TPU v7x, 512 devices: a whole 4x8x8 slice. The times are simulated.
512 devices in a mesh: row: 16 (over z, core), col: 32 (over x, y).
Axes of the slice: x: 4, y: 8, z: 8, core: 2. Of those that a mesh axis runs over, the one named last changes fastest.
Arguments:
- kernel: float32 [16384, 16384], P('row', 'col'), may hold values from 0 to 1.5, as said below
- targets: float32 [16384, 128], P('row'), may hold values from -6 to 6
Outputs:
- factored: float32 [16384, 16384], P('row', 'col')
- solved: float32 [16384, 128], P('row')
Inputs may be any that keep to these rules, and one draw needn't show every extreme that they name: kernel is symmetric and positive definite in matrix order.
All inputs are finite; a program needn't handle non-finite values.
Results may differ from a plain program's by a relative error of at most 0.00018.
Values sent between devices are 32-bit elements; how exact they have to be, the bound alone decides.
No kernel may reach another device: no remote copies, remote signals or barrier semaphores. Data moves between devices by JAX's collectives and lax.ppermute only.
A program may use at most 64 MiB of HBM per device.

v0:
```python
import jax
import jax.numpy as jnp
from jax import lax
from jax.experimental import pallas as pl
from jax.experimental.pallas import tpu as pltpu
from jax.sharding import PartitionSpec as P

BLOCK = 128
ORDER = 512
X, Y = 4, 8
ROWS, COLS = 16, 32
HI = lax.Precision.HIGHEST


def over_col(value, pairs):
    return lax.ppermute(value, "col", pairs)


def over_row(value, pairs):
    return lax.ppermute(value, "row", pairs)


def dot(a, b):
    return lax.dot_general(
        a, b, (((1,), (0,)), ((), ())), precision=HI, preferred_element_type=jnp.float32
    )


def dot_nt(a, b):
    return lax.dot_general(
        a, b, (((1,), (1,)), ((), ())), precision=HI, preferred_element_type=jnp.float32
    )


def spread(value):
    return jnp.broadcast_to(value, (8, BLOCK))


def total(terms):
    terms = list(terms)
    while len(terms) > 1:
        terms = [sum(terms[i + 1 : i + 2], terms[i]) for i in range(0, len(terms), 2)]
    return terms[0]


def factor_block(s_ref, e_ref):
    ids = lax.broadcasted_iota(jnp.int32, (BLOCK, BLOCK), 0)
    lanes = lax.broadcasted_iota(jnp.int32, (BLOCK, BLOCK), 1)
    e_ref[...] = jnp.where(ids == lanes, 1.0, 0.0)
    sub = lax.broadcasted_iota(jnp.int32, (8, BLOCK), 0)
    for p in range(16):
        at = 8 * p
        own = s_ref[at : at + 8, :]
        own_e = e_ref[at : at + 8, :]
        cols = [spread(own[:, at + i : at + i + 1]) for i in range(8)]
        t = {(s, i): spread(cols[i][s : s + 1, :]) for i in range(8) for s in range(i, 8)}
        rows = [spread(own[q : q + 1, :]) for q in range(8)]
        rows_e = [spread(own_e[q : q + 1, :]) for q in range(8)]
        low, inv, root = {}, {}, []
        for i in range(8):
            rs = lax.rsqrt(t[i, i])
            root.append(rs)
            for s in range(i + 1, 8):
                low[s, i] = t[s, i] * rs
            for s in range(i + 1, 8):
                for q in range(i + 1, s + 1):
                    t[s, q] = t[s, q] - low[s, i] * low[q, i]
        for i in range(8):
            inv[i, i] = root[i]
            for s in range(i + 1, 8):
                inv[s, i] = -root[s] * total(low[s, q] * inv[q, i] for q in range(i, s))
        done = [total(inv[i, q] * rows[q] for q in range(i + 1)) for i in range(8)]
        done_e = [total(inv[i, q] * rows_e[q] for q in range(i + 1)) for i in range(8)]
        tile, tile_e = done[0], done_e[0]
        for i in range(1, 8):
            tile = jnp.where(sub == i, done[i], tile)
            tile_e = jnp.where(sub == i, done_e[i], tile_e)
        s_ref[at : at + 8, :] = tile
        e_ref[at : at + 8, :] = tile_e
        if p == 15:
            break
        back = [total(inv[i, j] * done[i] for i in range(j, 8)) for j in range(8)]
        back_e = [total(inv[i, j] * done_e[i] for i in range(j, 8)) for j in range(8)]
        for u in range(p + 1, 16):
            part = s_ref[8 * u : 8 * u + 8, :]
            left = [spread(part[:, at + j : at + j + 1]) for j in range(8)]
            s_ref[8 * u : 8 * u + 8, :] = part - total(left[j] * back[j] for j in range(8))
            e_ref[8 * u : 8 * u + 8, :] -= total(left[j] * back_e[j] for j in range(8))


def factor_kernel(at_ref, a_ref, f_ref, g_ref, work, s_ref, e_ref):
    k = pl.program_id(0)
    n = BLOCK

    @pl.when(k == 0)
    def _():
        for i in range(4):
            for j in range(i + 1):
                work[i * n : (i + 1) * n, j * n : (j + 1) * n] = a_ref[
                    at_ref[0] ^ i, at_ref[1] ^ j
                ]
        f_ref[...] = jnp.zeros_like(f_ref)
        g_ref[...] = jnp.zeros_like(g_ref)

    for step in range(4):
        @pl.when(k == step)
        def _(step=step):
            here = slice(step * n, (step + 1) * n)
            s_ref[...] = work[here, here]

    factor_block(s_ref, e_ref)

    for step in range(4):
        @pl.when(k == step)
        def _(step=step):
            here = slice(step * n, (step + 1) * n)
            ids = lax.broadcasted_iota(jnp.int32, (n, n), 0)
            lanes = lax.broadcasted_iota(jnp.int32, (n, n), 1)
            f_ref[here, here] = jnp.where(ids <= lanes, s_ref[...], 0.0).T
            inv = e_ref[...]
            g_ref[here, here] = inv
            if step < 3:
                f_ref[(step + 1) * n :, here] = dot_nt(work[(step + 1) * n :, here], inv)
            for j in range(step + 1, 4):
                there = slice(j * n, (j + 1) * n)
                work[j * n :, there] -= dot_nt(f_ref[j * n :, here], f_ref[there, here])
            if step:
                before = slice(0, step * n)
                g_ref[here, before] = -dot(inv, dot(f_ref[here, before], g_ref[before, before]))


def factor(at, blocks):
    return pl.pallas_call(
        factor_kernel,
        grid=(4,),
        out_shape=[jax.ShapeDtypeStruct((ORDER, ORDER), jnp.float32)] * 2,
        in_specs=[
            pl.BlockSpec(memory_space=pltpu.SMEM),
            pl.BlockSpec((4, 4, BLOCK, BLOCK), lambda k: (0, 0, 0, 0)),
        ],
        out_specs=[pl.BlockSpec((ORDER, ORDER), lambda k: (0, 0))] * 2,
        scratch_shapes=[
            pltpu.VMEM((ORDER, ORDER), jnp.float32),
            pltpu.VMEM((BLOCK, BLOCK), jnp.float32),
            pltpu.VMEM((BLOCK, BLOCK), jnp.float32),
        ],
        compiler_params=pltpu.CompilerParams(vmem_limit_bytes=24 * 2**20),
        cost_estimate=pl.CostEstimate(flops=2 * 10**10, bytes_accessed=3 * 2**20, transcendentals=0),
    )(at, blocks)


def update_kernel(at_ref, pan_ref, top_ref, f_ref, g_ref, k_ref, y_ref, out_ref, right_ref,
                  wc, tmp, pan, w):
    step = pl.program_id(0)
    row, col = at_ref[2], at_ref[3]
    n = BLOCK

    @pl.when(step == 0)
    def _():
        for i in range(4):
            tmp[i * n : (i + 1) * n, :] = top_ref[at_ref[0] ^ i]
        for i in range(4):
            here = slice(i * n, (i + 1) * n)
            wc[here, :] = dot(g_ref[here, : (i + 1) * n], tmp[: (i + 1) * n, :])

    for j in range(4):
        for b in range(2):
            pan[b * n : (b + 1) * n, j * n : (j + 1) * n] = pan_ref[0, b, j]
    for i in range(4):
        here = slice(i * n, (i + 1) * n)
        w[:, here] = dot_nt(pan[:, : (i + 1) * n], g_ref[here, : (i + 1) * n])

    first = (step == 0) & (row < 4)

    @pl.when(first)
    def _():
        w[:n, :] = f_ref[pl.ds(pl.multiple_of(row * n, n), n), :]

    out_ref[...] = k_ref[...] - dot(w[...], wc[:, :ORDER])
    right_ref[...] = y_ref[...] - dot(w[...], wc[:, ORDER:])

    @pl.when(first)
    def _():
        out_ref[:n, :] = jnp.zeros((n, ORDER), jnp.float32)
        right_ref[:n, :] = wc[pl.ds(pl.multiple_of(row * n, n), n), ORDER:]

    @pl.when(col < 4)
    def _():
        out_ref[:, :n] = w[:, pl.ds(pl.multiple_of(col * n, n), n)]


def update(at, pan, top, fac, inv, kernel, targets):
    rows = 256
    whole = lambda *shape: pl.BlockSpec(shape, lambda s: (0,) * len(shape))
    return pl.pallas_call(
        update_kernel,
        grid=(kernel.shape[0] // rows,),
        out_shape=[
            jax.ShapeDtypeStruct(kernel.shape, jnp.float32),
            jax.ShapeDtypeStruct(targets.shape, jnp.float32),
        ],
        in_specs=[
            pl.BlockSpec(memory_space=pltpu.SMEM),
            pl.BlockSpec((1, 2, 4, BLOCK, BLOCK), lambda s: (s, 0, 0, 0, 0)),
            whole(4, BLOCK, ORDER + BLOCK),
            whole(ORDER, ORDER),
            whole(ORDER, ORDER),
            pl.BlockSpec((rows, ORDER), lambda s: (s, 0)),
            pl.BlockSpec((rows, BLOCK), lambda s: (s, 0)),
        ],
        out_specs=[
            pl.BlockSpec((rows, ORDER), lambda s: (s, 0)),
            pl.BlockSpec((rows, BLOCK), lambda s: (s, 0)),
        ],
        scratch_shapes=[
            pltpu.VMEM((ORDER, ORDER + BLOCK), jnp.float32),
            pltpu.VMEM((ORDER, ORDER + BLOCK), jnp.float32),
            pltpu.VMEM((rows, ORDER), jnp.float32),
            pltpu.VMEM((rows, ORDER), jnp.float32),
        ],
        compiler_params=pltpu.CompilerParams(vmem_limit_bytes=40 * 2**20),
        cost_estimate=pl.CostEstimate(flops=10**10, bytes_accessed=9 * 2**20, transcendentals=0),
    )(at, pan, top, fac, inv, kernel, targets)


def per_device(kernel, targets):
    row_pos = lax.axis_index("row")
    col_pos = lax.axis_index("col")
    x_pos = col_pos // Y
    y_pos = col_pos % Y
    block = BLOCK
    at = jnp.stack([row_pos % 4, col_pos % 4, row_pos, col_pos]).astype(jnp.int32)

    a0 = jnp.where((col_pos < 4) & (row_pos < 4), kernel[:block, :block], 0.0)
    got = [a0]
    for x in range(X):
        for half in (0, 4):
            if x or half:
                pairs = [
                    (r * COLS + j, r * COLS + x * Y + half + j)
                    for r in range(4)
                    for j in range(4)
                ]
                got.append(lax.ppermute(a0, ("row", "col"), pairs))
    a1 = total(got)
    got = [a1]
    for shift in (4, 8, 12):
        got.append(over_row(a1, [(r, r + shift) for r in range(4)]))
    a2 = total(got)
    got = [a2]
    for t in (1, 2, 3):
        got.append(over_col(a2, [(c, c ^ t) for c in range(COLS)]))
    a3 = jnp.stack(got)
    a4 = jnp.stack([a3, over_row(a3, [(r, r ^ 2) for r in range(ROWS)])])
    a5 = jnp.stack([a4, over_row(a4, [(r, r ^ 1) for r in range(ROWS)])], axis=1)
    fac, inv = factor(at, a5.reshape(4, 4, block, block))

    panel = kernel[:, :block].reshape(8, block, block)
    got = [jnp.where(x_pos == 0, panel[:2], 0.0)]
    for x in (1, 2, 3):
        got.append(over_col(panel[2 * x : 2 * x + 2], [(j, x * Y + j) for j in range(4)]))
    pair = total(got)
    upper = over_col(pair[1], [(x * Y + j, x * Y + j + 4) for x in range(X) for j in range(4)])
    shard = jnp.where(y_pos >= 4, upper, pair[0])
    pan = lax.all_gather(shard, "col").reshape(4, 2, 4, block, block)

    strip = jnp.concatenate([kernel[:block], targets[:block]], axis=1)
    got = [jnp.where(row_pos < 4, strip, 0.0)]
    for shift in (4, 8, 12):
        got.append(over_row(strip, [(r, r + shift) for r in range(4)]))
    s1 = total(got)
    s2 = jnp.stack([s1, over_row(s1, [(r, r ^ 2) for r in range(ROWS)])])
    s3 = jnp.stack([s2, over_row(s2, [(r, r ^ 1) for r in range(ROWS)])], axis=1)
    top = s3.reshape(4, block, ORDER + block)

    return tuple(update(at, pan, top, fac, inv, kernel, targets))


def solution(mesh):
    in_specs = (P("row", "col"), P("row", None))
    out_specs = (P("row", "col"), P("row", None))
    return jax.shard_map(
        per_device, mesh=mesh, in_specs=in_specs, out_specs=out_specs, check_vma=False
    )
```

profile of v0, /device:TPU:1, one launch (start us, length us, event | category | flops | bytes accessed | tf_op | source)
XLA Modules:
  0.0 157.5 jit_solution(4150391225597627607)
XLA Ops:
  7.2 1.3 fusion.4
  8.5 5.2 %collective-permute-start.2 = (f32[2,128,128]{2,1,0:T(8,128)S(1)}, f32[2,128,128]{2,1,0:T(8,128)S(1)}, u32[]{:S(2)}, u32[]{:S(2)}) collective-permute-start(f32[2,128,128]{2,1,0:T(8,128)S(1)} %bitcast.43), channel_id=1, source_target_pairs={{0,24},{1,25},{2,26},{3,27},{32,56},{33,57},{34,58},{35,59},{64,88... | collective-permute-start | bytes 393224 | tf_op jit(solution)/shard_map/ppermute | solution.py:16
  13.7 1.3 collective-permute-start
  15.1 1.3 collective-permute-start.1
  16.4 0.8 slice_select_fusion.1
  17.2 1.3 collective-permute-start.14
  18.5 4.3 %collective-permute-start.13 = (f32[128,128]{1,0:T(8,128)S(1)}, f32[128,128]{1,0:T(8,128)S(1)}, u32[]{:S(2)}, u32[]{:S(2)}) collective-permute-start(f32[128,128]{1,0:T(8,128)S(1)} %slice_select_fusion.1), channel_id=1, source_target_pairs={{0,20},{1,21},{2,22},{3,23},{32,52},{33,53},{34,54},{35,55},{64,84... | collective-permute-start | bytes 196616 | tf_op jit(solution)/shard_map/ppermute | solution.py:244
  22.9 1.3 collective-permute-start.3
  24.2 2.2 %collective-permute-start.12 = (f32[128,128]{1,0:T(8,128)S(1)}, f32[128,128]{1,0:T(8,128)S(1)}, u32[]{:S(2)}, u32[]{:S(2)}) collective-permute-start(f32[128,128]{1,0:T(8,128)S(1)} %slice_select_fusion.1), channel_id=1, source_target_pairs={{0,16},{1,17},{2,18},{3,19},{32,48},{33,49},{34,50},{35,51},{64,80... | collective-permute-start | bytes 196616 | tf_op jit(solution)/shard_map/ppermute | solution.py:244
  26.4 1.3 collective-permute-start.11
  27.7 1.3 collective-permute-start.10
  29.0 1.3 collective-permute-start.15
  30.4 3.2 %collective-permute-start.9 = (f32[128,128]{1,0:T(8,128)S(1)}, f32[128,128]{1,0:T(8,128)S(1)}, u32[]{:S(2)}, u32[]{:S(2)}) collective-permute-start(f32[128,128]{1,0:T(8,128)S(1)} %slice_select_fusion.1), channel_id=1, source_target_pairs={{0,4},{1,5},{2,6},{3,7},{32,36},{33,37},{34,38},{35,39},{64,68},{6... | collective-permute-start | bytes 196616 | tf_op jit(solution)/shard_map/ppermute | solution.py:244
  33.6 0.6 fusion
  34.3 0.9 collective-permute-done.9
  35.2 1.3 collective-permute-start.18
  36.5 1.3 collective-permute-start.17
  37.8 1.3 collective-permute-start.16
  39.1 1.3 collective-permute-done.16
  40.4 5.0 %collective-permute-start.21 = (f32[128,128]{1,0:T(8,128)S(1)}, f32[128,128]{1,0:T(8,128)S(1)}, u32[]{:S(2)}, u32[]{:S(2)}) collective-permute-start(f32[128,128]{1,0:T(8,128)S(1)} %add_add_fusion.2), channel_id=1, source_target_pairs={{0,3},{1,2},{2,1},{3,0},{4,7},{5,6},{6,5},{7,4},{8,11},{9,10},{10,... | collective-permute-start | bytes 196616 | tf_op jit(solution)/shard_map/ppermute | solution.py:16
  45.4 4.6 %collective-permute-start.20 = (f32[128,128]{1,0:T(8,128)S(1)}, f32[128,128]{1,0:T(8,128)S(1)}, u32[]{:S(2)}, u32[]{:S(2)}) collective-permute-start(f32[128,128]{1,0:T(8,128)S(1)} %add_add_fusion.2), channel_id=1, source_target_pairs={{0,2},{1,3},{2,0},{3,1},{4,6},{5,7},{6,4},{7,5},{8,10},{9,11},{10,... | collective-permute-start | bytes 196616 | tf_op jit(solution)/shard_map/ppermute | solution.py:16
  49.9 1.9 %collective-permute-start.19 = (f32[128,128]{1,0:T(8,128)S(1)}, f32[128,128]{1,0:T(8,128)S(1)}, u32[]{:S(2)}, u32[]{:S(2)}) collective-permute-start(f32[128,128]{1,0:T(8,128)S(1)} %add_add_fusion.2), channel_id=1, source_target_pairs={{0,1},{1,0},{2,3},{3,2},{4,5},{5,4},{6,7},{7,6},{8,9},{9,8},{10,11... | collective-permute-start | bytes 196616 | tf_op jit(solution)/shard_map/ppermute | solution.py:16
  51.9 0.8 slice.52
  52.8 2.6 %collective-permute-done.19 = f32[128,128]{1,0:T(8,128)S(1)} collective-permute-done((f32[128,128]{1,0:T(8,128)S(1)}, f32[128,128]{1,0:T(8,128)S(1)}, u32[]{:S(2)}, u32[]{:S(2)}) %collective-permute-start.19) | collective-permute-done | bytes 65568 | tf_op jit(solution)/shard_map/ppermute | solution.py:16
  55.4 5.4 %collective-permute-start.22 = (f32[4,128,128]{2,1,0:T(8,128)S(1)}, f32[4,128,128]{2,1,0:T(8,128)S(1)}, u32[]{:S(2)}, u32[]{:S(2)}) collective-permute-start(f32[4,128,128]{2,1,0:T(8,128)S(1)} %get-tuple-element.15), channel_id=1, source_target_pairs={{0,64},{32,96},{64,0},{96,32},{128,192},{160,224},{192,128},{224,1... | collective-permute-start | bytes 786440 | tf_op jit(solution)/shard_map/ppermute | solution.py:20
  60.8 5.6 %collective-permute-start.5 = (f32[128,640]{1,0:T(8,128)S(1)}, f32[128,640]{1,0:T(8,128)S(1)}, u32[]{:S(2)}, u32[]{:S(2)}) collective-permute-start(f32[128,640]{1,0:T(8,128)S(1)} %pad_maximum_fusion.4), channel_id=1, source_target_pairs={{0,256},{32,288},{64,320},{96,352},{1,257},{33,289},{65,321},{97,3... | collective-permute-start | bytes 983048 | tf_op jit(solution)/shard_map/ppermute | solution.py:20
  66.3 1.3 collective-permute-start.4
  67.7 1.3 collective-permute-start.6
  69.0 0.9 fusion.1
  69.9 4.8 %collective-permute-start.23 = (f32[2,4,128,128]{3,2,1,0:T(8,128)}, f32[2,4,128,128]{3,2,1,0:T(8,128)}, u32[]{:S(2)}, u32[]{:S(2)}) collective-permute-start(f32[2,4,128,128]{3,2,1,0:T(8,128)} %get-tuple-element.13), channel_id=1, source_target_pairs={{0,32},{32,0},{64,96},{96,64},{128,160},{160,128},{192,224},{224,1... | collective-permute-start | bytes 1572872 | tf_op jit(solution)/shard_map/ppermute | solution.py:20
  74.7 3.2 %collective-permute-done.4 = f32[128,640]{1,0:T(8,128)S(1)} collective-permute-done((f32[128,640]{1,0:T(8,128)S(1)}, f32[128,640]{1,0:T(8,128)S(1)}, u32[]{:S(2)}, u32[]{:S(2)}) %collective-permute-start.4) | collective-permute-done | bytes 327712 | tf_op jit(solution)/shard_map/ppermute | solution.py:20
  78.0 9.6 %collective-permute-done.6 = f32[128,640]{1,0:T(8,128)S(1)} collective-permute-done((f32[128,640]{1,0:T(8,128)S(1)}, f32[128,640]{1,0:T(8,128)S(1)}, u32[]{:S(2)}, u32[]{:S(2)}) %collective-permute-start.6) | collective-permute-done | bytes 327712 | tf_op jit(solution)/shard_map/ppermute | solution.py:20
  87.6 3.4 %collective-permute-start.7 = (f32[128,640]{1,0:T(8,128)S(1)}, f32[128,640]{1,0:T(8,128)S(1)}, u32[]{:S(2)}, u32[]{:S(2)}) collective-permute-start(f32[128,640]{1,0:T(8,128)S(1)} %add_add_fusion), channel_id=1, source_target_pairs={{0,64},{32,96},{64,0},{96,32},{128,192},{160,224},{192,128},{224,1... | collective-permute-start | bytes 983048 | tf_op jit(solution)/shard_map/ppermute | solution.py:20
  91.1 7.3 %collective-permute-done.7 = f32[128,640]{1,0:T(8,128)S(1)} collective-permute-done((f32[128,640]{1,0:T(8,128)S(1)}, f32[128,640]{1,0:T(8,128)S(1)}, u32[]{:S(2)}, u32[]{:S(2)}) %collective-permute-start.7) | collective-permute-done | bytes 327712 | tf_op jit(solution)/shard_map/ppermute | solution.py:20
  98.4 0.1 fusion.3
  98.5 3.4 %collective-permute-start.8 = (f32[2,128,640]{2,1,0:T(8,128)S(1)}, f32[2,128,640]{2,1,0:T(8,128)S(1)}, u32[]{:S(2)}, u32[]{:S(2)}) collective-permute-start(f32[2,128,640]{2,1,0:T(8,128)S(1)} %get-tuple-element.11), channel_id=1, source_target_pairs={{0,32},{32,0},{64,96},{96,64},{128,160},{160,128},{192,224},{224,1... | collective-permute-start | bytes 1966088 | tf_op jit(solution)/shard_map/ppermute | solution.py:20
  101.9 1.1 pad_maximum_fusion.1
  103.0 0.1 copy.5
  103.1 23.1 %shard_map.41 = (f32[512,512]{1,0:T(8,128)S(1)}, f32[512,512]{1,0:T(8,128)S(1)}) custom-call(s32[4]{0:T(128)S(1)} %pad_add_fusion.at_ref, f32[4,4,128,128]{3,2,1,0:T(8,128)S(1)} %bitcast.33), custom_call_target="tpu_custom_call" | custom-call | flops 20000000000 | bytes 3145728 | tf_op jit(solution)/shard_map/pallas_call | solution.py:133
  126.3 1.0 copy-done.3
  127.2 1.0 copy-done.5
  128.2 0.1 pad_maximum_fusion
  128.3 0.1 copy.4
  128.5 1.0 copy-done.1
  129.5 1.6 %copy-done.2 = f32[4096,128]{1,0:T(8,128)S(1)} copy-done((f32[4096,128]{1,0:T(8,128)S(1)}, f32[4096,128]{1,0:T(8,128)}, u32[]{:S(2)}) %copy-start.2) | copy-done | bytes 2097176
  131.1 1.2 copy-done.4
  132.3 1.2 copy-done.6
  133.5 17.2 %shard_map.42 = (f32[1024,512]{1,0:T(8,128)}, f32[1024,128]{1,0:T(8,128)}) custom-call(s32[4]{0:T(128)S(1)} %pad_add_fusion.at_ref, f32[4,2,4,128,128]{4,3,2,1,0:T(8,128)S(1)} %bitcast.34, f32[4,128,640]{2,1,0:T(8,128)S(1)} %bitcast.32, f32[512,512]{1,0:T(8,128)S(1)} %copy-done.4, f32[512,512]{1,0:T(8,128)S(1)} %copy-done.6, f32[1024,512]{1,0:T(8,128)S(1)} %copy-done, ...), custom_call_target="tpu_custom_call" | custom-call | flops 10000000000 | bytes 9437184 | tf_op jit(solution)/shard_map/pallas_call | solution.py:195
  (38 shorter events, 0.4 us)
Async XLA Ops:
  7.2 28.0 %copy-start = (f32[1024,512]{1,0:T(8,128)S(1)}, f32[1024,512]{1,0:T(8,128)}, u32[]{:S(2)}) copy-start(f32[1024,512]{1,0:T(8,128)} %k_ref.1) | copy-start | bytes 6291460
  7.2 121.3 %all-gather.3.cloned.1.call-start = ((), (), s32[]{:S(2)}) async-start(), calls=%async_computation | async-start | bytes 2162688 | tf_op jit(solution)/shard_map/all_gather | solution.py:265
  8.5 14.3 %collective-permute-start.2 = (f32[2,128,128]{2,1,0:T(8,128)S(1)}, f32[2,128,128]{2,1,0:T(8,128)S(1)}, u32[]{:S(2)}, u32[]{:S(2)}) collective-permute-start(f32[2,128,128]{2,1,0:T(8,128)S(1)} %bitcast.43), channel_id=1, source_target_pairs={{0,24},{1,25},{2,26},{3,27},{32,56},{33,57},{34,58},{35,59},{64,88... | collective-permute-start | bytes 393224 | tf_op jit(solution)/shard_map/ppermute | solution.py:16
  13.7 9.1 %collective-permute-start = (f32[2,128,128]{2,1,0:T(8,128)S(1)}, f32[2,128,128]{2,1,0:T(8,128)S(1)}, u32[]{:S(2)}, u32[]{:S(2)}) collective-permute-start(f32[2,128,128]{2,1,0:T(8,128)S(1)} %bitcast.42), channel_id=1, source_target_pairs={{0,8},{1,9},{2,10},{3,11},{32,40},{33,41},{34,42},{35,43},{64,72},... | collective-permute-start | bytes 393224 | tf_op jit(solution)/shard_map/ppermute | solution.py:16
  15.1 7.8 %collective-permute-start.1 = (f32[2,128,128]{2,1,0:T(8,128)S(1)}, f32[2,128,128]{2,1,0:T(8,128)S(1)}, u32[]{:S(2)}, u32[]{:S(2)}) collective-permute-start(f32[2,128,128]{2,1,0:T(8,128)S(1)} %bitcast.41), channel_id=1, source_target_pairs={{0,16},{1,17},{2,18},{3,19},{32,48},{33,49},{34,50},{35,51},{64,80... | collective-permute-start | bytes 393224 | tf_op jit(solution)/shard_map/ppermute | solution.py:16
  17.2 10.5 %collective-permute-start.14 = (f32[128,128]{1,0:T(8,128)S(1)}, f32[128,128]{1,0:T(8,128)S(1)}, u32[]{:S(2)}, u32[]{:S(2)}) collective-permute-start(f32[128,128]{1,0:T(8,128)S(1)} %slice_select_fusion.1), channel_id=1, source_target_pairs={{0,24},{1,25},{2,26},{3,27},{32,56},{33,57},{34,58},{35,59},{64,88... | collective-permute-start | bytes 196616 | tf_op jit(solution)/shard_map/ppermute | solution.py:244
  18.5 10.5 %collective-permute-start.13 = (f32[128,128]{1,0:T(8,128)S(1)}, f32[128,128]{1,0:T(8,128)S(1)}, u32[]{:S(2)}, u32[]{:S(2)}) collective-permute-start(f32[128,128]{1,0:T(8,128)S(1)} %slice_select_fusion.1), channel_id=1, source_target_pairs={{0,20},{1,21},{2,22},{3,23},{32,52},{33,53},{34,54},{35,55},{64,84... | collective-permute-start | bytes 196616 | tf_op jit(solution)/shard_map/ppermute | solution.py:244
  22.9 7.4 %collective-permute-start.3 = (f32[128,128]{1,0:T(8,128)S(1)}, f32[128,128]{1,0:T(8,128)S(1)}, u32[]{:S(2)}, u32[]{:S(2)}) collective-permute-start(f32[128,128]{1,0:T(8,128)S(1)} %slice_bitcast_fusion.1), channel_id=1, source_target_pairs={{0,4},{1,5},{2,6},{3,7},{8,12},{9,13},{10,14},{11,15},{16,20},{17,... | collective-permute-start | bytes 196616 | tf_op jit(solution)/shard_map/ppermute | solution.py:16
  24.2 10.0 %collective-permute-start.12 = (f32[128,128]{1,0:T(8,128)S(1)}, f32[128,128]{1,0:T(8,128)S(1)}, u32[]{:S(2)}, u32[]{:S(2)}) collective-permute-start(f32[128,128]{1,0:T(8,128)S(1)} %slice_select_fusion.1), channel_id=1, source_target_pairs={{0,16},{1,17},{2,18},{3,19},{32,48},{33,49},{34,50},{35,51},{64,80... | collective-permute-start | bytes 196616 | tf_op jit(solution)/shard_map/ppermute | solution.py:244
  26.4 7.8 %collective-permute-start.11 = (f32[128,128]{1,0:T(8,128)S(1)}, f32[128,128]{1,0:T(8,128)S(1)}, u32[]{:S(2)}, u32[]{:S(2)}) collective-permute-start(f32[128,128]{1,0:T(8,128)S(1)} %slice_select_fusion.1), channel_id=1, source_target_pairs={{0,12},{1,13},{2,14},{3,15},{32,44},{33,45},{34,46},{35,47},{64,76... | collective-permute-start | bytes 196616 | tf_op jit(solution)/shard_map/ppermute | solution.py:244
  27.7 6.5 %collective-permute-start.10 = (f32[128,128]{1,0:T(8,128)S(1)}, f32[128,128]{1,0:T(8,128)S(1)}, u32[]{:S(2)}, u32[]{:S(2)}) collective-permute-start(f32[128,128]{1,0:T(8,128)S(1)} %slice_select_fusion.1), channel_id=1, source_target_pairs={{0,8},{1,9},{2,10},{3,11},{32,40},{33,41},{34,42},{35,43},{64,72},... | collective-permute-start | bytes 196616 | tf_op jit(solution)/shard_map/ppermute | solution.py:244
  29.0 5.2 %collective-permute-start.15 = (f32[128,128]{1,0:T(8,128)S(1)}, f32[128,128]{1,0:T(8,128)S(1)}, u32[]{:S(2)}, u32[]{:S(2)}) collective-permute-start(f32[128,128]{1,0:T(8,128)S(1)} %slice_select_fusion.1), channel_id=1, source_target_pairs={{0,28},{1,29},{2,30},{3,31},{32,60},{33,61},{34,62},{35,63},{64,92... | collective-permute-start | bytes 196616 | tf_op jit(solution)/shard_map/ppermute | solution.py:244
  30.4 4.8 %collective-permute-start.9 = (f32[128,128]{1,0:T(8,128)S(1)}, f32[128,128]{1,0:T(8,128)S(1)}, u32[]{:S(2)}, u32[]{:S(2)}) collective-permute-start(f32[128,128]{1,0:T(8,128)S(1)} %slice_select_fusion.1), channel_id=1, source_target_pairs={{0,4},{1,5},{2,6},{3,7},{32,36},{33,37},{34,38},{35,39},{64,68},{6... | collective-permute-start | bytes 196616 | tf_op jit(solution)/shard_map/ppermute | solution.py:244
  35.2 3.9 %collective-permute-start.18 = (f32[128,128]{1,0:T(8,128)S(1)}, f32[128,128]{1,0:T(8,128)S(1)}, u32[]{:S(2)}, u32[]{:S(2)}) collective-permute-start(f32[128,128]{1,0:T(8,128)S(1)} %add_add_fusion.3), channel_id=1, source_target_pairs={{0,384},{32,416},{64,448},{96,480},{1,385},{33,417},{65,449},{97,4... | collective-permute-start | bytes 196616 | tf_op jit(solution)/shard_map/ppermute | solution.py:20
  36.5 2.6 %collective-permute-start.17 = (f32[128,128]{1,0:T(8,128)S(1)}, f32[128,128]{1,0:T(8,128)S(1)}, u32[]{:S(2)}, u32[]{:S(2)}) collective-permute-start(f32[128,128]{1,0:T(8,128)S(1)} %add_add_fusion.3), channel_id=1, source_target_pairs={{0,256},{32,288},{64,320},{96,352},{1,257},{33,289},{65,321},{97,3... | collective-permute-start | bytes 196616 | tf_op jit(solution)/shard_map/ppermute | solution.py:20
  37.8 2.6 %collective-permute-start.16 = (f32[128,128]{1,0:T(8,128)S(1)}, f32[128,128]{1,0:T(8,128)S(1)}, u32[]{:S(2)}, u32[]{:S(2)}) collective-permute-start(f32[128,128]{1,0:T(8,128)S(1)} %add_add_fusion.3), channel_id=1, source_target_pairs={{0,128},{32,160},{64,192},{96,224},{1,129},{33,161},{65,193},{97,2... | collective-permute-start | bytes 196616 | tf_op jit(solution)/shard_map/ppermute | solution.py:20
  40.4 12.3 %collective-permute-start.21 = (f32[128,128]{1,0:T(8,128)S(1)}, f32[128,128]{1,0:T(8,128)S(1)}, u32[]{:S(2)}, u32[]{:S(2)}) collective-permute-start(f32[128,128]{1,0:T(8,128)S(1)} %add_add_fusion.2), channel_id=1, source_target_pairs={{0,3},{1,2},{2,1},{3,0},{4,7},{5,6},{6,5},{7,4},{8,11},{9,10},{10,... | collective-permute-start | bytes 196616 | tf_op jit(solution)/shard_map/ppermute | solution.py:16
  45.4 7.4 %collective-permute-start.20 = (f32[128,128]{1,0:T(8,128)S(1)}, f32[128,128]{1,0:T(8,128)S(1)}, u32[]{:S(2)}, u32[]{:S(2)}) collective-permute-start(f32[128,128]{1,0:T(8,128)S(1)} %add_add_fusion.2), channel_id=1, source_target_pairs={{0,2},{1,3},{2,0},{3,1},{4,6},{5,7},{6,4},{7,5},{8,10},{9,11},{10,... | collective-permute-start | bytes 196616 | tf_op jit(solution)/shard_map/ppermute | solution.py:16
  49.9 5.4 %collective-permute-start.19 = (f32[128,128]{1,0:T(8,128)S(1)}, f32[128,128]{1,0:T(8,128)S(1)}, u32[]{:S(2)}, u32[]{:S(2)}) collective-permute-start(f32[128,128]{1,0:T(8,128)S(1)} %add_add_fusion.2), channel_id=1, source_target_pairs={{0,1},{1,0},{2,3},{3,2},{4,5},{5,4},{6,7},{7,6},{8,9},{9,8},{10,11... | collective-permute-start | bytes 196616 | tf_op jit(solution)/shard_map/ppermute | solution.py:16
  55.4 13.6 %collective-permute-start.22 = (f32[4,128,128]{2,1,0:T(8,128)S(1)}, f32[4,128,128]{2,1,0:T(8,128)S(1)}, u32[]{:S(2)}, u32[]{:S(2)}) collective-permute-start(f32[4,128,128]{2,1,0:T(8,128)S(1)} %get-tuple-element.15), channel_id=1, source_target_pairs={{0,64},{32,96},{64,0},{96,32},{128,192},{160,224},{192,128},{224,1... | collective-permute-start | bytes 786440 | tf_op jit(solution)/shard_map/ppermute | solution.py:20
  60.8 13.9 %collective-permute-start.5 = (f32[128,640]{1,0:T(8,128)S(1)}, f32[128,640]{1,0:T(8,128)S(1)}, u32[]{:S(2)}, u32[]{:S(2)}) collective-permute-start(f32[128,640]{1,0:T(8,128)S(1)} %pad_maximum_fusion.4), channel_id=1, source_target_pairs={{0,256},{32,288},{64,320},{96,352},{1,257},{33,289},{65,321},{97,3... | collective-permute-start | bytes 983048 | tf_op jit(solution)/shard_map/ppermute | solution.py:20
  66.3 11.6 %collective-permute-start.4 = (f32[128,640]{1,0:T(8,128)S(1)}, f32[128,640]{1,0:T(8,128)S(1)}, u32[]{:S(2)}, u32[]{:S(2)}) collective-permute-start(f32[128,640]{1,0:T(8,128)S(1)} %pad_maximum_fusion.4), channel_id=1, source_target_pairs={{0,128},{32,160},{64,192},{96,224},{1,129},{33,161},{65,193},{97,2... | collective-permute-start | bytes 983048 | tf_op jit(solution)/shard_map/ppermute | solution.py:20
  67.7 19.9 %collective-permute-start.6 = (f32[128,640]{1,0:T(8,128)S(1)}, f32[128,640]{1,0:T(8,128)S(1)}, u32[]{:S(2)}, u32[]{:S(2)}) collective-permute-start(f32[128,640]{1,0:T(8,128)S(1)} %pad_maximum_fusion.4), channel_id=1, source_target_pairs={{0,384},{32,416},{64,448},{96,480},{1,385},{33,417},{65,449},{97,4... | collective-permute-start | bytes 983048 | tf_op jit(solution)/shard_map/ppermute | solution.py:20
  69.9 32.0 %collective-permute-start.23 = (f32[2,4,128,128]{3,2,1,0:T(8,128)}, f32[2,4,128,128]{3,2,1,0:T(8,128)}, u32[]{:S(2)}, u32[]{:S(2)}) collective-permute-start(f32[2,4,128,128]{3,2,1,0:T(8,128)} %get-tuple-element.13), channel_id=1, source_target_pairs={{0,32},{32,0},{64,96},{96,64},{128,160},{160,128},{192,224},{224,1... | collective-permute-start | bytes 1572872 | tf_op jit(solution)/shard_map/ppermute | solution.py:20
  87.6 10.8 %collective-permute-start.7 = (f32[128,640]{1,0:T(8,128)S(1)}, f32[128,640]{1,0:T(8,128)S(1)}, u32[]{:S(2)}, u32[]{:S(2)}) collective-permute-start(f32[128,640]{1,0:T(8,128)S(1)} %add_add_fusion), channel_id=1, source_target_pairs={{0,64},{32,96},{64,0},{96,32},{128,192},{160,224},{192,128},{224,1... | collective-permute-start | bytes 983048 | tf_op jit(solution)/shard_map/ppermute | solution.py:20
  98.5 29.7 %collective-permute-start.8 = (f32[2,128,640]{2,1,0:T(8,128)S(1)}, f32[2,128,640]{2,1,0:T(8,128)S(1)}, u32[]{:S(2)}, u32[]{:S(2)}) collective-permute-start(f32[2,128,640]{2,1,0:T(8,128)S(1)} %get-tuple-element.11), channel_id=1, source_target_pairs={{0,32},{32,0},{64,96},{96,64},{128,160},{160,128},{192,224},{224,1... | collective-permute-start | bytes 1966088 | tf_op jit(solution)/shard_map/ppermute | solution.py:20
  126.2 1.0 copy-start.3
  127.2 1.0 copy-start.5
  128.4 1.0 copy-start.1
  129.5 1.6 %copy-start.2 = (f32[4096,128]{1,0:T(8,128)S(1)}, f32[4096,128]{1,0:T(8,128)}, u32[]{:S(2)}) copy-start(f32[4096,128]{1,0:T(8,128)} %all-gather.3.cloned.1.call-done) | copy-start | bytes 6291460
  131.1 1.2 copy-start.4
  132.3 1.2 copy-start.6
Sparse Core Ops, SparseCore 0:
  34.4 77.5 all-gather.2
where the time goes:
time: 159 us; the launch traced here: 158 us
  starting transfers between devices  64.5 us (41%)
  Pallas kernels  40.3 us (25%)
  waiting for transfers between devices  24.9 us (16%)
  between operations  14.5 us (9%)
  local copies, waits for them, and re-layouts  8.08 us (5%)
  other arithmetic  5.24 us (3%)
    ppermute x10, starting transfers between devices, over_row(): return lax.ppermute(value, 'row', pairs)  29 us
    pallas_call x1, Pallas kernels, factor(): pl.pallas_call(factor_kernel, grid=(4,), out_shape=[jax.ShapeDtypeStruct(...  23.1 us
    ppermute x10, waiting for transfers between devices, over_row(): return lax.ppermute(value, 'row', pairs)  21.4 us
    ppermute x7, starting transfers between devices, over_col(): return lax.ppermute(value, 'col', pairs)  20.6 us
    pallas_call x1, Pallas kernels, update(): pl.pallas_call(update_kernel, grid=(kernel.shape[0] // rows,), out_shape=...  17.2 us
    ppermute x7, starting transfers between devices, per_device(): got.append(lax.ppermute(a0, ('row', 'col'), pairs))  14.9 us
    unnamed x14, local copies, waits for them, and re-layouts  7.03 us
  transfers between devices with their start and end apart: 25, of which 6 were waited for; matrix products, arithmetic and copies ran while one was open for 3% of the time, Pallas kernels for 15%

commit v1 on v0

v1 whole, which is shorter than its diff:
```python
import functools

import jax
import jax.numpy as jnp
from jax import lax
from jax.experimental import pallas as pl
from jax.experimental.pallas import tpu as pltpu
from jax.sharding import PartitionSpec as P

BLOCK = 128
ORDER = 512
X, Y = 4, 8
ROWS, COLS = 16, 32
HI = lax.Precision.HIGHEST


def over_col(value, pairs):
    return lax.ppermute(value, "col", pairs)


def over_row(value, pairs):
    return lax.ppermute(value, "row", pairs)


def dot(a, b):
    return lax.dot_general(
        a, b, (((1,), (0,)), ((), ())), precision=HI, preferred_element_type=jnp.float32
    )


def dot_nt(a, b):
    return lax.dot_general(
        a, b, (((1,), (1,)), ((), ())), precision=HI, preferred_element_type=jnp.float32
    )


def spread(value):
    return jnp.broadcast_to(value, (8, BLOCK))


def total(terms):
    terms = list(terms)
    while len(terms) > 1:
        terms = [sum(terms[i + 1 : i + 2], terms[i]) for i in range(0, len(terms), 2)]
    return terms[0]


def factor_block(s_ref, e_ref):
    ids = lax.broadcasted_iota(jnp.int32, (BLOCK, BLOCK), 0)
    lanes = lax.broadcasted_iota(jnp.int32, (BLOCK, BLOCK), 1)
    e_ref[...] = jnp.where(ids == lanes, 1.0, 0.0)
    sub = lax.broadcasted_iota(jnp.int32, (8, BLOCK), 0)
    for p in range(16):
        at = 8 * p
        own = s_ref[at : at + 8, :]
        own_e = e_ref[at : at + 8, :]
        cols = [spread(own[:, at + i : at + i + 1]) for i in range(8)]
        t = {(s, i): spread(cols[i][s : s + 1, :]) for i in range(8) for s in range(i, 8)}
        rows = [spread(own[q : q + 1, :]) for q in range(8)]
        rows_e = [spread(own_e[q : q + 1, :]) for q in range(8)]
        low, inv, root = {}, {}, []
        for i in range(8):
            rs = lax.rsqrt(t[i, i])
            root.append(rs)
            for s in range(i + 1, 8):
                low[s, i] = t[s, i] * rs
            for s in range(i + 1, 8):
                for q in range(i + 1, s + 1):
                    t[s, q] = t[s, q] - low[s, i] * low[q, i]
        for i in range(8):
            inv[i, i] = root[i]
            for s in range(i + 1, 8):
                inv[s, i] = -root[s] * total(low[s, q] * inv[q, i] for q in range(i, s))
        done = [total(inv[i, q] * rows[q] for q in range(i + 1)) for i in range(8)]
        done_e = [total(inv[i, q] * rows_e[q] for q in range(i + 1)) for i in range(8)]
        tile, tile_e = done[0], done_e[0]
        for i in range(1, 8):
            tile = jnp.where(sub == i, done[i], tile)
            tile_e = jnp.where(sub == i, done_e[i], tile_e)
        s_ref[at : at + 8, :] = tile
        e_ref[at : at + 8, :] = tile_e
        if p == 15:
            break
        back = [total(inv[i, j] * done[i] for i in range(j, 8)) for j in range(8)]
        back_e = [total(inv[i, j] * done_e[i] for i in range(j, 8)) for j in range(8)]
        for u in range(p + 1, 16):
            part = s_ref[8 * u : 8 * u + 8, :]
            left = [spread(part[:, at + j : at + j + 1]) for j in range(8)]
            s_ref[8 * u : 8 * u + 8, :] = part - total(left[j] * back[j] for j in range(8))
            e_ref[8 * u : 8 * u + 8, :] -= total(left[j] * back_e[j] for j in range(8))


def invert_block(work, s_ref, e_ref, k):
    n = BLOCK
    here = slice(k * n, (k + 1) * n)
    s_ref[...] = work[here, here]
    factor_block(s_ref, e_ref)
    ids = lax.broadcasted_iota(jnp.int32, (n, n), 0)
    lanes = lax.broadcasted_iota(jnp.int32, (n, n), 1)
    return jnp.where(ids <= lanes, s_ref[...], 0.0).T, e_ref[...]


def first_kernel(at_ref, own_ref, got_ref, f_ref, g_ref, rest_ref, work, s_ref, e_ref):
    n = BLOCK
    for i in range(4):
        u = at_ref[0] ^ i
        for j in range(i + 1):
            t = at_ref[1] ^ j
            work[i * n : (i + 1) * n, j * n : (j + 1) * n] = jnp.where(
                u % 2 == 0,
                own_ref[u // 2, t % 2, t // 2],
                got_ref[u // 2, t % 2, t // 2],
            )
    fac, inv = invert_block(work, s_ref, e_ref, 0)
    f_ref[:n, :] = fac
    g_ref[...] = inv
    f_ref[n:, :] = dot_nt(work[n:, :n], inv)
    for j in range(1, 4):
        rest_ref[(j - 1) * n :, (j - 1) * n : j * n] = work[
            j * n :, j * n : (j + 1) * n
        ] - dot_nt(f_ref[j * n :, :], f_ref[j * n : (j + 1) * n, :])


def second_kernel(f0_ref, g0_ref, rest_ref, f_ref, g_ref, work, s_ref, e_ref):
    k = pl.program_id(0) + 1
    n = BLOCK

    @pl.when(k == 1)
    def _():
        f_ref[...] = jnp.zeros_like(f_ref)
        g_ref[...] = jnp.zeros_like(g_ref)
        f_ref[:, :n] = f0_ref[...]
        g_ref[:n, :n] = g0_ref[...]
        for j in range(1, 4):
            there = slice(j * n, (j + 1) * n)
            work[j * n :, there] = rest_ref[(j - 1) * n :, (j - 1) * n : j * n]

    for step in range(1, 4):
        @pl.when(k == step)
        def _(step=step):
            here = slice(step * n, (step + 1) * n)
            s_ref[...] = work[here, here]

    factor_block(s_ref, e_ref)

    for step in range(1, 4):
        @pl.when(k == step)
        def _(step=step):
            here = slice(step * n, (step + 1) * n)
            ids = lax.broadcasted_iota(jnp.int32, (n, n), 0)
            lanes = lax.broadcasted_iota(jnp.int32, (n, n), 1)
            f_ref[here, here] = jnp.where(ids <= lanes, s_ref[...], 0.0).T
            inv = e_ref[...]
            g_ref[here, here] = inv
            if step < 3:
                f_ref[(step + 1) * n :, here] = dot_nt(work[(step + 1) * n :, here], inv)
            for j in range(step + 1, 4):
                there = slice(j * n, (j + 1) * n)
                work[j * n :, there] -= dot_nt(f_ref[j * n :, here], f_ref[there, here])
            before = slice(0, step * n)
            g_ref[here, before] = -dot(inv, dot(f_ref[here, before], g_ref[before, before]))


def f32(*shape):
    return jax.ShapeDtypeStruct(shape, jnp.float32)


VMEM = pl.BlockSpec(memory_space=pltpu.VMEM)
SMEM = pl.BlockSpec(memory_space=pltpu.SMEM)
WORK = [
    pltpu.VMEM((ORDER, ORDER), jnp.float32),
    pltpu.VMEM((BLOCK, BLOCK), jnp.float32),
    pltpu.VMEM((BLOCK, BLOCK), jnp.float32),
]


def factor_first(at, own, got):
    return pl.pallas_call(
        first_kernel,
        out_shape=[f32(ORDER, BLOCK), f32(BLOCK, BLOCK), f32(ORDER - BLOCK, ORDER - BLOCK)],
        in_specs=[SMEM, VMEM, VMEM],
        out_specs=[VMEM] * 3,
        scratch_shapes=WORK,
        compiler_params=pltpu.CompilerParams(vmem_limit_bytes=8 * 2**20),
        cost_estimate=pl.CostEstimate(flops=6 * 10**9, bytes_accessed=2**20, transcendentals=0),
    )(at, own, got)


def factor_rest(f0, g0, rest):
    return pl.pallas_call(
        second_kernel,
        grid=(3,),
        out_shape=[f32(ORDER, ORDER)] * 2,
        in_specs=[VMEM] * 3,
        out_specs=[VMEM] * 2,
        scratch_shapes=WORK,
        compiler_params=pltpu.CompilerParams(vmem_limit_bytes=8 * 2**20),
        cost_estimate=pl.CostEstimate(flops=18 * 10**9, bytes_accessed=2**20, transcendentals=0),
    )(f0, g0, rest)


def strip_kernel(top_ref, g_ref, wc_ref, tmp):
    n = BLOCK
    for i in range(4):
        for a in range(4):
            tmp[i * n + a * 32 : i * n + (a + 1) * 32, :] = top_ref[4 * a + i]
    for i in range(4):
        here = slice(i * n, (i + 1) * n)
        wc_ref[here, :] = dot(g_ref[here, : (i + 1) * n], tmp[: (i + 1) * n, :])


def strip_solve(top, inv):
    shape = (ORDER, ORDER + BLOCK)
    return pl.pallas_call(
        strip_kernel,
        out_shape=f32(*shape),
        in_specs=[VMEM] * 2,
        out_specs=VMEM,
        scratch_shapes=[pltpu.VMEM(shape, jnp.float32)],
        compiler_params=pltpu.CompilerParams(vmem_limit_bytes=8 * 2**20),
        cost_estimate=pl.CostEstimate(flops=4 * 10**9, bytes_accessed=4 * 2**20, transcendentals=0),
    )(top, inv)


def update_kernel(at_ref, q0_ref, q1_ref, q2_ref, low_ref, high_ref, f_ref, g_ref, wc_ref,
                  k_ref, y_ref, out_ref, right_ref, pan, w):
    step = pl.program_id(0)
    row, col = at_ref[2], at_ref[3]
    n = BLOCK

    def fill(read):
        for j in range(4):
            t = at_ref[1] ^ j
            for b in range(2):
                pan[b * n : (b + 1) * n, j * n : (j + 1) * n] = read(t % 2, t // 2, b)

    for s, ref in enumerate((q0_ref, q1_ref, q2_ref)):
        @pl.when(step == s)
        def _(ref=ref):
            fill(lambda t1, t2, b: ref[t1, t2, b])

    @pl.when(step == 3)
    def _():
        fill(lambda t1, t2, b: jnp.where(t1 == 0, low_ref[t2, b], high_ref[t2, b]))

    for i in range(4):
        here = slice(i * n, (i + 1) * n)
        w[:, here] = dot_nt(pan[:, : (i + 1) * n], g_ref[here, : (i + 1) * n])

    first = (at_ref[4 + step] == 0) & (row < 4)

    @pl.when(first)
    def _():
        w[:n, :] = f_ref[pl.ds(pl.multiple_of(row * n, n), n), :]

    out_ref[...] = k_ref[...] - dot(w[...], wc_ref[:, :ORDER])
    right_ref[...] = y_ref[...] - dot(w[...], wc_ref[:, ORDER:])

    @pl.when(first)
    def _():
        out_ref[:n, :] = jnp.zeros((n, ORDER), jnp.float32)
        right_ref[:n, :] = wc_ref[pl.ds(pl.multiple_of(row * n, n), n), ORDER:]

    @pl.when(col < 4)
    def _():
        out_ref[:, :n] = w[:, pl.ds(pl.multiple_of(col * n, n), n)]


def update(at, parts, fac, inv, wc, kernel, targets):
    rows = 256
    moved = lambda width: pl.BlockSpec((rows, width), lambda s, at: (at[4 + s], 0))
    return pl.pallas_call(
        update_kernel,
        out_shape=[f32(*kernel.shape), f32(*targets.shape)],
        grid_spec=pltpu.PrefetchScalarGridSpec(
            num_scalar_prefetch=1,
            grid=(4,),
            in_specs=[VMEM] * 8 + [moved(ORDER), moved(BLOCK)],
            out_specs=[moved(ORDER), moved(BLOCK)],
            scratch_shapes=[pltpu.VMEM((rows, ORDER), jnp.float32)] * 2,
        ),
        compiler_params=pltpu.CompilerParams(vmem_limit_bytes=16 * 2**20),
        cost_estimate=pl.CostEstimate(flops=10**10, bytes_accessed=6 * 2**20, transcendentals=0),
    )(at, *parts, fac, inv, wc, kernel, targets)


def after(value, *others):
    return lax.optimization_barrier((value, *others))[0]


def per_device(kernel, targets):
    row_pos = lax.axis_index("row")
    col_pos = lax.axis_index("col")
    x_pos = col_pos // Y
    y_pos = col_pos % Y
    n = BLOCK
    base = jnp.where(y_pos < 4, y_pos, 7 - y_pos)
    shifts = jnp.array([0, 3, 1, 2], jnp.int32)
    at = jnp.concatenate(
        [jnp.stack([row_pos % 4, base, row_pos, col_pos]), (x_pos + shifts) % 4]
    ).astype(jnp.int32)
    mirror = [(x * Y + j, x * Y + 7 - j) for x in range(X) for j in range(4)]
    by_two = [(c, c ^ 2) for c in range(COLS)]
    by_one = [(c, c ^ 1) for c in range(COLS)]

    a0 = jnp.where((col_pos < 4) & (row_pos < 4), kernel[:n, :n], 0.0)
    got = [a0]
    for x in (1, 2, 3):
        pairs = [(r * COLS + j, r * COLS + x * Y + j) for r in range(4) for j in range(4)]
        got.append(lax.ppermute(a0, ("row", "col"), pairs))
    a1 = total(got)

    strip = jnp.concatenate([kernel[:n], targets[:n]], axis=1)
    got = [jnp.where(row_pos < 4, strip[:32], 0.0)]
    for a in (1, 2, 3):
        got.append(over_row(strip[32 * a : 32 * a + 32], [(r, r + 4 * a) for r in range(4)]))
    piece = total(got)
    top = lax.all_gather(piece, "row")

    panel = kernel[:, :n].reshape(8, n, n)
    got = [jnp.where(x_pos == 0, panel[:2], 0.0)]
    for x in (1, 2, 3):
        got.append(over_col(panel[2 * x : 2 * x + 2], [(j, x * Y + j) for j in range(4)]))
    p1 = total(got)

    a2 = after(a1 + over_col(a1, mirror), piece, p1)
    got = [a2]
    for a in (1, 2, 3):
        got.append(over_row(a2, [(r, r + 4 * a) for r in range(4)]))
    a3 = total(got)
    p2 = jnp.where(y_pos >= 4, over_col(after(p1, a2), mirror), p1)
    a4 = jnp.stack([a3, over_col(a3, by_two)])
    a5 = jnp.stack([a4, over_col(a4, by_one)])
    p3 = jnp.stack([p2, over_col(after(p2, a5), by_two)])
    a6 = jnp.stack([a5, over_row(a5, [(r, r ^ 2) for r in range(ROWS)])])
    p4 = jnp.stack([p3, over_col(after(p3, a6), by_one)])
    a7 = over_row(a6, [(r, r ^ 1) for r in range(ROWS)])

    state = factor_first(at, a6, a7)
    p4 = after(p4, state[1])
    down = over_col(p4, [(c, (c + Y) % COLS) for c in range(COLS)])
    up = over_col(p4, [(c, (c - Y) % COLS) for c in range(COLS)])
    fac, inv = factor_rest(*state)
    low = over_col(after(up[0], inv), [(c, (c - Y) % COLS) for c in range(COLS)])
    high = over_col(after(down[1], inv), [(c, (c + Y) % COLS) for c in range(COLS)])
    wc = strip_solve(top, inv)
    return tuple(update(at, (p4, down, up, low, high), fac, inv, wc, kernel, targets))


def solution(mesh):
    in_specs = (P("row", "col"), P("row", None))
    out_specs = (P("row", "col"), P("row", None))
    return jax.shard_map(
        per_device, mesh=mesh, in_specs=in_specs, out_specs=out_specs, check_vma=False
    )
```

time: 159 us -> 163 us (1.025)
  the two profiles are of different devices: /device:TPU:1 before, /device:TPU:56 now
where the time goes in v1:
time: 163 us; the launch traced here: 162 us
  starting transfers between devices  61.4 us (38%)
  Pallas kernels  42.9 us (26%)
  waiting for transfers between devices  26.3 us (16%)
  between operations  14.5 us (9%)
  local copies, waits for them, and re-layouts  9.32 us (6%)
  other arithmetic  7.27 us (4%)
    ppermute x13, starting transfers between devices, over_col(): return lax.ppermute(value, 'col', pairs)  34.8 us
    ppermute x13, waiting for transfers between devices, over_col(): return lax.ppermute(value, 'col', pairs)  24.4 us
    ppermute x8, starting transfers between devices, over_row(): return lax.ppermute(value, 'row', pairs)  24 us
    pallas_call x1, Pallas kernels, factor_rest(): pl.pallas_call(second_kernel, grid=(3,), out_shape=[f32(ORDER, ORDER)] *...  16.9 us
    pallas_call x1, Pallas kernels, update(): pl.pallas_call(update_kernel, out_shape=[f32(*kernel.shape), f32(*targets...  16.6 us
    pallas_call x1, Pallas kernels, factor_first(): pl.pallas_call(first_kernel, out_shape=[f32(ORDER, BLOCK), f32(BLOCK, BLO...  7.41 us
    unnamed x26, local copies, waits for them, and re-layouts  5.93 us
  transfers between devices with their start and end apart: 25, of which 9 were waited for; matrix products, arithmetic and copies ran while one was open for 6% of the time, Pallas kernels for 16%

profile of v1, /device:TPU:56, one launch (start us, length us, event | category | flops | bytes accessed | tf_op | source)
XLA Modules:
  0.0 161.7 jit_solution(11788652552984496478)
XLA Ops:
  7.2 1.0 slice_select_fusion.1
  9.6 1.3 collective-permute-start.3
  10.8 1.0 slice.62
  11.8 0.8 slice.63
  12.7 0.7 pad_maximum_fusion.5
  13.3 10.9 %collective-permute-start.9 = (f32[32,640]{1,0:T(8,128)S(1)}, f32[32,640]{1,0:T(8,128)S(1)}, u32[]{:S(2)}, u32[]{:S(2)}) collective-permute-start(f32[32,640]{1,0:T(8,128)S(1)} %get-tuple-element.30), channel_id=1, source_target_pairs={{0,384},{32,416},{64,448},{96,480},{1,385},{33,417},{65,449},{97,4... | collective-permute-start | bytes 245768 | tf_op jit(solution)/shard_map/ppermute | solution.py:22
  24.3 1.9 %collective-permute-start.7 = (f32[32,640]{1,0:T(8,128)}, f32[32,640]{1,0:T(8,128)}, u32[]{:S(2)}, u32[]{:S(2)}) collective-permute-start(f32[32,640]{1,0:T(8,128)} %get-tuple-element.31), channel_id=1, source_target_pairs={{0,128},{32,160},{64,192},{96,224},{1,129},{33,161},{65,193},{97,2... | collective-permute-start | bytes 245768 | tf_op jit(solution)/shard_map/ppermute | solution.py:22
  26.2 1.1 fusion.10
  27.3 1.3 collective-permute-start.8
  30.6 0.9 add_add_fusion.2
  31.5 0.7 collective-permute-start.1
  32.2 1.3 collective-permute-start.6
  33.5 1.5 fusion.4
  35.1 6.1 %collective-permute-done.6 = f32[128,128]{1,0:T(8,128)} collective-permute-done((f32[128,128]{1,0:T(8,128)S(1)}, f32[128,128]{1,0:T(8,128)}, u32[]{:S(2)}, u32[]{:S(2)}) %collective-permute-start.6) | collective-permute-done | bytes 65568 | tf_op jit(solution)/shard_map/ppermute | solution.py:18
  41.2 0.8 add.70
  42.1 1.4 collective-permute-start.13
  43.5 1.3 collective-permute-start.12
  44.8 1.3 collective-permute-start.11
  46.7 1.3 collective-permute-done.11
  48.0 5.8 %collective-permute-start.14 = (f32[128,128]{1,0:T(8,128)S(1)}, f32[128,128]{1,0:T(8,128)S(1)}, u32[]{:S(2)}, u32[]{:S(2)}) collective-permute-start(f32[128,128]{1,0:T(8,128)S(1)} %add_add_fusion.1), channel_id=1, source_target_pairs={{0,2},{1,3},{2,0},{3,1},{4,6},{5,7},{6,4},{7,5},{8,10},{9,11},{10,... | collective-permute-start | bytes 196616 | tf_op jit(solution)/shard_map/ppermute | solution.py:18
  53.8 2.2 %collective-permute-done.14 = f32[128,128]{1,0:T(8,128)S(1)} collective-permute-done((f32[128,128]{1,0:T(8,128)S(1)}, f32[128,128]{1,0:T(8,128)S(1)}, u32[]{:S(2)}, u32[]{:S(2)}) %collective-permute-start.14) | collective-permute-done | bytes 65568 | tf_op jit(solution)/shard_map/ppermute | solution.py:18
  56.0 3.9 %collective-permute-start.15 = (f32[2,128,128]{2,1,0:T(8,128)S(1)}, f32[2,128,128]{2,1,0:T(8,128)S(1)}, u32[]{:S(2)}, u32[]{:S(2)}) collective-permute-start(f32[2,128,128]{2,1,0:T(8,128)S(1)} %get-tuple-element.38), channel_id=1, source_target_pairs={{0,1},{1,0},{2,3},{3,2},{4,5},{5,4},{6,7},{7,6},{8,9},{9,8},{10,11... | collective-permute-start | bytes 393224 | tf_op jit(solution)/shard_map/ppermute | solution.py:18
  60.0 1.3 collective-permute-start.10
  61.3 2.6 %collective-permute-done.15 = f32[2,128,128]{2,1,0:T(8,128)S(1)} collective-permute-done((f32[2,128,128]{2,1,0:T(8,128)S(1)}, f32[2,128,128]{2,1,0:T(8,128)S(1)}, u32[]{:S(2)}, u32[]{:S(2)}) %collective-permute-start.15) | collective-permute-done | bytes 131104 | tf_op jit(solution)/shard_map/ppermute | solution.py:18
  63.9 4.0 %collective-permute-start.17 = (f32[2,2,128,128]{3,2,1,0:T(8,128)S(1)}, f32[2,2,128,128]{3,2,1,0:T(8,128)S(1)}, u32[]{:S(2)}, u32[]{:S(2)}) collective-permute-start(f32[2,2,128,128]{3,2,1,0:T(8,128)S(1)} %get-tuple-element.36), channel_id=1, source_target_pairs={{0,64},{32,96},{64,0},{96,32},{128,192},{160,224},{192,128},{224,1... | collective-permute-start | bytes 786440 | tf_op jit(solution)/shard_map/ppermute | solution.py:22
  67.8 1.6 collective-permute-done.10
  69.5 6.3 %collective-permute-start.16 = (f32[2,128,128]{2,1,0:T(8,128)S(1)}, f32[2,128,128]{2,1,0:T(8,128)S(1)}, u32[]{:S(2)}, u32[]{:S(2)}) collective-permute-start(f32[2,128,128]{2,1,0:T(8,128)S(1)} %broadcast_select_fusion), channel_id=1, source_target_pairs={{0,2},{1,3},{2,0},{3,1},{4,6},{5,7},{6,4},{7,5},{8,10},{9,11},{10,... | collective-permute-start | bytes 393224 | tf_op jit(solution)/shard_map/ppermute | solution.py:18
  75.8 1.9 %collective-permute-start.19 = (f32[2,2,2,128,128]{4,3,2,1,0:T(8,128)S(1)}, f32[2,2,2,128,128]{4,3,2,1,0:T(8,128)}, u32[]{:S(2)}, u32[]{:S(2)}) collective-permute-start(f32[2,2,2,128,128]{4,3,2,1,0:T(8,128)S(1)} %pad_maximum_fusion.own_ref), channel_id=1, source_target_pairs={{0,32},{32,0},{64,96},{96,64},{128,160},{160,128},{192,224},{224,1... | collective-permute-start | bytes 1572872 | tf_op jit(solution)/shard_map/ppermute | solution.py:22
  77.8 1.2 collective-permute-done.16
  79.0 1.9 %collective-permute-start.18 = (f32[2,2,128,128]{3,2,1,0:T(8,128)S(1)}, f32[2,2,128,128]{3,2,1,0:T(8,128)S(1)}, u32[]{:S(2)}, u32[]{:S(2)}) collective-permute-start(f32[2,2,128,128]{3,2,1,0:T(8,128)S(1)} %get-tuple-element.17), channel_id=1, source_target_pairs={{0,1},{1,0},{2,3},{3,2},{4,5},{5,4},{6,7},{7,6},{8,9},{9,8},{10,11... | collective-permute-start | bytes 786440 | tf_op jit(solution)/shard_map/ppermute | solution.py:18
  81.1 7.3 %collective-permute-done.18 = f32[2,2,128,128]{3,2,1,0:T(8,128)S(1)} collective-permute-done((f32[2,2,128,128]{3,2,1,0:T(8,128)S(1)}, f32[2,2,128,128]{3,2,1,0:T(8,128)S(1)}, u32[]{:S(2)}, u32[]{:S(2)}) %collective-permute-start.18) | collective-permute-done | bytes 262176 | tf_op jit(solution)/shard_map/ppermute | solution.py:18
  88.4 0.7 copy-done.10
  89.1 1.0 pad_maximum_fusion.1.q0_ref
  90.1 7.4 %shard_map.50 = (f32[512,128]{1,0:T(8,128)S(1)}, f32[128,128]{1,0:T(8,128)S(1)}, f32[384,384]{1,0:T(8,128)S(1)}) custom-call(s32[8]{0:T(128)S(1)} %concatenate.6.at_ref, f32[2,2,2,128,128]{4,3,2,1,0:T(8,128)S(1)} %pad_maximum_fusion.own_ref, f32[2,2,2,128,128]{4,3,2,1,0:T(8,128)} %collective-permute-done.19.got_ref), custom_call_target="tpu_custom_call" | custom-call | flops 6000000000 | bytes 1048576 | tf_op jit(solution)/shard_map/pallas_call | solution.py:178
  97.6 3.1 %collective-permute-start.21 = (f32[2,2,2,128,128]{4,3,2,1,0:T(8,128)S(1)}, f32[2,2,2,128,128]{4,3,2,1,0:T(8,128)S(1)}, u32[]{:S(2)}, u32[]{:S(2)}) collective-permute-start(f32[2,2,2,128,128]{4,3,2,1,0:T(8,128)S(1)} %pad_maximum_fusion.1.q0_ref), channel_id=1, source_target_pairs={{0,24},{1,25},{2,26},{3,27},{4,28},{5,29},{6,30},{7,31},{8,0},{9,1... | collective-permute-start | bytes 1572872 | tf_op jit(solution)/shard_map/ppermute | solution.py:18
  100.7 2.9 %collective-permute-start.20 = (f32[2,2,2,128,128]{4,3,2,1,0:T(8,128)S(1)}, f32[2,2,2,128,128]{4,3,2,1,0:T(8,128)S(1)}, u32[]{:S(2)}, u32[]{:S(2)}) collective-permute-start(f32[2,2,2,128,128]{4,3,2,1,0:T(8,128)S(1)} %pad_maximum_fusion.1.q0_ref), channel_id=1, source_target_pairs={{0,8},{1,9},{2,10},{3,11},{4,12},{5,13},{6,14},{7,15},{8,16},{9,17... | collective-permute-start | bytes 1572872 | tf_op jit(solution)/shard_map/ppermute | solution.py:18
  103.6 16.9 %shard_map.51 = (f32[512,512]{1,0:T(8,128)S(1)}, f32[512,512]{1,0:T(8,128)S(1)}) custom-call(f32[512,128]{1,0:T(8,128)S(1)} %get-tuple-element.20.f0_ref, f32[128,128]{1,0:T(8,128)S(1)} %get-tuple-element.18.g0_ref, f32[384,384]{1,0:T(8,128)S(1)} %get-tuple-element.21.rest_ref), custom_call_target="tpu_custom_call" | custom-call | flops 17999998976 | bytes 1048576 | tf_op jit(solution)/shard_map/pallas_call | solution.py:190
  120.5 1.0 copy-done.5
  121.5 1.0 copy-done.8
  122.4 0.8 slice_bitcast_fusion
  123.3 0.7 slice_bitcast_fusion.1
  124.0 4.3 %collective-permute-start.22 = (f32[2,2,128,128]{3,2,1,0:T(8,128)}, f32[2,2,128,128]{3,2,1,0:T(8,128)S(1)}, u32[]{:S(2)}, u32[]{:S(2)}) collective-permute-start(f32[2,2,128,128]{3,2,1,0:T(8,128)} %slice_bitcast_fusion.1), channel_id=1, source_target_pairs={{0,24},{1,25},{2,26},{3,27},{4,28},{5,29},{6,30},{7,31},{8,0},{9,1... | collective-permute-start | bytes 786440 | tf_op jit(solution)/shard_map/ppermute | solution.py:18
  128.4 1.9 %collective-permute-start.23 = (f32[2,2,128,128]{3,2,1,0:T(8,128)}, f32[2,2,128,128]{3,2,1,0:T(8,128)}, u32[]{:S(2)}, u32[]{:S(2)}) collective-permute-start(f32[2,2,128,128]{3,2,1,0:T(8,128)} %slice_bitcast_fusion), channel_id=1, source_target_pairs={{0,8},{1,9},{2,10},{3,11},{4,12},{5,13},{6,14},{7,15},{8,16},{9,17... | collective-permute-start | bytes 786440 | tf_op jit(solution)/shard_map/ppermute | solution.py:18
  130.3 1.3 copy-done.4
  131.6 1.2 copy-done.6
  132.9 1.9 %shard_map.52.wc_ref = f32[512,640]{1,0:T(8,128)S(1)} custom-call(f32[16,32,640]{2,1,0:T(8,128)S(1)} %bitcast.26, f32[512,512]{1,0:T(8,128)S(1)} %copy-done.6), custom_call_target="tpu_custom_call" | custom-call | flops 4000000000 | bytes 4194304 | tf_op jit(solution)/shard_map/pallas_call | solution.py:214
  134.8 3.3 %collective-permute-done.23.high_ref = f32[2,2,128,128]{3,2,1,0:T(8,128)} collective-permute-done((f32[2,2,128,128]{3,2,1,0:T(8,128)}, f32[2,2,128,128]{3,2,1,0:T(8,128)}, u32[]{:S(2)}, u32[]{:S(2)}) %collective-permute-start.23) | collective-permute-done | bytes 262176 | tf_op jit(solution)/shard_map/ppermute | solution.py:18
  138.2 16.6 %shard_map.53 = (f32[1024,512]{1,0:T(8,128)}, f32[1024,128]{1,0:T(8,128)}) custom-call(s32[8]{0:T(128)S(1)} %concatenate.6.at_ref, f32[2,2,2,128,128]{4,3,2,1,0:T(8,128)S(1)} %pad_maximum_fusion.1.q0_ref, f32[2,2,2,128,128]{4,3,2,1,0:T(8,128)S(1)} %copy-done.2, f32[2,2,2,128,128]{4,3,2,1,0:T(8,128)S(1)} %collective-permute-done.21.q2_ref, ...), custom_call_target="tpu_custom_call" | custom-call | flops 10000000000 | bytes 6291456 | tf_op jit(solution)/shard_map/pallas_call | solution.py:272
  (53 shorter events, 4.4 us)
Async XLA Ops:
  7.2 23.5 %copy-start = (f32[1024,512]{1,0:T(8,128)S(1)}, f32[1024,512]{1,0:T(8,128)}, u32[]{:S(2)}) copy-start(f32[1024,512]{1,0:T(8,128)} %k_ref.1) | copy-start | bytes 6291460
  7.2 123.1 %all-gather.3.cloned.1.call-start = ((), (), s32[]{:S(2)}) async-start(), calls=%async_computation | async-start | bytes 1392640 | tf_op jit(solution)/shard_map/all_gather | solution.py:318
  8.2 19.1 %collective-permute-start.4 = (f32[128,128]{1,0:T(8,128)S(1)}, f32[128,128]{1,0:T(8,128)S(1)}, u32[]{:S(2)}, u32[]{:S(2)}) collective-permute-start(f32[128,128]{1,0:T(8,128)S(1)} %slice_select_fusion.1), channel_id=1, source_target_pairs={{0,16},{1,17},{2,18},{3,19},{32,48},{33,49},{34,50},{35,51},{64,80... | collective-permute-start | bytes 196616 | tf_op jit(solution)/shard_map/ppermute | solution.py:310
  8.9 19.8 %collective-permute-start.5 = (f32[128,128]{1,0:T(8,128)S(1)}, f32[128,128]{1,0:T(8,128)S(1)}, u32[]{:S(2)}, u32[]{:S(2)}) collective-permute-start(f32[128,128]{1,0:T(8,128)S(1)} %slice_select_fusion.1), channel_id=1, source_target_pairs={{0,24},{1,25},{2,26},{3,27},{32,56},{33,57},{34,58},{35,59},{64,88... | collective-permute-start | bytes 196616 | tf_op jit(solution)/shard_map/ppermute | solution.py:310
  9.6 20.4 %collective-permute-start.3 = (f32[128,128]{1,0:T(8,128)S(1)}, f32[128,128]{1,0:T(8,128)}, u32[]{:S(2)}, u32[]{:S(2)}) collective-permute-start(f32[128,128]{1,0:T(8,128)S(1)} %slice_select_fusion.1), channel_id=1, source_target_pairs={{0,8},{1,9},{2,10},{3,11},{32,40},{33,41},{34,42},{35,43},{64,72},... | collective-permute-start | bytes 196616 | tf_op jit(solution)/shard_map/ppermute | solution.py:310
  13.3 18.2 %collective-permute-start.9 = (f32[32,640]{1,0:T(8,128)S(1)}, f32[32,640]{1,0:T(8,128)S(1)}, u32[]{:S(2)}, u32[]{:S(2)}) collective-permute-start(f32[32,640]{1,0:T(8,128)S(1)} %get-tuple-element.30), channel_id=1, source_target_pairs={{0,384},{32,416},{64,448},{96,480},{1,385},{33,417},{65,449},{97,4... | collective-permute-start | bytes 245768 | tf_op jit(solution)/shard_map/ppermute | solution.py:22
  24.3 7.9 %collective-permute-start.7 = (f32[32,640]{1,0:T(8,128)}, f32[32,640]{1,0:T(8,128)}, u32[]{:S(2)}, u32[]{:S(2)}) collective-permute-start(f32[32,640]{1,0:T(8,128)} %get-tuple-element.31), channel_id=1, source_target_pairs={{0,128},{32,160},{64,192},{96,224},{1,129},{33,161},{65,193},{97,2... | collective-permute-start | bytes 245768 | tf_op jit(solution)/shard_map/ppermute | solution.py:22
  27.3 6.2 %collective-permute-start.8 = (f32[32,640]{1,0:T(8,128)}, f32[32,640]{1,0:T(8,128)S(1)}, u32[]{:S(2)}, u32[]{:S(2)}) collective-permute-start(f32[32,640]{1,0:T(8,128)} %get-tuple-element.32), channel_id=1, source_target_pairs={{0,256},{32,288},{64,320},{96,352},{1,257},{33,289},{65,321},{97,3... | collective-permute-start | bytes 245768 | tf_op jit(solution)/shard_map/ppermute | solution.py:22
  28.6 0.6 copy-start.11
  29.3 12.8 %collective-permute-start.2 = (f32[2,128,128]{2,1,0:T(8,128)S(1)}, f32[2,128,128]{2,1,0:T(8,128)S(1)}, u32[]{:S(2)}, u32[]{:S(2)}) collective-permute-start(f32[2,128,128]{2,1,0:T(8,128)S(1)} %bitcast.36), channel_id=1, source_target_pairs={{0,24},{1,25},{2,26},{3,27},{32,56},{33,57},{34,58},{35,59},{64,88... | collective-permute-start | bytes 393224 | tf_op jit(solution)/shard_map/ppermute | solution.py:18
  29.9 12.1 %collective-permute-start = (f32[2,128,128]{2,1,0:T(8,128)S(1)}, f32[2,128,128]{2,1,0:T(8,128)S(1)}, u32[]{:S(2)}, u32[]{:S(2)}) collective-permute-start(f32[2,128,128]{2,1,0:T(8,128)S(1)} %bitcast.35), channel_id=1, source_target_pairs={{0,8},{1,9},{2,10},{3,11},{32,40},{33,41},{34,42},{35,43},{64,72},... | collective-permute-start | bytes 393224 | tf_op jit(solution)/shard_map/ppermute | solution.py:18
  31.5 10.5 %collective-permute-start.1 = (f32[2,128,128]{2,1,0:T(8,128)S(1)}, f32[2,128,128]{2,1,0:T(8,128)S(1)}, u32[]{:S(2)}, u32[]{:S(2)}) collective-permute-start(f32[2,128,128]{2,1,0:T(8,128)S(1)} %bitcast.34), channel_id=1, source_target_pairs={{0,16},{1,17},{2,18},{3,19},{32,48},{33,49},{34,50},{35,51},{64,80... | collective-permute-start | bytes 393224 | tf_op jit(solution)/shard_map/ppermute | solution.py:18
  32.2 9.0 %collective-permute-start.6 = (f32[128,128]{1,0:T(8,128)S(1)}, f32[128,128]{1,0:T(8,128)}, u32[]{:S(2)}, u32[]{:S(2)}) collective-permute-start(f32[128,128]{1,0:T(8,128)S(1)} %add_add_fusion.2), channel_id=1, source_target_pairs={{0,7},{1,6},{2,5},{3,4},{8,15},{9,14},{10,13},{11,12},{16,23},{17,... | collective-permute-start | bytes 196616 | tf_op jit(solution)/shard_map/ppermute | solution.py:18
  42.0 38.9 %copy-start.12 = (s32[4]{0:T(128)S(1)}, s32[4]{0:T(128)}, u32[]{:S(2)}) copy-start(s32[4]{0:T(128)} %constant.58.clone) | copy-start | bytes 52
  42.1 4.0 %collective-permute-start.13 = (f32[128,128]{1,0:T(8,128)S(1)}, f32[128,128]{1,0:T(8,128)S(1)}, u32[]{:S(2)}, u32[]{:S(2)}) collective-permute-start(f32[128,128]{1,0:T(8,128)S(1)} %add.70), channel_id=1, source_target_pairs={{0,384},{32,416},{64,448},{96,480},{1,385},{33,417},{65,449},{97,4... | collective-permute-start | bytes 196616 | tf_op jit(solution)/shard_map/ppermute | solution.py:22
  43.5 3.2 %collective-permute-start.12 = (f32[128,128]{1,0:T(8,128)S(1)}, f32[128,128]{1,0:T(8,128)S(1)}, u32[]{:S(2)}, u32[]{:S(2)}) collective-permute-start(f32[128,128]{1,0:T(8,128)S(1)} %add.70), channel_id=1, source_target_pairs={{0,256},{32,288},{64,320},{96,352},{1,257},{33,289},{65,321},{97,3... | collective-permute-start | bytes 196616 | tf_op jit(solution)/shard_map/ppermute | solution.py:22
  44.8 3.2 %collective-permute-start.11 = (f32[128,128]{1,0:T(8,128)S(1)}, f32[128,128]{1,0:T(8,128)S(1)}, u32[]{:S(2)}, u32[]{:S(2)}) collective-permute-start(f32[128,128]{1,0:T(8,128)S(1)} %add.70), channel_id=1, source_target_pairs={{0,128},{32,160},{64,192},{96,224},{1,129},{33,161},{65,193},{97,2... | collective-permute-start | bytes 196616 | tf_op jit(solution)/shard_map/ppermute | solution.py:22
  48.0 8.0 %collective-permute-start.14 = (f32[128,128]{1,0:T(8,128)S(1)}, f32[128,128]{1,0:T(8,128)S(1)}, u32[]{:S(2)}, u32[]{:S(2)}) collective-permute-start(f32[128,128]{1,0:T(8,128)S(1)} %add_add_fusion.1), channel_id=1, source_target_pairs={{0,2},{1,3},{2,0},{3,1},{4,6},{5,7},{6,4},{7,5},{8,10},{9,11},{10,... | collective-permute-start | bytes 196616 | tf_op jit(solution)/shard_map/ppermute | solution.py:18
  56.0 7.8 %collective-permute-start.15 = (f32[2,128,128]{2,1,0:T(8,128)S(1)}, f32[2,128,128]{2,1,0:T(8,128)S(1)}, u32[]{:S(2)}, u32[]{:S(2)}) collective-permute-start(f32[2,128,128]{2,1,0:T(8,128)S(1)} %get-tuple-element.38), channel_id=1, source_target_pairs={{0,1},{1,0},{2,3},{3,2},{4,5},{5,4},{6,7},{7,6},{8,9},{9,8},{10,11... | collective-permute-start | bytes 393224 | tf_op jit(solution)/shard_map/ppermute | solution.py:18
  60.0 9.5 %collective-permute-start.10 = (f32[2,128,128]{2,1,0:T(8,128)S(1)}, f32[2,128,128]{2,1,0:T(8,128)S(1)}, u32[]{:S(2)}, u32[]{:S(2)}) collective-permute-start(f32[2,128,128]{2,1,0:T(8,128)S(1)} %add_add_fusion), channel_id=1, source_target_pairs={{0,7},{1,6},{2,5},{3,4},{8,15},{9,14},{10,13},{11,12},{16,23},{17,... | collective-permute-start | bytes 393224 | tf_op jit(solution)/shard_map/ppermute | solution.py:18
  63.9 11.9 %collective-permute-start.17 = (f32[2,2,128,128]{3,2,1,0:T(8,128)S(1)}, f32[2,2,128,128]{3,2,1,0:T(8,128)S(1)}, u32[]{:S(2)}, u32[]{:S(2)}) collective-permute-start(f32[2,2,128,128]{3,2,1,0:T(8,128)S(1)} %get-tuple-element.36), channel_id=1, source_target_pairs={{0,64},{32,96},{64,0},{96,32},{128,192},{160,224},{192,128},{224,1... | collective-permute-start | bytes 786440 | tf_op jit(solution)/shard_map/ppermute | solution.py:22
  69.5 9.5 %collective-permute-start.16 = (f32[2,128,128]{2,1,0:T(8,128)S(1)}, f32[2,128,128]{2,1,0:T(8,128)S(1)}, u32[]{:S(2)}, u32[]{:S(2)}) collective-permute-start(f32[2,128,128]{2,1,0:T(8,128)S(1)} %broadcast_select_fusion), channel_id=1, source_target_pairs={{0,2},{1,3},{2,0},{3,1},{4,6},{5,7},{6,4},{7,5},{8,10},{9,11},{10,... | collective-permute-start | bytes 393224 | tf_op jit(solution)/shard_map/ppermute | solution.py:18
  75.8 14.3 %collective-permute-start.19 = (f32[2,2,2,128,128]{4,3,2,1,0:T(8,128)S(1)}, f32[2,2,2,128,128]{4,3,2,1,0:T(8,128)}, u32[]{:S(2)}, u32[]{:S(2)}) collective-permute-start(f32[2,2,2,128,128]{4,3,2,1,0:T(8,128)S(1)} %pad_maximum_fusion.own_ref), channel_id=1, source_target_pairs={{0,32},{32,0},{64,96},{96,64},{128,160},{160,128},{192,224},{224,1... | collective-permute-start | bytes 1572872 | tf_op jit(solution)/shard_map/ppermute | solution.py:22
  79.0 9.4 %collective-permute-start.18 = (f32[2,2,128,128]{3,2,1,0:T(8,128)S(1)}, f32[2,2,128,128]{3,2,1,0:T(8,128)S(1)}, u32[]{:S(2)}, u32[]{:S(2)}) collective-permute-start(f32[2,2,128,128]{3,2,1,0:T(8,128)S(1)} %get-tuple-element.17), channel_id=1, source_target_pairs={{0,1},{1,0},{2,3},{3,2},{4,5},{5,4},{6,7},{7,6},{8,9},{9,8},{10,11... | collective-permute-start | bytes 786440 | tf_op jit(solution)/shard_map/ppermute | solution.py:18
  88.4 0.7 copy-start.10
  97.6 25.7 %collective-permute-start.21 = (f32[2,2,2,128,128]{4,3,2,1,0:T(8,128)S(1)}, f32[2,2,2,128,128]{4,3,2,1,0:T(8,128)S(1)}, u32[]{:S(2)}, u32[]{:S(2)}) collective-permute-start(f32[2,2,2,128,128]{4,3,2,1,0:T(8,128)S(1)} %pad_maximum_fusion.1.q0_ref), channel_id=1, source_target_pairs={{0,24},{1,25},{2,26},{3,27},{4,28},{5,29},{6,30},{7,31},{8,0},{9,1... | collective-permute-start | bytes 1572872 | tf_op jit(solution)/shard_map/ppermute | solution.py:18
  100.7 21.8 %collective-permute-start.20 = (f32[2,2,2,128,128]{4,3,2,1,0:T(8,128)S(1)}, f32[2,2,2,128,128]{4,3,2,1,0:T(8,128)S(1)}, u32[]{:S(2)}, u32[]{:S(2)}) collective-permute-start(f32[2,2,2,128,128]{4,3,2,1,0:T(8,128)S(1)} %pad_maximum_fusion.1.q0_ref), channel_id=1, source_target_pairs={{0,8},{1,9},{2,10},{3,11},{4,12},{5,13},{6,14},{7,15},{8,16},{9,17... | collective-permute-start | bytes 1572872 | tf_op jit(solution)/shard_map/ppermute | solution.py:18
  120.5 1.0 copy-start.5
  121.5 1.0 copy-start.8
  122.4 0.9 copy-start.1
  124.0 10.8 %collective-permute-start.22 = (f32[2,2,128,128]{3,2,1,0:T(8,128)}, f32[2,2,128,128]{3,2,1,0:T(8,128)S(1)}, u32[]{:S(2)}, u32[]{:S(2)}) collective-permute-start(f32[2,2,128,128]{3,2,1,0:T(8,128)} %slice_bitcast_fusion.1), channel_id=1, source_target_pairs={{0,24},{1,25},{2,26},{3,27},{4,28},{5,29},{6,30},{7,31},{8,0},{9,1... | collective-permute-start | bytes 786440 | tf_op jit(solution)/shard_map/ppermute | solution.py:18
  128.4 9.8 %collective-permute-start.23 = (f32[2,2,128,128]{3,2,1,0:T(8,128)}, f32[2,2,128,128]{3,2,1,0:T(8,128)}, u32[]{:S(2)}, u32[]{:S(2)}) collective-permute-start(f32[2,2,128,128]{3,2,1,0:T(8,128)} %slice_bitcast_fusion), channel_id=1, source_target_pairs={{0,8},{1,9},{2,10},{3,11},{4,12},{5,13},{6,14},{7,15},{8,16},{9,17... | collective-permute-start | bytes 786440 | tf_op jit(solution)/shard_map/ppermute | solution.py:18
  130.3 1.3 copy-start.4
  131.6 1.2 copy-start.6
  132.9 5.3 %copy-start.2 = (f32[2,2,2,128,128]{4,3,2,1,0:T(8,128)S(1)}, f32[2,2,2,128,128]{4,3,2,1,0:T(8,128)}, u32[]{:S(2)}) copy-start(f32[2,2,2,128,128]{4,3,2,1,0:T(8,128)} %copy-done.1) | copy-start | bytes 1572868
  132.9 5.3 %copy-start.3 = (f32[1024,128]{1,0:T(8,128)S(1)}, f32[1024,128]{1,0:T(8,128)}, u32[]{:S(2)}) copy-start(f32[1024,128]{1,0:T(8,128)} %y_ref.1) | copy-start | bytes 1572868
  132.9 5.3 %copy-start.7 = (f32[512,512]{1,0:T(8,128)S(1)}, f32[512,512]{1,0:T(8,128)}, u32[]{:S(2)}) copy-start(f32[512,512]{1,0:T(8,128)} %copy-done.5) | copy-start | bytes 3145732
  132.9 5.3 %copy-start.9 = (f32[512,512]{1,0:T(8,128)S(1)}, f32[512,512]{1,0:T(8,128)}, u32[]{:S(2)}) copy-start(f32[512,512]{1,0:T(8,128)} %copy-done.8) | copy-start | bytes 3145732
Sparse Core Ops, SparseCore 0:
  81.2 42.1 all-gather.2

commit v2 on v1

--- a/solution.py
+++ b/solution.py
@@ -121,7 +121,7 @@
         ] - dot_nt(f_ref[j * n :, :], f_ref[j * n : (j + 1) * n, :])
 
 
-def second_kernel(f0_ref, g0_ref, rest_ref, f_ref, g_ref, work, s_ref, e_ref):
+def middle_kernel(f0_ref, g0_ref, rest_ref, f_ref, g_ref, left_ref, work, s_ref, e_ref):
     k = pl.program_id(0) + 1
     n = BLOCK
 
@@ -135,7 +135,7 @@
             there = slice(j * n, (j + 1) * n)
             work[j * n :, there] = rest_ref[(j - 1) * n :, (j - 1) * n : j * n]
 
-    for step in range(1, 4):
+    for step in (1, 2):
         @pl.when(k == step)
         def _(step=step):
             here = slice(step * n, (step + 1) * n)
@@ -143,7 +143,7 @@
 
     factor_block(s_ref, e_ref)
 
-    for step in range(1, 4):
+    for step in (1, 2):
         @pl.when(k == step)
         def _(step=step):
             here = slice(step * n, (step + 1) * n)
@@ -152,13 +152,28 @@
             f_ref[here, here] = jnp.where(ids <= lanes, s_ref[...], 0.0).T
             inv = e_ref[...]
             g_ref[here, here] = inv
-            if step < 3:
-                f_ref[(step + 1) * n :, here] = dot_nt(work[(step + 1) * n :, here], inv)
+            f_ref[(step + 1) * n :, here] = dot_nt(work[(step + 1) * n :, here], inv)
             for j in range(step + 1, 4):
                 there = slice(j * n, (j + 1) * n)
                 work[j * n :, there] -= dot_nt(f_ref[j * n :, here], f_ref[there, here])
             before = slice(0, step * n)
             g_ref[here, before] = -dot(inv, dot(f_ref[here, before], g_ref[before, before]))
+            if step == 2:
+                left_ref[...] = work[3 * n :, 3 * n :]
+
+
+def last_kernel(f_ref, g_ref, left_ref, f3_ref, g3_ref, s_ref, e_ref):
+    n = BLOCK
+    old = 3 * n
+    s_ref[...] = left_ref[...]
+    factor_block(s_ref, e_ref)
+    ids = lax.broadcasted_iota(jnp.int32, (n, n), 0)
+    lanes = lax.broadcasted_iota(jnp.int32, (n, n), 1)
+    inv = e_ref[...]
+    f3_ref[:, :old] = f_ref[old:, :old]
+    f3_ref[:, old:] = jnp.where(ids <= lanes, s_ref[...], 0.0).T
+    g3_ref[:, :old] = -dot(inv, dot(f_ref[old:, :old], g_ref[:old, :old]))
+    g3_ref[:, old:] = inv
 
 
 def f32(*shape):
@@ -186,44 +201,70 @@
     )(at, own, got)
 
 
-def factor_rest(f0, g0, rest):
+def factor_middle(f0, g0, rest):
     return pl.pallas_call(
-        second_kernel,
-        grid=(3,),
-        out_shape=[f32(ORDER, ORDER)] * 2,
+        middle_kernel,
+        grid=(2,),
+        out_shape=[f32(ORDER, ORDER), f32(ORDER, ORDER), f32(BLOCK, BLOCK)],
+        in_specs=[VMEM] * 3,
+        out_specs=[VMEM] * 3,
+        scratch_shapes=WORK,
+        compiler_params=pltpu.CompilerParams(vmem_limit_bytes=8 * 2**20),
+        cost_estimate=pl.CostEstimate(flops=12 * 10**9, bytes_accessed=2**20, transcendentals=0),
+    )(f0, g0, rest)
+
+
+def factor_last(fac, inv, left):
+    return pl.pallas_call(
+        last_kernel,
+        out_shape=[f32(BLOCK, ORDER)] * 2,
         in_specs=[VMEM] * 3,
         out_specs=[VMEM] * 2,
-        scratch_shapes=WORK,
+        scratch_shapes=WORK[1:],
         compiler_params=pltpu.CompilerParams(vmem_limit_bytes=8 * 2**20),
-        cost_estimate=pl.CostEstimate(flops=18 * 10**9, bytes_accessed=2**20, transcendentals=0),
-    )(f0, g0, rest)
-
-
-def strip_kernel(top_ref, g_ref, wc_ref, tmp):
+        cost_estimate=pl.CostEstimate(flops=6 * 10**9, bytes_accessed=2**20, transcendentals=0),
+    )(fac, inv, left)
+
+
+def halves(value):
+    high = value.astype(jnp.bfloat16)
+    return high, (value - high.astype(jnp.float32)).astype(jnp.bfloat16)
+
+
+def inverse_rows(g_ref, g3_ref, i):
+    n = BLOCK
+    if i == 3:
+        return g3_ref[...]
+    return g_ref[i * n : (i + 1) * n, : (i + 1) * n]
+
+
+def strip_kernel(at_ref, own_ref, got_ref, g_ref, g3_ref, high_ref, low_ref, z_ref, tmp):
     n = BLOCK
     for i in range(4):
-        for a in range(4):
-            tmp[i * n + a * 32 : i * n + (a + 1) * 32, :] = top_ref[4 * a + i]
+        u = at_ref[0] ^ i
+        tmp[i * n : (i + 1) * n, :] = jnp.where(u % 2 == 0, own_ref[u // 2], got_ref[u // 2])
     for i in range(4):
         here = slice(i * n, (i + 1) * n)
-        wc_ref[here, :] = dot(g_ref[here, : (i + 1) * n], tmp[: (i + 1) * n, :])
-
-
-def strip_solve(top, inv):
-    shape = (ORDER, ORDER + BLOCK)
+        value = dot(inverse_rows(g_ref, g3_ref, i), tmp[: (i + 1) * n, :])
+        high_ref[here, :], low_ref[here, :] = halves(value)
+        z_ref[here, :] = value[:, ORDER:]
+
+
+def strip_solve(at, own, got, inv, inv3):
+    wide = (ORDER, ORDER + BLOCK)
     return pl.pallas_call(
         strip_kernel,
-        out_shape=f32(*shape),
-        in_specs=[VMEM] * 2,
-        out_specs=VMEM,
-        scratch_shapes=[pltpu.VMEM(shape, jnp.float32)],
+        out_shape=[jax.ShapeDtypeStruct(wide, jnp.bfloat16)] * 2 + [f32(ORDER, BLOCK)],
+        in_specs=[SMEM] + [VMEM] * 4,
+        out_specs=[VMEM] * 3,
+        scratch_shapes=[pltpu.VMEM(wide, jnp.float32)],
         compiler_params=pltpu.CompilerParams(vmem_limit_bytes=8 * 2**20),
         cost_estimate=pl.CostEstimate(flops=4 * 10**9, bytes_accessed=4 * 2**20, transcendentals=0),
-    )(top, inv)
-
-
-def update_kernel(at_ref, q0_ref, q1_ref, q2_ref, low_ref, high_ref, f_ref, g_ref, wc_ref,
-                  k_ref, y_ref, out_ref, right_ref, pan, w):
+    )(at, own, got, inv, inv3)
+
+
+def update_kernel(at_ref, q0_ref, q1_ref, q2_ref, low_ref, high_ref, f_ref, f3_ref, g_ref, g3_ref,
+                  wh_ref, wl_ref, z_ref, k_ref, y_ref, out_ref, right_ref, pan, w):
     step = pl.program_id(0)
     row, col = at_ref[2], at_ref[3]
     n = BLOCK
@@ -245,28 +286,35 @@
 
     for i in range(4):
         here = slice(i * n, (i + 1) * n)
-        w[:, here] = dot_nt(pan[:, : (i + 1) * n], g_ref[here, : (i + 1) * n])
+        w[:, here] = dot_nt(pan[:, : (i + 1) * n], inverse_rows(g_ref, g3_ref, i))
 
     first = (at_ref[4 + step] == 0) & (row < 4)
 
+    @pl.when(first & (row < 3))
+    def _():
+        w[:n, :] = f_ref[pl.ds(pl.multiple_of(row * n, n), n), :]
+
+    @pl.when(first & (row == 3))
+    def _():
+        w[:n, :] = f3_ref[...]
+
+    high, low = halves(w[...])
+    once = functools.partial(jnp.dot, preferred_element_type=jnp.float32)
+    change = once(high, wh_ref[...]) + (once(high, wl_ref[...]) + once(low, wh_ref[...]))
+    out_ref[...] = k_ref[...] - change[:, :ORDER]
+    right_ref[...] = y_ref[...] - change[:, ORDER:]
+
     @pl.when(first)
     def _():
-        w[:n, :] = f_ref[pl.ds(pl.multiple_of(row * n, n), n), :]
-
-    out_ref[...] = k_ref[...] - dot(w[...], wc_ref[:, :ORDER])
-    right_ref[...] = y_ref[...] - dot(w[...], wc_ref[:, ORDER:])
-
-    @pl.when(first)
-    def _():
         out_ref[:n, :] = jnp.zeros((n, ORDER), jnp.float32)
-        right_ref[:n, :] = wc_ref[pl.ds(pl.multiple_of(row * n, n), n), ORDER:]
+        right_ref[:n, :] = z_ref[pl.ds(pl.multiple_of(row * n, n), n), :]
 
     @pl.when(col < 4)
     def _():
         out_ref[:, :n] = w[:, pl.ds(pl.multiple_of(col * n, n), n)]
 
 
-def update(at, parts, fac, inv, wc, kernel, targets):
+def update(at, parts, factors, strips, kernel, targets):
     rows = 256
     moved = lambda width: pl.BlockSpec((rows, width), lambda s, at: (at[4 + s], 0))
     return pl.pallas_call(
@@ -275,13 +323,13 @@
         grid_spec=pltpu.PrefetchScalarGridSpec(
             num_scalar_prefetch=1,
             grid=(4,),
-            in_specs=[VMEM] * 8 + [moved(ORDER), moved(BLOCK)],
+            in_specs=[VMEM] * 12 + [moved(ORDER), moved(BLOCK)],
             out_specs=[moved(ORDER), moved(BLOCK)],
             scratch_shapes=[pltpu.VMEM((rows, ORDER), jnp.float32)] * 2,
         ),
         compiler_params=pltpu.CompilerParams(vmem_limit_bytes=16 * 2**20),
         cost_estimate=pl.CostEstimate(flops=10**10, bytes_accessed=6 * 2**20, transcendentals=0),
-    )(at, *parts, fac, inv, wc, kernel, targets)
+    )(at, *parts, *factors, *strips, kernel, targets)
 
 
 def after(value, *others):
@@ -302,6 +350,8 @@
     mirror = [(x * Y + j, x * Y + 7 - j) for x in range(X) for j in range(4)]
     by_two = [(c, c ^ 2) for c in range(COLS)]
     by_one = [(c, c ^ 1) for c in range(COLS)]
+    by_z = [(r, r ^ 2) for r in range(ROWS)]
+    by_core = [(r, r ^ 1) for r in range(ROWS)]
 
     a0 = jnp.where((col_pos < 4) & (row_pos < 4), kernel[:n, :n], 0.0)
     got = [a0]
@@ -310,41 +360,49 @@
         got.append(lax.ppermute(a0, ("row", "col"), pairs))
     a1 = total(got)
 
-    strip = jnp.concatenate([kernel[:n], targets[:n]], axis=1)
-    got = [jnp.where(row_pos < 4, strip[:32], 0.0)]
-    for a in (1, 2, 3):
-        got.append(over_row(strip[32 * a : 32 * a + 32], [(r, r + 4 * a) for r in range(4)]))
-    piece = total(got)
-    top = lax.all_gather(piece, "row")
-
-    panel = kernel[:, :n].reshape(8, n, n)
+    panel = after(kernel[:, :n].reshape(8, n, n), a0)
     got = [jnp.where(x_pos == 0, panel[:2], 0.0)]
     for x in (1, 2, 3):
         got.append(over_col(panel[2 * x : 2 * x + 2], [(j, x * Y + j) for j in range(4)]))
     p1 = total(got)
-
-    a2 = after(a1 + over_col(a1, mirror), piece, p1)
+    a2 = after(a1 + over_col(a1, mirror), p1)
+    p2 = jnp.where(y_pos >= 4, over_col(after(p1, a1), mirror), p1)
     got = [a2]
     for a in (1, 2, 3):
         got.append(over_row(a2, [(r, r + 4 * a) for r in range(4)]))
-    a3 = total(got)
-    p2 = jnp.where(y_pos >= 4, over_col(after(p1, a2), mirror), p1)
+    a3 = after(total(got), p2)
+
+    strip = jnp.concatenate([kernel[:n], targets[:n]], axis=1)
+    strip = after(jnp.where(row_pos < 4, strip, 0.0), a3)
+    c1 = strip + over_row(strip, [(r, r + 12) for r in range(4)])
+
     a4 = jnp.stack([a3, over_col(a3, by_two)])
-    a5 = jnp.stack([a4, over_col(a4, by_one)])
+    a5 = after(jnp.stack([a4, over_col(a4, by_one)]), c1)
     p3 = jnp.stack([p2, over_col(after(p2, a5), by_two)])
-    a6 = jnp.stack([a5, over_row(a5, [(r, r ^ 2) for r in range(ROWS)])])
-    p4 = jnp.stack([p3, over_col(after(p3, a6), by_one)])
-    a7 = over_row(a6, [(r, r ^ 1) for r in range(ROWS)])
+    a6 = after(jnp.stack([a5, over_row(a5, by_z)]), p3)
+    a7 = over_row(a6, by_core)
+    p4_got = over_col(after(p3, a6), by_one)
+    c1 = after(c1, a6)
+    c2_got = over_row(c1, [(r, r + 4) for r in range(4)] + [(r, r - 4) for r in range(12, 16)])
 
     state = factor_first(at, a6, a7)
-    p4 = after(p4, state[1])
+    p4 = jnp.stack([p3, after(p4_got, state[1])])
+    c2 = c1 + after(c2_got, state[1])
     down = over_col(p4, [(c, (c + Y) % COLS) for c in range(COLS)])
     up = over_col(p4, [(c, (c - Y) % COLS) for c in range(COLS)])
-    fac, inv = factor_rest(*state)
-    low = over_col(after(up[0], inv), [(c, (c - Y) % COLS) for c in range(COLS)])
-    high = over_col(after(down[1], inv), [(c, (c + Y) % COLS) for c in range(COLS)])
-    wc = strip_solve(top, inv)
-    return tuple(update(at, (p4, down, up, low, high), fac, inv, wc, kernel, targets))
+    c3_got = over_row(c2, by_z)
+    fac, inv, left = factor_middle(*state)
+    down, up = after(down, left), after(up, left)
+    c3 = jnp.stack([c2, after(c3_got, left)])
+    near, far = up[0], down[1]
+    low = over_col(near, [(c, (c - Y) % COLS) for c in range(COLS)])
+    high = over_col(far, [(c, (c + Y) % COLS) for c in range(COLS)])
+    c4 = over_row(c3, by_core)
+    fac3, inv3 = factor_last(fac, inv, after(left, near, far, c3))
+    strips = strip_solve(at, c3, c4, inv, inv3)
+    return tuple(
+        update(at, (p4, down, up, low, high), (fac, fac3, inv, inv3), strips, kernel, targets)
+    )
 
 
 def solution(mesh):

time: 163 us -> 138 us (0.85)
  the two profiles are of different devices: /device:TPU:56 before, /device:TPU:1 now
where the time goes in v2:
time: 138 us; the launch traced here: 137 us
  starting transfers between devices  78.4 us (57%)
  Pallas kernels  40.1 us (29%)
  waiting for transfers between devices  14.4 us (10%)
  other arithmetic  2.12 us (2%)
    ppermute x13, starting transfers between devices, over_col(): return lax.ppermute(value, 'col', pairs)  42.1 us
    ppermute x9, starting transfers between devices, over_row(): return lax.ppermute(value, 'row', pairs)  28.1 us
    pallas_call x1, Pallas kernels, update(): pl.pallas_call(update_kernel, out_shape=[f32(*kernel.shape), f32(*targets...  13.7 us
    pallas_call x1, Pallas kernels, factor_middle(): pl.pallas_call(middle_kernel, grid=(2,), out_shape=[f32(ORDER, ORDER), f3...  11.3 us
    ppermute x13, waiting for transfers between devices, over_col(): return lax.ppermute(value, 'col', pairs)  10.5 us
    ppermute x3, starting transfers between devices, per_device(): got.append(lax.ppermute(a0, ('row', 'col'), pairs))  8.2 us
    pallas_call x1, Pallas kernels, factor_first(): pl.pallas_call(first_kernel, out_shape=[f32(ORDER, BLOCK), f32(BLOCK, BLO...  6.92 us
    pallas_call x1, Pallas kernels, factor_last(): pl.pallas_call(last_kernel, out_shape=[f32(BLOCK, ORDER)] * 2, in_specs=[...  5.47 us
  transfers between devices with their start and end apart: 25, of which 6 were waited for; matrix products, arithmetic and copies ran while one was open for 2% of the time, Pallas kernels for 19%

profile of v2, /device:TPU:1, one launch (start us, length us, event | category | flops | bytes accessed | tf_op | source)
XLA Modules:
  0.0 137.5 jit_solution(10676097379608892117)
XLA Ops:
  0.6 0.8 slice_select_fusion
  1.5 5.6 %collective-permute-start.4 = (f32[128,128]{1,0:T(8,128)S(1)}, f32[128,128]{1,0:T(8,128)S(1)}, u32[]{:S(2)}, u32[]{:S(2)}) collective-permute-start(f32[128,128]{1,0:T(8,128)S(1)} %slice_select_fusion), channel_id=1, source_target_pairs={{0,16},{1,17},{2,18},{3,19},{32,48},{33,49},{34,50},{35,51},{64,80... | collective-permute-start | bytes 196616 | tf_op jit(solution)/shard_map/ppermute | solution.py:360
  7.1 1.3 collective-permute-start.5
  8.4 1.3 collective-permute-start.3
  9.7 1.1 slice.30
  10.8 1.3 collective-permute-start
  12.1 1.3 collective-permute-start.2
  13.4 0.0 collective-permute-done.4
  13.5 1.3 collective-permute-start.1
  14.8 0.0 collective-permute-done.3
  14.8 0.9 add_add_fusion.2
  15.7 1.3 collective-permute-start.7
  17.0 1.3 collective-permute-done.7
  18.3 0.0 collective-permute-done.2
  18.3 0.0 collective-permute-done.1
  18.3 7.9 %collective-permute-start.10 = (f32[128,128]{1,0:T(8,128)S(1)}, f32[128,128]{1,0:T(8,128)S(1)}, u32[]{:S(2)}, u32[]{:S(2)}) collective-permute-start(f32[128,128]{1,0:T(8,128)S(1)} %add.67), channel_id=1, source_target_pairs={{0,384},{32,416},{64,448},{96,480},{1,385},{33,417},{65,449},{97,4... | collective-permute-start | bytes 196616 | tf_op jit(solution)/shard_map/ppermute | solution.py:22
  26.2 1.3 collective-permute-start.9
  27.5 1.3 collective-permute-start.8
  28.8 4.9 %collective-permute-start.6 = (f32[2,128,128]{2,1,0:T(8,128)S(1)}, f32[2,128,128]{2,1,0:T(8,128)S(1)}, u32[]{:S(2)}, u32[]{:S(2)}) collective-permute-start(f32[2,128,128]{2,1,0:T(8,128)S(1)} %add_add_fusion), channel_id=1, source_target_pairs={{0,7},{1,6},{2,5},{3,4},{8,15},{9,14},{10,13},{11,12},{16,23},{17,... | collective-permute-start | bytes 393224 | tf_op jit(solution)/shard_map/ppermute | solution.py:18
  33.8 1.9 %collective-permute-done.6 = f32[2,128,128]{2,1,0:T(8,128)S(1)} collective-permute-done((f32[2,128,128]{2,1,0:T(8,128)S(1)}, f32[2,128,128]{2,1,0:T(8,128)S(1)}, u32[]{:S(2)}, u32[]{:S(2)}) %collective-permute-start.6) | collective-permute-done | bytes 131104 | tf_op jit(solution)/shard_map/ppermute | solution.py:18
  35.7 0.0 copy-start.2
  35.7 6.1 %collective-permute-start.11 = (f32[128,128]{1,0:T(8,128)S(1)}, f32[128,128]{1,0:T(8,128)S(1)}, u32[]{:S(2)}, u32[]{:S(2)}) collective-permute-start(f32[128,128]{1,0:T(8,128)S(1)} %add_add_fusion.1), channel_id=1, source_target_pairs={{0,2},{1,3},{2,0},{3,1},{4,6},{5,7},{6,4},{7,5},{8,10},{9,11},{10,... | collective-permute-start | bytes 196616 | tf_op jit(solution)/shard_map/ppermute | solution.py:18
  41.9 1.3 collective-permute-start.13
  43.2 0.3 collective-permute-done.11
  43.5 6.9 %collective-permute-start.12 = (f32[2,128,128]{2,1,0:T(8,128)S(1)}, f32[2,128,128]{2,1,0:T(8,128)S(1)}, u32[]{:S(2)}, u32[]{:S(2)}) collective-permute-start(f32[2,128,128]{2,1,0:T(8,128)S(1)} %get-tuple-element.62), channel_id=1, source_target_pairs={{0,1},{1,0},{2,3},{3,2},{4,5},{5,4},{6,7},{7,6},{8,9},{9,8},{10,11... | collective-permute-start | bytes 393224 | tf_op jit(solution)/shard_map/ppermute | solution.py:18
  50.4 2.3 %collective-permute-done.12 = f32[2,128,128]{2,1,0:T(8,128)S(1)} collective-permute-done((f32[2,128,128]{2,1,0:T(8,128)S(1)}, f32[2,128,128]{2,1,0:T(8,128)S(1)}, u32[]{:S(2)}, u32[]{:S(2)}) %collective-permute-start.12) | collective-permute-done | bytes 131104 | tf_op jit(solution)/shard_map/ppermute | solution.py:18
  52.7 3.9 %collective-permute-done.13 = f32[128,640]{1,0:T(8,128)S(1)} collective-permute-done((f32[128,640]{1,0:T(8,128)S(1)}, f32[128,640]{1,0:T(8,128)S(1)}, u32[]{:S(2)}, u32[]{:S(2)}) %collective-permute-start.13) | collective-permute-done | bytes 327712 | tf_op jit(solution)/shard_map/ppermute | solution.py:22
  56.7 1.9 %collective-permute-start.15 = (f32[2,2,128,128]{3,2,1,0:T(8,128)S(1)}, f32[2,2,128,128]{3,2,1,0:T(8,128)S(1)}, u32[]{:S(2)}, u32[]{:S(2)}) collective-permute-start(f32[2,2,128,128]{3,2,1,0:T(8,128)S(1)} %pad_maximum_fusion.3), channel_id=1, source_target_pairs={{0,64},{32,96},{64,0},{96,32},{128,192},{160,224},{192,128},{224,1... | collective-permute-start | bytes 786440 | tf_op jit(solution)/shard_map/ppermute | solution.py:22
  58.6 1.9 %collective-permute-start.14 = (f32[2,128,128]{2,1,0:T(8,128)S(1)}, f32[2,128,128]{2,1,0:T(8,128)S(1)}, u32[]{:S(2)}, u32[]{:S(2)}) collective-permute-start(f32[2,128,128]{2,1,0:T(8,128)S(1)} %broadcast_select_fusion), channel_id=1, source_target_pairs={{0,2},{1,3},{2,0},{3,1},{4,6},{5,7},{6,4},{7,5},{8,10},{9,11},{10,... | collective-permute-start | bytes 393224 | tf_op jit(solution)/shard_map/ppermute | solution.py:18
  60.5 4.7 %collective-permute-done.14 = f32[2,128,128]{2,1,0:T(8,128)S(1)} collective-permute-done((f32[2,128,128]{2,1,0:T(8,128)S(1)}, f32[2,128,128]{2,1,0:T(8,128)S(1)}, u32[]{:S(2)}, u32[]{:S(2)}) %collective-permute-start.14) | collective-permute-done | bytes 131104 | tf_op jit(solution)/shard_map/ppermute | solution.py:18
  65.3 0.1 pad_maximum_fusion.1.own_ref
  65.3 5.0 %collective-permute-start.17 = (f32[2,2,2,128,128]{4,3,2,1,0:T(8,128)S(1)}, f32[2,2,2,128,128]{4,3,2,1,0:T(8,128)S(1)}, u32[]{:S(2)}, u32[]{:S(2)}) collective-permute-start(f32[2,2,2,128,128]{4,3,2,1,0:T(8,128)S(1)} %pad_maximum_fusion.1.own_ref), channel_id=1, source_target_pairs={{0,32},{32,0},{64,96},{96,64},{128,160},{160,128},{192,224},{224,1... | collective-permute-start | bytes 1572872 | tf_op jit(solution)/shard_map/ppermute | solution.py:22
  70.4 0.1 concatenate.6.at_ref
  70.5 6.3 %collective-permute-start.16 = (f32[2,2,128,128]{3,2,1,0:T(8,128)S(1)}, f32[2,2,128,128]{3,2,1,0:T(8,128)S(1)}, u32[]{:S(2)}, u32[]{:S(2)}) collective-permute-start(f32[2,2,128,128]{3,2,1,0:T(8,128)S(1)} %get-tuple-element.37), channel_id=1, source_target_pairs={{0,1},{1,0},{2,3},{3,2},{4,5},{5,4},{6,7},{7,6},{8,9},{9,8},{10,11... | collective-permute-start | bytes 786440 | tf_op jit(solution)/shard_map/ppermute | solution.py:18
  76.8 1.3 collective-permute-start.22
  78.1 6.9 %shard_map.50 = (f32[512,128]{1,0:T(8,128)S(1)}, f32[128,128]{1,0:T(8,128)S(1)}, f32[384,384]{1,0:T(8,128)S(1)}) custom-call(s32[8]{0:T(128)S(1)} %concatenate.6.at_ref, f32[2,2,2,128,128]{4,3,2,1,0:T(8,128)S(1)} %pad_maximum_fusion.1.own_ref, f32[2,2,2,128,128]{4,3,2,1,0:T(8,128)S(1)} %collective-permute-done.17.got_ref), custom_call_target="tpu_custom_call" | custom-call | flops 6000000000 | bytes 1048576 | tf_op jit(solution)/shard_map/pallas_call | solution.py:193
  85.1 1.9 %collective-permute-start.19 = (f32[2,2,2,128,128]{4,3,2,1,0:T(8,128)S(1)}, f32[2,2,2,128,128]{4,3,2,1,0:T(8,128)S(1)}, u32[]{:S(2)}, u32[]{:S(2)}) collective-permute-start(f32[2,2,2,128,128]{4,3,2,1,0:T(8,128)S(1)} %pad_maximum_fusion.2.q0_ref), channel_id=1, source_target_pairs={{0,24},{1,25},{2,26},{3,27},{4,28},{5,29},{6,30},{7,31},{8,0},{9,1... | collective-permute-start | bytes 1572872 | tf_op jit(solution)/shard_map/ppermute | solution.py:18
  87.1 3.4 %collective-permute-start.18 = (f32[2,2,2,128,128]{4,3,2,1,0:T(8,128)S(1)}, f32[2,2,2,128,128]{4,3,2,1,0:T(8,128)S(1)}, u32[]{:S(2)}, u32[]{:S(2)}) collective-permute-start(f32[2,2,2,128,128]{4,3,2,1,0:T(8,128)S(1)} %pad_maximum_fusion.2.q0_ref), channel_id=1, source_target_pairs={{0,8},{1,9},{2,10},{3,11},{4,12},{5,13},{6,14},{7,15},{8,16},{9,17... | collective-permute-start | bytes 1572872 | tf_op jit(solution)/shard_map/ppermute | solution.py:18
  90.5 5.4 %collective-permute-start.23 = (f32[128,640]{1,0:T(8,128)S(1)}, f32[128,640]{1,0:T(8,128)S(1)}, u32[]{:S(2)}, u32[]{:S(2)}) collective-permute-start(f32[128,640]{1,0:T(8,128)S(1)} %add.72), channel_id=1, source_target_pairs={{0,64},{32,96},{64,0},{96,32},{128,192},{160,224},{192,128},{224,1... | collective-permute-start | bytes 983048 | tf_op jit(solution)/shard_map/ppermute | solution.py:22
  95.9 11.3 %shard_map.51 = (f32[512,512]{1,0:T(8,128)S(1)}, f32[512,512]{1,0:T(8,128)S(1)}, f32[128,128]{1,0:T(8,128)S(1)}) custom-call(f32[512,128]{1,0:T(8,128)S(1)} %get-tuple-element.40.f0_ref, f32[128,128]{1,0:T(8,128)S(1)} %get-tuple-element.38.g0_ref, f32[384,384]{1,0:T(8,128)S(1)} %get-tuple-element.41.rest_ref), custom_call_target="tpu_custom_call" | custom-call | flops 12000000000 | bytes 1048576 | tf_op jit(solution)/shard_map/pallas_call | solution.py:205
  107.3 2.6 %collective-permute-start.24 = (f32[2,128,640]{2,1,0:T(8,128)S(1)}, f32[2,128,640]{2,1,0:T(8,128)S(1)}, u32[]{:S(2)}, u32[]{:S(2)}) collective-permute-start(f32[2,128,640]{2,1,0:T(8,128)S(1)} %pad_maximum_fusion.own_ref), channel_id=1, source_target_pairs={{0,32},{32,0},{64,96},{96,64},{128,160},{160,128},{192,224},{224,1... | collective-permute-start | bytes 1966088 | tf_op jit(solution)/shard_map/ppermute | solution.py:22
  110.0 1.9 %collective-permute-start.20 = (f32[2,2,128,128]{3,2,1,0:T(8,128)S(1)}, f32[2,2,128,128]{3,2,1,0:T(8,128)S(1)}, u32[]{:S(2)}, u32[]{:S(2)}) collective-permute-start(f32[2,2,128,128]{3,2,1,0:T(8,128)S(1)} %slice_bitcast_fusion.1), channel_id=1, source_target_pairs={{0,24},{1,25},{2,26},{3,27},{4,28},{5,29},{6,30},{7,31},{8,0},{9,1... | collective-permute-start | bytes 786440 | tf_op jit(solution)/shard_map/ppermute | solution.py:18
  112.0 3.6 %collective-permute-start.21 = (f32[2,2,128,128]{3,2,1,0:T(8,128)S(1)}, f32[2,2,128,128]{3,2,1,0:T(8,128)S(1)}, u32[]{:S(2)}, u32[]{:S(2)}) collective-permute-start(f32[2,2,128,128]{3,2,1,0:T(8,128)S(1)} %slice_bitcast_fusion), channel_id=1, source_target_pairs={{0,8},{1,9},{2,10},{3,11},{4,12},{5,13},{6,14},{7,15},{8,16},{9,17... | collective-permute-start | bytes 786440 | tf_op jit(solution)/shard_map/ppermute | solution.py:18
  115.6 5.5 %shard_map.52 = (f32[128,512]{1,0:T(8,128)S(1)}, f32[128,512]{1,0:T(8,128)S(1)}) custom-call(f32[512,512]{1,0:T(8,128)S(1)} %get-tuple-element.45.f_ref, f32[512,512]{1,0:T(8,128)S(1)} %get-tuple-element.46.g_ref, f32[128,128]{1,0:T(8,128)S(1)} %get-tuple-element.50.left_ref), custom_call_target="tpu_custom_call" | custom-call | flops 6000000000 | bytes 1048576 | tf_op jit(solution)/shard_map/pallas_call | solution.py:218
  121.1 0.0 copy-start
  121.1 0.0 copy-start.1
  121.1 2.6 %shard_map.53 = (bf16[512,640]{1,0:T(8,128)(2,1)S(1)}, bf16[512,640]{1,0:T(8,128)(2,1)S(1)}, f32[512,128]{1,0:T(8,128)S(1)}) custom-call(s32[8]{0:T(128)S(1)} %concatenate.6.at_ref, f32[2,128,640]{2,1,0:T(8,128)S(1)} %pad_maximum_fusion.own_ref, f32[2,128,640]{2,1,0:T(8,128)S(1)} %collective-permute-done.24.got_ref, f32[512,512]{1,0:T(8,128)S(1)} %get-tuple-element.46.g_ref, ...), custom_call_target="tpu_custom_call" | custom-call | flops 4000000000 | bytes 4194304 | tf_op jit(solution)/shard_map/pallas_call | solution.py:255
  123.7 13.7 %shard_map.54 = (f32[1024,512]{1,0:T(8,128)}, f32[1024,128]{1,0:T(8,128)}) custom-call(s32[8]{0:T(128)S(1)} %concatenate.6.at_ref, f32[2,2,2,128,128]{4,3,2,1,0:T(8,128)S(1)} %pad_maximum_fusion.2.q0_ref, f32[2,2,2,128,128]{4,3,2,1,0:T(8,128)S(1)} %collective-permute-done.18.q1_ref, f32[2,2,2,128,128]{4,3,2,1,0:T(8,128)S(1)} %collective-permute-done.19.q2_ref, ...), custom_call_target="tpu_custom_call" | custom-call | flops 10000000000 | bytes 6291456 | tf_op jit(solution)/shard_map/pallas_call | solution.py:320
  (38 shorter events, 0.5 us)
Async XLA Ops:
  1.5 40.3 %slice-start = ((f32[1024,512]{1,0:T(8,128)}), f32[128,512]{1,0:T(8,128)S(1)}, s32[]{:S(2)}) async-start(f32[1024,512]{1,0:T(8,128)} %k_ref.1), calls=%async_computation | async-start | bytes 524288 | tf_op jit(solution)/shard_map/slice | solution.py:375
  1.5 40.3 %slice-start.1 = ((f32[1024,128]{1,0:T(8,128)}), f32[128,128]{1,0:T(8,128)S(1)}, s32[]{:S(2)}) async-start(f32[1024,128]{1,0:T(8,128)} %y_ref.1), calls=%async_computation.1 | async-start | bytes 131072 | tf_op jit(solution)/shard_map/slice | solution.py:375
  1.5 12.0 %collective-permute-start.4 = (f32[128,128]{1,0:T(8,128)S(1)}, f32[128,128]{1,0:T(8,128)S(1)}, u32[]{:S(2)}, u32[]{:S(2)}) collective-permute-start(f32[128,128]{1,0:T(8,128)S(1)} %slice_select_fusion), channel_id=1, source_target_pairs={{0,16},{1,17},{2,18},{3,19},{32,48},{33,49},{34,50},{35,51},{64,80... | collective-permute-start | bytes 196616 | tf_op jit(solution)/shard_map/ppermute | solution.py:360
  7.1 7.6 %collective-permute-start.5 = (f32[128,128]{1,0:T(8,128)S(1)}, f32[128,128]{1,0:T(8,128)S(1)}, u32[]{:S(2)}, u32[]{:S(2)}) collective-permute-start(f32[128,128]{1,0:T(8,128)S(1)} %slice_select_fusion), channel_id=1, source_target_pairs={{0,24},{1,25},{2,26},{3,27},{32,56},{33,57},{34,58},{35,59},{64,88... | collective-permute-start | bytes 196616 | tf_op jit(solution)/shard_map/ppermute | solution.py:360
  8.4 6.4 %collective-permute-start.3 = (f32[128,128]{1,0:T(8,128)S(1)}, f32[128,128]{1,0:T(8,128)S(1)}, u32[]{:S(2)}, u32[]{:S(2)}) collective-permute-start(f32[128,128]{1,0:T(8,128)S(1)} %slice_select_fusion), channel_id=1, source_target_pairs={{0,8},{1,9},{2,10},{3,11},{32,40},{33,41},{34,42},{35,43},{64,72},... | collective-permute-start | bytes 196616 | tf_op jit(solution)/shard_map/ppermute | solution.py:360
  10.8 7.4 %collective-permute-start = (f32[2,128,128]{2,1,0:T(8,128)S(1)}, f32[2,128,128]{2,1,0:T(8,128)S(1)}, u32[]{:S(2)}, u32[]{:S(2)}) collective-permute-start(f32[2,128,128]{2,1,0:T(8,128)S(1)} %get-tuple-element.56), channel_id=1, source_target_pairs={{0,8},{1,9},{2,10},{3,11},{32,40},{33,41},{34,42},{35,43},{64,72},... | collective-permute-start | bytes 393224 | tf_op jit(solution)/shard_map/ppermute | solution.py:18
  12.1 6.1 %collective-permute-start.2 = (f32[2,128,128]{2,1,0:T(8,128)S(1)}, f32[2,128,128]{2,1,0:T(8,128)S(1)}, u32[]{:S(2)}, u32[]{:S(2)}) collective-permute-start(f32[2,128,128]{2,1,0:T(8,128)S(1)} %get-tuple-element.57), channel_id=1, source_target_pairs={{0,24},{1,25},{2,26},{3,27},{32,56},{33,57},{34,58},{35,59},{64,88... | collective-permute-start | bytes 393224 | tf_op jit(solution)/shard_map/ppermute | solution.py:18
  13.5 4.8 %collective-permute-start.1 = (f32[2,128,128]{2,1,0:T(8,128)S(1)}, f32[2,128,128]{2,1,0:T(8,128)S(1)}, u32[]{:S(2)}, u32[]{:S(2)}) collective-permute-start(f32[2,128,128]{2,1,0:T(8,128)S(1)} %get-tuple-element.58), channel_id=1, source_target_pairs={{0,16},{1,17},{2,18},{3,19},{32,48},{33,49},{34,50},{35,51},{64,80... | collective-permute-start | bytes 393224 | tf_op jit(solution)/shard_map/ppermute | solution.py:18
  15.7 2.6 %collective-permute-start.7 = (f32[128,128]{1,0:T(8,128)S(1)}, f32[128,128]{1,0:T(8,128)S(1)}, u32[]{:S(2)}, u32[]{:S(2)}) collective-permute-start(f32[128,128]{1,0:T(8,128)S(1)} %add_add_fusion.2), channel_id=1, source_target_pairs={{0,7},{1,6},{2,5},{3,4},{8,15},{9,14},{10,13},{11,12},{16,23},{17,... | collective-permute-start | bytes 196616 | tf_op jit(solution)/shard_map/ppermute | solution.py:18
  18.3 15.4 %collective-permute-start.10 = (f32[128,128]{1,0:T(8,128)S(1)}, f32[128,128]{1,0:T(8,128)S(1)}, u32[]{:S(2)}, u32[]{:S(2)}) collective-permute-start(f32[128,128]{1,0:T(8,128)S(1)} %add.67), channel_id=1, source_target_pairs={{0,384},{32,416},{64,448},{96,480},{1,385},{33,417},{65,449},{97,4... | collective-permute-start | bytes 196616 | tf_op jit(solution)/shard_map/ppermute | solution.py:22
  26.2 7.5 %collective-permute-start.9 = (f32[128,128]{1,0:T(8,128)S(1)}, f32[128,128]{1,0:T(8,128)S(1)}, u32[]{:S(2)}, u32[]{:S(2)}) collective-permute-start(f32[128,128]{1,0:T(8,128)S(1)} %add.67), channel_id=1, source_target_pairs={{0,256},{32,288},{64,320},{96,352},{1,257},{33,289},{65,321},{97,3... | collective-permute-start | bytes 196616 | tf_op jit(solution)/shard_map/ppermute | solution.py:22
  27.5 6.3 %collective-permute-start.8 = (f32[128,128]{1,0:T(8,128)S(1)}, f32[128,128]{1,0:T(8,128)S(1)}, u32[]{:S(2)}, u32[]{:S(2)}) collective-permute-start(f32[128,128]{1,0:T(8,128)S(1)} %add.67), channel_id=1, source_target_pairs={{0,128},{32,160},{64,192},{96,224},{1,129},{33,161},{65,193},{97,2... | collective-permute-start | bytes 196616 | tf_op jit(solution)/shard_map/ppermute | solution.py:22
  28.8 6.8 %collective-permute-start.6 = (f32[2,128,128]{2,1,0:T(8,128)S(1)}, f32[2,128,128]{2,1,0:T(8,128)S(1)}, u32[]{:S(2)}, u32[]{:S(2)}) collective-permute-start(f32[2,128,128]{2,1,0:T(8,128)S(1)} %add_add_fusion), channel_id=1, source_target_pairs={{0,7},{1,6},{2,5},{3,4},{8,15},{9,14},{10,13},{11,12},{16,23},{17,... | collective-permute-start | bytes 393224 | tf_op jit(solution)/shard_map/ppermute | solution.py:18
  35.7 34.7 %copy-start.2 = (s32[4]{0:T(128)S(1)}, s32[4]{0:T(128)}, u32[]{:S(2)}) copy-start(s32[4]{0:T(128)} %constant.58.clone) | copy-start | bytes 52
  35.7 7.7 %collective-permute-start.11 = (f32[128,128]{1,0:T(8,128)S(1)}, f32[128,128]{1,0:T(8,128)S(1)}, u32[]{:S(2)}, u32[]{:S(2)}) collective-permute-start(f32[128,128]{1,0:T(8,128)S(1)} %add_add_fusion.1), channel_id=1, source_target_pairs={{0,2},{1,3},{2,0},{3,1},{4,6},{5,7},{6,4},{7,5},{8,10},{9,11},{10,... | collective-permute-start | bytes 196616 | tf_op jit(solution)/shard_map/ppermute | solution.py:18
  41.9 14.8 %collective-permute-start.13 = (f32[128,640]{1,0:T(8,128)S(1)}, f32[128,640]{1,0:T(8,128)S(1)}, u32[]{:S(2)}, u32[]{:S(2)}) collective-permute-start(f32[128,640]{1,0:T(8,128)S(1)} %maximum_select_fusion), channel_id=1, source_target_pairs={{0,384},{32,416},{64,448},{96,480},{1,385},{33,417},{65,449},{97,4... | collective-permute-start | bytes 983048 | tf_op jit(solution)/shard_map/ppermute | solution.py:22
  43.5 9.3 %collective-permute-start.12 = (f32[2,128,128]{2,1,0:T(8,128)S(1)}, f32[2,128,128]{2,1,0:T(8,128)S(1)}, u32[]{:S(2)}, u32[]{:S(2)}) collective-permute-start(f32[2,128,128]{2,1,0:T(8,128)S(1)} %get-tuple-element.62), channel_id=1, source_target_pairs={{0,1},{1,0},{2,3},{3,2},{4,5},{5,4},{6,7},{7,6},{8,9},{9,8},{10,11... | collective-permute-start | bytes 393224 | tf_op jit(solution)/shard_map/ppermute | solution.py:18
  56.7 8.6 %collective-permute-start.15 = (f32[2,2,128,128]{3,2,1,0:T(8,128)S(1)}, f32[2,2,128,128]{3,2,1,0:T(8,128)S(1)}, u32[]{:S(2)}, u32[]{:S(2)}) collective-permute-start(f32[2,2,128,128]{3,2,1,0:T(8,128)S(1)} %pad_maximum_fusion.3), channel_id=1, source_target_pairs={{0,64},{32,96},{64,0},{96,32},{128,192},{160,224},{192,128},{224,1... | collective-permute-start | bytes 786440 | tf_op jit(solution)/shard_map/ppermute | solution.py:22
  58.6 6.6 %collective-permute-start.14 = (f32[2,128,128]{2,1,0:T(8,128)S(1)}, f32[2,128,128]{2,1,0:T(8,128)S(1)}, u32[]{:S(2)}, u32[]{:S(2)}) collective-permute-start(f32[2,128,128]{2,1,0:T(8,128)S(1)} %broadcast_select_fusion), channel_id=1, source_target_pairs={{0,2},{1,3},{2,0},{3,1},{4,6},{5,7},{6,4},{7,5},{8,10},{9,11},{10,... | collective-permute-start | bytes 393224 | tf_op jit(solution)/shard_map/ppermute | solution.py:18
  65.3 12.8 %collective-permute-start.17 = (f32[2,2,2,128,128]{4,3,2,1,0:T(8,128)S(1)}, f32[2,2,2,128,128]{4,3,2,1,0:T(8,128)S(1)}, u32[]{:S(2)}, u32[]{:S(2)}) collective-permute-start(f32[2,2,2,128,128]{4,3,2,1,0:T(8,128)S(1)} %pad_maximum_fusion.1.own_ref), channel_id=1, source_target_pairs={{0,32},{32,0},{64,96},{96,64},{128,160},{160,128},{192,224},{224,1... | collective-permute-start | bytes 1572872 | tf_op jit(solution)/shard_map/ppermute | solution.py:22
  70.5 14.6 %collective-permute-start.16 = (f32[2,2,128,128]{3,2,1,0:T(8,128)S(1)}, f32[2,2,128,128]{3,2,1,0:T(8,128)S(1)}, u32[]{:S(2)}, u32[]{:S(2)}) collective-permute-start(f32[2,2,128,128]{3,2,1,0:T(8,128)S(1)} %get-tuple-element.37), channel_id=1, source_target_pairs={{0,1},{1,0},{2,3},{3,2},{4,5},{5,4},{6,7},{7,6},{8,9},{9,8},{10,11... | collective-permute-start | bytes 786440 | tf_op jit(solution)/shard_map/ppermute | solution.py:18
  76.8 13.6 %collective-permute-start.22 = (f32[128,640]{1,0:T(8,128)S(1)}, f32[128,640]{1,0:T(8,128)S(1)}, u32[]{:S(2)}, u32[]{:S(2)}) collective-permute-start(f32[128,640]{1,0:T(8,128)S(1)} %add.71), channel_id=1, source_target_pairs={{0,128},{32,160},{64,192},{96,224},{384,256},{416,288},{448,320},{... | collective-permute-start | bytes 983048 | tf_op jit(solution)/shard_map/ppermute | solution.py:22
  85.1 24.9 %collective-permute-start.19 = (f32[2,2,2,128,128]{4,3,2,1,0:T(8,128)S(1)}, f32[2,2,2,128,128]{4,3,2,1,0:T(8,128)S(1)}, u32[]{:S(2)}, u32[]{:S(2)}) collective-permute-start(f32[2,2,2,128,128]{4,3,2,1,0:T(8,128)S(1)} %pad_maximum_fusion.2.q0_ref), channel_id=1, source_target_pairs={{0,24},{1,25},{2,26},{3,27},{4,28},{5,29},{6,30},{7,31},{8,0},{9,1... | collective-permute-start | bytes 1572872 | tf_op jit(solution)/shard_map/ppermute | solution.py:18
  87.1 22.9 %collective-permute-start.18 = (f32[2,2,2,128,128]{4,3,2,1,0:T(8,128)S(1)}, f32[2,2,2,128,128]{4,3,2,1,0:T(8,128)S(1)}, u32[]{:S(2)}, u32[]{:S(2)}) collective-permute-start(f32[2,2,2,128,128]{4,3,2,1,0:T(8,128)S(1)} %pad_maximum_fusion.2.q0_ref), channel_id=1, source_target_pairs={{0,8},{1,9},{2,10},{3,11},{4,12},{5,13},{6,14},{7,15},{8,16},{9,17... | collective-permute-start | bytes 1572872 | tf_op jit(solution)/shard_map/ppermute | solution.py:18
  90.5 16.8 %collective-permute-start.23 = (f32[128,640]{1,0:T(8,128)S(1)}, f32[128,640]{1,0:T(8,128)S(1)}, u32[]{:S(2)}, u32[]{:S(2)}) collective-permute-start(f32[128,640]{1,0:T(8,128)S(1)} %add.72), channel_id=1, source_target_pairs={{0,64},{32,96},{64,0},{96,32},{128,192},{160,224},{192,128},{224,1... | collective-permute-start | bytes 983048 | tf_op jit(solution)/shard_map/ppermute | solution.py:22
  107.3 13.7 %collective-permute-start.24 = (f32[2,128,640]{2,1,0:T(8,128)S(1)}, f32[2,128,640]{2,1,0:T(8,128)S(1)}, u32[]{:S(2)}, u32[]{:S(2)}) collective-permute-start(f32[2,128,640]{2,1,0:T(8,128)S(1)} %pad_maximum_fusion.own_ref), channel_id=1, source_target_pairs={{0,32},{32,0},{64,96},{96,64},{128,160},{160,128},{192,224},{224,1... | collective-permute-start | bytes 1966088 | tf_op jit(solution)/shard_map/ppermute | solution.py:22
  110.0 13.6 %collective-permute-start.20 = (f32[2,2,128,128]{3,2,1,0:T(8,128)S(1)}, f32[2,2,128,128]{3,2,1,0:T(8,128)S(1)}, u32[]{:S(2)}, u32[]{:S(2)}) collective-permute-start(f32[2,2,128,128]{3,2,1,0:T(8,128)S(1)} %slice_bitcast_fusion.1), channel_id=1, source_target_pairs={{0,24},{1,25},{2,26},{3,27},{4,28},{5,29},{6,30},{7,31},{8,0},{9,1... | collective-permute-start | bytes 786440 | tf_op jit(solution)/shard_map/ppermute | solution.py:18
  112.0 11.7 %collective-permute-start.21 = (f32[2,2,128,128]{3,2,1,0:T(8,128)S(1)}, f32[2,2,128,128]{3,2,1,0:T(8,128)S(1)}, u32[]{:S(2)}, u32[]{:S(2)}) collective-permute-start(f32[2,2,128,128]{3,2,1,0:T(8,128)S(1)} %slice_bitcast_fusion), channel_id=1, source_target_pairs={{0,8},{1,9},{2,10},{3,11},{4,12},{5,13},{6,14},{7,15},{8,16},{9,17... | collective-permute-start | bytes 786440 | tf_op jit(solution)/shard_map/ppermute | solution.py:18
  121.1 2.6 %copy-start = (f32[1024,512]{1,0:T(8,128)S(1)}, f32[1024,512]{1,0:T(8,128)}, u32[]{:S(2)}) copy-start(f32[1024,512]{1,0:T(8,128)} %k_ref.1) | copy-start | bytes 6291460
  121.1 2.6 %copy-start.1 = (f32[1024,128]{1,0:T(8,128)S(1)}, f32[1024,128]{1,0:T(8,128)}, u32[]{:S(2)}) copy-start(f32[1024,128]{1,0:T(8,128)} %y_ref.1) | copy-start | bytes 1572868

commit v3 on v1

v3 whole, which is shorter than its diff:
```python
import functools

import jax
import jax.numpy as jnp
from jax import lax
from jax.experimental import pallas as pl
from jax.experimental.pallas import tpu as pltpu
from jax.sharding import PartitionSpec as P

BLOCK = 128
ORDER = 512
X, Y = 4, 8
ROWS, COLS = 16, 32
HI = lax.Precision.HIGHEST


def over_col(value, pairs):
    return lax.ppermute(value, "col", pairs)


def over_row(value, pairs):
    return lax.ppermute(value, "row", pairs)


def dot(a, b):
    return lax.dot_general(
        a, b, (((1,), (0,)), ((), ())), precision=HI, preferred_element_type=jnp.float32
    )


def dot_nt(a, b):
    return lax.dot_general(
        a, b, (((1,), (1,)), ((), ())), precision=HI, preferred_element_type=jnp.float32
    )


def spread(value):
    return jnp.broadcast_to(value, (8, BLOCK))


def total(terms):
    terms = list(terms)
    while len(terms) > 1:
        terms = [sum(terms[i + 1 : i + 2], terms[i]) for i in range(0, len(terms), 2)]
    return terms[0]


def factor_block(s_ref, e_ref):
    ids = lax.broadcasted_iota(jnp.int32, (BLOCK, BLOCK), 0)
    lanes = lax.broadcasted_iota(jnp.int32, (BLOCK, BLOCK), 1)
    e_ref[...] = jnp.where(ids == lanes, 1.0, 0.0)
    sub = lax.broadcasted_iota(jnp.int32, (8, BLOCK), 0)
    for p in range(16):
        at = 8 * p
        own = s_ref[at : at + 8, :]
        own_e = e_ref[at : at + 8, :]
        cols = [spread(own[:, at + i : at + i + 1]) for i in range(8)]
        t = {(s, i): spread(cols[i][s : s + 1, :]) for i in range(8) for s in range(i, 8)}
        rows = [spread(own[q : q + 1, :]) for q in range(8)]
        rows_e = [spread(own_e[q : q + 1, :]) for q in range(8)]
        low, inv, root = {}, {}, []
        for i in range(8):
            rs = lax.rsqrt(t[i, i])
            root.append(rs)
            for s in range(i + 1, 8):
                low[s, i] = t[s, i] * rs
            for s in range(i + 1, 8):
                for q in range(i + 1, s + 1):
                    t[s, q] = t[s, q] - low[s, i] * low[q, i]
        for i in range(8):
            inv[i, i] = root[i]
            for s in range(i + 1, 8):
                inv[s, i] = -root[s] * total(low[s, q] * inv[q, i] for q in range(i, s))
        done = [total(inv[i, q] * rows[q] for q in range(i + 1)) for i in range(8)]
        done_e = [total(inv[i, q] * rows_e[q] for q in range(i + 1)) for i in range(8)]
        tile, tile_e = done[0], done_e[0]
        for i in range(1, 8):
            tile = jnp.where(sub == i, done[i], tile)
            tile_e = jnp.where(sub == i, done_e[i], tile_e)
        s_ref[at : at + 8, :] = tile
        e_ref[at : at + 8, :] = tile_e
        if p == 15:
            break
        back = [total(inv[i, j] * done[i] for i in range(j, 8)) for j in range(8)]
        back_e = [total(inv[i, j] * done_e[i] for i in range(j, 8)) for j in range(8)]
        for u in range(p + 1, 16):
            part = s_ref[8 * u : 8 * u + 8, :]
            left = [spread(part[:, at + j : at + j + 1]) for j in range(8)]
            s_ref[8 * u : 8 * u + 8, :] = part - total(left[j] * back[j] for j in range(8))
            e_ref[8 * u : 8 * u + 8, :] -= total(left[j] * back_e[j] for j in range(8))


def invert_block(s_ref, e_ref):
    factor_block(s_ref, e_ref)
    ids = lax.broadcasted_iota(jnp.int32, (BLOCK, BLOCK), 0)
    lanes = lax.broadcasted_iota(jnp.int32, (BLOCK, BLOCK), 1)
    return jnp.where(ids <= lanes, s_ref[...], 0.0).T, e_ref[...]


def first_kernel(at_ref, own_ref, got_ref, f_ref, g_ref, rest_ref, work, s_ref, e_ref):
    n = BLOCK
    for i in range(4):
        u = at_ref[0] ^ i
        for j in range(i + 1):
            t = at_ref[1] ^ j
            work[i * n : (i + 1) * n, j * n : (j + 1) * n] = jnp.where(
                u % 2 == 0,
                own_ref[u // 2, t % 2, t // 2],
                got_ref[u // 2, t % 2, t // 2],
            )
    s_ref[...] = work[:n, :n]
    fac, inv = invert_block(s_ref, e_ref)
    f_ref[:n, :] = fac
    g_ref[...] = inv
    f_ref[n:, :] = dot_nt(work[n:, :n], inv)
    for j in range(1, 4):
        rest_ref[(j - 1) * n :, (j - 1) * n : j * n] = work[
            j * n :, j * n : (j + 1) * n
        ] - dot_nt(f_ref[j * n :, :], f_ref[j * n : (j + 1) * n, :])


def step_kernel(k, *refs):
    n = BLOCK
    old_f, old_g, rest_ref = refs[:k], refs[k : 2 * k], refs[2 * k]
    f_ref, g_ref = refs[2 * k + 1], refs[2 * k + 2]
    s_ref, e_ref = refs[-2], refs[-1]
    s_ref[...] = rest_ref[:n, :n]
    fac, inv = invert_block(s_ref, e_ref)
    f_ref[:n, :] = fac
    g_ref[:, k * n :] = inv
    if k < 3:
        left_ref = refs[2 * k + 3]
        f_ref[n:, :] = dot_nt(rest_ref[n:, :n], inv)
        for j in range(1, 4 - k):
            left_ref[(j - 1) * n :, (j - 1) * n : j * n] = rest_ref[
                j * n :, j * n : (j + 1) * n
            ] - dot_nt(f_ref[j * n :, :], f_ref[j * n : (j + 1) * n, :])
    for j in range(k):
        here = slice(j * n, (j + 1) * n)
        part = total(
            dot(old_f[m][(k - m) * n : (k - m + 1) * n, :], old_g[m][:, here])
            for m in range(j, k)
        )
        g_ref[:, here] = -dot(inv, part)


def f32(*shape):
    return jax.ShapeDtypeStruct(shape, jnp.float32)


def b16(*shape):
    return jax.ShapeDtypeStruct(shape, jnp.bfloat16)


VMEM = pl.BlockSpec(memory_space=pltpu.VMEM)
SMEM = pl.BlockSpec(memory_space=pltpu.SMEM)
PAIR = [pltpu.VMEM((BLOCK, BLOCK), jnp.float32)] * 2
COST = pl.CostEstimate(flops=6 * 10**9, bytes_accessed=2**20, transcendentals=0)


def factor_first(at, own, got):
    return pl.pallas_call(
        first_kernel,
        out_shape=[f32(ORDER, BLOCK), f32(BLOCK, BLOCK), f32(ORDER - BLOCK, ORDER - BLOCK)],
        in_specs=[SMEM, VMEM, VMEM],
        out_specs=[VMEM] * 3,
        scratch_shapes=[pltpu.VMEM((ORDER, ORDER), jnp.float32)] + PAIR,
        compiler_params=pltpu.CompilerParams(vmem_limit_bytes=8 * 2**20),
        cost_estimate=COST,
    )(at, own, got)


def factor_step(k, fs, gs, rest):
    shapes = [f32((4 - k) * BLOCK, BLOCK), f32(BLOCK, (k + 1) * BLOCK)]
    if k < 3:
        shapes.append(f32((3 - k) * BLOCK, (3 - k) * BLOCK))
    return pl.pallas_call(
        functools.partial(step_kernel, k),
        out_shape=shapes,
        in_specs=[VMEM] * (2 * k + 1),
        out_specs=[VMEM] * len(shapes),
        scratch_shapes=PAIR,
        compiler_params=pltpu.CompilerParams(vmem_limit_bytes=8 * 2**20),
        cost_estimate=COST,
    )(*fs, *gs, rest)


def split(value, parts):
    out = []
    for _ in range(parts):
        out.append(value.astype(jnp.bfloat16))
        value = value - out[-1].astype(jnp.float32)
    return out


def once(a, b):
    return jnp.dot(a, b, preferred_element_type=jnp.float32)


def strip_kernel(at_ref, own_ref, got_ref, g0, g1, g2, g3, high_ref, low_ref, z_ref,
                 t0, t1, t2, tmp):
    n = BLOCK
    for i in range(4):
        u = at_ref[0] ^ i
        tmp[i * n : (i + 1) * n, :] = jnp.where(u % 2 == 0, own_ref[u // 2], got_ref[u // 2])
    for t_ref in (t0, t1, t2):
        t_ref[...] = jnp.zeros_like(t_ref)
    for i, g_ref in enumerate((g0, g1, g2, g3)):
        here = slice(i * n, (i + 1) * n)
        value = dot(g_ref[...], tmp[: (i + 1) * n, :])
        high_ref[here, :], low_ref[here, :] = split(value, 2)
        z_ref[here, :] = value[:, ORDER:]
        for j in range(i + 1):
            there = slice(j * n, (j + 1) * n)
            for t_ref, part in zip((t0, t1, t2), split(g_ref[:, there].T, 3)):
                t_ref[there, here] = part


def strip_solve(at, own, got, gs):
    wide = (ORDER, ORDER + BLOCK)
    return pl.pallas_call(
        strip_kernel,
        out_shape=[b16(*wide)] * 2 + [f32(ORDER, BLOCK)] + [b16(ORDER, ORDER)] * 3,
        in_specs=[SMEM] + [VMEM] * 6,
        out_specs=[VMEM] * 6,
        scratch_shapes=[pltpu.VMEM(wide, jnp.float32)],
        compiler_params=pltpu.CompilerParams(vmem_limit_bytes=8 * 2**20),
        cost_estimate=pl.CostEstimate(flops=4 * 10**9, bytes_accessed=4 * 2**20, transcendentals=0),
    )(at, own, got, *gs)


def update_kernel(at_ref, q0_ref, q1_ref, q2_ref, low_ref, high_ref, f0, f1, f2, f3,
                  wh_ref, wl_ref, z_ref, t0, t1, t2, k_ref, y_ref, out_ref, right_ref, pan, w):
    step = pl.program_id(0)
    row, col = at_ref[2], at_ref[3]
    n = BLOCK

    def fill(read):
        for j in range(4):
            t = at_ref[1] ^ j
            for b in range(2):
                pan[b * n : (b + 1) * n, j * n : (j + 1) * n] = read(t % 2, t // 2, b)

    for s, ref in enumerate((q0_ref, q1_ref, q2_ref)):
        @pl.when(step == s)
        def _(ref=ref):
            fill(lambda t1, t2, b: ref[t1, t2, b])

    @pl.when(step == 3)
    def _():
        fill(lambda t1, t2, b: jnp.where(t1 == 0, low_ref[t2, b], high_ref[t2, b]))

    p = split(pan[...], 3)
    for cols, depth in ((slice(0, 256), 256), (slice(256, 512), 512)):
        a = [part[:, :depth] for part in p]
        b = [t_ref[:depth, cols] for t_ref in (t0, t1, t2)]
        small = once(a[0], b[2]) + once(a[1], b[1]) + once(a[2], b[0])
        w[:, cols] = once(a[0], b[0]) + ((once(a[0], b[1]) + once(a[1], b[0])) + small)

    first = (at_ref[4 + step] == 0) & (row < 4)
    for i in range(4):
        @pl.when(first & (row == i))
        def _(i=i):
            w[:n, :] = jnp.zeros((n, ORDER), jnp.float32)
            for m, f_ref in enumerate((f0, f1, f2, f3)[: i + 1]):
                w[:n, m * n : (m + 1) * n] = f_ref[(i - m) * n : (i - m + 1) * n, :]

    high, low = split(w[...], 2)
    change = once(high, wh_ref[...]) + (once(high, wl_ref[...]) + once(low, wh_ref[...]))
    out_ref[...] = k_ref[...] - change[:, :ORDER]
    right_ref[...] = y_ref[...] - change[:, ORDER:]

    @pl.when(first)
    def _():
        out_ref[:n, :] = jnp.zeros((n, ORDER), jnp.float32)
        right_ref[:n, :] = z_ref[pl.ds(pl.multiple_of(row * n, n), n), :]

    @pl.when(col < 4)
    def _():
        out_ref[:, :n] = w[:, pl.ds(pl.multiple_of(col * n, n), n)]


def update(at, parts, fs, strips, kernel, targets):
    rows = 256
    moved = lambda width: pl.BlockSpec((rows, width), lambda s, at: (at[4 + s], 0))
    return pl.pallas_call(
        update_kernel,
        out_shape=[f32(*kernel.shape), f32(*targets.shape)],
        grid_spec=pltpu.PrefetchScalarGridSpec(
            num_scalar_prefetch=1,
            grid=(4,),
            in_specs=[VMEM] * 15 + [moved(ORDER), moved(BLOCK)],
            out_specs=[moved(ORDER), moved(BLOCK)],
            scratch_shapes=[pltpu.VMEM((rows, ORDER), jnp.float32)] * 2,
        ),
        compiler_params=pltpu.CompilerParams(vmem_limit_bytes=16 * 2**20),
        cost_estimate=pl.CostEstimate(flops=10**10, bytes_accessed=6 * 2**20, transcendentals=0),
    )(at, *parts, *fs, *strips, kernel, targets)


def after(value, *others):
    return lax.optimization_barrier((value, *others))[0]


def per_device(kernel, targets):
    row_pos = lax.axis_index("row")
    col_pos = lax.axis_index("col")
    x_pos = col_pos // Y
    y_pos = col_pos % Y
    n = BLOCK
    base = jnp.where(y_pos < 4, y_pos, 7 - y_pos)
    shifts = jnp.array([0, 3, 1, 2], jnp.int32)
    at = jnp.concatenate(
        [jnp.stack([row_pos % 4, base, row_pos, col_pos]), (x_pos + shifts) % 4]
    ).astype(jnp.int32)
    mirror = [(x * Y + j, x * Y + 7 - j) for x in range(X) for j in range(4)]
    by_two = [(c, c ^ 2) for c in range(COLS)]
    by_one = [(c, c ^ 1) for c in range(COLS)]
    by_z = [(r, r ^ 2) for r in range(ROWS)]
    by_core = [(r, r ^ 1) for r in range(ROWS)]

    a0 = jnp.where((col_pos < 4) & (row_pos < 4), kernel[:n, :n], 0.0)
    got = [a0]
    for x in (1, 2, 3):
        pairs = [(r * COLS + j, r * COLS + x * Y + j) for r in range(4) for j in range(4)]
        got.append(lax.ppermute(a0, ("row", "col"), pairs))
    a1 = total(got)

    pairs = [(r * COLS + a, r * COLS + b) for r in range(4) for a, b in mirror]
    a2 = a1 + lax.ppermute(a1, ("row", "col"), pairs)
    got = [a2]
    for a in (1, 2, 3):
        got.append(over_row(a2, [(r, r + 4 * a) for r in range(4)]))
    a3 = total(got)

    panel = after(kernel[:, :n].reshape(8, n, n), a2)
    got = [jnp.where(x_pos == 0, panel[:2], 0.0)]
    for x in (1, 2, 3):
        got.append(over_col(panel[2 * x : 2 * x + 2], [(j, x * Y + j) for j in range(4)]))
    p1 = total(got)
    a3 = after(a3, p1)

    strip = jnp.concatenate([kernel[:n], targets[:n]], axis=1)
    strip = after(jnp.where(row_pos < 4, strip, 0.0), a3)
    c1 = strip + over_row(strip, [(r, r + 12) for r in range(4)])

    a4 = jnp.stack([a3, over_col(a3, by_two)])
    a5 = after(jnp.stack([a4, over_col(a4, by_one)]), c1)
    p2 = jnp.where(y_pos >= 4, over_col(after(p1, a5), mirror), p1)
    a6 = after(jnp.stack([a5, over_row(a5, by_z)]), p2)
    a7 = over_row(a6, by_core)
    p2, c1 = after(p2, a6), after(c1, a6)
    p3_got = over_col(p2, by_two)
    c2_got = over_row(c1, [(r, r + 4) for r in range(4)] + [(r, r - 4) for r in range(12, 16)])

    f0, g0, rest = factor_first(at, a6, a7)
    p3 = jnp.stack([p2, after(p3_got, rest)])
    c2 = c1 + after(c2_got, rest)
    p4_got = over_col(p3, by_one)
    c3_got = over_row(c2, by_z)
    f1, g1, rest = factor_step(1, [f0], [g0], after(rest, p3, c2))
    p4 = jnp.stack([p3, after(p4_got, rest)])
    down = over_col(p4, [(c, (c + Y) % COLS) for c in range(COLS)])
    up = over_col(p4, [(c, (c - Y) % COLS) for c in range(COLS)])
    f2, g2, rest = factor_step(2, [f0, f1], [g0, g1], after(rest, p4))
    c3 = jnp.stack([c2, after(c3_got, rest)])
    c4 = over_row(c3, by_core)
    f3, g3 = factor_step(3, [f0, f1, f2], [g0, g1, g2], after(rest, c3))
    near, far = after(up, g3)[0], after(down, g3)[1]
    low = over_col(near, [(c, (c - Y) % COLS) for c in range(COLS)])
    high = over_col(far, [(c, (c + Y) % COLS) for c in range(COLS)])
    strips = strip_solve(at, c3, c4, (g0, g1, g2, after(g3, near, far)))
    return tuple(
        update(at, (p4, down, up, low, high), (f0, f1, f2, f3), strips, kernel, targets)
    )


def solution(mesh):
    in_specs = (P("row", "col"), P("row", None))
    out_specs = (P("row", "col"), P("row", None))
    return jax.shard_map(
        per_device, mesh=mesh, in_specs=in_specs, out_specs=out_specs, check_vma=False
    )
```

time: 163 us -> 142 us (0.87)
  the two profiles are of different devices: /device:TPU:56 before, /device:TPU:1 now
where the time goes in v3:
time: 142 us; the launch traced here: 141 us
  starting transfers between devices  69.3 us (49%)
  Pallas kernels  39.7 us (28%)
  waiting for transfers between devices  27.6 us (19%)
  other arithmetic  2.14 us (2%)
    ppermute x12, starting transfers between devices, over_col(): return lax.ppermute(value, 'col', pairs)  31.6 us
    ppermute x9, starting transfers between devices, over_row(): return lax.ppermute(value, 'row', pairs)  28.3 us
    pallas_call x3, Pallas kernels, factor_step(): pl.pallas_call(functools.partial(step_kernel, k), out_shape=shapes, in_sp...  18.9 us
    ppermute x12, waiting for transfers between devices, over_col(): return lax.ppermute(value, 'col', pairs)  14.3 us
    ppermute x9, waiting for transfers between devices, over_row(): return lax.ppermute(value, 'row', pairs)  11.5 us
    pallas_call x1, Pallas kernels, update(): pl.pallas_call(update_kernel, out_shape=[f32(*kernel.shape), f32(*targets...  11.1 us
    ppermute x3, starting transfers between devices, per_device(): got.append(lax.ppermute(a0, ('row', 'col'), pairs))  8.05 us
    pallas_call x1, Pallas kernels, factor_first(): pl.pallas_call(first_kernel, out_shape=[f32(ORDER, BLOCK), f32(BLOCK, BLO...  6.92 us
  transfers between devices with their start and end apart: 25, of which 13 were waited for; matrix products, arithmetic and copies ran while one was open for 1% of the time, Pallas kernels for 20%

profile of v3, /device:TPU:1, one launch (start us, length us, event | category | flops | bytes accessed | tf_op | source)
XLA Modules:
  0.0 141.2 jit_solution(17319170456871869942)
XLA Ops:
  0.7 0.9 slice_select_fusion
  1.6 5.5 %collective-permute-start.1 = (f32[128,128]{1,0:T(8,128)S(1)}, f32[128,128]{1,0:T(8,128)S(1)}, u32[]{:S(2)}, u32[]{:S(2)}) collective-permute-start(f32[128,128]{1,0:T(8,128)S(1)} %slice_select_fusion), channel_id=1, source_target_pairs={{0,16},{1,17},{2,18},{3,19},{32,48},{33,49},{34,50},{35,51},{64,80... | collective-permute-start | bytes 196616 | tf_op jit(solution)/shard_map/ppermute | solution.py:326
  7.0 1.3 collective-permute-start.2
  8.3 1.3 collective-permute-start
  9.7 1.6 %collective-permute-done = f32[128,128]{1,0:T(8,128)S(1)} collective-permute-done((f32[128,128]{1,0:T(8,128)S(1)}, f32[128,128]{1,0:T(8,128)S(1)}, u32[]{:S(2)}, u32[]{:S(2)}) %collective-permute-start) | collective-permute-done | bytes 65568 | tf_op jit(solution)/shard_map/ppermute | solution.py:326
  11.3 0.9 add_add_fusion.2
  12.1 1.3 collective-permute-start.3
  13.4 1.1 slice.30
  14.5 0.2 collective-permute-done.3
  14.7 3.0 %collective-permute-start.9 = (f32[128,128]{1,0:T(8,128)S(1)}, f32[128,128]{1,0:T(8,128)S(1)}, u32[]{:S(2)}, u32[]{:S(2)}) collective-permute-start(f32[128,128]{1,0:T(8,128)S(1)} %add.64), channel_id=1, source_target_pairs={{0,384},{32,416},{64,448},{96,480},{1,385},{33,417},{65,449},{97,4... | collective-permute-start | bytes 196616 | tf_op jit(solution)/shard_map/ppermute | solution.py:22
  17.8 1.3 collective-permute-start.8
  19.1 1.3 collective-permute-start.7
  20.4 3.1 %collective-permute-start.4 = (f32[2,128,128]{2,1,0:T(8,128)S(1)}, f32[2,128,128]{2,1,0:T(8,128)S(1)}, u32[]{:S(2)}, u32[]{:S(2)}) collective-permute-start(f32[2,128,128]{2,1,0:T(8,128)S(1)} %get-tuple-element.72), channel_id=1, source_target_pairs={{0,8},{1,9},{2,10},{3,11},{32,40},{33,41},{34,42},{35,43},{64,72},... | collective-permute-start | bytes 393224 | tf_op jit(solution)/shard_map/ppermute | solution.py:18
  23.5 1.9 %collective-permute-start.6 = (f32[2,128,128]{2,1,0:T(8,128)S(1)}, f32[2,128,128]{2,1,0:T(8,128)S(1)}, u32[]{:S(2)}, u32[]{:S(2)}) collective-permute-start(f32[2,128,128]{2,1,0:T(8,128)S(1)} %get-tuple-element.73), channel_id=1, source_target_pairs={{0,24},{1,25},{2,26},{3,27},{32,56},{33,57},{34,58},{35,59},{64,88... | collective-permute-start | bytes 393224 | tf_op jit(solution)/shard_map/ppermute | solution.py:18
  25.5 1.3 collective-permute-start.5
  26.9 0.5 collective-permute-done.6
  27.4 2.7 %collective-permute-done.5 = f32[2,128,128]{2,1,0:T(8,128)S(1)} collective-permute-done((f32[2,128,128]{2,1,0:T(8,128)S(1)}, f32[2,128,128]{2,1,0:T(8,128)S(1)}, u32[]{:S(2)}, u32[]{:S(2)}) %collective-permute-start.5) | collective-permute-done | bytes 131104 | tf_op jit(solution)/shard_map/ppermute | solution.py:18
  30.1 2.9 %collective-permute-start.10 = (f32[128,128]{1,0:T(8,128)S(1)}, f32[128,128]{1,0:T(8,128)S(1)}, u32[]{:S(2)}, u32[]{:S(2)}) collective-permute-start(f32[128,128]{1,0:T(8,128)S(1)} %add_add_fusion.1), channel_id=1, source_target_pairs={{0,2},{1,3},{2,0},{3,1},{4,6},{5,7},{6,4},{7,5},{8,10},{9,11},{10,... | collective-permute-start | bytes 196616 | tf_op jit(solution)/shard_map/ppermute | solution.py:18
  33.0 2.8 %collective-permute-start.12 = (f32[128,640]{1,0:T(8,128)S(1)}, f32[128,640]{1,0:T(8,128)S(1)}, u32[]{:S(2)}, u32[]{:S(2)}) collective-permute-start(f32[128,640]{1,0:T(8,128)S(1)} %maximum_select_fusion), channel_id=1, source_target_pairs={{0,384},{32,416},{64,448},{96,480},{1,385},{33,417},{65,449},{97,4... | collective-permute-start | bytes 983048 | tf_op jit(solution)/shard_map/ppermute | solution.py:22
  35.8 0.6 collective-permute-done.10
  36.4 2.6 %collective-permute-start.11 = (f32[2,128,128]{2,1,0:T(8,128)S(1)}, f32[2,128,128]{2,1,0:T(8,128)S(1)}, u32[]{:S(2)}, u32[]{:S(2)}) collective-permute-start(f32[2,128,128]{2,1,0:T(8,128)S(1)} %get-tuple-element.78), channel_id=1, source_target_pairs={{0,1},{1,0},{2,3},{3,2},{4,5},{5,4},{6,7},{7,6},{8,9},{9,8},{10,11... | collective-permute-start | bytes 393224 | tf_op jit(solution)/shard_map/ppermute | solution.py:18
  39.1 3.1 %collective-permute-done.11 = f32[2,128,128]{2,1,0:T(8,128)S(1)} collective-permute-done((f32[2,128,128]{2,1,0:T(8,128)S(1)}, f32[2,128,128]{2,1,0:T(8,128)S(1)}, u32[]{:S(2)}, u32[]{:S(2)}) %collective-permute-start.11) | collective-permute-done | bytes 131104 | tf_op jit(solution)/shard_map/ppermute | solution.py:18
  42.1 6.8 %collective-permute-done.12 = f32[128,640]{1,0:T(8,128)S(1)} collective-permute-done((f32[128,640]{1,0:T(8,128)S(1)}, f32[128,640]{1,0:T(8,128)S(1)}, u32[]{:S(2)}, u32[]{:S(2)}) %collective-permute-start.12) | collective-permute-done | bytes 327712 | tf_op jit(solution)/shard_map/ppermute | solution.py:22
  48.9 1.3 collective-permute-start.13
  50.2 1.9 %collective-permute-start.14 = (f32[2,2,128,128]{3,2,1,0:T(8,128)S(1)}, f32[2,2,128,128]{3,2,1,0:T(8,128)S(1)}, u32[]{:S(2)}, u32[]{:S(2)}) collective-permute-start(f32[2,2,128,128]{3,2,1,0:T(8,128)S(1)} %pad_maximum_fusion.3), channel_id=1, source_target_pairs={{0,64},{32,96},{64,0},{96,32},{128,192},{160,224},{192,128},{224,1... | collective-permute-start | bytes 786440 | tf_op jit(solution)/shard_map/ppermute | solution.py:22
  52.2 1.4 %collective-permute-done.13 = f32[2,128,128]{2,1,0:T(8,128)S(1)} collective-permute-done((f32[2,128,128]{2,1,0:T(8,128)S(1)}, f32[2,128,128]{2,1,0:T(8,128)S(1)}, u32[]{:S(2)}, u32[]{:S(2)}) %collective-permute-start.13) | collective-permute-done | bytes 131104 | tf_op jit(solution)/shard_map/ppermute | solution.py:18
  53.6 4.5 %collective-permute-done.14 = f32[2,2,128,128]{3,2,1,0:T(8,128)S(1)} collective-permute-done((f32[2,2,128,128]{3,2,1,0:T(8,128)S(1)}, f32[2,2,128,128]{3,2,1,0:T(8,128)S(1)}, u32[]{:S(2)}, u32[]{:S(2)}) %collective-permute-start.14) | collective-permute-done | bytes 262176 | tf_op jit(solution)/shard_map/ppermute | solution.py:22
  58.2 4.6 %collective-permute-start.16 = (f32[2,2,2,128,128]{4,3,2,1,0:T(8,128)S(1)}, f32[2,2,2,128,128]{4,3,2,1,0:T(8,128)S(1)}, u32[]{:S(2)}, u32[]{:S(2)}) collective-permute-start(f32[2,2,2,128,128]{4,3,2,1,0:T(8,128)S(1)} %pad_maximum_fusion.1.own_ref), channel_id=1, source_target_pairs={{0,32},{32,0},{64,96},{96,64},{128,160},{160,128},{192,224},{224,1... | collective-permute-start | bytes 1572872 | tf_op jit(solution)/shard_map/ppermute | solution.py:22
  62.9 0.1 concatenate.6.at_ref
  63.0 2.0 %collective-permute-start.15 = (f32[2,128,128]{2,1,0:T(8,128)S(1)}, f32[2,128,128]{2,1,0:T(8,128)S(1)}, u32[]{:S(2)}, u32[]{:S(2)}) collective-permute-start(f32[2,128,128]{2,1,0:T(8,128)S(1)} %broadcast_select_fusion), channel_id=1, source_target_pairs={{0,2},{1,3},{2,0},{3,1},{4,6},{5,7},{6,4},{7,5},{8,10},{9,11},{10,... | collective-permute-start | bytes 393224 | tf_op jit(solution)/shard_map/ppermute | solution.py:18
  64.9 1.3 collective-permute-start.18
  66.3 6.9 %shard_map.50 = (f32[512,128]{1,0:T(8,128)S(1)}, f32[128,128]{1,0:T(8,128)S(1)}, f32[384,384]{1,0:T(8,128)S(1)}) custom-call(s32[8]{0:T(128)S(1)} %concatenate.6.at_ref, f32[2,2,2,128,128]{4,3,2,1,0:T(8,128)S(1)} %pad_maximum_fusion.1.own_ref, f32[2,2,2,128,128]{4,3,2,1,0:T(8,128)S(1)} %collective-permute-done.16.got_ref), custom_call_target="tpu_custom_call" | custom-call | flops 6000000000 | bytes 1048576 | tf_op jit(solution)/shard_map/pallas_call | solution.py:162
  73.2 0.2 collective-permute-done.18
  73.4 0.3 collective-permute-done.15
  73.7 3.0 %collective-permute-start.17 = (f32[2,2,128,128]{3,2,1,0:T(8,128)S(1)}, f32[2,2,128,128]{3,2,1,0:T(8,128)S(1)}, u32[]{:S(2)}, u32[]{:S(2)}) collective-permute-start(f32[2,2,128,128]{3,2,1,0:T(8,128)S(1)} %get-tuple-element.76), channel_id=1, source_target_pairs={{0,1},{1,0},{2,3},{3,2},{4,5},{5,4},{6,7},{7,6},{8,9},{9,8},{10,11... | collective-permute-start | bytes 786440 | tf_op jit(solution)/shard_map/ppermute | solution.py:18
  76.7 8.9 %collective-permute-start.21 = (f32[128,640]{1,0:T(8,128)S(1)}, f32[128,640]{1,0:T(8,128)S(1)}, u32[]{:S(2)}, u32[]{:S(2)}) collective-permute-start(f32[128,640]{1,0:T(8,128)S(1)} %add.72), channel_id=1, source_target_pairs={{0,64},{32,96},{64,0},{96,32},{128,192},{160,224},{192,128},{224,1... | collective-permute-start | bytes 983048 | tf_op jit(solution)/shard_map/ppermute | solution.py:22
  85.6 6.3 %shard_map.51 = (f32[384,128]{1,0:T(8,128)S(1)}, f32[128,256]{1,0:T(8,128)S(1)}, f32[256,256]{1,0:T(8,128)S(1)}) custom-call(f32[512,128]{1,0:T(8,128)S(1)} %get-tuple-element.46.refs_0_.f0, f32[128,128]{1,0:T(8,128)S(1)} %get-tuple-element.47.refs_1_.refs_2_.refs_3_.g0, f32[384,384]{1,0:T(8,128)S(1)} %get-tuple-element.50.refs_2_), custom_call_target="tpu_custom_call" | custom-call | flops 6000000000 | bytes 1048576 | tf_op jit(solution)/shard_map/pallas_call | solution.py:177
  91.9 4.3 %collective-permute-start.20 = (f32[2,2,2,128,128]{4,3,2,1,0:T(8,128)S(1)}, f32[2,2,2,128,128]{4,3,2,1,0:T(8,128)S(1)}, u32[]{:S(2)}, u32[]{:S(2)}) collective-permute-start(f32[2,2,2,128,128]{4,3,2,1,0:T(8,128)S(1)} %pad_maximum_fusion.2.q0_ref), channel_id=1, source_target_pairs={{0,24},{1,25},{2,26},{3,27},{4,28},{5,29},{6,30},{7,31},{8,0},{9,1... | collective-permute-start | bytes 1572872 | tf_op jit(solution)/shard_map/ppermute | solution.py:18
  96.3 2.1 %collective-permute-start.19 = (f32[2,2,2,128,128]{4,3,2,1,0:T(8,128)S(1)}, f32[2,2,2,128,128]{4,3,2,1,0:T(8,128)S(1)}, u32[]{:S(2)}, u32[]{:S(2)}) collective-permute-start(f32[2,2,2,128,128]{4,3,2,1,0:T(8,128)S(1)} %pad_maximum_fusion.2.q0_ref), channel_id=1, source_target_pairs={{0,8},{1,9},{2,10},{3,11},{4,12},{5,13},{6,14},{7,15},{8,16},{9,17... | collective-permute-start | bytes 1572872 | tf_op jit(solution)/shard_map/ppermute | solution.py:18
  98.4 6.5 %shard_map.52 = (f32[256,128]{1,0:T(8,128)S(1)}, f32[128,384]{1,0:T(8,128)S(1)}, f32[128,128]{1,0:T(8,128)S(1)}) custom-call(f32[512,128]{1,0:T(8,128)S(1)} %get-tuple-element.46.refs_0_.f0, f32[384,128]{1,0:T(8,128)S(1)} %get-tuple-element.53.refs_1_.f1, f32[128,128]{1,0:T(8,128)S(1)} %get-tuple-element.47.refs_1_.refs_2_.refs_3_.g0, ...), custom_call_target="tpu_custom_call" | custom-call | flops 6000000000 | bytes 1048576 | tf_op jit(solution)/shard_map/pallas_call | solution.py:177
  105.0 3.2 %collective-permute-start.24 = (f32[2,128,640]{2,1,0:T(8,128)S(1)}, f32[2,128,640]{2,1,0:T(8,128)S(1)}, u32[]{:S(2)}, u32[]{:S(2)}) collective-permute-start(f32[2,128,640]{2,1,0:T(8,128)S(1)} %pad_maximum_fusion.own_ref), channel_id=1, source_target_pairs={{0,32},{32,0},{64,96},{96,64},{128,160},{160,128},{192,224},{224,1... | collective-permute-start | bytes 1966088 | tf_op jit(solution)/shard_map/ppermute | solution.py:22
  108.2 6.1 %shard_map.53 = (f32[128,128]{1,0:T(8,128)S(1)}, f32[128,512]{1,0:T(8,128)S(1)}) custom-call(f32[512,128]{1,0:T(8,128)S(1)} %get-tuple-element.46.refs_0_.f0, f32[384,128]{1,0:T(8,128)S(1)} %get-tuple-element.53.refs_1_.f1, f32[256,128]{1,0:T(8,128)S(1)} %get-tuple-element.56.refs_2_.f2, f32[128,128]{1,0:T(8,128)S(1)} %get-tuple-element.47.refs_1_.refs_2_.refs_3_.g0, ...), custom_call_target="tpu_custom_call" | custom-call | flops 6000000000 | bytes 1048576 | tf_op jit(solution)/shard_map/pallas_call | solution.py:177
  114.3 4.9 %collective-permute-start.22 = (f32[2,2,128,128]{3,2,1,0:T(8,128)S(1)}, f32[2,2,128,128]{3,2,1,0:T(8,128)S(1)}, u32[]{:S(2)}, u32[]{:S(2)}) collective-permute-start(f32[2,2,128,128]{3,2,1,0:T(8,128)S(1)} %slice_bitcast_fusion.1), channel_id=1, source_target_pairs={{0,24},{1,25},{2,26},{3,27},{4,28},{5,29},{6,30},{7,31},{8,0},{9,1... | collective-permute-start | bytes 786440 | tf_op jit(solution)/shard_map/ppermute | solution.py:18
  119.2 2.3 %collective-permute-start.23 = (f32[2,2,128,128]{3,2,1,0:T(8,128)S(1)}, f32[2,2,128,128]{3,2,1,0:T(8,128)S(1)}, u32[]{:S(2)}, u32[]{:S(2)}) collective-permute-start(f32[2,2,128,128]{3,2,1,0:T(8,128)S(1)} %slice_bitcast_fusion), channel_id=1, source_target_pairs={{0,8},{1,9},{2,10},{3,11},{4,12},{5,13},{6,14},{7,15},{8,16},{9,17... | collective-permute-start | bytes 786440 | tf_op jit(solution)/shard_map/ppermute | solution.py:18
  121.5 2.8 %shard_map.54 = (bf16[512,640]{1,0:T(8,128)(2,1)S(1)}, bf16[512,640]{1,0:T(8,128)(2,1)S(1)}, f32[512,128]{1,0:T(8,128)S(1)}, bf16[512,512]{1,0:T(8,128)(2,1)S(1)...) custom-call(s32[8]{0:T(128)S(1)} %concatenate.6.at_ref, f32[2,128,640]{2,1,0:T(8,128)S(1)} %pad_maximum_fusion.own_ref, ...), custom_call_target="tpu_custom_call" | custom-call | flops 4000000000 | bytes 4194304 | tf_op jit(solution)/shard_map/pallas_call | solution.py:221
  124.3 0.6 collective-permute-done.22.low_ref
  124.9 5.2 %collective-permute-done.23.high_ref = f32[2,2,128,128]{3,2,1,0:T(8,128)S(1)} collective-permute-done((f32[2,2,128,128]{3,2,1,0:T(8,128)S(1)}, f32[2,2,128,128]{3,2,1,0:T(8,128)S(1)}, u32[]{:S(2)}, u32[]{:S(2)}) %collective-permute-start.23) | collective-permute-done | bytes 262176 | tf_op jit(solution)/shard_map/ppermute | solution.py:18
  130.1 11.1 %shard_map.55 = (f32[1024,512]{1,0:T(8,128)}, f32[1024,128]{1,0:T(8,128)}) custom-call(s32[8]{0:T(128)S(1)} %concatenate.6.at_ref, f32[2,2,2,128,128]{4,3,2,1,0:T(8,128)S(1)} %pad_maximum_fusion.2.q0_ref, f32[2,2,2,128,128]{4,3,2,1,0:T(8,128)S(1)} %collective-permute-done.19.q1_ref, f32[2,2,2,128,128]{4,3,2,1,0:T(8,128)S(1)} %collective-permute-done.20.q2_ref, ...), custom_call_target="tpu_custom_call" | custom-call | flops 10000000000 | bytes 6291456 | tf_op jit(solution)/shard_map/pallas_call | solution.py:286
  (39 shorter events, 0.5 us)
Async XLA Ops:
  0.6 32.4 %slice-start = ((f32[1024,512]{1,0:T(8,128)}), f32[128,512]{1,0:T(8,128)S(1)}, s32[]{:S(2)}) async-start(f32[1024,512]{1,0:T(8,128)} %k_ref.1), calls=%async_computation | async-start | bytes 524288 | tf_op jit(solution)/shard_map/slice | solution.py:343
  0.6 32.4 %slice-start.1 = ((f32[1024,128]{1,0:T(8,128)}), f32[128,128]{1,0:T(8,128)S(1)}, s32[]{:S(2)}) async-start(f32[1024,128]{1,0:T(8,128)} %y_ref.1), calls=%async_computation.1 | async-start | bytes 131072 | tf_op jit(solution)/shard_map/slice | solution.py:343
  1.6 8.1 %collective-permute-start.1 = (f32[128,128]{1,0:T(8,128)S(1)}, f32[128,128]{1,0:T(8,128)S(1)}, u32[]{:S(2)}, u32[]{:S(2)}) collective-permute-start(f32[128,128]{1,0:T(8,128)S(1)} %slice_select_fusion), channel_id=1, source_target_pairs={{0,16},{1,17},{2,18},{3,19},{32,48},{33,49},{34,50},{35,51},{64,80... | collective-permute-start | bytes 196616 | tf_op jit(solution)/shard_map/ppermute | solution.py:326
  7.0 2.6 %collective-permute-start.2 = (f32[128,128]{1,0:T(8,128)S(1)}, f32[128,128]{1,0:T(8,128)S(1)}, u32[]{:S(2)}, u32[]{:S(2)}) collective-permute-start(f32[128,128]{1,0:T(8,128)S(1)} %slice_select_fusion), channel_id=1, source_target_pairs={{0,24},{1,25},{2,26},{3,27},{32,56},{33,57},{34,58},{35,59},{64,88... | collective-permute-start | bytes 196616 | tf_op jit(solution)/shard_map/ppermute | solution.py:326
  8.3 2.9 %collective-permute-start = (f32[128,128]{1,0:T(8,128)S(1)}, f32[128,128]{1,0:T(8,128)S(1)}, u32[]{:S(2)}, u32[]{:S(2)}) collective-permute-start(f32[128,128]{1,0:T(8,128)S(1)} %slice_select_fusion), channel_id=1, source_target_pairs={{0,8},{1,9},{2,10},{3,11},{32,40},{33,41},{34,42},{35,43},{64,72},... | collective-permute-start | bytes 196616 | tf_op jit(solution)/shard_map/ppermute | solution.py:326
  12.1 2.6 %collective-permute-start.3 = (f32[128,128]{1,0:T(8,128)S(1)}, f32[128,128]{1,0:T(8,128)S(1)}, u32[]{:S(2)}, u32[]{:S(2)}) collective-permute-start(f32[128,128]{1,0:T(8,128)S(1)} %add_add_fusion.2), channel_id=1, source_target_pairs={{0,7},{1,6},{2,5},{3,4},{8,15},{9,14},{10,13},{11,12},{16,23},{17,... | collective-permute-start | bytes 196616 | tf_op jit(solution)/shard_map/ppermute | solution.py:330
  14.7 10.7 %collective-permute-start.9 = (f32[128,128]{1,0:T(8,128)S(1)}, f32[128,128]{1,0:T(8,128)S(1)}, u32[]{:S(2)}, u32[]{:S(2)}) collective-permute-start(f32[128,128]{1,0:T(8,128)S(1)} %add.64), channel_id=1, source_target_pairs={{0,384},{32,416},{64,448},{96,480},{1,385},{33,417},{65,449},{97,4... | collective-permute-start | bytes 196616 | tf_op jit(solution)/shard_map/ppermute | solution.py:22
  17.8 9.0 %collective-permute-start.8 = (f32[128,128]{1,0:T(8,128)S(1)}, f32[128,128]{1,0:T(8,128)S(1)}, u32[]{:S(2)}, u32[]{:S(2)}) collective-permute-start(f32[128,128]{1,0:T(8,128)S(1)} %add.64), channel_id=1, source_target_pairs={{0,256},{32,288},{64,320},{96,352},{1,257},{33,289},{65,321},{97,3... | collective-permute-start | bytes 196616 | tf_op jit(solution)/shard_map/ppermute | solution.py:22
  19.1 7.7 %collective-permute-start.7 = (f32[128,128]{1,0:T(8,128)S(1)}, f32[128,128]{1,0:T(8,128)S(1)}, u32[]{:S(2)}, u32[]{:S(2)}) collective-permute-start(f32[128,128]{1,0:T(8,128)S(1)} %add.64), channel_id=1, source_target_pairs={{0,128},{32,160},{64,192},{96,224},{1,129},{33,161},{65,193},{97,2... | collective-permute-start | bytes 196616 | tf_op jit(solution)/shard_map/ppermute | solution.py:22
  20.4 6.4 %collective-permute-start.4 = (f32[2,128,128]{2,1,0:T(8,128)S(1)}, f32[2,128,128]{2,1,0:T(8,128)S(1)}, u32[]{:S(2)}, u32[]{:S(2)}) collective-permute-start(f32[2,128,128]{2,1,0:T(8,128)S(1)} %get-tuple-element.72), channel_id=1, source_target_pairs={{0,8},{1,9},{2,10},{3,11},{32,40},{33,41},{34,42},{35,43},{64,72},... | collective-permute-start | bytes 393224 | tf_op jit(solution)/shard_map/ppermute | solution.py:18
  23.5 3.9 %collective-permute-start.6 = (f32[2,128,128]{2,1,0:T(8,128)S(1)}, f32[2,128,128]{2,1,0:T(8,128)S(1)}, u32[]{:S(2)}, u32[]{:S(2)}) collective-permute-start(f32[2,128,128]{2,1,0:T(8,128)S(1)} %get-tuple-element.73), channel_id=1, source_target_pairs={{0,24},{1,25},{2,26},{3,27},{32,56},{33,57},{34,58},{35,59},{64,88... | collective-permute-start | bytes 393224 | tf_op jit(solution)/shard_map/ppermute | solution.py:18
  25.5 4.6 %collective-permute-start.5 = (f32[2,128,128]{2,1,0:T(8,128)S(1)}, f32[2,128,128]{2,1,0:T(8,128)S(1)}, u32[]{:S(2)}, u32[]{:S(2)}) collective-permute-start(f32[2,128,128]{2,1,0:T(8,128)S(1)} %get-tuple-element.74), channel_id=1, source_target_pairs={{0,16},{1,17},{2,18},{3,19},{32,48},{33,49},{34,50},{35,51},{64,80... | collective-permute-start | bytes 393224 | tf_op jit(solution)/shard_map/ppermute | solution.py:18
  30.1 32.7 %copy-start.2 = (s32[4]{0:T(128)S(1)}, s32[4]{0:T(128)}, u32[]{:S(2)}) copy-start(s32[4]{0:T(128)} %constant.58.clone) | copy-start | bytes 52
  30.1 6.3 %collective-permute-start.10 = (f32[128,128]{1,0:T(8,128)S(1)}, f32[128,128]{1,0:T(8,128)S(1)}, u32[]{:S(2)}, u32[]{:S(2)}) collective-permute-start(f32[128,128]{1,0:T(8,128)S(1)} %add_add_fusion.1), channel_id=1, source_target_pairs={{0,2},{1,3},{2,0},{3,1},{4,6},{5,7},{6,4},{7,5},{8,10},{9,11},{10,... | collective-permute-start | bytes 196616 | tf_op jit(solution)/shard_map/ppermute | solution.py:18
  33.0 15.9 %collective-permute-start.12 = (f32[128,640]{1,0:T(8,128)S(1)}, f32[128,640]{1,0:T(8,128)S(1)}, u32[]{:S(2)}, u32[]{:S(2)}) collective-permute-start(f32[128,640]{1,0:T(8,128)S(1)} %maximum_select_fusion), channel_id=1, source_target_pairs={{0,384},{32,416},{64,448},{96,480},{1,385},{33,417},{65,449},{97,4... | collective-permute-start | bytes 983048 | tf_op jit(solution)/shard_map/ppermute | solution.py:22
  36.4 5.7 %collective-permute-start.11 = (f32[2,128,128]{2,1,0:T(8,128)S(1)}, f32[2,128,128]{2,1,0:T(8,128)S(1)}, u32[]{:S(2)}, u32[]{:S(2)}) collective-permute-start(f32[2,128,128]{2,1,0:T(8,128)S(1)} %get-tuple-element.78), channel_id=1, source_target_pairs={{0,1},{1,0},{2,3},{3,2},{4,5},{5,4},{6,7},{7,6},{8,9},{9,8},{10,11... | collective-permute-start | bytes 393224 | tf_op jit(solution)/shard_map/ppermute | solution.py:18
  48.9 4.7 %collective-permute-start.13 = (f32[2,128,128]{2,1,0:T(8,128)S(1)}, f32[2,128,128]{2,1,0:T(8,128)S(1)}, u32[]{:S(2)}, u32[]{:S(2)}) collective-permute-start(f32[2,128,128]{2,1,0:T(8,128)S(1)} %add_add_fusion), channel_id=1, source_target_pairs={{0,7},{1,6},{2,5},{3,4},{8,15},{9,14},{10,13},{11,12},{16,23},{17,... | collective-permute-start | bytes 393224 | tf_op jit(solution)/shard_map/ppermute | solution.py:18
  50.2 7.9 %collective-permute-start.14 = (f32[2,2,128,128]{3,2,1,0:T(8,128)S(1)}, f32[2,2,128,128]{3,2,1,0:T(8,128)S(1)}, u32[]{:S(2)}, u32[]{:S(2)}) collective-permute-start(f32[2,2,128,128]{3,2,1,0:T(8,128)S(1)} %pad_maximum_fusion.3), channel_id=1, source_target_pairs={{0,64},{32,96},{64,0},{96,32},{128,192},{160,224},{192,128},{224,1... | collective-permute-start | bytes 786440 | tf_op jit(solution)/shard_map/ppermute | solution.py:22
  58.2 8.1 %collective-permute-start.16 = (f32[2,2,2,128,128]{4,3,2,1,0:T(8,128)S(1)}, f32[2,2,2,128,128]{4,3,2,1,0:T(8,128)S(1)}, u32[]{:S(2)}, u32[]{:S(2)}) collective-permute-start(f32[2,2,2,128,128]{4,3,2,1,0:T(8,128)S(1)} %pad_maximum_fusion.1.own_ref), channel_id=1, source_target_pairs={{0,32},{32,0},{64,96},{96,64},{128,160},{160,128},{192,224},{224,1... | collective-permute-start | bytes 1572872 | tf_op jit(solution)/shard_map/ppermute | solution.py:22
  63.0 10.7 %collective-permute-start.15 = (f32[2,128,128]{2,1,0:T(8,128)S(1)}, f32[2,128,128]{2,1,0:T(8,128)S(1)}, u32[]{:S(2)}, u32[]{:S(2)}) collective-permute-start(f32[2,128,128]{2,1,0:T(8,128)S(1)} %broadcast_select_fusion), channel_id=1, source_target_pairs={{0,2},{1,3},{2,0},{3,1},{4,6},{5,7},{6,4},{7,5},{8,10},{9,11},{10,... | collective-permute-start | bytes 393224 | tf_op jit(solution)/shard_map/ppermute | solution.py:18
  64.9 8.5 %collective-permute-start.18 = (f32[128,640]{1,0:T(8,128)S(1)}, f32[128,640]{1,0:T(8,128)S(1)}, u32[]{:S(2)}, u32[]{:S(2)}) collective-permute-start(f32[128,640]{1,0:T(8,128)S(1)} %add.71), channel_id=1, source_target_pairs={{0,128},{32,160},{64,192},{96,224},{384,256},{416,288},{448,320},{... | collective-permute-start | bytes 983048 | tf_op jit(solution)/shard_map/ppermute | solution.py:22
  73.7 18.2 %collective-permute-start.17 = (f32[2,2,128,128]{3,2,1,0:T(8,128)S(1)}, f32[2,2,128,128]{3,2,1,0:T(8,128)S(1)}, u32[]{:S(2)}, u32[]{:S(2)}) collective-permute-start(f32[2,2,128,128]{3,2,1,0:T(8,128)S(1)} %get-tuple-element.76), channel_id=1, source_target_pairs={{0,1},{1,0},{2,3},{3,2},{4,5},{5,4},{6,7},{7,6},{8,9},{9,8},{10,11... | collective-permute-start | bytes 786440 | tf_op jit(solution)/shard_map/ppermute | solution.py:18
  76.7 28.2 %collective-permute-start.21 = (f32[128,640]{1,0:T(8,128)S(1)}, f32[128,640]{1,0:T(8,128)S(1)}, u32[]{:S(2)}, u32[]{:S(2)}) collective-permute-start(f32[128,640]{1,0:T(8,128)S(1)} %add.72), channel_id=1, source_target_pairs={{0,64},{32,96},{64,0},{96,32},{128,192},{160,224},{192,128},{224,1... | collective-permute-start | bytes 983048 | tf_op jit(solution)/shard_map/ppermute | solution.py:22
  91.9 22.3 %collective-permute-start.20 = (f32[2,2,2,128,128]{4,3,2,1,0:T(8,128)S(1)}, f32[2,2,2,128,128]{4,3,2,1,0:T(8,128)S(1)}, u32[]{:S(2)}, u32[]{:S(2)}) collective-permute-start(f32[2,2,2,128,128]{4,3,2,1,0:T(8,128)S(1)} %pad_maximum_fusion.2.q0_ref), channel_id=1, source_target_pairs={{0,24},{1,25},{2,26},{3,27},{4,28},{5,29},{6,30},{7,31},{8,0},{9,1... | collective-permute-start | bytes 1572872 | tf_op jit(solution)/shard_map/ppermute | solution.py:18
  96.3 22.9 %collective-permute-start.19 = (f32[2,2,2,128,128]{4,3,2,1,0:T(8,128)S(1)}, f32[2,2,2,128,128]{4,3,2,1,0:T(8,128)S(1)}, u32[]{:S(2)}, u32[]{:S(2)}) collective-permute-start(f32[2,2,2,128,128]{4,3,2,1,0:T(8,128)S(1)} %pad_maximum_fusion.2.q0_ref), channel_id=1, source_target_pairs={{0,8},{1,9},{2,10},{3,11},{4,12},{5,13},{6,14},{7,15},{8,16},{9,17... | collective-permute-start | bytes 1572872 | tf_op jit(solution)/shard_map/ppermute | solution.py:18
  105.0 16.6 %collective-permute-start.24 = (f32[2,128,640]{2,1,0:T(8,128)S(1)}, f32[2,128,640]{2,1,0:T(8,128)S(1)}, u32[]{:S(2)}, u32[]{:S(2)}) collective-permute-start(f32[2,128,640]{2,1,0:T(8,128)S(1)} %pad_maximum_fusion.own_ref), channel_id=1, source_target_pairs={{0,32},{32,0},{64,96},{96,64},{128,160},{160,128},{192,224},{224,1... | collective-permute-start | bytes 1966088 | tf_op jit(solution)/shard_map/ppermute | solution.py:22
  114.3 10.6 %collective-permute-start.22 = (f32[2,2,128,128]{3,2,1,0:T(8,128)S(1)}, f32[2,2,128,128]{3,2,1,0:T(8,128)S(1)}, u32[]{:S(2)}, u32[]{:S(2)}) collective-permute-start(f32[2,2,128,128]{3,2,1,0:T(8,128)S(1)} %slice_bitcast_fusion.1), channel_id=1, source_target_pairs={{0,24},{1,25},{2,26},{3,27},{4,28},{5,29},{6,30},{7,31},{8,0},{9,1... | collective-permute-start | bytes 786440 | tf_op jit(solution)/shard_map/ppermute | solution.py:18
  119.2 10.9 %copy-start = (f32[1024,512]{1,0:T(8,128)S(1)}, f32[1024,512]{1,0:T(8,128)}, u32[]{:S(2)}) copy-start(f32[1024,512]{1,0:T(8,128)} %k_ref.1) | copy-start | bytes 6291460
  119.2 10.9 %copy-start.1 = (f32[1024,128]{1,0:T(8,128)S(1)}, f32[1024,128]{1,0:T(8,128)}, u32[]{:S(2)}) copy-start(f32[1024,128]{1,0:T(8,128)} %y_ref.1) | copy-start | bytes 1572868
  119.2 10.8 %collective-permute-start.23 = (f32[2,2,128,128]{3,2,1,0:T(8,128)S(1)}, f32[2,2,128,128]{3,2,1,0:T(8,128)S(1)}, u32[]{:S(2)}, u32[]{:S(2)}) collective-permute-start(f32[2,2,128,128]{3,2,1,0:T(8,128)S(1)} %slice_bitcast_fusion), channel_id=1, source_target_pairs={{0,8},{1,9},{2,10},{3,11},{4,12},{5,13},{6,14},{7,15},{8,16},{9,17... | collective-permute-start | bytes 786440 | tf_op jit(solution)/shard_map/ppermute | solution.py:18

commit v4 on v3

--- a/solution.py
+++ b/solution.py
@@ -340,36 +340,34 @@
     p1 = total(got)
     a3 = after(a3, p1)
 
+    a4 = jnp.stack([a3, over_col(a3, by_two)])
+    p2 = jnp.where(y_pos >= 4, over_col(after(p1, a3), mirror), p1)
+    a5 = after(jnp.stack([a4, over_col(a4, by_one)]), p2)
+    p3 = jnp.stack([p2, over_col(after(p2, a5), by_two)])
+    a6 = after(jnp.stack([a5, over_row(a5, by_z)]), p3)
+    a7 = over_row(a6, by_core)
+    p4_got = over_col(after(p3, a6), by_one)
+
     strip = jnp.concatenate([kernel[:n], targets[:n]], axis=1)
-    strip = after(jnp.where(row_pos < 4, strip, 0.0), a3)
-    c1 = strip + over_row(strip, [(r, r + 12) for r in range(4)])
-
-    a4 = jnp.stack([a3, over_col(a3, by_two)])
-    a5 = after(jnp.stack([a4, over_col(a4, by_one)]), c1)
-    p2 = jnp.where(y_pos >= 4, over_col(after(p1, a5), mirror), p1)
-    a6 = after(jnp.stack([a5, over_row(a5, by_z)]), p2)
-    a7 = over_row(a6, by_core)
-    p2, c1 = after(p2, a6), after(c1, a6)
-    p3_got = over_col(p2, by_two)
-    c2_got = over_row(c1, [(r, r + 4) for r in range(4)] + [(r, r - 4) for r in range(12, 16)])
+    strip = after(jnp.where(row_pos < 4, strip, 0.0), a6)
+    strip_got = [over_row(strip, [(r, r + 4 * a) for r in range(4)]) for a in (1, 2, 3)]
 
     f0, g0, rest = factor_first(at, a6, a7)
-    p3 = jnp.stack([p2, after(p3_got, rest)])
-    c2 = c1 + after(c2_got, rest)
-    p4_got = over_col(p3, by_one)
-    c3_got = over_row(c2, by_z)
-    f1, g1, rest = factor_step(1, [f0], [g0], after(rest, p3, c2))
     p4 = jnp.stack([p3, after(p4_got, rest)])
     down = over_col(p4, [(c, (c + Y) % COLS) for c in range(COLS)])
     up = over_col(p4, [(c, (c - Y) % COLS) for c in range(COLS)])
-    f2, g2, rest = factor_step(2, [f0, f1], [g0, g1], after(rest, p4))
-    c3 = jnp.stack([c2, after(c3_got, rest)])
-    c4 = over_row(c3, by_core)
-    f3, g3 = factor_step(3, [f0, f1, f2], [g0, g1, g2], after(rest, c3))
-    near, far = after(up, g3)[0], after(down, g3)[1]
+    f1, g1, rest = factor_step(1, [f0], [g0], after(rest, p4))
+    f2, g2, rest = factor_step(2, [f0, f1], [g0, g1], rest)
+    down, up = after(down, rest), after(up, rest)
+    near, far = up[0], down[1]
     low = over_col(near, [(c, (c - Y) % COLS) for c in range(COLS)])
     high = over_col(far, [(c, (c + Y) % COLS) for c in range(COLS)])
-    strips = strip_solve(at, c3, c4, (g0, g1, g2, after(g3, near, far)))
+    c2 = total([strip] + [after(got, rest) for got in strip_got])
+    c3_got = over_row(c2, by_z)
+    f3, g3 = factor_step(3, [f0, f1, f2], [g0, g1, g2], after(rest, near, far, c2))
+    c3 = after(jnp.stack([c2, after(c3_got, g3)]), low, high)
+    c4 = over_row(c3, by_core)
+    strips = strip_solve(at, c3, c4, (g0, g1, g2, g3))
     return tuple(
         update(at, (p4, down, up, low, high), (f0, f1, f2, f3), strips, kernel, targets)
     )

time: 142 us -> 133 us (0.937)
  waiting for transfers between devices: 27.6 us -> 18.2 us
    ppermute x9 -> x10, waiting for transfers between devices: 11.5 us -> 1.73 us  [over_row(): return lax.ppermute(value, 'row', pairs)]
    ppermute x9 -> x10, starting transfers between devices: 28.3 us -> 30.6 us  [over_row(): return lax.ppermute(value, 'row', pairs)]
    ppermute x12, starting transfers between devices: 31.6 us -> 30 us  [over_col(): return lax.ppermute(value, 'col', pairs)]
  transfers between devices with their start and end apart: 25 -> 26, of which waited for: 13 -> 9; matrix products, arithmetic and copies ran while one was open for 1% -> 1% of each run, Pallas kernels for 20% -> 19%
where the time goes in v4:
time: 133 us; the launch traced here: 132 us
  starting transfers between devices  69.9 us (53%)
  Pallas kernels  39.7 us (30%)
  waiting for transfers between devices  18.2 us (14%)
  other arithmetic  2.1 us (2%)
    ppermute x10, starting transfers between devices, over_row(): return lax.ppermute(value, 'row', pairs)  30.6 us
    ppermute x12, starting transfers between devices, over_col(): return lax.ppermute(value, 'col', pairs)  30 us
    pallas_call x3, Pallas kernels, factor_step(): pl.pallas_call(functools.partial(step_kernel, k), out_shape=shapes, in_sp...  18.9 us
    ppermute x12, waiting for transfers between devices, over_col(): return lax.ppermute(value, 'col', pairs)  14.7 us
    pallas_call x1, Pallas kernels, update(): pl.pallas_call(update_kernel, out_shape=[f32(*kernel.shape), f32(*targets...  11.1 us
    ppermute x3, starting transfers between devices, per_device(): got.append(lax.ppermute(a0, ('row', 'col'), pairs))  8.05 us
    pallas_call x1, Pallas kernels, factor_first(): pl.pallas_call(first_kernel, out_shape=[f32(ORDER, BLOCK), f32(BLOCK, BLO...  6.91 us
    pallas_call x1, Pallas kernels, strip_solve(): pl.pallas_call(strip_kernel, out_shape=[b16(*wide)] * 2 + [f32(ORDER, BLO...  2.77 us
  transfers between devices with their start and end apart: 26, of which 9 were waited for; matrix products, arithmetic and copies ran while one was open for 1% of the time, Pallas kernels for 19%

profile of v4, /device:TPU:1, one launch (start us, length us, event | category | flops | bytes accessed | tf_op | source)
XLA Modules:
  0.0 132.4 jit_solution(3385669700235291417)
XLA Ops:
  0.6 0.8 slice_select_fusion
  1.5 5.5 %collective-permute-start.1 = (f32[128,128]{1,0:T(8,128)S(1)}, f32[128,128]{1,0:T(8,128)S(1)}, u32[]{:S(2)}, u32[]{:S(2)}) collective-permute-start(f32[128,128]{1,0:T(8,128)S(1)} %slice_select_fusion), channel_id=1, source_target_pairs={{0,16},{1,17},{2,18},{3,19},{32,48},{33,49},{34,50},{35,51},{64,80... | collective-permute-start | bytes 196616 | tf_op jit(solution)/shard_map/ppermute | solution.py:326
  7.0 1.3 collective-permute-start.2
  8.3 1.3 collective-permute-start
  9.6 1.6 %collective-permute-done = f32[128,128]{1,0:T(8,128)S(1)} collective-permute-done((f32[128,128]{1,0:T(8,128)S(1)}, f32[128,128]{1,0:T(8,128)S(1)}, u32[]{:S(2)}, u32[]{:S(2)}) %collective-permute-start) | collective-permute-done | bytes 65568 | tf_op jit(solution)/shard_map/ppermute | solution.py:326
  11.2 0.9 add_add_fusion.3
  12.0 1.3 collective-permute-start.3
  13.4 1.1 slice.30
  14.5 0.2 collective-permute-done.3
  14.7 3.0 %collective-permute-start.9 = (f32[128,128]{1,0:T(8,128)S(1)}, f32[128,128]{1,0:T(8,128)S(1)}, u32[]{:S(2)}, u32[]{:S(2)}) collective-permute-start(f32[128,128]{1,0:T(8,128)S(1)} %add.67), channel_id=1, source_target_pairs={{0,384},{32,416},{64,448},{96,480},{1,385},{33,417},{65,449},{97,4... | collective-permute-start | bytes 196616 | tf_op jit(solution)/shard_map/ppermute | solution.py:22
  17.7 1.3 collective-permute-start.8
  19.0 1.3 collective-permute-start.7
  20.3 3.1 %collective-permute-start.4 = (f32[2,128,128]{2,1,0:T(8,128)S(1)}, f32[2,128,128]{2,1,0:T(8,128)S(1)}, u32[]{:S(2)}, u32[]{:S(2)}) collective-permute-start(f32[2,128,128]{2,1,0:T(8,128)S(1)} %get-tuple-element.72), channel_id=1, source_target_pairs={{0,8},{1,9},{2,10},{3,11},{32,40},{33,41},{34,42},{35,43},{64,72},... | collective-permute-start | bytes 393224 | tf_op jit(solution)/shard_map/ppermute | solution.py:18
  23.5 1.9 %collective-permute-start.6 = (f32[2,128,128]{2,1,0:T(8,128)S(1)}, f32[2,128,128]{2,1,0:T(8,128)S(1)}, u32[]{:S(2)}, u32[]{:S(2)}) collective-permute-start(f32[2,128,128]{2,1,0:T(8,128)S(1)} %get-tuple-element.73), channel_id=1, source_target_pairs={{0,24},{1,25},{2,26},{3,27},{32,56},{33,57},{34,58},{35,59},{64,88... | collective-permute-start | bytes 393224 | tf_op jit(solution)/shard_map/ppermute | solution.py:18
  25.4 1.3 collective-permute-start.5
  26.8 0.5 collective-permute-done.6
  27.3 2.7 %collective-permute-done.5 = f32[2,128,128]{2,1,0:T(8,128)S(1)} collective-permute-done((f32[2,128,128]{2,1,0:T(8,128)S(1)}, f32[2,128,128]{2,1,0:T(8,128)S(1)}, u32[]{:S(2)}, u32[]{:S(2)}) %collective-permute-start.5) | collective-permute-done | bytes 131104 | tf_op jit(solution)/shard_map/ppermute | solution.py:18
  30.1 0.0 slice-start.1
  30.1 3.0 %collective-permute-start.11 = (f32[128,128]{1,0:T(8,128)S(1)}, f32[128,128]{1,0:T(8,128)S(1)}, u32[]{:S(2)}, u32[]{:S(2)}) collective-permute-start(f32[128,128]{1,0:T(8,128)S(1)} %add_add_fusion.2), channel_id=1, source_target_pairs={{0,2},{1,3},{2,0},{3,1},{4,6},{5,7},{6,4},{7,5},{8,10},{9,11},{10,... | collective-permute-start | bytes 196616 | tf_op jit(solution)/shard_map/ppermute | solution.py:18
  33.1 1.3 collective-permute-start.10
  34.4 2.1 %collective-permute-done.11 = f32[128,128]{1,0:T(8,128)S(1)} collective-permute-done((f32[128,128]{1,0:T(8,128)S(1)}, f32[128,128]{1,0:T(8,128)S(1)}, u32[]{:S(2)}, u32[]{:S(2)}) %collective-permute-start.11) | collective-permute-done | bytes 65568 | tf_op jit(solution)/shard_map/ppermute | solution.py:18
  36.5 1.9 %collective-permute-start.12 = (f32[2,128,128]{2,1,0:T(8,128)S(1)}, f32[2,128,128]{2,1,0:T(8,128)S(1)}, u32[]{:S(2)}, u32[]{:S(2)}) collective-permute-start(f32[2,128,128]{2,1,0:T(8,128)S(1)} %get-tuple-element.78), channel_id=1, source_target_pairs={{0,1},{1,0},{2,3},{3,2},{4,5},{5,4},{6,7},{7,6},{8,9},{9,8},{10,11... | collective-permute-start | bytes 393224 | tf_op jit(solution)/shard_map/ppermute | solution.py:18
  38.5 3.7 %collective-permute-done.12 = f32[2,128,128]{2,1,0:T(8,128)S(1)} collective-permute-done((f32[2,128,128]{2,1,0:T(8,128)S(1)}, f32[2,128,128]{2,1,0:T(8,128)S(1)}, u32[]{:S(2)}, u32[]{:S(2)}) %collective-permute-start.12) | collective-permute-done | bytes 131104 | tf_op jit(solution)/shard_map/ppermute | solution.py:18
  42.2 3.5 %collective-permute-start.14 = (f32[2,2,128,128]{3,2,1,0:T(8,128)S(1)}, f32[2,2,128,128]{3,2,1,0:T(8,128)S(1)}, u32[]{:S(2)}, u32[]{:S(2)}) collective-permute-start(f32[2,2,128,128]{3,2,1,0:T(8,128)S(1)} %pad_maximum_fusion.3), channel_id=1, source_target_pairs={{0,64},{32,96},{64,0},{96,32},{128,192},{160,224},{192,128},{224,1... | collective-permute-start | bytes 786440 | tf_op jit(solution)/shard_map/ppermute | solution.py:22
  45.7 3.0 %collective-permute-start.13 = (f32[2,128,128]{2,1,0:T(8,128)S(1)}, f32[2,128,128]{2,1,0:T(8,128)S(1)}, u32[]{:S(2)}, u32[]{:S(2)}) collective-permute-start(f32[2,128,128]{2,1,0:T(8,128)S(1)} %broadcast_select_fusion), channel_id=1, source_target_pairs={{0,2},{1,3},{2,0},{3,1},{4,6},{5,7},{6,4},{7,5},{8,10},{9,11},{10,... | collective-permute-start | bytes 393224 | tf_op jit(solution)/shard_map/ppermute | solution.py:18
  48.7 4.9 %collective-permute-done.13 = f32[2,128,128]{2,1,0:T(8,128)S(1)} collective-permute-done((f32[2,128,128]{2,1,0:T(8,128)S(1)}, f32[2,128,128]{2,1,0:T(8,128)S(1)}, u32[]{:S(2)}, u32[]{:S(2)}) %collective-permute-start.13) | collective-permute-done | bytes 131104 | tf_op jit(solution)/shard_map/ppermute | solution.py:18
  53.7 0.1 pad_maximum_fusion.1.own_ref
  53.7 5.9 %collective-permute-start.16 = (f32[2,2,2,128,128]{4,3,2,1,0:T(8,128)S(1)}, f32[2,2,2,128,128]{4,3,2,1,0:T(8,128)S(1)}, u32[]{:S(2)}, u32[]{:S(2)}) collective-permute-start(f32[2,2,2,128,128]{4,3,2,1,0:T(8,128)S(1)} %pad_maximum_fusion.1.own_ref), channel_id=1, source_target_pairs={{0,32},{32,0},{64,96},{96,64},{128,160},{160,128},{192,224},{224,1... | collective-permute-start | bytes 1572872 | tf_op jit(solution)/shard_map/ppermute | solution.py:22
  59.6 0.1 concatenate.6.at_ref
  59.8 4.7 %collective-permute-start.23 = (f32[128,640]{1,0:T(8,128)S(1)}, f32[128,640]{1,0:T(8,128)S(1)}, u32[]{:S(2)}, u32[]{:S(2)}) collective-permute-start(f32[128,640]{1,0:T(8,128)S(1)} %maximum_select_fusion), channel_id=1, source_target_pairs={{0,384},{32,416},{64,448},{96,480},{1,385},{33,417},{65,449},{97,4... | collective-permute-start | bytes 983048 | tf_op jit(solution)/shard_map/ppermute | solution.py:22
  64.4 1.3 collective-permute-start.22
  65.8 1.3 collective-permute-start.21
  67.1 2.6 %collective-permute-start.15 = (f32[2,2,128,128]{3,2,1,0:T(8,128)S(1)}, f32[2,2,128,128]{3,2,1,0:T(8,128)S(1)}, u32[]{:S(2)}, u32[]{:S(2)}) collective-permute-start(f32[2,2,128,128]{3,2,1,0:T(8,128)S(1)} %get-tuple-element.43), channel_id=1, source_target_pairs={{0,1},{1,0},{2,3},{3,2},{4,5},{5,4},{6,7},{7,6},{8,9},{9,8},{10,11... | collective-permute-start | bytes 786440 | tf_op jit(solution)/shard_map/ppermute | solution.py:18
  69.7 6.9 %shard_map.50 = (f32[512,128]{1,0:T(8,128)S(1)}, f32[128,128]{1,0:T(8,128)S(1)}, f32[384,384]{1,0:T(8,128)S(1)}) custom-call(s32[8]{0:T(128)S(1)} %concatenate.6.at_ref, f32[2,2,2,128,128]{4,3,2,1,0:T(8,128)S(1)} %pad_maximum_fusion.1.own_ref, f32[2,2,2,128,128]{4,3,2,1,0:T(8,128)S(1)} %collective-permute-done.16.got_ref), custom_call_target="tpu_custom_call" | custom-call | flops 6000000000 | bytes 1048576 | tf_op jit(solution)/shard_map/pallas_call | solution.py:162
  76.7 1.9 %collective-permute-start.18 = (f32[2,2,2,128,128]{4,3,2,1,0:T(8,128)S(1)}, f32[2,2,2,128,128]{4,3,2,1,0:T(8,128)S(1)}, u32[]{:S(2)}, u32[]{:S(2)}) collective-permute-start(f32[2,2,2,128,128]{4,3,2,1,0:T(8,128)S(1)} %pad_maximum_fusion.2.q0_ref), channel_id=1, source_target_pairs={{0,24},{1,25},{2,26},{3,27},{4,28},{5,29},{6,30},{7,31},{8,0},{9,1... | collective-permute-start | bytes 1572872 | tf_op jit(solution)/shard_map/ppermute | solution.py:18
  78.6 3.5 %collective-permute-start.17 = (f32[2,2,2,128,128]{4,3,2,1,0:T(8,128)S(1)}, f32[2,2,2,128,128]{4,3,2,1,0:T(8,128)S(1)}, u32[]{:S(2)}, u32[]{:S(2)}) collective-permute-start(f32[2,2,2,128,128]{4,3,2,1,0:T(8,128)S(1)} %pad_maximum_fusion.2.q0_ref), channel_id=1, source_target_pairs={{0,8},{1,9},{2,10},{3,11},{4,12},{5,13},{6,14},{7,15},{8,16},{9,17... | collective-permute-start | bytes 1572872 | tf_op jit(solution)/shard_map/ppermute | solution.py:18
  82.2 6.3 %shard_map.51 = (f32[384,128]{1,0:T(8,128)S(1)}, f32[128,256]{1,0:T(8,128)S(1)}, f32[256,256]{1,0:T(8,128)S(1)}) custom-call(f32[512,128]{1,0:T(8,128)S(1)} %get-tuple-element.46.refs_0_.f0, f32[128,128]{1,0:T(8,128)S(1)} %get-tuple-element.47.refs_1_.refs_2_.refs_3_.g0, f32[384,384]{1,0:T(8,128)S(1)} %get-tuple-element.48.refs_2_), custom_call_target="tpu_custom_call" | custom-call | flops 6000000000 | bytes 1048576 | tf_op jit(solution)/shard_map/pallas_call | solution.py:177
  88.5 6.5 %shard_map.52 = (f32[256,128]{1,0:T(8,128)S(1)}, f32[128,384]{1,0:T(8,128)S(1)}, f32[128,128]{1,0:T(8,128)S(1)}) custom-call(f32[512,128]{1,0:T(8,128)S(1)} %get-tuple-element.46.refs_0_.f0, f32[384,128]{1,0:T(8,128)S(1)} %get-tuple-element.49.refs_1_.f1, f32[128,128]{1,0:T(8,128)S(1)} %get-tuple-element.47.refs_1_.refs_2_.refs_3_.g0, ...), custom_call_target="tpu_custom_call" | custom-call | flops 6000000000 | bytes 1048576 | tf_op jit(solution)/shard_map/pallas_call | solution.py:177
  95.0 0.1 add_add_fusion
  95.1 3.6 %collective-permute-start.24 = (f32[128,640]{1,0:T(8,128)S(1)}, f32[128,640]{1,0:T(8,128)S(1)}, u32[]{:S(2)}, u32[]{:S(2)}) collective-permute-start(f32[128,640]{1,0:T(8,128)S(1)} %add_add_fusion), channel_id=1, source_target_pairs={{0,64},{32,96},{64,0},{96,32},{128,192},{160,224},{192,128},{224,1... | collective-permute-start | bytes 983048 | tf_op jit(solution)/shard_map/ppermute | solution.py:22
  98.8 4.3 %collective-permute-start.19 = (f32[2,2,128,128]{3,2,1,0:T(8,128)S(1)}, f32[2,2,128,128]{3,2,1,0:T(8,128)S(1)}, u32[]{:S(2)}, u32[]{:S(2)}) collective-permute-start(f32[2,2,128,128]{3,2,1,0:T(8,128)S(1)} %slice_bitcast_fusion.1), channel_id=1, source_target_pairs={{0,24},{1,25},{2,26},{3,27},{4,28},{5,29},{6,30},{7,31},{8,0},{9,1... | collective-permute-start | bytes 786440 | tf_op jit(solution)/shard_map/ppermute | solution.py:18
  103.1 2.1 %collective-permute-start.20 = (f32[2,2,128,128]{3,2,1,0:T(8,128)S(1)}, f32[2,2,128,128]{3,2,1,0:T(8,128)S(1)}, u32[]{:S(2)}, u32[]{:S(2)}) collective-permute-start(f32[2,2,128,128]{3,2,1,0:T(8,128)S(1)} %slice_bitcast_fusion), channel_id=1, source_target_pairs={{0,8},{1,9},{2,10},{3,11},{4,12},{5,13},{6,14},{7,15},{8,16},{9,17... | collective-permute-start | bytes 786440 | tf_op jit(solution)/shard_map/ppermute | solution.py:18
  105.2 6.1 %shard_map.53 = (f32[128,128]{1,0:T(8,128)S(1)}, f32[128,512]{1,0:T(8,128)S(1)}) custom-call(f32[512,128]{1,0:T(8,128)S(1)} %get-tuple-element.46.refs_0_.f0, f32[384,128]{1,0:T(8,128)S(1)} %get-tuple-element.49.refs_1_.f1, f32[256,128]{1,0:T(8,128)S(1)} %get-tuple-element.55.refs_2_.f2, f32[128,128]{1,0:T(8,128)S(1)} %get-tuple-element.47.refs_1_.refs_2_.refs_3_.g0, ...), custom_call_target="tpu_custom_call" | custom-call | flops 6000000000 | bytes 1048576 | tf_op jit(solution)/shard_map/pallas_call | solution.py:177
  111.4 0.7 collective-permute-done.20.high_ref
  112.1 4.7 %collective-permute-start.25 = (f32[2,128,640]{2,1,0:T(8,128)S(1)}, f32[2,128,640]{2,1,0:T(8,128)S(1)}, u32[]{:S(2)}, u32[]{:S(2)}) collective-permute-start(f32[2,128,640]{2,1,0:T(8,128)S(1)} %pad_maximum_fusion.own_ref), channel_id=1, source_target_pairs={{0,32},{32,0},{64,96},{96,64},{128,160},{160,128},{192,224},{224,1... | collective-permute-start | bytes 1966088 | tf_op jit(solution)/shard_map/ppermute | solution.py:22
  116.8 1.7 %collective-permute-done.25.got_ref = f32[2,128,640]{2,1,0:T(8,128)S(1)} collective-permute-done((f32[2,128,640]{2,1,0:T(8,128)S(1)}, f32[2,128,640]{2,1,0:T(8,128)S(1)}, u32[]{:S(2)}, u32[]{:S(2)}) %collective-permute-start.25) | collective-permute-done | bytes 655392 | tf_op jit(solution)/shard_map/ppermute | solution.py:22
  118.5 2.8 %shard_map.54 = (bf16[512,640]{1,0:T(8,128)(2,1)S(1)}, bf16[512,640]{1,0:T(8,128)(2,1)S(1)}, f32[512,128]{1,0:T(8,128)S(1)}, bf16[512,512]{1,0:T(8,128)(2,1)S(1)...) custom-call(s32[8]{0:T(128)S(1)} %concatenate.6.at_ref, f32[2,128,640]{2,1,0:T(8,128)S(1)} %pad_maximum_fusion.own_ref, ...), custom_call_target="tpu_custom_call" | custom-call | flops 4000000000 | bytes 4194304 | tf_op jit(solution)/shard_map/pallas_call | solution.py:221
  121.3 11.1 %shard_map.55 = (f32[1024,512]{1,0:T(8,128)}, f32[1024,128]{1,0:T(8,128)}) custom-call(s32[8]{0:T(128)S(1)} %concatenate.6.at_ref, f32[2,2,2,128,128]{4,3,2,1,0:T(8,128)S(1)} %pad_maximum_fusion.2.q0_ref, f32[2,2,2,128,128]{4,3,2,1,0:T(8,128)S(1)} %collective-permute-done.17.q1_ref, f32[2,2,2,128,128]{4,3,2,1,0:T(8,128)S(1)} %collective-permute-done.18.q2_ref, ...), custom_call_target="tpu_custom_call" | custom-call | flops 10000000000 | bytes 6291456 | tf_op jit(solution)/shard_map/pallas_call | solution.py:286
  (40 shorter events, 0.4 us)
Async XLA Ops:
  1.5 8.1 %collective-permute-start.1 = (f32[128,128]{1,0:T(8,128)S(1)}, f32[128,128]{1,0:T(8,128)S(1)}, u32[]{:S(2)}, u32[]{:S(2)}) collective-permute-start(f32[128,128]{1,0:T(8,128)S(1)} %slice_select_fusion), channel_id=1, source_target_pairs={{0,16},{1,17},{2,18},{3,19},{32,48},{33,49},{34,50},{35,51},{64,80... | collective-permute-start | bytes 196616 | tf_op jit(solution)/shard_map/ppermute | solution.py:326
  7.0 2.6 %collective-permute-start.2 = (f32[128,128]{1,0:T(8,128)S(1)}, f32[128,128]{1,0:T(8,128)S(1)}, u32[]{:S(2)}, u32[]{:S(2)}) collective-permute-start(f32[128,128]{1,0:T(8,128)S(1)} %slice_select_fusion), channel_id=1, source_target_pairs={{0,24},{1,25},{2,26},{3,27},{32,56},{33,57},{34,58},{35,59},{64,88... | collective-permute-start | bytes 196616 | tf_op jit(solution)/shard_map/ppermute | solution.py:326
  8.3 2.9 %collective-permute-start = (f32[128,128]{1,0:T(8,128)S(1)}, f32[128,128]{1,0:T(8,128)S(1)}, u32[]{:S(2)}, u32[]{:S(2)}) collective-permute-start(f32[128,128]{1,0:T(8,128)S(1)} %slice_select_fusion), channel_id=1, source_target_pairs={{0,8},{1,9},{2,10},{3,11},{32,40},{33,41},{34,42},{35,43},{64,72},... | collective-permute-start | bytes 196616 | tf_op jit(solution)/shard_map/ppermute | solution.py:326
  12.0 2.6 %collective-permute-start.3 = (f32[128,128]{1,0:T(8,128)S(1)}, f32[128,128]{1,0:T(8,128)S(1)}, u32[]{:S(2)}, u32[]{:S(2)}) collective-permute-start(f32[128,128]{1,0:T(8,128)S(1)} %add_add_fusion.3), channel_id=1, source_target_pairs={{0,7},{1,6},{2,5},{3,4},{8,15},{9,14},{10,13},{11,12},{16,23},{17,... | collective-permute-start | bytes 196616 | tf_op jit(solution)/shard_map/ppermute | solution.py:330
  14.7 10.7 %collective-permute-start.9 = (f32[128,128]{1,0:T(8,128)S(1)}, f32[128,128]{1,0:T(8,128)S(1)}, u32[]{:S(2)}, u32[]{:S(2)}) collective-permute-start(f32[128,128]{1,0:T(8,128)S(1)} %add.67), channel_id=1, source_target_pairs={{0,384},{32,416},{64,448},{96,480},{1,385},{33,417},{65,449},{97,4... | collective-permute-start | bytes 196616 | tf_op jit(solution)/shard_map/ppermute | solution.py:22
  17.7 9.0 %collective-permute-start.8 = (f32[128,128]{1,0:T(8,128)S(1)}, f32[128,128]{1,0:T(8,128)S(1)}, u32[]{:S(2)}, u32[]{:S(2)}) collective-permute-start(f32[128,128]{1,0:T(8,128)S(1)} %add.67), channel_id=1, source_target_pairs={{0,256},{32,288},{64,320},{96,352},{1,257},{33,289},{65,321},{97,3... | collective-permute-start | bytes 196616 | tf_op jit(solution)/shard_map/ppermute | solution.py:22
  19.0 7.7 %collective-permute-start.7 = (f32[128,128]{1,0:T(8,128)S(1)}, f32[128,128]{1,0:T(8,128)S(1)}, u32[]{:S(2)}, u32[]{:S(2)}) collective-permute-start(f32[128,128]{1,0:T(8,128)S(1)} %add.67), channel_id=1, source_target_pairs={{0,128},{32,160},{64,192},{96,224},{1,129},{33,161},{65,193},{97,2... | collective-permute-start | bytes 196616 | tf_op jit(solution)/shard_map/ppermute | solution.py:22
  20.3 6.5 %collective-permute-start.4 = (f32[2,128,128]{2,1,0:T(8,128)S(1)}, f32[2,128,128]{2,1,0:T(8,128)S(1)}, u32[]{:S(2)}, u32[]{:S(2)}) collective-permute-start(f32[2,128,128]{2,1,0:T(8,128)S(1)} %get-tuple-element.72), channel_id=1, source_target_pairs={{0,8},{1,9},{2,10},{3,11},{32,40},{33,41},{34,42},{35,43},{64,72},... | collective-permute-start | bytes 393224 | tf_op jit(solution)/shard_map/ppermute | solution.py:18
  23.5 3.9 %collective-permute-start.6 = (f32[2,128,128]{2,1,0:T(8,128)S(1)}, f32[2,128,128]{2,1,0:T(8,128)S(1)}, u32[]{:S(2)}, u32[]{:S(2)}) collective-permute-start(f32[2,128,128]{2,1,0:T(8,128)S(1)} %get-tuple-element.73), channel_id=1, source_target_pairs={{0,24},{1,25},{2,26},{3,27},{32,56},{33,57},{34,58},{35,59},{64,88... | collective-permute-start | bytes 393224 | tf_op jit(solution)/shard_map/ppermute | solution.py:18
  25.4 4.6 %collective-permute-start.5 = (f32[2,128,128]{2,1,0:T(8,128)S(1)}, f32[2,128,128]{2,1,0:T(8,128)S(1)}, u32[]{:S(2)}, u32[]{:S(2)}) collective-permute-start(f32[2,128,128]{2,1,0:T(8,128)S(1)} %get-tuple-element.74), channel_id=1, source_target_pairs={{0,16},{1,17},{2,18},{3,19},{32,48},{33,49},{34,50},{35,51},{64,80... | collective-permute-start | bytes 393224 | tf_op jit(solution)/shard_map/ppermute | solution.py:18
  26.8 32.8 %copy-start.2 = (s32[4]{0:T(128)S(1)}, s32[4]{0:T(128)}, u32[]{:S(2)}) copy-start(s32[4]{0:T(128)} %constant.58.clone) | copy-start | bytes 52
  30.1 29.7 %slice-start = ((f32[1024,512]{1,0:T(8,128)}), f32[128,512]{1,0:T(8,128)S(1)}, s32[]{:S(2)}) async-start(f32[1024,512]{1,0:T(8,128)} %k_ref.1), calls=%async_computation | async-start | bytes 524288 | tf_op jit(solution)/shard_map/slice | solution.py:351
  30.1 29.7 %slice-start.1 = ((f32[1024,128]{1,0:T(8,128)}), f32[128,128]{1,0:T(8,128)S(1)}, s32[]{:S(2)}) async-start(f32[1024,128]{1,0:T(8,128)} %y_ref.1), calls=%async_computation.1 | async-start | bytes 131072 | tf_op jit(solution)/shard_map/slice | solution.py:351
  30.1 6.4 %collective-permute-start.11 = (f32[128,128]{1,0:T(8,128)S(1)}, f32[128,128]{1,0:T(8,128)S(1)}, u32[]{:S(2)}, u32[]{:S(2)}) collective-permute-start(f32[128,128]{1,0:T(8,128)S(1)} %add_add_fusion.2), channel_id=1, source_target_pairs={{0,2},{1,3},{2,0},{3,1},{4,6},{5,7},{6,4},{7,5},{8,10},{9,11},{10,... | collective-permute-start | bytes 196616 | tf_op jit(solution)/shard_map/ppermute | solution.py:18
  33.1 5.4 %collective-permute-start.10 = (f32[2,128,128]{2,1,0:T(8,128)S(1)}, f32[2,128,128]{2,1,0:T(8,128)S(1)}, u32[]{:S(2)}, u32[]{:S(2)}) collective-permute-start(f32[2,128,128]{2,1,0:T(8,128)S(1)} %add_add_fusion.1), channel_id=1, source_target_pairs={{0,7},{1,6},{2,5},{3,4},{8,15},{9,14},{10,13},{11,12},{16,23},{17,... | collective-permute-start | bytes 393224 | tf_op jit(solution)/shard_map/ppermute | solution.py:18
  36.5 5.7 %collective-permute-start.12 = (f32[2,128,128]{2,1,0:T(8,128)S(1)}, f32[2,128,128]{2,1,0:T(8,128)S(1)}, u32[]{:S(2)}, u32[]{:S(2)}) collective-permute-start(f32[2,128,128]{2,1,0:T(8,128)S(1)} %get-tuple-element.78), channel_id=1, source_target_pairs={{0,1},{1,0},{2,3},{3,2},{4,5},{5,4},{6,7},{7,6},{8,9},{9,8},{10,11... | collective-permute-start | bytes 393224 | tf_op jit(solution)/shard_map/ppermute | solution.py:18
  42.2 11.4 %collective-permute-start.14 = (f32[2,2,128,128]{3,2,1,0:T(8,128)S(1)}, f32[2,2,128,128]{3,2,1,0:T(8,128)S(1)}, u32[]{:S(2)}, u32[]{:S(2)}) collective-permute-start(f32[2,2,128,128]{3,2,1,0:T(8,128)S(1)} %pad_maximum_fusion.3), channel_id=1, source_target_pairs={{0,64},{32,96},{64,0},{96,32},{128,192},{160,224},{192,128},{224,1... | collective-permute-start | bytes 786440 | tf_op jit(solution)/shard_map/ppermute | solution.py:22
  45.7 7.9 %collective-permute-start.13 = (f32[2,128,128]{2,1,0:T(8,128)S(1)}, f32[2,128,128]{2,1,0:T(8,128)S(1)}, u32[]{:S(2)}, u32[]{:S(2)}) collective-permute-start(f32[2,128,128]{2,1,0:T(8,128)S(1)} %broadcast_select_fusion), channel_id=1, source_target_pairs={{0,2},{1,3},{2,0},{3,1},{4,6},{5,7},{6,4},{7,5},{8,10},{9,11},{10,... | collective-permute-start | bytes 393224 | tf_op jit(solution)/shard_map/ppermute | solution.py:18
  53.7 16.0 %collective-permute-start.16 = (f32[2,2,2,128,128]{4,3,2,1,0:T(8,128)S(1)}, f32[2,2,2,128,128]{4,3,2,1,0:T(8,128)S(1)}, u32[]{:S(2)}, u32[]{:S(2)}) collective-permute-start(f32[2,2,2,128,128]{4,3,2,1,0:T(8,128)S(1)} %pad_maximum_fusion.1.own_ref), channel_id=1, source_target_pairs={{0,32},{32,0},{64,96},{96,64},{128,160},{160,128},{192,224},{224,1... | collective-permute-start | bytes 1572872 | tf_op jit(solution)/shard_map/ppermute | solution.py:22
  59.8 35.2 %collective-permute-start.23 = (f32[128,640]{1,0:T(8,128)S(1)}, f32[128,640]{1,0:T(8,128)S(1)}, u32[]{:S(2)}, u32[]{:S(2)}) collective-permute-start(f32[128,640]{1,0:T(8,128)S(1)} %maximum_select_fusion), channel_id=1, source_target_pairs={{0,384},{32,416},{64,448},{96,480},{1,385},{33,417},{65,449},{97,4... | collective-permute-start | bytes 983048 | tf_op jit(solution)/shard_map/ppermute | solution.py:22
  64.4 30.6 %collective-permute-start.22 = (f32[128,640]{1,0:T(8,128)S(1)}, f32[128,640]{1,0:T(8,128)S(1)}, u32[]{:S(2)}, u32[]{:S(2)}) collective-permute-start(f32[128,640]{1,0:T(8,128)S(1)} %maximum_select_fusion), channel_id=1, source_target_pairs={{0,256},{32,288},{64,320},{96,352},{1,257},{33,289},{65,321},{97,3... | collective-permute-start | bytes 983048 | tf_op jit(solution)/shard_map/ppermute | solution.py:22
  65.8 29.2 %collective-permute-start.21 = (f32[128,640]{1,0:T(8,128)S(1)}, f32[128,640]{1,0:T(8,128)S(1)}, u32[]{:S(2)}, u32[]{:S(2)}) collective-permute-start(f32[128,640]{1,0:T(8,128)S(1)} %maximum_select_fusion), channel_id=1, source_target_pairs={{0,128},{32,160},{64,192},{96,224},{1,129},{33,161},{65,193},{97,2... | collective-permute-start | bytes 983048 | tf_op jit(solution)/shard_map/ppermute | solution.py:22
  67.1 9.6 %collective-permute-start.15 = (f32[2,2,128,128]{3,2,1,0:T(8,128)S(1)}, f32[2,2,128,128]{3,2,1,0:T(8,128)S(1)}, u32[]{:S(2)}, u32[]{:S(2)}) collective-permute-start(f32[2,2,128,128]{3,2,1,0:T(8,128)S(1)} %get-tuple-element.43), channel_id=1, source_target_pairs={{0,1},{1,0},{2,3},{3,2},{4,5},{5,4},{6,7},{7,6},{8,9},{9,8},{10,11... | collective-permute-start | bytes 786440 | tf_op jit(solution)/shard_map/ppermute | solution.py:18
  76.7 22.0 %collective-permute-start.18 = (f32[2,2,2,128,128]{4,3,2,1,0:T(8,128)S(1)}, f32[2,2,2,128,128]{4,3,2,1,0:T(8,128)S(1)}, u32[]{:S(2)}, u32[]{:S(2)}) collective-permute-start(f32[2,2,2,128,128]{4,3,2,1,0:T(8,128)S(1)} %pad_maximum_fusion.2.q0_ref), channel_id=1, source_target_pairs={{0,24},{1,25},{2,26},{3,27},{4,28},{5,29},{6,30},{7,31},{8,0},{9,1... | collective-permute-start | bytes 1572872 | tf_op jit(solution)/shard_map/ppermute | solution.py:18
  78.6 24.4 %collective-permute-start.17 = (f32[2,2,2,128,128]{4,3,2,1,0:T(8,128)S(1)}, f32[2,2,2,128,128]{4,3,2,1,0:T(8,128)S(1)}, u32[]{:S(2)}, u32[]{:S(2)}) collective-permute-start(f32[2,2,2,128,128]{4,3,2,1,0:T(8,128)S(1)} %pad_maximum_fusion.2.q0_ref), channel_id=1, source_target_pairs={{0,8},{1,9},{2,10},{3,11},{4,12},{5,13},{6,14},{7,15},{8,16},{9,17... | collective-permute-start | bytes 1572872 | tf_op jit(solution)/shard_map/ppermute | solution.py:18
  95.1 16.2 %collective-permute-start.24 = (f32[128,640]{1,0:T(8,128)S(1)}, f32[128,640]{1,0:T(8,128)S(1)}, u32[]{:S(2)}, u32[]{:S(2)}) collective-permute-start(f32[128,640]{1,0:T(8,128)S(1)} %add_add_fusion), channel_id=1, source_target_pairs={{0,64},{32,96},{64,0},{96,32},{128,192},{160,224},{192,128},{224,1... | collective-permute-start | bytes 983048 | tf_op jit(solution)/shard_map/ppermute | solution.py:22
  98.8 12.6 %collective-permute-start.19 = (f32[2,2,128,128]{3,2,1,0:T(8,128)S(1)}, f32[2,2,128,128]{3,2,1,0:T(8,128)S(1)}, u32[]{:S(2)}, u32[]{:S(2)}) collective-permute-start(f32[2,2,128,128]{3,2,1,0:T(8,128)S(1)} %slice_bitcast_fusion.1), channel_id=1, source_target_pairs={{0,24},{1,25},{2,26},{3,27},{4,28},{5,29},{6,30},{7,31},{8,0},{9,1... | collective-permute-start | bytes 786440 | tf_op jit(solution)/shard_map/ppermute | solution.py:18
  103.1 9.0 %collective-permute-start.20 = (f32[2,2,128,128]{3,2,1,0:T(8,128)S(1)}, f32[2,2,128,128]{3,2,1,0:T(8,128)S(1)}, u32[]{:S(2)}, u32[]{:S(2)}) collective-permute-start(f32[2,2,128,128]{3,2,1,0:T(8,128)S(1)} %slice_bitcast_fusion), channel_id=1, source_target_pairs={{0,8},{1,9},{2,10},{3,11},{4,12},{5,13},{6,14},{7,15},{8,16},{9,17... | collective-permute-start | bytes 786440 | tf_op jit(solution)/shard_map/ppermute | solution.py:18
  111.4 9.9 %copy-start = (f32[1024,512]{1,0:T(8,128)S(1)}, f32[1024,512]{1,0:T(8,128)}, u32[]{:S(2)}) copy-start(f32[1024,512]{1,0:T(8,128)} %k_ref.1) | copy-start | bytes 6291460
  111.4 9.9 %copy-start.1 = (f32[1024,128]{1,0:T(8,128)S(1)}, f32[1024,128]{1,0:T(8,128)}, u32[]{:S(2)}) copy-start(f32[1024,128]{1,0:T(8,128)} %y_ref.1) | copy-start | bytes 1572868
  112.1 6.4 %collective-permute-start.25 = (f32[2,128,640]{2,1,0:T(8,128)S(1)}, f32[2,128,640]{2,1,0:T(8,128)S(1)}, u32[]{:S(2)}, u32[]{:S(2)}) collective-permute-start(f32[2,128,640]{2,1,0:T(8,128)S(1)} %pad_maximum_fusion.own_ref), channel_id=1, source_target_pairs={{0,32},{32,0},{64,96},{96,64},{128,160},{160,128},{192,224},{224,1... | collective-permute-start | bytes 1966088 | tf_op jit(solution)/shard_map/ppermute | solution.py:22

commit v5 on v4

--- a/solution.py
+++ b/solution.py
@@ -234,30 +234,29 @@
     step = pl.program_id(0)
     row, col = at_ref[2], at_ref[3]
     n = BLOCK
-
-    def fill(read):
-        for j in range(4):
-            t = at_ref[1] ^ j
+    rows = w.shape[0]
+
+    @pl.when(step == 0)
+    def _():
+        for s in range(4):
             for b in range(2):
-                pan[b * n : (b + 1) * n, j * n : (j + 1) * n] = read(t % 2, t // 2, b)
-
-    for s, ref in enumerate((q0_ref, q1_ref, q2_ref)):
-        @pl.when(step == s)
-        def _(ref=ref):
-            fill(lambda t1, t2, b: ref[t1, t2, b])
-
-    @pl.when(step == 3)
-    def _():
-        fill(lambda t1, t2, b: jnp.where(t1 == 0, low_ref[t2, b], high_ref[t2, b]))
-
-    p = split(pan[...], 3)
+                here = pl.ds(pl.multiple_of(at_ref[4 + s] * 2 * n + b * n, n), n)
+                for j in range(4):
+                    t = at_ref[1] ^ j
+                    if s < 3:
+                        value = (q0_ref, q1_ref, q2_ref)[s][t % 2, t // 2, b]
+                    else:
+                        value = jnp.where(t % 2 == 0, low_ref[t // 2, b], high_ref[t // 2, b])
+                    pan[here, j * n : (j + 1) * n] = value
+
+    p = split(pan[pl.ds(pl.multiple_of(step * rows, rows), rows), :], 3)
     for cols, depth in ((slice(0, 256), 256), (slice(256, 512), 512)):
         a = [part[:, :depth] for part in p]
         b = [t_ref[:depth, cols] for t_ref in (t0, t1, t2)]
         small = once(a[0], b[2]) + once(a[1], b[1]) + once(a[2], b[0])
         w[:, cols] = once(a[0], b[0]) + ((once(a[0], b[1]) + once(a[1], b[0])) + small)
 
-    first = (at_ref[4 + step] == 0) & (row < 4)
+    first = (step == 0) & (row < 4)
     for i in range(4):
         @pl.when(first & (row == i))
         def _(i=i):
@@ -281,19 +280,19 @@
 
 
 def update(at, parts, fs, strips, kernel, targets):
-    rows = 256
-    moved = lambda width: pl.BlockSpec((rows, width), lambda s, at: (at[4 + s], 0))
+    rows = 512
+    moved = lambda width: pl.BlockSpec((rows, width), lambda s: (s, 0))
     return pl.pallas_call(
         update_kernel,
         out_shape=[f32(*kernel.shape), f32(*targets.shape)],
-        grid_spec=pltpu.PrefetchScalarGridSpec(
-            num_scalar_prefetch=1,
-            grid=(4,),
-            in_specs=[VMEM] * 15 + [moved(ORDER), moved(BLOCK)],
-            out_specs=[moved(ORDER), moved(BLOCK)],
-            scratch_shapes=[pltpu.VMEM((rows, ORDER), jnp.float32)] * 2,
-        ),
-        compiler_params=pltpu.CompilerParams(vmem_limit_bytes=16 * 2**20),
+        grid=(kernel.shape[0] // rows,),
+        in_specs=[SMEM] + [VMEM] * 15 + [moved(ORDER), moved(BLOCK)],
+        out_specs=[moved(ORDER), moved(BLOCK)],
+        scratch_shapes=[
+            pltpu.VMEM((kernel.shape[0], ORDER), jnp.float32),
+            pltpu.VMEM((rows, ORDER), jnp.float32),
+        ],
+        compiler_params=pltpu.CompilerParams(vmem_limit_bytes=24 * 2**20),
         cost_estimate=pl.CostEstimate(flops=10**10, bytes_accessed=6 * 2**20, transcendentals=0),
     )(at, *parts, *fs, *strips, kernel, targets)
 
@@ -357,17 +356,17 @@
     down = over_col(p4, [(c, (c + Y) % COLS) for c in range(COLS)])
     up = over_col(p4, [(c, (c - Y) % COLS) for c in range(COLS)])
     f1, g1, rest = factor_step(1, [f0], [g0], after(rest, p4))
-    f2, g2, rest = factor_step(2, [f0, f1], [g0, g1], rest)
+    c2 = total([strip] + [after(got, rest) for got in strip_got])
+    c3_got = over_row(c2, by_z)
+    f2, g2, rest = factor_step(2, [f0, f1], [g0, g1], after(rest, c2))
     down, up = after(down, rest), after(up, rest)
     near, far = up[0], down[1]
     low = over_col(near, [(c, (c - Y) % COLS) for c in range(COLS)])
     high = over_col(far, [(c, (c + Y) % COLS) for c in range(COLS)])
-    c2 = total([strip] + [after(got, rest) for got in strip_got])
-    c3_got = over_row(c2, by_z)
-    f3, g3 = factor_step(3, [f0, f1, f2], [g0, g1, g2], after(rest, near, far, c2))
-    c3 = after(jnp.stack([c2, after(c3_got, g3)]), low, high)
+    c3 = jnp.stack([c2, after(c3_got, rest)])
     c4 = over_row(c3, by_core)
-    strips = strip_solve(at, c3, c4, (g0, g1, g2, g3))
+    f3, g3 = factor_step(3, [f0, f1, f2], [g0, g1, g2], after(rest, near, far, c3))
+    strips = strip_solve(at, c3, after(c4, g3, low, high), (g0, g1, g2, g3))
     return tuple(
         update(at, (p4, down, up, low, high), (f0, f1, f2, f3), strips, kernel, targets)
     )

time: 133 us -> 136 us (1.023)
  waiting for transfers between devices: 18.2 us -> 20.1 us
  Pallas kernels: 39.7 us -> 41.1 us
    pallas_call x1, Pallas kernels: 11.1 us -> 12.5 us  [update(): pl.pallas_call(update_kernel, out_shape=[f32(*kernel.shape), f32(*targets...]
where the time goes in v5:
time: 136 us; the launch traced here: 135 us
  starting transfers between devices  69.1 us (51%)
  Pallas kernels  41.1 us (30%)
  waiting for transfers between devices  20.1 us (15%)
  other arithmetic  2.14 us (2%)
    ppermute x10, starting transfers between devices, over_row(): return lax.ppermute(value, 'row', pairs)  30.2 us
    ppermute x12, starting transfers between devices, over_col(): return lax.ppermute(value, 'col', pairs)  29.5 us
    pallas_call x3, Pallas kernels, factor_step(): pl.pallas_call(functools.partial(step_kernel, k), out_shape=shapes, in_sp...  18.9 us
    ppermute x12, waiting for transfers between devices, over_col(): return lax.ppermute(value, 'col', pairs)  15.7 us
    pallas_call x1, Pallas kernels, update(): pl.pallas_call(update_kernel, out_shape=[f32(*kernel.shape), f32(*targets...  12.5 us
    ppermute x3, starting transfers between devices, per_device(): got.append(lax.ppermute(a0, ('row', 'col'), pairs))  8.05 us
    pallas_call x1, Pallas kernels, factor_first(): pl.pallas_call(first_kernel, out_shape=[f32(ORDER, BLOCK), f32(BLOCK, BLO...  6.91 us
    pallas_call x1, Pallas kernels, strip_solve(): pl.pallas_call(strip_kernel, out_shape=[b16(*wide)] * 2 + [f32(ORDER, BLO...  2.77 us
  transfers between devices with their start and end apart: 26, of which 9 were waited for; matrix products, arithmetic and copies ran while one was open for 1% of the time, Pallas kernels for 19%

profile of v5, /device:TPU:1, one launch (start us, length us, event | category | flops | bytes accessed | tf_op | source)
XLA Modules:
  0.0 134.8 jit_solution(9997872239753774345)
XLA Ops:
  0.6 0.8 slice_select_fusion
  1.5 5.5 %collective-permute-start.1 = (f32[128,128]{1,0:T(8,128)S(1)}, f32[128,128]{1,0:T(8,128)S(1)}, u32[]{:S(2)}, u32[]{:S(2)}) collective-permute-start(f32[128,128]{1,0:T(8,128)S(1)} %slice_select_fusion), channel_id=1, source_target_pairs={{0,16},{1,17},{2,18},{3,19},{32,48},{33,49},{34,50},{35,51},{64,80... | collective-permute-start | bytes 196616 | tf_op jit(solution)/shard_map/ppermute | solution.py:325
  7.0 1.3 collective-permute-start.2
  8.3 1.3 collective-permute-start
  9.6 1.6 %collective-permute-done = f32[128,128]{1,0:T(8,128)S(1)} collective-permute-done((f32[128,128]{1,0:T(8,128)S(1)}, f32[128,128]{1,0:T(8,128)S(1)}, u32[]{:S(2)}, u32[]{:S(2)}) %collective-permute-start) | collective-permute-done | bytes 65568 | tf_op jit(solution)/shard_map/ppermute | solution.py:325
  11.2 0.9 add_add_fusion.3
  12.0 1.3 collective-permute-start.3
  13.4 1.1 slice.30
  14.5 0.2 collective-permute-done.3
  14.7 3.0 %collective-permute-start.9 = (f32[128,128]{1,0:T(8,128)S(1)}, f32[128,128]{1,0:T(8,128)S(1)}, u32[]{:S(2)}, u32[]{:S(2)}) collective-permute-start(f32[128,128]{1,0:T(8,128)S(1)} %add.67), channel_id=1, source_target_pairs={{0,384},{32,416},{64,448},{96,480},{1,385},{33,417},{65,449},{97,4... | collective-permute-start | bytes 196616 | tf_op jit(solution)/shard_map/ppermute | solution.py:22
  17.7 1.3 collective-permute-start.8
  19.0 1.3 collective-permute-start.7
  20.3 3.1 %collective-permute-start.4 = (f32[2,128,128]{2,1,0:T(8,128)S(1)}, f32[2,128,128]{2,1,0:T(8,128)S(1)}, u32[]{:S(2)}, u32[]{:S(2)}) collective-permute-start(f32[2,128,128]{2,1,0:T(8,128)S(1)} %get-tuple-element.74), channel_id=1, source_target_pairs={{0,8},{1,9},{2,10},{3,11},{32,40},{33,41},{34,42},{35,43},{64,72},... | collective-permute-start | bytes 393224 | tf_op jit(solution)/shard_map/ppermute | solution.py:18
  23.5 1.9 %collective-permute-start.6 = (f32[2,128,128]{2,1,0:T(8,128)S(1)}, f32[2,128,128]{2,1,0:T(8,128)S(1)}, u32[]{:S(2)}, u32[]{:S(2)}) collective-permute-start(f32[2,128,128]{2,1,0:T(8,128)S(1)} %get-tuple-element.75), channel_id=1, source_target_pairs={{0,24},{1,25},{2,26},{3,27},{32,56},{33,57},{34,58},{35,59},{64,88... | collective-permute-start | bytes 393224 | tf_op jit(solution)/shard_map/ppermute | solution.py:18
  25.4 1.3 collective-permute-start.5
  26.8 0.5 collective-permute-done.6
  27.3 2.7 %collective-permute-done.5 = f32[2,128,128]{2,1,0:T(8,128)S(1)} collective-permute-done((f32[2,128,128]{2,1,0:T(8,128)S(1)}, f32[2,128,128]{2,1,0:T(8,128)S(1)}, u32[]{:S(2)}, u32[]{:S(2)}) %collective-permute-start.5) | collective-permute-done | bytes 131104 | tf_op jit(solution)/shard_map/ppermute | solution.py:18
  30.1 3.0 %collective-permute-start.11 = (f32[128,128]{1,0:T(8,128)S(1)}, f32[128,128]{1,0:T(8,128)S(1)}, u32[]{:S(2)}, u32[]{:S(2)}) collective-permute-start(f32[128,128]{1,0:T(8,128)S(1)} %add_add_fusion.2), channel_id=1, source_target_pairs={{0,2},{1,3},{2,0},{3,1},{4,6},{5,7},{6,4},{7,5},{8,10},{9,11},{10,... | collective-permute-start | bytes 196616 | tf_op jit(solution)/shard_map/ppermute | solution.py:18
  33.1 1.3 collective-permute-start.10
  34.4 2.1 %collective-permute-done.11 = f32[128,128]{1,0:T(8,128)S(1)} collective-permute-done((f32[128,128]{1,0:T(8,128)S(1)}, f32[128,128]{1,0:T(8,128)S(1)}, u32[]{:S(2)}, u32[]{:S(2)}) %collective-permute-start.11) | collective-permute-done | bytes 65568 | tf_op jit(solution)/shard_map/ppermute | solution.py:18
  36.5 1.9 %collective-permute-start.12 = (f32[2,128,128]{2,1,0:T(8,128)S(1)}, f32[2,128,128]{2,1,0:T(8,128)S(1)}, u32[]{:S(2)}, u32[]{:S(2)}) collective-permute-start(f32[2,128,128]{2,1,0:T(8,128)S(1)} %get-tuple-element.80), channel_id=1, source_target_pairs={{0,1},{1,0},{2,3},{3,2},{4,5},{5,4},{6,7},{7,6},{8,9},{9,8},{10,11... | collective-permute-start | bytes 393224 | tf_op jit(solution)/shard_map/ppermute | solution.py:18
  38.5 3.7 %collective-permute-done.12 = f32[2,128,128]{2,1,0:T(8,128)S(1)} collective-permute-done((f32[2,128,128]{2,1,0:T(8,128)S(1)}, f32[2,128,128]{2,1,0:T(8,128)S(1)}, u32[]{:S(2)}, u32[]{:S(2)}) %collective-permute-start.12) | collective-permute-done | bytes 131104 | tf_op jit(solution)/shard_map/ppermute | solution.py:18
  42.2 3.5 %collective-permute-start.14 = (f32[2,2,128,128]{3,2,1,0:T(8,128)S(1)}, f32[2,2,128,128]{3,2,1,0:T(8,128)S(1)}, u32[]{:S(2)}, u32[]{:S(2)}) collective-permute-start(f32[2,2,128,128]{3,2,1,0:T(8,128)S(1)} %pad_maximum_fusion.3), channel_id=1, source_target_pairs={{0,64},{32,96},{64,0},{96,32},{128,192},{160,224},{192,128},{224,1... | collective-permute-start | bytes 786440 | tf_op jit(solution)/shard_map/ppermute | solution.py:22
  45.7 3.0 %collective-permute-start.13 = (f32[2,128,128]{2,1,0:T(8,128)S(1)}, f32[2,128,128]{2,1,0:T(8,128)S(1)}, u32[]{:S(2)}, u32[]{:S(2)}) collective-permute-start(f32[2,128,128]{2,1,0:T(8,128)S(1)} %broadcast_select_fusion), channel_id=1, source_target_pairs={{0,2},{1,3},{2,0},{3,1},{4,6},{5,7},{6,4},{7,5},{8,10},{9,11},{10,... | collective-permute-start | bytes 393224 | tf_op jit(solution)/shard_map/ppermute | solution.py:18
  48.7 4.9 %collective-permute-done.13 = f32[2,128,128]{2,1,0:T(8,128)S(1)} collective-permute-done((f32[2,128,128]{2,1,0:T(8,128)S(1)}, f32[2,128,128]{2,1,0:T(8,128)S(1)}, u32[]{:S(2)}, u32[]{:S(2)}) %collective-permute-start.13) | collective-permute-done | bytes 131104 | tf_op jit(solution)/shard_map/ppermute | solution.py:18
  53.7 0.1 pad_maximum_fusion.1.own_ref
  53.7 5.9 %collective-permute-start.16 = (f32[2,2,2,128,128]{4,3,2,1,0:T(8,128)S(1)}, f32[2,2,2,128,128]{4,3,2,1,0:T(8,128)S(1)}, u32[]{:S(2)}, u32[]{:S(2)}) collective-permute-start(f32[2,2,2,128,128]{4,3,2,1,0:T(8,128)S(1)} %pad_maximum_fusion.1.own_ref), channel_id=1, source_target_pairs={{0,32},{32,0},{64,96},{96,64},{128,160},{160,128},{192,224},{224,1... | collective-permute-start | bytes 1572872 | tf_op jit(solution)/shard_map/ppermute | solution.py:22
  59.6 0.1 concatenate.6.at_ref
  59.8 4.7 %collective-permute-start.20 = (f32[128,640]{1,0:T(8,128)S(1)}, f32[128,640]{1,0:T(8,128)S(1)}, u32[]{:S(2)}, u32[]{:S(2)}) collective-permute-start(f32[128,640]{1,0:T(8,128)S(1)} %maximum_select_fusion), channel_id=1, source_target_pairs={{0,384},{32,416},{64,448},{96,480},{1,385},{33,417},{65,449},{97,4... | collective-permute-start | bytes 983048 | tf_op jit(solution)/shard_map/ppermute | solution.py:22
  64.4 1.3 collective-permute-start.19
  65.8 1.3 collective-permute-start.18
  67.1 2.6 %collective-permute-start.15 = (f32[2,2,128,128]{3,2,1,0:T(8,128)S(1)}, f32[2,2,128,128]{3,2,1,0:T(8,128)S(1)}, u32[]{:S(2)}, u32[]{:S(2)}) collective-permute-start(f32[2,2,128,128]{3,2,1,0:T(8,128)S(1)} %get-tuple-element.44), channel_id=1, source_target_pairs={{0,1},{1,0},{2,3},{3,2},{4,5},{5,4},{6,7},{7,6},{8,9},{9,8},{10,11... | collective-permute-start | bytes 786440 | tf_op jit(solution)/shard_map/ppermute | solution.py:18
  69.7 6.9 %shard_map.50 = (f32[512,128]{1,0:T(8,128)S(1)}, f32[128,128]{1,0:T(8,128)S(1)}, f32[384,384]{1,0:T(8,128)S(1)}) custom-call(s32[8]{0:T(128)S(1)} %concatenate.6.at_ref, f32[2,2,2,128,128]{4,3,2,1,0:T(8,128)S(1)} %pad_maximum_fusion.1.own_ref, f32[2,2,2,128,128]{4,3,2,1,0:T(8,128)S(1)} %collective-permute-done.16.got_ref), custom_call_target="tpu_custom_call" | custom-call | flops 6000000000 | bytes 1048576 | tf_op jit(solution)/shard_map/pallas_call | solution.py:162
  76.7 6.3 %shard_map.51 = (f32[384,128]{1,0:T(8,128)S(1)}, f32[128,256]{1,0:T(8,128)S(1)}, f32[256,256]{1,0:T(8,128)S(1)}) custom-call(f32[512,128]{1,0:T(8,128)S(1)} %get-tuple-element.47.refs_0_.f0, f32[128,128]{1,0:T(8,128)S(1)} %get-tuple-element.48.refs_1_.refs_2_.refs_3_.g0, f32[384,384]{1,0:T(8,128)S(1)} %get-tuple-element.49.refs_2_), custom_call_target="tpu_custom_call" | custom-call | flops 6000000000 | bytes 1048576 | tf_op jit(solution)/shard_map/pallas_call | solution.py:177
  83.0 2.6 %collective-permute-done.20 = f32[128,640]{1,0:T(8,128)S(1)} collective-permute-done((f32[128,640]{1,0:T(8,128)S(1)}, f32[128,640]{1,0:T(8,128)S(1)}, u32[]{:S(2)}, u32[]{:S(2)}) %collective-permute-start.20) | collective-permute-done | bytes 327712 | tf_op jit(solution)/shard_map/ppermute | solution.py:22
  85.6 0.1 add_add_fusion
  85.7 4.8 %collective-permute-start.24 = (f32[128,640]{1,0:T(8,128)S(1)}, f32[128,640]{1,0:T(8,128)S(1)}, u32[]{:S(2)}, u32[]{:S(2)}) collective-permute-start(f32[128,640]{1,0:T(8,128)S(1)} %add_add_fusion), channel_id=1, source_target_pairs={{0,64},{32,96},{64,0},{96,32},{128,192},{160,224},{192,128},{224,1... | collective-permute-start | bytes 983048 | tf_op jit(solution)/shard_map/ppermute | solution.py:22
  90.4 1.9 %collective-permute-start.21 = (f32[2,2,2,128,128]{4,3,2,1,0:T(8,128)S(1)}, f32[2,2,2,128,128]{4,3,2,1,0:T(8,128)S(1)}, u32[]{:S(2)}, u32[]{:S(2)}) collective-permute-start(f32[2,2,2,128,128]{4,3,2,1,0:T(8,128)S(1)} %pad_maximum_fusion.2.q0_ref), channel_id=1, source_target_pairs={{0,24},{1,25},{2,26},{3,27},{4,28},{5,29},{6,30},{7,31},{8,0},{9,1... | collective-permute-start | bytes 1572872 | tf_op jit(solution)/shard_map/ppermute | solution.py:18
  92.4 3.5 %collective-permute-start.17 = (f32[2,2,2,128,128]{4,3,2,1,0:T(8,128)S(1)}, f32[2,2,2,128,128]{4,3,2,1,0:T(8,128)S(1)}, u32[]{:S(2)}, u32[]{:S(2)}) collective-permute-start(f32[2,2,2,128,128]{4,3,2,1,0:T(8,128)S(1)} %pad_maximum_fusion.2.q0_ref), channel_id=1, source_target_pairs={{0,8},{1,9},{2,10},{3,11},{4,12},{5,13},{6,14},{7,15},{8,16},{9,17... | collective-permute-start | bytes 1572872 | tf_op jit(solution)/shard_map/ppermute | solution.py:18
  95.9 6.5 %shard_map.52 = (f32[256,128]{1,0:T(8,128)S(1)}, f32[128,384]{1,0:T(8,128)S(1)}, f32[128,128]{1,0:T(8,128)S(1)}) custom-call(f32[512,128]{1,0:T(8,128)S(1)} %get-tuple-element.47.refs_0_.f0, f32[384,128]{1,0:T(8,128)S(1)} %get-tuple-element.50.refs_1_.f1, f32[128,128]{1,0:T(8,128)S(1)} %get-tuple-element.48.refs_1_.refs_2_.refs_3_.g0, ...), custom_call_target="tpu_custom_call" | custom-call | flops 6000000000 | bytes 1048576 | tf_op jit(solution)/shard_map/pallas_call | solution.py:177
  102.4 0.1 pad_maximum_fusion.own_ref
  102.5 3.2 %collective-permute-start.25 = (f32[2,128,640]{2,1,0:T(8,128)S(1)}, f32[2,128,640]{2,1,0:T(8,128)S(1)}, u32[]{:S(2)}, u32[]{:S(2)}) collective-permute-start(f32[2,128,640]{2,1,0:T(8,128)S(1)} %pad_maximum_fusion.own_ref), channel_id=1, source_target_pairs={{0,32},{32,0},{64,96},{96,64},{128,160},{160,128},{192,224},{224,1... | collective-permute-start | bytes 1966088 | tf_op jit(solution)/shard_map/ppermute | solution.py:22
  105.7 4.0 %collective-permute-start.22 = (f32[2,2,128,128]{3,2,1,0:T(8,128)S(1)}, f32[2,2,128,128]{3,2,1,0:T(8,128)S(1)}, u32[]{:S(2)}, u32[]{:S(2)}) collective-permute-start(f32[2,2,128,128]{3,2,1,0:T(8,128)S(1)} %slice_bitcast_fusion.1), channel_id=1, source_target_pairs={{0,24},{1,25},{2,26},{3,27},{4,28},{5,29},{6,30},{7,31},{8,0},{9,1... | collective-permute-start | bytes 786440 | tf_op jit(solution)/shard_map/ppermute | solution.py:18
  109.8 1.9 %collective-permute-start.23 = (f32[2,2,128,128]{3,2,1,0:T(8,128)S(1)}, f32[2,2,128,128]{3,2,1,0:T(8,128)S(1)}, u32[]{:S(2)}, u32[]{:S(2)}) collective-permute-start(f32[2,2,128,128]{3,2,1,0:T(8,128)S(1)} %slice_bitcast_fusion), channel_id=1, source_target_pairs={{0,8},{1,9},{2,10},{3,11},{4,12},{5,13},{6,14},{7,15},{8,16},{9,17... | collective-permute-start | bytes 786440 | tf_op jit(solution)/shard_map/ppermute | solution.py:18
  111.7 6.1 %shard_map.53 = (f32[128,128]{1,0:T(8,128)S(1)}, f32[128,512]{1,0:T(8,128)S(1)}) custom-call(f32[512,128]{1,0:T(8,128)S(1)} %get-tuple-element.47.refs_0_.f0, f32[384,128]{1,0:T(8,128)S(1)} %get-tuple-element.50.refs_1_.f1, f32[256,128]{1,0:T(8,128)S(1)} %get-tuple-element.61.refs_2_.f2, f32[128,128]{1,0:T(8,128)S(1)} %get-tuple-element.48.refs_1_.refs_2_.refs_3_.g0, ...), custom_call_target="tpu_custom_call" | custom-call | flops 6000000000 | bytes 1048576 | tf_op jit(solution)/shard_map/pallas_call | solution.py:177
  117.8 1.7 %collective-permute-done.23.high_ref = f32[2,2,128,128]{3,2,1,0:T(8,128)S(1)} collective-permute-done((f32[2,2,128,128]{3,2,1,0:T(8,128)S(1)}, f32[2,2,128,128]{3,2,1,0:T(8,128)S(1)}, u32[]{:S(2)}, u32[]{:S(2)}) %collective-permute-start.23) | collective-permute-done | bytes 262176 | tf_op jit(solution)/shard_map/ppermute | solution.py:18
  119.5 2.8 %shard_map.54 = (bf16[512,640]{1,0:T(8,128)(2,1)S(1)}, bf16[512,640]{1,0:T(8,128)(2,1)S(1)}, f32[512,128]{1,0:T(8,128)S(1)}, bf16[512,512]{1,0:T(8,128)(2,1)S(1)...) custom-call(s32[8]{0:T(128)S(1)} %concatenate.6.at_ref, f32[2,128,640]{2,1,0:T(8,128)S(1)} %pad_maximum_fusion.own_ref, ...), custom_call_target="tpu_custom_call" | custom-call | flops 4000000000 | bytes 4194304 | tf_op jit(solution)/shard_map/pallas_call | solution.py:221
  122.3 12.5 %shard_map.55 = (f32[1024,512]{1,0:T(8,128)}, f32[1024,128]{1,0:T(8,128)}) custom-call(s32[8]{0:T(128)S(1)} %concatenate.6.at_ref, f32[2,2,2,128,128]{4,3,2,1,0:T(8,128)S(1)} %pad_maximum_fusion.2.q0_ref, f32[2,2,2,128,128]{4,3,2,1,0:T(8,128)S(1)} %collective-permute-done.17.q1_ref, f32[2,2,2,128,128]{4,3,2,1,0:T(8,128)S(1)} %collective-permute-done.21.q2_ref, ...), custom_call_target="tpu_custom_call" | custom-call | flops 10000000000 | bytes 6291456 | tf_op jit(solution)/shard_map/pallas_call | solution.py:285
  (40 shorter events, 0.4 us)
Async XLA Ops:
  1.5 8.1 %collective-permute-start.1 = (f32[128,128]{1,0:T(8,128)S(1)}, f32[128,128]{1,0:T(8,128)S(1)}, u32[]{:S(2)}, u32[]{:S(2)}) collective-permute-start(f32[128,128]{1,0:T(8,128)S(1)} %slice_select_fusion), channel_id=1, source_target_pairs={{0,16},{1,17},{2,18},{3,19},{32,48},{33,49},{34,50},{35,51},{64,80... | collective-permute-start | bytes 196616 | tf_op jit(solution)/shard_map/ppermute | solution.py:325
  7.0 2.6 %collective-permute-start.2 = (f32[128,128]{1,0:T(8,128)S(1)}, f32[128,128]{1,0:T(8,128)S(1)}, u32[]{:S(2)}, u32[]{:S(2)}) collective-permute-start(f32[128,128]{1,0:T(8,128)S(1)} %slice_select_fusion), channel_id=1, source_target_pairs={{0,24},{1,25},{2,26},{3,27},{32,56},{33,57},{34,58},{35,59},{64,88... | collective-permute-start | bytes 196616 | tf_op jit(solution)/shard_map/ppermute | solution.py:325
  8.3 2.9 %collective-permute-start = (f32[128,128]{1,0:T(8,128)S(1)}, f32[128,128]{1,0:T(8,128)S(1)}, u32[]{:S(2)}, u32[]{:S(2)}) collective-permute-start(f32[128,128]{1,0:T(8,128)S(1)} %slice_select_fusion), channel_id=1, source_target_pairs={{0,8},{1,9},{2,10},{3,11},{32,40},{33,41},{34,42},{35,43},{64,72},... | collective-permute-start | bytes 196616 | tf_op jit(solution)/shard_map/ppermute | solution.py:325
  12.0 2.6 %collective-permute-start.3 = (f32[128,128]{1,0:T(8,128)S(1)}, f32[128,128]{1,0:T(8,128)S(1)}, u32[]{:S(2)}, u32[]{:S(2)}) collective-permute-start(f32[128,128]{1,0:T(8,128)S(1)} %add_add_fusion.3), channel_id=1, source_target_pairs={{0,7},{1,6},{2,5},{3,4},{8,15},{9,14},{10,13},{11,12},{16,23},{17,... | collective-permute-start | bytes 196616 | tf_op jit(solution)/shard_map/ppermute | solution.py:329
  14.7 10.7 %collective-permute-start.9 = (f32[128,128]{1,0:T(8,128)S(1)}, f32[128,128]{1,0:T(8,128)S(1)}, u32[]{:S(2)}, u32[]{:S(2)}) collective-permute-start(f32[128,128]{1,0:T(8,128)S(1)} %add.67), channel_id=1, source_target_pairs={{0,384},{32,416},{64,448},{96,480},{1,385},{33,417},{65,449},{97,4... | collective-permute-start | bytes 196616 | tf_op jit(solution)/shard_map/ppermute | solution.py:22
  17.7 9.0 %collective-permute-start.8 = (f32[128,128]{1,0:T(8,128)S(1)}, f32[128,128]{1,0:T(8,128)S(1)}, u32[]{:S(2)}, u32[]{:S(2)}) collective-permute-start(f32[128,128]{1,0:T(8,128)S(1)} %add.67), channel_id=1, source_target_pairs={{0,256},{32,288},{64,320},{96,352},{1,257},{33,289},{65,321},{97,3... | collective-permute-start | bytes 196616 | tf_op jit(solution)/shard_map/ppermute | solution.py:22
  19.0 7.7 %collective-permute-start.7 = (f32[128,128]{1,0:T(8,128)S(1)}, f32[128,128]{1,0:T(8,128)S(1)}, u32[]{:S(2)}, u32[]{:S(2)}) collective-permute-start(f32[128,128]{1,0:T(8,128)S(1)} %add.67), channel_id=1, source_target_pairs={{0,128},{32,160},{64,192},{96,224},{1,129},{33,161},{65,193},{97,2... | collective-permute-start | bytes 196616 | tf_op jit(solution)/shard_map/ppermute | solution.py:22
  20.3 6.5 %collective-permute-start.4 = (f32[2,128,128]{2,1,0:T(8,128)S(1)}, f32[2,128,128]{2,1,0:T(8,128)S(1)}, u32[]{:S(2)}, u32[]{:S(2)}) collective-permute-start(f32[2,128,128]{2,1,0:T(8,128)S(1)} %get-tuple-element.74), channel_id=1, source_target_pairs={{0,8},{1,9},{2,10},{3,11},{32,40},{33,41},{34,42},{35,43},{64,72},... | collective-permute-start | bytes 393224 | tf_op jit(solution)/shard_map/ppermute | solution.py:18
  23.5 3.9 %collective-permute-start.6 = (f32[2,128,128]{2,1,0:T(8,128)S(1)}, f32[2,128,128]{2,1,0:T(8,128)S(1)}, u32[]{:S(2)}, u32[]{:S(2)}) collective-permute-start(f32[2,128,128]{2,1,0:T(8,128)S(1)} %get-tuple-element.75), channel_id=1, source_target_pairs={{0,24},{1,25},{2,26},{3,27},{32,56},{33,57},{34,58},{35,59},{64,88... | collective-permute-start | bytes 393224 | tf_op jit(solution)/shard_map/ppermute | solution.py:18
  25.4 4.6 %collective-permute-start.5 = (f32[2,128,128]{2,1,0:T(8,128)S(1)}, f32[2,128,128]{2,1,0:T(8,128)S(1)}, u32[]{:S(2)}, u32[]{:S(2)}) collective-permute-start(f32[2,128,128]{2,1,0:T(8,128)S(1)} %get-tuple-element.76), channel_id=1, source_target_pairs={{0,16},{1,17},{2,18},{3,19},{32,48},{33,49},{34,50},{35,51},{64,80... | collective-permute-start | bytes 393224 | tf_op jit(solution)/shard_map/ppermute | solution.py:18
  26.8 32.8 %copy-start.2 = (s32[4]{0:T(128)S(1)}, s32[4]{0:T(128)}, u32[]{:S(2)}) copy-start(s32[4]{0:T(128)} %constant.58.clone) | copy-start | bytes 52
  30.1 29.7 %slice-start = ((f32[1024,512]{1,0:T(8,128)}), f32[128,512]{1,0:T(8,128)S(1)}, s32[]{:S(2)}) async-start(f32[1024,512]{1,0:T(8,128)} %k_ref.1), calls=%async_computation | async-start | bytes 524288 | tf_op jit(solution)/shard_map/slice | solution.py:350
  30.1 29.7 %slice-start.1 = ((f32[1024,128]{1,0:T(8,128)}), f32[128,128]{1,0:T(8,128)S(1)}, s32[]{:S(2)}) async-start(f32[1024,128]{1,0:T(8,128)} %y_ref.1), calls=%async_computation.1 | async-start | bytes 131072 | tf_op jit(solution)/shard_map/slice | solution.py:350
  30.1 6.4 %collective-permute-start.11 = (f32[128,128]{1,0:T(8,128)S(1)}, f32[128,128]{1,0:T(8,128)S(1)}, u32[]{:S(2)}, u32[]{:S(2)}) collective-permute-start(f32[128,128]{1,0:T(8,128)S(1)} %add_add_fusion.2), channel_id=1, source_target_pairs={{0,2},{1,3},{2,0},{3,1},{4,6},{5,7},{6,4},{7,5},{8,10},{9,11},{10,... | collective-permute-start | bytes 196616 | tf_op jit(solution)/shard_map/ppermute | solution.py:18
  33.1 5.4 %collective-permute-start.10 = (f32[2,128,128]{2,1,0:T(8,128)S(1)}, f32[2,128,128]{2,1,0:T(8,128)S(1)}, u32[]{:S(2)}, u32[]{:S(2)}) collective-permute-start(f32[2,128,128]{2,1,0:T(8,128)S(1)} %add_add_fusion.1), channel_id=1, source_target_pairs={{0,7},{1,6},{2,5},{3,4},{8,15},{9,14},{10,13},{11,12},{16,23},{17,... | collective-permute-start | bytes 393224 | tf_op jit(solution)/shard_map/ppermute | solution.py:18
  36.5 5.7 %collective-permute-start.12 = (f32[2,128,128]{2,1,0:T(8,128)S(1)}, f32[2,128,128]{2,1,0:T(8,128)S(1)}, u32[]{:S(2)}, u32[]{:S(2)}) collective-permute-start(f32[2,128,128]{2,1,0:T(8,128)S(1)} %get-tuple-element.80), channel_id=1, source_target_pairs={{0,1},{1,0},{2,3},{3,2},{4,5},{5,4},{6,7},{7,6},{8,9},{9,8},{10,11... | collective-permute-start | bytes 393224 | tf_op jit(solution)/shard_map/ppermute | solution.py:18
  42.2 11.4 %collective-permute-start.14 = (f32[2,2,128,128]{3,2,1,0:T(8,128)S(1)}, f32[2,2,128,128]{3,2,1,0:T(8,128)S(1)}, u32[]{:S(2)}, u32[]{:S(2)}) collective-permute-start(f32[2,2,128,128]{3,2,1,0:T(8,128)S(1)} %pad_maximum_fusion.3), channel_id=1, source_target_pairs={{0,64},{32,96},{64,0},{96,32},{128,192},{160,224},{192,128},{224,1... | collective-permute-start | bytes 786440 | tf_op jit(solution)/shard_map/ppermute | solution.py:22
  45.7 7.9 %collective-permute-start.13 = (f32[2,128,128]{2,1,0:T(8,128)S(1)}, f32[2,128,128]{2,1,0:T(8,128)S(1)}, u32[]{:S(2)}, u32[]{:S(2)}) collective-permute-start(f32[2,128,128]{2,1,0:T(8,128)S(1)} %broadcast_select_fusion), channel_id=1, source_target_pairs={{0,2},{1,3},{2,0},{3,1},{4,6},{5,7},{6,4},{7,5},{8,10},{9,11},{10,... | collective-permute-start | bytes 393224 | tf_op jit(solution)/shard_map/ppermute | solution.py:18
  53.7 16.0 %collective-permute-start.16 = (f32[2,2,2,128,128]{4,3,2,1,0:T(8,128)S(1)}, f32[2,2,2,128,128]{4,3,2,1,0:T(8,128)S(1)}, u32[]{:S(2)}, u32[]{:S(2)}) collective-permute-start(f32[2,2,2,128,128]{4,3,2,1,0:T(8,128)S(1)} %pad_maximum_fusion.1.own_ref), channel_id=1, source_target_pairs={{0,32},{32,0},{64,96},{96,64},{128,160},{160,128},{192,224},{224,1... | collective-permute-start | bytes 1572872 | tf_op jit(solution)/shard_map/ppermute | solution.py:22
  59.8 25.8 %collective-permute-start.20 = (f32[128,640]{1,0:T(8,128)S(1)}, f32[128,640]{1,0:T(8,128)S(1)}, u32[]{:S(2)}, u32[]{:S(2)}) collective-permute-start(f32[128,640]{1,0:T(8,128)S(1)} %maximum_select_fusion), channel_id=1, source_target_pairs={{0,384},{32,416},{64,448},{96,480},{1,385},{33,417},{65,449},{97,4... | collective-permute-start | bytes 983048 | tf_op jit(solution)/shard_map/ppermute | solution.py:22
  64.4 21.1 %collective-permute-start.19 = (f32[128,640]{1,0:T(8,128)S(1)}, f32[128,640]{1,0:T(8,128)S(1)}, u32[]{:S(2)}, u32[]{:S(2)}) collective-permute-start(f32[128,640]{1,0:T(8,128)S(1)} %maximum_select_fusion), channel_id=1, source_target_pairs={{0,256},{32,288},{64,320},{96,352},{1,257},{33,289},{65,321},{97,3... | collective-permute-start | bytes 983048 | tf_op jit(solution)/shard_map/ppermute | solution.py:22
  65.8 19.8 %collective-permute-start.18 = (f32[128,640]{1,0:T(8,128)S(1)}, f32[128,640]{1,0:T(8,128)S(1)}, u32[]{:S(2)}, u32[]{:S(2)}) collective-permute-start(f32[128,640]{1,0:T(8,128)S(1)} %maximum_select_fusion), channel_id=1, source_target_pairs={{0,128},{32,160},{64,192},{96,224},{1,129},{33,161},{65,193},{97,2... | collective-permute-start | bytes 983048 | tf_op jit(solution)/shard_map/ppermute | solution.py:22
  67.1 9.6 %collective-permute-start.15 = (f32[2,2,128,128]{3,2,1,0:T(8,128)S(1)}, f32[2,2,128,128]{3,2,1,0:T(8,128)S(1)}, u32[]{:S(2)}, u32[]{:S(2)}) collective-permute-start(f32[2,2,128,128]{3,2,1,0:T(8,128)S(1)} %get-tuple-element.44), channel_id=1, source_target_pairs={{0,1},{1,0},{2,3},{3,2},{4,5},{5,4},{6,7},{7,6},{8,9},{9,8},{10,11... | collective-permute-start | bytes 786440 | tf_op jit(solution)/shard_map/ppermute | solution.py:18
  85.7 16.7 %collective-permute-start.24 = (f32[128,640]{1,0:T(8,128)S(1)}, f32[128,640]{1,0:T(8,128)S(1)}, u32[]{:S(2)}, u32[]{:S(2)}) collective-permute-start(f32[128,640]{1,0:T(8,128)S(1)} %add_add_fusion), channel_id=1, source_target_pairs={{0,64},{32,96},{64,0},{96,32},{128,192},{160,224},{192,128},{224,1... | collective-permute-start | bytes 983048 | tf_op jit(solution)/shard_map/ppermute | solution.py:22
  90.4 15.3 %collective-permute-start.21 = (f32[2,2,2,128,128]{4,3,2,1,0:T(8,128)S(1)}, f32[2,2,2,128,128]{4,3,2,1,0:T(8,128)S(1)}, u32[]{:S(2)}, u32[]{:S(2)}) collective-permute-start(f32[2,2,2,128,128]{4,3,2,1,0:T(8,128)S(1)} %pad_maximum_fusion.2.q0_ref), channel_id=1, source_target_pairs={{0,24},{1,25},{2,26},{3,27},{4,28},{5,29},{6,30},{7,31},{8,0},{9,1... | collective-permute-start | bytes 1572872 | tf_op jit(solution)/shard_map/ppermute | solution.py:18
  92.4 17.4 %collective-permute-start.17 = (f32[2,2,2,128,128]{4,3,2,1,0:T(8,128)S(1)}, f32[2,2,2,128,128]{4,3,2,1,0:T(8,128)S(1)}, u32[]{:S(2)}, u32[]{:S(2)}) collective-permute-start(f32[2,2,2,128,128]{4,3,2,1,0:T(8,128)S(1)} %pad_maximum_fusion.2.q0_ref), channel_id=1, source_target_pairs={{0,8},{1,9},{2,10},{3,11},{4,12},{5,13},{6,14},{7,15},{8,16},{9,17... | collective-permute-start | bytes 1572872 | tf_op jit(solution)/shard_map/ppermute | solution.py:18
  102.5 17.0 %collective-permute-start.25 = (f32[2,128,640]{2,1,0:T(8,128)S(1)}, f32[2,128,640]{2,1,0:T(8,128)S(1)}, u32[]{:S(2)}, u32[]{:S(2)}) collective-permute-start(f32[2,128,640]{2,1,0:T(8,128)S(1)} %pad_maximum_fusion.own_ref), channel_id=1, source_target_pairs={{0,32},{32,0},{64,96},{96,64},{128,160},{160,128},{192,224},{224,1... | collective-permute-start | bytes 1966088 | tf_op jit(solution)/shard_map/ppermute | solution.py:22
  105.7 12.1 %collective-permute-start.22 = (f32[2,2,128,128]{3,2,1,0:T(8,128)S(1)}, f32[2,2,128,128]{3,2,1,0:T(8,128)S(1)}, u32[]{:S(2)}, u32[]{:S(2)}) collective-permute-start(f32[2,2,128,128]{3,2,1,0:T(8,128)S(1)} %slice_bitcast_fusion.1), channel_id=1, source_target_pairs={{0,24},{1,25},{2,26},{3,27},{4,28},{5,29},{6,30},{7,31},{8,0},{9,1... | collective-permute-start | bytes 786440 | tf_op jit(solution)/shard_map/ppermute | solution.py:18
  109.8 9.7 %collective-permute-start.23 = (f32[2,2,128,128]{3,2,1,0:T(8,128)S(1)}, f32[2,2,128,128]{3,2,1,0:T(8,128)S(1)}, u32[]{:S(2)}, u32[]{:S(2)}) collective-permute-start(f32[2,2,128,128]{3,2,1,0:T(8,128)S(1)} %slice_bitcast_fusion), channel_id=1, source_target_pairs={{0,8},{1,9},{2,10},{3,11},{4,12},{5,13},{6,14},{7,15},{8,16},{9,17... | collective-permute-start | bytes 786440 | tf_op jit(solution)/shard_map/ppermute | solution.py:18
  119.5 2.8 %copy-start = (f32[1024,512]{1,0:T(8,128)S(1)}, f32[1024,512]{1,0:T(8,128)}, u32[]{:S(2)}) copy-start(f32[1024,512]{1,0:T(8,128)} %k_ref.1) | copy-start | bytes 6291460
  119.5 2.8 %copy-start.1 = (f32[1024,128]{1,0:T(8,128)S(1)}, f32[1024,128]{1,0:T(8,128)}, u32[]{:S(2)}) copy-start(f32[1024,128]{1,0:T(8,128)} %y_ref.1) | copy-start | bytes 1572868

commit v6 on v4

--- a/solution.py
+++ b/solution.py
@@ -59,14 +59,23 @@
         rows = [spread(own[q : q + 1, :]) for q in range(8)]
         rows_e = [spread(own_e[q : q + 1, :]) for q in range(8)]
         low, inv, root = {}, {}, []
-        for i in range(8):
-            rs = lax.rsqrt(t[i, i])
-            root.append(rs)
+        scale = [lax.rsqrt(t[i, i]) for i in range(8)]
+        for i in range(0, 8, 2):
+            a = t[i, i] * (scale[i] * scale[i])
+            b = t[i + 1, i] * (scale[i] * scale[i + 1])
+            c = t[i + 1, i + 1] * (scale[i + 1] * scale[i + 1])
+            ra = lax.rsqrt(a)
+            rd = lax.rsqrt(a * c - b * b)
+            one = scale[i] * ra
+            two = scale[i + 1] * ((a * ra) * rd)
+            root += [one, two]
             for s in range(i + 1, 8):
-                low[s, i] = t[s, i] * rs
-            for s in range(i + 1, 8):
-                for q in range(i + 1, s + 1):
-                    t[s, q] = t[s, q] - low[s, i] * low[q, i]
+                low[s, i] = t[s, i] * one
+            for s in range(i + 2, 8):
+                low[s, i + 1] = (t[s, i + 1] - low[s, i] * low[i + 1, i]) * two
+            for s in range(i + 2, 8):
+                for q in range(i + 2, s + 1):
+                    t[s, q] = t[s, q] - (low[s, i] * low[q, i] + low[s, i + 1] * low[q, i + 1])
         for i in range(8):
             inv[i, i] = root[i]
             for s in range(i + 1, 8):
@@ -112,36 +121,29 @@
     fac, inv = invert_block(s_ref, e_ref)
     f_ref[:n, :] = fac
     g_ref[...] = inv
-    f_ref[n:, :] = dot_nt(work[n:, :n], inv)
-    for j in range(1, 4):
-        rest_ref[(j - 1) * n :, (j - 1) * n : j * n] = work[
-            j * n :, j * n : (j + 1) * n
-        ] - dot_nt(f_ref[j * n :, :], f_ref[j * n : (j + 1) * n, :])
+    below = dot_nt(work[n:, :n], inv)
+    f_ref[n:, :] = below
+    rest_ref[...] = work[n:, n:] - dot_nt(below, below)
 
 
 def step_kernel(k, *refs):
     n = BLOCK
     old_f, old_g, rest_ref = refs[:k], refs[k : 2 * k], refs[2 * k]
     f_ref, g_ref = refs[2 * k + 1], refs[2 * k + 2]
-    s_ref, e_ref = refs[-2], refs[-1]
+    sum_ref, s_ref, e_ref = refs[-3:]
+    for m in reversed(range(k)):
+        part = dot(old_f[m][(k - m) * n : (k - m + 1) * n, :], old_g[m][...])
+        here = slice(0, (m + 1) * n)
+        sum_ref[:, here] = part if m == k - 1 else sum_ref[:, here] + part
     s_ref[...] = rest_ref[:n, :n]
     fac, inv = invert_block(s_ref, e_ref)
     f_ref[:n, :] = fac
     g_ref[:, k * n :] = inv
     if k < 3:
-        left_ref = refs[2 * k + 3]
-        f_ref[n:, :] = dot_nt(rest_ref[n:, :n], inv)
-        for j in range(1, 4 - k):
-            left_ref[(j - 1) * n :, (j - 1) * n : j * n] = rest_ref[
-                j * n :, j * n : (j + 1) * n
-            ] - dot_nt(f_ref[j * n :, :], f_ref[j * n : (j + 1) * n, :])
-    for j in range(k):
-        here = slice(j * n, (j + 1) * n)
-        part = total(
-            dot(old_f[m][(k - m) * n : (k - m + 1) * n, :], old_g[m][:, here])
-            for m in range(j, k)
-        )
-        g_ref[:, here] = -dot(inv, part)
+        below = dot_nt(rest_ref[n:, :n], inv)
+        f_ref[n:, :] = below
+        refs[2 * k + 3][...] = rest_ref[n:, n:] - dot_nt(below, below)
+    g_ref[:, : k * n] = -dot(inv, sum_ref[...])
 
 
 def f32(*shape):
@@ -179,7 +181,7 @@
         out_shape=shapes,
         in_specs=[VMEM] * (2 * k + 1),
         out_specs=[VMEM] * len(shapes),
-        scratch_shapes=PAIR,
+        scratch_shapes=[pltpu.VMEM((BLOCK, k * BLOCK), jnp.float32)] + PAIR,
         compiler_params=pltpu.CompilerParams(vmem_limit_bytes=8 * 2**20),
         cost_estimate=COST,
     )(*fs, *gs, rest)
@@ -197,32 +199,48 @@
     return jnp.dot(a, b, preferred_element_type=jnp.float32)
 
 
-def strip_kernel(at_ref, own_ref, got_ref, g0, g1, g2, g3, high_ref, low_ref, z_ref,
-                 t0, t1, t2, tmp):
+def split_kernel(g0, g1, g2, g3, t0, t1, t2):
+    n = BLOCK
+    for t_ref in (t0, t1, t2):
+        t_ref[...] = jnp.zeros_like(t_ref)
+    for i, g_ref in enumerate((g0, g1, g2, g3)):
+        here = slice(i * n, (i + 1) * n)
+        for j in range(i + 1):
+            there = slice(j * n, (j + 1) * n)
+            for t_ref, part in zip((t0, t1, t2), split(g_ref[:, there].T, 3)):
+                t_ref[there, here] = part
+
+
+def split_inverse(gs):
+    return pl.pallas_call(
+        split_kernel,
+        out_shape=[b16(ORDER, ORDER)] * 3,
+        in_specs=[VMEM] * 4,
+        out_specs=[VMEM] * 3,
+        compiler_params=pltpu.CompilerParams(vmem_limit_bytes=8 * 2**20),
+        cost_estimate=pl.CostEstimate(flops=10**9, bytes_accessed=2**21, transcendentals=0),
+    )(*gs)
+
+
+def strip_kernel(at_ref, own_ref, got_ref, g0, g1, g2, g3, high_ref, low_ref, z_ref, tmp):
     n = BLOCK
     for i in range(4):
         u = at_ref[0] ^ i
         tmp[i * n : (i + 1) * n, :] = jnp.where(u % 2 == 0, own_ref[u // 2], got_ref[u // 2])
-    for t_ref in (t0, t1, t2):
-        t_ref[...] = jnp.zeros_like(t_ref)
     for i, g_ref in enumerate((g0, g1, g2, g3)):
         here = slice(i * n, (i + 1) * n)
         value = dot(g_ref[...], tmp[: (i + 1) * n, :])
         high_ref[here, :], low_ref[here, :] = split(value, 2)
         z_ref[here, :] = value[:, ORDER:]
-        for j in range(i + 1):
-            there = slice(j * n, (j + 1) * n)
-            for t_ref, part in zip((t0, t1, t2), split(g_ref[:, there].T, 3)):
-                t_ref[there, here] = part
 
 
 def strip_solve(at, own, got, gs):
     wide = (ORDER, ORDER + BLOCK)
     return pl.pallas_call(
         strip_kernel,
-        out_shape=[b16(*wide)] * 2 + [f32(ORDER, BLOCK)] + [b16(ORDER, ORDER)] * 3,
+        out_shape=[b16(*wide)] * 2 + [f32(ORDER, BLOCK)],
         in_specs=[SMEM] + [VMEM] * 6,
-        out_specs=[VMEM] * 6,
+        out_specs=[VMEM] * 3,
         scratch_shapes=[pltpu.VMEM(wide, jnp.float32)],
         compiler_params=pltpu.CompilerParams(vmem_limit_bytes=8 * 2**20),
         cost_estimate=pl.CostEstimate(flops=4 * 10**9, bytes_accessed=4 * 2**20, transcendentals=0),
@@ -367,7 +385,8 @@
     f3, g3 = factor_step(3, [f0, f1, f2], [g0, g1, g2], after(rest, near, far, c2))
     c3 = after(jnp.stack([c2, after(c3_got, g3)]), low, high)
     c4 = over_row(c3, by_core)
-    strips = strip_solve(at, c3, c4, (g0, g1, g2, g3))
+    parts = split_inverse((g0, g1, g2, g3))
+    strips = strip_solve(at, c3, after(c4, *parts), (g0, g1, g2, g3)) + parts
     return tuple(
         update(at, (p4, down, up, low, high), (f0, f1, f2, f3), strips, kernel, targets)
     )

time: 133 us -> 132 us (level)
    pallas_call x3, Pallas kernels: 18.9 us -> 17.5 us  [factor_step(): pl.pallas_call(functools.partial(step_kernel, k), out_shape=shapes, in_sp...]
where the time goes in v6:
time: 132 us
  starting transfers between devices  69.8 us (53%)
  Pallas kernels  38.6 us (29%)
  waiting for transfers between devices  18.7 us (14%)
  other arithmetic  2.1 us (2%)
    ppermute x10, starting transfers between devices, over_row(): return lax.ppermute(value, 'row', pairs)  30.5 us
    ppermute x12, starting transfers between devices, over_col(): return lax.ppermute(value, 'col', pairs)  30 us
    pallas_call x3, Pallas kernels, factor_step(): pl.pallas_call(functools.partial(step_kernel, k), out_shape=shapes, in_sp...  17.5 us
    ppermute x12, waiting for transfers between devices, over_col(): return lax.ppermute(value, 'col', pairs)  15.4 us
    pallas_call x1, Pallas kernels, update(): pl.pallas_call(update_kernel, out_shape=[f32(*kernel.shape), f32(*targets...  11.1 us
    ppermute x3, starting transfers between devices, per_device(): got.append(lax.ppermute(a0, ('row', 'col'), pairs))  8.05 us
    pallas_call x1, Pallas kernels, factor_first(): pl.pallas_call(first_kernel, out_shape=[f32(ORDER, BLOCK), f32(BLOCK, BLO...  7.04 us
  transfers between devices with their start and end apart: 26, of which 9 were waited for; matrix products, arithmetic and copies ran while one was open for 1% of the time, Pallas kernels for 19%

profile of v6, /device:TPU:1, one launch (start us, length us, event | category | flops | bytes accessed | tf_op | source)
XLA Modules:
  0.0 131.6 jit_solution(17743031269237468228)
XLA Ops:
  0.6 0.8 slice_select_fusion
  1.5 5.5 %collective-permute-start.1 = (f32[128,128]{1,0:T(8,128)S(1)}, f32[128,128]{1,0:T(8,128)S(1)}, u32[]{:S(2)}, u32[]{:S(2)}) collective-permute-start(f32[128,128]{1,0:T(8,128)S(1)} %slice_select_fusion), channel_id=1, source_target_pairs={{0,16},{1,17},{2,18},{3,19},{32,48},{33,49},{34,50},{35,51},{64,80... | collective-permute-start | bytes 196616 | tf_op jit(solution)/shard_map/ppermute | solution.py:344
  7.0 1.3 collective-permute-start.2
  8.3 1.3 collective-permute-start
  9.6 1.6 %collective-permute-done = f32[128,128]{1,0:T(8,128)S(1)} collective-permute-done((f32[128,128]{1,0:T(8,128)S(1)}, f32[128,128]{1,0:T(8,128)S(1)}, u32[]{:S(2)}, u32[]{:S(2)}) %collective-permute-start) | collective-permute-done | bytes 65568 | tf_op jit(solution)/shard_map/ppermute | solution.py:344
  11.2 0.9 add_add_fusion.3
  12.0 1.3 collective-permute-start.3
  13.4 1.1 slice.30
  14.5 0.2 collective-permute-done.3
  14.7 3.0 %collective-permute-start.9 = (f32[128,128]{1,0:T(8,128)S(1)}, f32[128,128]{1,0:T(8,128)S(1)}, u32[]{:S(2)}, u32[]{:S(2)}) collective-permute-start(f32[128,128]{1,0:T(8,128)S(1)} %add.67), channel_id=1, source_target_pairs={{0,384},{32,416},{64,448},{96,480},{1,385},{33,417},{65,449},{97,4... | collective-permute-start | bytes 196616 | tf_op jit(solution)/shard_map/ppermute | solution.py:22
  17.7 1.3 collective-permute-start.8
  19.0 1.3 collective-permute-start.7
  20.3 3.1 %collective-permute-start.4 = (f32[2,128,128]{2,1,0:T(8,128)S(1)}, f32[2,128,128]{2,1,0:T(8,128)S(1)}, u32[]{:S(2)}, u32[]{:S(2)}) collective-permute-start(f32[2,128,128]{2,1,0:T(8,128)S(1)} %get-tuple-element.74), channel_id=1, source_target_pairs={{0,8},{1,9},{2,10},{3,11},{32,40},{33,41},{34,42},{35,43},{64,72},... | collective-permute-start | bytes 393224 | tf_op jit(solution)/shard_map/ppermute | solution.py:18
  23.5 1.9 %collective-permute-start.6 = (f32[2,128,128]{2,1,0:T(8,128)S(1)}, f32[2,128,128]{2,1,0:T(8,128)S(1)}, u32[]{:S(2)}, u32[]{:S(2)}) collective-permute-start(f32[2,128,128]{2,1,0:T(8,128)S(1)} %get-tuple-element.75), channel_id=1, source_target_pairs={{0,24},{1,25},{2,26},{3,27},{32,56},{33,57},{34,58},{35,59},{64,88... | collective-permute-start | bytes 393224 | tf_op jit(solution)/shard_map/ppermute | solution.py:18
  25.4 1.3 collective-permute-start.5
  26.8 0.5 collective-permute-done.6
  27.3 2.7 %collective-permute-done.5 = f32[2,128,128]{2,1,0:T(8,128)S(1)} collective-permute-done((f32[2,128,128]{2,1,0:T(8,128)S(1)}, f32[2,128,128]{2,1,0:T(8,128)S(1)}, u32[]{:S(2)}, u32[]{:S(2)}) %collective-permute-start.5) | collective-permute-done | bytes 131104 | tf_op jit(solution)/shard_map/ppermute | solution.py:18
  30.1 3.0 %collective-permute-start.11 = (f32[128,128]{1,0:T(8,128)S(1)}, f32[128,128]{1,0:T(8,128)S(1)}, u32[]{:S(2)}, u32[]{:S(2)}) collective-permute-start(f32[128,128]{1,0:T(8,128)S(1)} %add_add_fusion.2), channel_id=1, source_target_pairs={{0,2},{1,3},{2,0},{3,1},{4,6},{5,7},{6,4},{7,5},{8,10},{9,11},{10,... | collective-permute-start | bytes 196616 | tf_op jit(solution)/shard_map/ppermute | solution.py:18
  33.1 1.3 collective-permute-start.10
  34.4 2.1 %collective-permute-done.11 = f32[128,128]{1,0:T(8,128)S(1)} collective-permute-done((f32[128,128]{1,0:T(8,128)S(1)}, f32[128,128]{1,0:T(8,128)S(1)}, u32[]{:S(2)}, u32[]{:S(2)}) %collective-permute-start.11) | collective-permute-done | bytes 65568 | tf_op jit(solution)/shard_map/ppermute | solution.py:18
  36.5 1.9 %collective-permute-start.12 = (f32[2,128,128]{2,1,0:T(8,128)S(1)}, f32[2,128,128]{2,1,0:T(8,128)S(1)}, u32[]{:S(2)}, u32[]{:S(2)}) collective-permute-start(f32[2,128,128]{2,1,0:T(8,128)S(1)} %get-tuple-element.80), channel_id=1, source_target_pairs={{0,1},{1,0},{2,3},{3,2},{4,5},{5,4},{6,7},{7,6},{8,9},{9,8},{10,11... | collective-permute-start | bytes 393224 | tf_op jit(solution)/shard_map/ppermute | solution.py:18
  38.5 3.7 %collective-permute-done.12 = f32[2,128,128]{2,1,0:T(8,128)S(1)} collective-permute-done((f32[2,128,128]{2,1,0:T(8,128)S(1)}, f32[2,128,128]{2,1,0:T(8,128)S(1)}, u32[]{:S(2)}, u32[]{:S(2)}) %collective-permute-start.12) | collective-permute-done | bytes 131104 | tf_op jit(solution)/shard_map/ppermute | solution.py:18
  42.2 3.5 %collective-permute-start.14 = (f32[2,2,128,128]{3,2,1,0:T(8,128)S(1)}, f32[2,2,128,128]{3,2,1,0:T(8,128)S(1)}, u32[]{:S(2)}, u32[]{:S(2)}) collective-permute-start(f32[2,2,128,128]{3,2,1,0:T(8,128)S(1)} %pad_maximum_fusion.3), channel_id=1, source_target_pairs={{0,64},{32,96},{64,0},{96,32},{128,192},{160,224},{192,128},{224,1... | collective-permute-start | bytes 786440 | tf_op jit(solution)/shard_map/ppermute | solution.py:22
  45.7 3.0 %collective-permute-start.13 = (f32[2,128,128]{2,1,0:T(8,128)S(1)}, f32[2,128,128]{2,1,0:T(8,128)S(1)}, u32[]{:S(2)}, u32[]{:S(2)}) collective-permute-start(f32[2,128,128]{2,1,0:T(8,128)S(1)} %broadcast_select_fusion), channel_id=1, source_target_pairs={{0,2},{1,3},{2,0},{3,1},{4,6},{5,7},{6,4},{7,5},{8,10},{9,11},{10,... | collective-permute-start | bytes 393224 | tf_op jit(solution)/shard_map/ppermute | solution.py:18
  48.7 4.9 %collective-permute-done.13 = f32[2,128,128]{2,1,0:T(8,128)S(1)} collective-permute-done((f32[2,128,128]{2,1,0:T(8,128)S(1)}, f32[2,128,128]{2,1,0:T(8,128)S(1)}, u32[]{:S(2)}, u32[]{:S(2)}) %collective-permute-start.13) | collective-permute-done | bytes 131104 | tf_op jit(solution)/shard_map/ppermute | solution.py:18
  53.7 0.1 pad_maximum_fusion.1.own_ref
  53.7 5.9 %collective-permute-start.16 = (f32[2,2,2,128,128]{4,3,2,1,0:T(8,128)S(1)}, f32[2,2,2,128,128]{4,3,2,1,0:T(8,128)S(1)}, u32[]{:S(2)}, u32[]{:S(2)}) collective-permute-start(f32[2,2,2,128,128]{4,3,2,1,0:T(8,128)S(1)} %pad_maximum_fusion.1.own_ref), channel_id=1, source_target_pairs={{0,32},{32,0},{64,96},{96,64},{128,160},{160,128},{192,224},{224,1... | collective-permute-start | bytes 1572872 | tf_op jit(solution)/shard_map/ppermute | solution.py:22
  59.6 0.1 concatenate.6.at_ref
  59.8 4.7 %collective-permute-start.23 = (f32[128,640]{1,0:T(8,128)S(1)}, f32[128,640]{1,0:T(8,128)S(1)}, u32[]{:S(2)}, u32[]{:S(2)}) collective-permute-start(f32[128,640]{1,0:T(8,128)S(1)} %maximum_select_fusion), channel_id=1, source_target_pairs={{0,384},{32,416},{64,448},{96,480},{1,385},{33,417},{65,449},{97,4... | collective-permute-start | bytes 983048 | tf_op jit(solution)/shard_map/ppermute | solution.py:22
  64.4 1.3 collective-permute-start.22
  65.8 1.3 collective-permute-start.21
  67.1 2.6 %collective-permute-start.15 = (f32[2,2,128,128]{3,2,1,0:T(8,128)S(1)}, f32[2,2,128,128]{3,2,1,0:T(8,128)S(1)}, u32[]{:S(2)}, u32[]{:S(2)}) collective-permute-start(f32[2,2,128,128]{3,2,1,0:T(8,128)S(1)} %get-tuple-element.44), channel_id=1, source_target_pairs={{0,1},{1,0},{2,3},{3,2},{4,5},{5,4},{6,7},{7,6},{8,9},{9,8},{10,11... | collective-permute-start | bytes 786440 | tf_op jit(solution)/shard_map/ppermute | solution.py:18
  69.7 7.0 %shard_map.50 = (f32[512,128]{1,0:T(8,128)S(1)}, f32[128,128]{1,0:T(8,128)S(1)}, f32[384,384]{1,0:T(8,128)S(1)}) custom-call(s32[8]{0:T(128)S(1)} %concatenate.6.at_ref, f32[2,2,2,128,128]{4,3,2,1,0:T(8,128)S(1)} %pad_maximum_fusion.1.own_ref, f32[2,2,2,128,128]{4,3,2,1,0:T(8,128)S(1)} %collective-permute-done.16.got_ref), custom_call_target="tpu_custom_call" | custom-call | flops 6000000000 | bytes 1048576 | tf_op jit(solution)/shard_map/pallas_call | solution.py:164
  76.8 1.9 %collective-permute-start.18 = (f32[2,2,2,128,128]{4,3,2,1,0:T(8,128)S(1)}, f32[2,2,2,128,128]{4,3,2,1,0:T(8,128)S(1)}, u32[]{:S(2)}, u32[]{:S(2)}) collective-permute-start(f32[2,2,2,128,128]{4,3,2,1,0:T(8,128)S(1)} %pad_maximum_fusion.2.q0_ref), channel_id=1, source_target_pairs={{0,24},{1,25},{2,26},{3,27},{4,28},{5,29},{6,30},{7,31},{8,0},{9,1... | collective-permute-start | bytes 1572872 | tf_op jit(solution)/shard_map/ppermute | solution.py:18
  78.8 3.5 %collective-permute-start.17 = (f32[2,2,2,128,128]{4,3,2,1,0:T(8,128)S(1)}, f32[2,2,2,128,128]{4,3,2,1,0:T(8,128)S(1)}, u32[]{:S(2)}, u32[]{:S(2)}) collective-permute-start(f32[2,2,2,128,128]{4,3,2,1,0:T(8,128)S(1)} %pad_maximum_fusion.2.q0_ref), channel_id=1, source_target_pairs={{0,8},{1,9},{2,10},{3,11},{4,12},{5,13},{6,14},{7,15},{8,16},{9,17... | collective-permute-start | bytes 1572872 | tf_op jit(solution)/shard_map/ppermute | solution.py:18
  82.3 6.1 %shard_map.51 = (f32[384,128]{1,0:T(8,128)S(1)}, f32[128,256]{1,0:T(8,128)S(1)}, f32[256,256]{1,0:T(8,128)S(1)}) custom-call(f32[512,128]{1,0:T(8,128)S(1)} %get-tuple-element.47.refs_0_.f0, f32[128,128]{1,0:T(8,128)S(1)} %get-tuple-element.48.refs_1_.refs_2_.refs_3_.g0, f32[384,384]{1,0:T(8,128)S(1)} %get-tuple-element.49.refs_2_), custom_call_target="tpu_custom_call" | custom-call | flops 6000000000 | bytes 1048576 | tf_op jit(solution)/shard_map/pallas_call | solution.py:179
  88.4 5.9 %shard_map.52 = (f32[256,128]{1,0:T(8,128)S(1)}, f32[128,384]{1,0:T(8,128)S(1)}, f32[128,128]{1,0:T(8,128)S(1)}) custom-call(f32[512,128]{1,0:T(8,128)S(1)} %get-tuple-element.47.refs_0_.f0, f32[384,128]{1,0:T(8,128)S(1)} %get-tuple-element.50.refs_1_.f1, f32[128,128]{1,0:T(8,128)S(1)} %get-tuple-element.48.refs_1_.refs_2_.refs_3_.g0, ...), custom_call_target="tpu_custom_call" | custom-call | flops 6000000000 | bytes 1048576 | tf_op jit(solution)/shard_map/pallas_call | solution.py:179
  94.4 0.1 add_add_fusion
  94.5 3.6 %collective-permute-start.24 = (f32[128,640]{1,0:T(8,128)S(1)}, f32[128,640]{1,0:T(8,128)S(1)}, u32[]{:S(2)}, u32[]{:S(2)}) collective-permute-start(f32[128,640]{1,0:T(8,128)S(1)} %add_add_fusion), channel_id=1, source_target_pairs={{0,64},{32,96},{64,0},{96,32},{128,192},{160,224},{192,128},{224,1... | collective-permute-start | bytes 983048 | tf_op jit(solution)/shard_map/ppermute | solution.py:22
  98.2 4.3 %collective-permute-start.19 = (f32[2,2,128,128]{3,2,1,0:T(8,128)S(1)}, f32[2,2,128,128]{3,2,1,0:T(8,128)S(1)}, u32[]{:S(2)}, u32[]{:S(2)}) collective-permute-start(f32[2,2,128,128]{3,2,1,0:T(8,128)S(1)} %slice_bitcast_fusion.1), channel_id=1, source_target_pairs={{0,24},{1,25},{2,26},{3,27},{4,28},{5,29},{6,30},{7,31},{8,0},{9,1... | collective-permute-start | bytes 786440 | tf_op jit(solution)/shard_map/ppermute | solution.py:18
  102.5 2.1 %collective-permute-start.20 = (f32[2,2,128,128]{3,2,1,0:T(8,128)S(1)}, f32[2,2,128,128]{3,2,1,0:T(8,128)S(1)}, u32[]{:S(2)}, u32[]{:S(2)}) collective-permute-start(f32[2,2,128,128]{3,2,1,0:T(8,128)S(1)} %slice_bitcast_fusion), channel_id=1, source_target_pairs={{0,8},{1,9},{2,10},{3,11},{4,12},{5,13},{6,14},{7,15},{8,16},{9,17... | collective-permute-start | bytes 786440 | tf_op jit(solution)/shard_map/ppermute | solution.py:18
  104.6 5.5 %shard_map.53 = (f32[128,128]{1,0:T(8,128)S(1)}, f32[128,512]{1,0:T(8,128)S(1)}) custom-call(f32[512,128]{1,0:T(8,128)S(1)} %get-tuple-element.47.refs_0_.f0, f32[384,128]{1,0:T(8,128)S(1)} %get-tuple-element.50.refs_1_.f1, f32[256,128]{1,0:T(8,128)S(1)} %get-tuple-element.56.refs_2_.f2, f32[128,128]{1,0:T(8,128)S(1)} %get-tuple-element.48.refs_1_.refs_2_.refs_3_.g0, ...), custom_call_target="tpu_custom_call" | custom-call | flops 6000000000 | bytes 1048576 | tf_op jit(solution)/shard_map/pallas_call | solution.py:179
  110.1 1.5 %collective-permute-done.20.high_ref = f32[2,2,128,128]{3,2,1,0:T(8,128)S(1)} collective-permute-done((f32[2,2,128,128]{3,2,1,0:T(8,128)S(1)}, f32[2,2,128,128]{3,2,1,0:T(8,128)S(1)}, u32[]{:S(2)}, u32[]{:S(2)}) %collective-permute-start.20) | collective-permute-done | bytes 262176 | tf_op jit(solution)/shard_map/ppermute | solution.py:18
  111.6 4.6 %collective-permute-start.25 = (f32[2,128,640]{2,1,0:T(8,128)S(1)}, f32[2,128,640]{2,1,0:T(8,128)S(1)}, u32[]{:S(2)}, u32[]{:S(2)}) collective-permute-start(f32[2,128,640]{2,1,0:T(8,128)S(1)} %pad_maximum_fusion.own_ref), channel_id=1, source_target_pairs={{0,32},{32,0},{64,96},{96,64},{128,160},{160,128},{192,224},{224,1... | collective-permute-start | bytes 1966088 | tf_op jit(solution)/shard_map/ppermute | solution.py:22
  116.2 0.3 shard_map.54
  116.5 1.4 %collective-permute-done.25.got_ref = f32[2,128,640]{2,1,0:T(8,128)S(1)} collective-permute-done((f32[2,128,640]{2,1,0:T(8,128)S(1)}, f32[2,128,640]{2,1,0:T(8,128)S(1)}, u32[]{:S(2)}, u32[]{:S(2)}) %collective-permute-start.25) | collective-permute-done | bytes 655392 | tf_op jit(solution)/shard_map/ppermute | solution.py:22
  117.9 2.6 %shard_map.55 = (bf16[512,640]{1,0:T(8,128)(2,1)S(1)}, bf16[512,640]{1,0:T(8,128)(2,1)S(1)}, f32[512,128]{1,0:T(8,128)S(1)}) custom-call(s32[8]{0:T(128)S(1)} %concatenate.6.at_ref, f32[2,128,640]{2,1,0:T(8,128)S(1)} %pad_maximum_fusion.own_ref, f32[2,128,640]{2,1,0:T(8,128)S(1)} %collective-permute-done.25.got_ref, ...), custom_call_target="tpu_custom_call" | custom-call | flops 4000000000 | bytes 4194304 | tf_op jit(solution)/shard_map/pallas_call | solution.py:239
  120.5 11.1 %shard_map.56 = (f32[1024,512]{1,0:T(8,128)}, f32[1024,128]{1,0:T(8,128)}) custom-call(s32[8]{0:T(128)S(1)} %concatenate.6.at_ref, f32[2,2,2,128,128]{4,3,2,1,0:T(8,128)S(1)} %pad_maximum_fusion.2.q0_ref, f32[2,2,2,128,128]{4,3,2,1,0:T(8,128)S(1)} %collective-permute-done.17.q1_ref, f32[2,2,2,128,128]{4,3,2,1,0:T(8,128)S(1)} %collective-permute-done.18.q2_ref, ...), custom_call_target="tpu_custom_call" | custom-call | flops 10000000000 | bytes 6291456 | tf_op jit(solution)/shard_map/pallas_call | solution.py:304
  (41 shorter events, 0.4 us)
Async XLA Ops:
  1.5 8.1 %collective-permute-start.1 = (f32[128,128]{1,0:T(8,128)S(1)}, f32[128,128]{1,0:T(8,128)S(1)}, u32[]{:S(2)}, u32[]{:S(2)}) collective-permute-start(f32[128,128]{1,0:T(8,128)S(1)} %slice_select_fusion), channel_id=1, source_target_pairs={{0,16},{1,17},{2,18},{3,19},{32,48},{33,49},{34,50},{35,51},{64,80... | collective-permute-start | bytes 196616 | tf_op jit(solution)/shard_map/ppermute | solution.py:344
  7.0 2.6 %collective-permute-start.2 = (f32[128,128]{1,0:T(8,128)S(1)}, f32[128,128]{1,0:T(8,128)S(1)}, u32[]{:S(2)}, u32[]{:S(2)}) collective-permute-start(f32[128,128]{1,0:T(8,128)S(1)} %slice_select_fusion), channel_id=1, source_target_pairs={{0,24},{1,25},{2,26},{3,27},{32,56},{33,57},{34,58},{35,59},{64,88... | collective-permute-start | bytes 196616 | tf_op jit(solution)/shard_map/ppermute | solution.py:344
  8.3 2.9 %collective-permute-start = (f32[128,128]{1,0:T(8,128)S(1)}, f32[128,128]{1,0:T(8,128)S(1)}, u32[]{:S(2)}, u32[]{:S(2)}) collective-permute-start(f32[128,128]{1,0:T(8,128)S(1)} %slice_select_fusion), channel_id=1, source_target_pairs={{0,8},{1,9},{2,10},{3,11},{32,40},{33,41},{34,42},{35,43},{64,72},... | collective-permute-start | bytes 196616 | tf_op jit(solution)/shard_map/ppermute | solution.py:344
  12.0 2.6 %collective-permute-start.3 = (f32[128,128]{1,0:T(8,128)S(1)}, f32[128,128]{1,0:T(8,128)S(1)}, u32[]{:S(2)}, u32[]{:S(2)}) collective-permute-start(f32[128,128]{1,0:T(8,128)S(1)} %add_add_fusion.3), channel_id=1, source_target_pairs={{0,7},{1,6},{2,5},{3,4},{8,15},{9,14},{10,13},{11,12},{16,23},{17,... | collective-permute-start | bytes 196616 | tf_op jit(solution)/shard_map/ppermute | solution.py:348
  14.7 10.7 %collective-permute-start.9 = (f32[128,128]{1,0:T(8,128)S(1)}, f32[128,128]{1,0:T(8,128)S(1)}, u32[]{:S(2)}, u32[]{:S(2)}) collective-permute-start(f32[128,128]{1,0:T(8,128)S(1)} %add.67), channel_id=1, source_target_pairs={{0,384},{32,416},{64,448},{96,480},{1,385},{33,417},{65,449},{97,4... | collective-permute-start | bytes 196616 | tf_op jit(solution)/shard_map/ppermute | solution.py:22
  17.7 9.0 %collective-permute-start.8 = (f32[128,128]{1,0:T(8,128)S(1)}, f32[128,128]{1,0:T(8,128)S(1)}, u32[]{:S(2)}, u32[]{:S(2)}) collective-permute-start(f32[128,128]{1,0:T(8,128)S(1)} %add.67), channel_id=1, source_target_pairs={{0,256},{32,288},{64,320},{96,352},{1,257},{33,289},{65,321},{97,3... | collective-permute-start | bytes 196616 | tf_op jit(solution)/shard_map/ppermute | solution.py:22
  19.0 7.7 %collective-permute-start.7 = (f32[128,128]{1,0:T(8,128)S(1)}, f32[128,128]{1,0:T(8,128)S(1)}, u32[]{:S(2)}, u32[]{:S(2)}) collective-permute-start(f32[128,128]{1,0:T(8,128)S(1)} %add.67), channel_id=1, source_target_pairs={{0,128},{32,160},{64,192},{96,224},{1,129},{33,161},{65,193},{97,2... | collective-permute-start | bytes 196616 | tf_op jit(solution)/shard_map/ppermute | solution.py:22
  20.3 6.5 %collective-permute-start.4 = (f32[2,128,128]{2,1,0:T(8,128)S(1)}, f32[2,128,128]{2,1,0:T(8,128)S(1)}, u32[]{:S(2)}, u32[]{:S(2)}) collective-permute-start(f32[2,128,128]{2,1,0:T(8,128)S(1)} %get-tuple-element.74), channel_id=1, source_target_pairs={{0,8},{1,9},{2,10},{3,11},{32,40},{33,41},{34,42},{35,43},{64,72},... | collective-permute-start | bytes 393224 | tf_op jit(solution)/shard_map/ppermute | solution.py:18
  23.5 3.9 %collective-permute-start.6 = (f32[2,128,128]{2,1,0:T(8,128)S(1)}, f32[2,128,128]{2,1,0:T(8,128)S(1)}, u32[]{:S(2)}, u32[]{:S(2)}) collective-permute-start(f32[2,128,128]{2,1,0:T(8,128)S(1)} %get-tuple-element.75), channel_id=1, source_target_pairs={{0,24},{1,25},{2,26},{3,27},{32,56},{33,57},{34,58},{35,59},{64,88... | collective-permute-start | bytes 393224 | tf_op jit(solution)/shard_map/ppermute | solution.py:18
  25.4 4.6 %collective-permute-start.5 = (f32[2,128,128]{2,1,0:T(8,128)S(1)}, f32[2,128,128]{2,1,0:T(8,128)S(1)}, u32[]{:S(2)}, u32[]{:S(2)}) collective-permute-start(f32[2,128,128]{2,1,0:T(8,128)S(1)} %get-tuple-element.76), channel_id=1, source_target_pairs={{0,16},{1,17},{2,18},{3,19},{32,48},{33,49},{34,50},{35,51},{64,80... | collective-permute-start | bytes 393224 | tf_op jit(solution)/shard_map/ppermute | solution.py:18
  26.8 32.8 %copy-start.2 = (s32[4]{0:T(128)S(1)}, s32[4]{0:T(128)}, u32[]{:S(2)}) copy-start(s32[4]{0:T(128)} %constant.58.clone) | copy-start | bytes 52
  30.1 29.7 %slice-start = ((f32[1024,512]{1,0:T(8,128)}), f32[128,512]{1,0:T(8,128)S(1)}, s32[]{:S(2)}) async-start(f32[1024,512]{1,0:T(8,128)} %k_ref.1), calls=%async_computation | async-start | bytes 524288 | tf_op jit(solution)/shard_map/slice | solution.py:369
  30.1 29.7 %slice-start.1 = ((f32[1024,128]{1,0:T(8,128)}), f32[128,128]{1,0:T(8,128)S(1)}, s32[]{:S(2)}) async-start(f32[1024,128]{1,0:T(8,128)} %y_ref.1), calls=%async_computation.1 | async-start | bytes 131072 | tf_op jit(solution)/shard_map/slice | solution.py:369
  30.1 6.4 %collective-permute-start.11 = (f32[128,128]{1,0:T(8,128)S(1)}, f32[128,128]{1,0:T(8,128)S(1)}, u32[]{:S(2)}, u32[]{:S(2)}) collective-permute-start(f32[128,128]{1,0:T(8,128)S(1)} %add_add_fusion.2), channel_id=1, source_target_pairs={{0,2},{1,3},{2,0},{3,1},{4,6},{5,7},{6,4},{7,5},{8,10},{9,11},{10,... | collective-permute-start | bytes 196616 | tf_op jit(solution)/shard_map/ppermute | solution.py:18
  33.1 5.4 %collective-permute-start.10 = (f32[2,128,128]{2,1,0:T(8,128)S(1)}, f32[2,128,128]{2,1,0:T(8,128)S(1)}, u32[]{:S(2)}, u32[]{:S(2)}) collective-permute-start(f32[2,128,128]{2,1,0:T(8,128)S(1)} %add_add_fusion.1), channel_id=1, source_target_pairs={{0,7},{1,6},{2,5},{3,4},{8,15},{9,14},{10,13},{11,12},{16,23},{17,... | collective-permute-start | bytes 393224 | tf_op jit(solution)/shard_map/ppermute | solution.py:18
  36.5 5.7 %collective-permute-start.12 = (f32[2,128,128]{2,1,0:T(8,128)S(1)}, f32[2,128,128]{2,1,0:T(8,128)S(1)}, u32[]{:S(2)}, u32[]{:S(2)}) collective-permute-start(f32[2,128,128]{2,1,0:T(8,128)S(1)} %get-tuple-element.80), channel_id=1, source_target_pairs={{0,1},{1,0},{2,3},{3,2},{4,5},{5,4},{6,7},{7,6},{8,9},{9,8},{10,11... | collective-permute-start | bytes 393224 | tf_op jit(solution)/shard_map/ppermute | solution.py:18
  42.2 11.4 %collective-permute-start.14 = (f32[2,2,128,128]{3,2,1,0:T(8,128)S(1)}, f32[2,2,128,128]{3,2,1,0:T(8,128)S(1)}, u32[]{:S(2)}, u32[]{:S(2)}) collective-permute-start(f32[2,2,128,128]{3,2,1,0:T(8,128)S(1)} %pad_maximum_fusion.3), channel_id=1, source_target_pairs={{0,64},{32,96},{64,0},{96,32},{128,192},{160,224},{192,128},{224,1... | collective-permute-start | bytes 786440 | tf_op jit(solution)/shard_map/ppermute | solution.py:22
  45.7 7.9 %collective-permute-start.13 = (f32[2,128,128]{2,1,0:T(8,128)S(1)}, f32[2,128,128]{2,1,0:T(8,128)S(1)}, u32[]{:S(2)}, u32[]{:S(2)}) collective-permute-start(f32[2,128,128]{2,1,0:T(8,128)S(1)} %broadcast_select_fusion), channel_id=1, source_target_pairs={{0,2},{1,3},{2,0},{3,1},{4,6},{5,7},{6,4},{7,5},{8,10},{9,11},{10,... | collective-permute-start | bytes 393224 | tf_op jit(solution)/shard_map/ppermute | solution.py:18
  53.7 16.0 %collective-permute-start.16 = (f32[2,2,2,128,128]{4,3,2,1,0:T(8,128)S(1)}, f32[2,2,2,128,128]{4,3,2,1,0:T(8,128)S(1)}, u32[]{:S(2)}, u32[]{:S(2)}) collective-permute-start(f32[2,2,2,128,128]{4,3,2,1,0:T(8,128)S(1)} %pad_maximum_fusion.1.own_ref), channel_id=1, source_target_pairs={{0,32},{32,0},{64,96},{96,64},{128,160},{160,128},{192,224},{224,1... | collective-permute-start | bytes 1572872 | tf_op jit(solution)/shard_map/ppermute | solution.py:22
  59.8 34.6 %collective-permute-start.23 = (f32[128,640]{1,0:T(8,128)S(1)}, f32[128,640]{1,0:T(8,128)S(1)}, u32[]{:S(2)}, u32[]{:S(2)}) collective-permute-start(f32[128,640]{1,0:T(8,128)S(1)} %maximum_select_fusion), channel_id=1, source_target_pairs={{0,384},{32,416},{64,448},{96,480},{1,385},{33,417},{65,449},{97,4... | collective-permute-start | bytes 983048 | tf_op jit(solution)/shard_map/ppermute | solution.py:22
  64.4 29.9 %collective-permute-start.22 = (f32[128,640]{1,0:T(8,128)S(1)}, f32[128,640]{1,0:T(8,128)S(1)}, u32[]{:S(2)}, u32[]{:S(2)}) collective-permute-start(f32[128,640]{1,0:T(8,128)S(1)} %maximum_select_fusion), channel_id=1, source_target_pairs={{0,256},{32,288},{64,320},{96,352},{1,257},{33,289},{65,321},{97,3... | collective-permute-start | bytes 983048 | tf_op jit(solution)/shard_map/ppermute | solution.py:22
  65.8 28.6 %collective-permute-start.21 = (f32[128,640]{1,0:T(8,128)S(1)}, f32[128,640]{1,0:T(8,128)S(1)}, u32[]{:S(2)}, u32[]{:S(2)}) collective-permute-start(f32[128,640]{1,0:T(8,128)S(1)} %maximum_select_fusion), channel_id=1, source_target_pairs={{0,128},{32,160},{64,192},{96,224},{1,129},{33,161},{65,193},{97,2... | collective-permute-start | bytes 983048 | tf_op jit(solution)/shard_map/ppermute | solution.py:22
  67.1 9.7 %collective-permute-start.15 = (f32[2,2,128,128]{3,2,1,0:T(8,128)S(1)}, f32[2,2,128,128]{3,2,1,0:T(8,128)S(1)}, u32[]{:S(2)}, u32[]{:S(2)}) collective-permute-start(f32[2,2,128,128]{3,2,1,0:T(8,128)S(1)} %get-tuple-element.44), channel_id=1, source_target_pairs={{0,1},{1,0},{2,3},{3,2},{4,5},{5,4},{6,7},{7,6},{8,9},{9,8},{10,11... | collective-permute-start | bytes 786440 | tf_op jit(solution)/shard_map/ppermute | solution.py:18
  76.8 21.3 %collective-permute-start.18 = (f32[2,2,2,128,128]{4,3,2,1,0:T(8,128)S(1)}, f32[2,2,2,128,128]{4,3,2,1,0:T(8,128)S(1)}, u32[]{:S(2)}, u32[]{:S(2)}) collective-permute-start(f32[2,2,2,128,128]{4,3,2,1,0:T(8,128)S(1)} %pad_maximum_fusion.2.q0_ref), channel_id=1, source_target_pairs={{0,24},{1,25},{2,26},{3,27},{4,28},{5,29},{6,30},{7,31},{8,0},{9,1... | collective-permute-start | bytes 1572872 | tf_op jit(solution)/shard_map/ppermute | solution.py:18
  78.8 23.7 %collective-permute-start.17 = (f32[2,2,2,128,128]{4,3,2,1,0:T(8,128)S(1)}, f32[2,2,2,128,128]{4,3,2,1,0:T(8,128)S(1)}, u32[]{:S(2)}, u32[]{:S(2)}) collective-permute-start(f32[2,2,2,128,128]{4,3,2,1,0:T(8,128)S(1)} %pad_maximum_fusion.2.q0_ref), channel_id=1, source_target_pairs={{0,8},{1,9},{2,10},{3,11},{4,12},{5,13},{6,14},{7,15},{8,16},{9,17... | collective-permute-start | bytes 1572872 | tf_op jit(solution)/shard_map/ppermute | solution.py:18
  94.5 15.6 %collective-permute-start.24 = (f32[128,640]{1,0:T(8,128)S(1)}, f32[128,640]{1,0:T(8,128)S(1)}, u32[]{:S(2)}, u32[]{:S(2)}) collective-permute-start(f32[128,640]{1,0:T(8,128)S(1)} %add_add_fusion), channel_id=1, source_target_pairs={{0,64},{32,96},{64,0},{96,32},{128,192},{160,224},{192,128},{224,1... | collective-permute-start | bytes 983048 | tf_op jit(solution)/shard_map/ppermute | solution.py:22
  98.2 12.0 %collective-permute-start.19 = (f32[2,2,128,128]{3,2,1,0:T(8,128)S(1)}, f32[2,2,128,128]{3,2,1,0:T(8,128)S(1)}, u32[]{:S(2)}, u32[]{:S(2)}) collective-permute-start(f32[2,2,128,128]{3,2,1,0:T(8,128)S(1)} %slice_bitcast_fusion.1), channel_id=1, source_target_pairs={{0,24},{1,25},{2,26},{3,27},{4,28},{5,29},{6,30},{7,31},{8,0},{9,1... | collective-permute-start | bytes 786440 | tf_op jit(solution)/shard_map/ppermute | solution.py:18
  102.5 9.1 %collective-permute-start.20 = (f32[2,2,128,128]{3,2,1,0:T(8,128)S(1)}, f32[2,2,128,128]{3,2,1,0:T(8,128)S(1)}, u32[]{:S(2)}, u32[]{:S(2)}) collective-permute-start(f32[2,2,128,128]{3,2,1,0:T(8,128)S(1)} %slice_bitcast_fusion), channel_id=1, source_target_pairs={{0,8},{1,9},{2,10},{3,11},{4,12},{5,13},{6,14},{7,15},{8,16},{9,17... | collective-permute-start | bytes 786440 | tf_op jit(solution)/shard_map/ppermute | solution.py:18
  111.6 6.3 %collective-permute-start.25 = (f32[2,128,640]{2,1,0:T(8,128)S(1)}, f32[2,128,640]{2,1,0:T(8,128)S(1)}, u32[]{:S(2)}, u32[]{:S(2)}) collective-permute-start(f32[2,128,640]{2,1,0:T(8,128)S(1)} %pad_maximum_fusion.own_ref), channel_id=1, source_target_pairs={{0,32},{32,0},{64,96},{96,64},{128,160},{160,128},{192,224},{224,1... | collective-permute-start | bytes 1966088 | tf_op jit(solution)/shard_map/ppermute | solution.py:22
  117.9 2.6 %copy-start = (f32[1024,512]{1,0:T(8,128)S(1)}, f32[1024,512]{1,0:T(8,128)}, u32[]{:S(2)}) copy-start(f32[1024,512]{1,0:T(8,128)} %k_ref.1) | copy-start | bytes 6291460
  117.9 2.6 %copy-start.1 = (f32[1024,128]{1,0:T(8,128)S(1)}, f32[1024,128]{1,0:T(8,128)}, u32[]{:S(2)}) copy-start(f32[1024,128]{1,0:T(8,128)} %y_ref.1) | copy-start | bytes 1572868

commit v7 on v6

--- a/solution.py
+++ b/solution.py
@@ -272,8 +272,10 @@
     for cols, depth in ((slice(0, 256), 256), (slice(256, 512), 512)):
         a = [part[:, :depth] for part in p]
         b = [t_ref[:depth, cols] for t_ref in (t0, t1, t2)]
-        small = once(a[0], b[2]) + once(a[1], b[1]) + once(a[2], b[0])
-        w[:, cols] = once(a[0], b[0]) + ((once(a[0], b[1]) + once(a[1], b[0])) + small)
+        w[:, cols] = once(
+            jnp.concatenate([a[2], a[1], a[0], a[1], a[0], a[0]], 1),
+            jnp.concatenate([b[0], b[1], b[2], b[0], b[1], b[0]], 0),
+        )
 
     first = (at_ref[4 + step] == 0) & (row < 4)
     for i in range(4):
@@ -284,7 +286,10 @@
                 w[:n, m * n : (m + 1) * n] = f_ref[(i - m) * n : (i - m + 1) * n, :]
 
     high, low = split(w[...], 2)
-    change = once(high, wh_ref[...]) + (once(high, wl_ref[...]) + once(low, wh_ref[...]))
+    change = once(
+        jnp.concatenate([low, high, high], 1),
+        jnp.concatenate([wh_ref[...], wl_ref[...], wh_ref[...]], 0),
+    )
     out_ref[...] = k_ref[...] - change[:, :ORDER]
     right_ref[...] = y_ref[...] - change[:, ORDER:]
 
@@ -381,6 +386,7 @@
     low = over_col(near, [(c, (c - Y) % COLS) for c in range(COLS)])
     high = over_col(far, [(c, (c + Y) % COLS) for c in range(COLS)])
     c2 = total([strip] + [after(got, rest) for got in strip_got])
+    c2 = after(c2, near, far)
     c3_got = over_row(c2, by_z)
     f3, g3 = factor_step(3, [f0, f1, f2], [g0, g1, g2], after(rest, near, far, c2))
     c3 = after(jnp.stack([c2, after(c3_got, g3)]), low, high)

time: 132 us -> 130 us (0.985)
    ppermute x12, waiting for transfers between devices: 15.4 us -> 14 us  [over_col(): return lax.ppermute(value, 'col', pairs)]
where the time goes in v7:
time: 130 us; the launch traced here: 129 us
  starting transfers between devices  69.3 us (53%)
  Pallas kernels  37.5 us (29%)
  waiting for transfers between devices  18.1 us (14%)
  other arithmetic  2.1 us (2%)
    ppermute x10, starting transfers between devices, over_row(): return lax.ppermute(value, 'row', pairs)  30.1 us
    ppermute x12, starting transfers between devices, over_col(): return lax.ppermute(value, 'col', pairs)  29.8 us
    pallas_call x3, Pallas kernels, factor_step(): pl.pallas_call(functools.partial(step_kernel, k), out_shape=shapes, in_sp...  17.5 us
    ppermute x12, waiting for transfers between devices, over_col(): return lax.ppermute(value, 'col', pairs)  14 us
    pallas_call x1, Pallas kernels, update(): pl.pallas_call(update_kernel, out_shape=[f32(*kernel.shape), f32(*targets...  10.1 us
    ppermute x3, starting transfers between devices, per_device(): got.append(lax.ppermute(a0, ('row', 'col'), pairs))  8.05 us
    pallas_call x1, Pallas kernels, factor_first(): pl.pallas_call(first_kernel, out_shape=[f32(ORDER, BLOCK), f32(BLOCK, BLO...  7.04 us
  transfers between devices with their start and end apart: 26, of which 9 were waited for; matrix products, arithmetic and copies ran while one was open for 1% of the time, Pallas kernels for 19%

profile of v7, /device:TPU:1, one launch (start us, length us, event | category | flops | bytes accessed | tf_op | source)
XLA Modules:
  0.0 129.4 jit_solution(4008754876028292465)
XLA Ops:
  0.6 0.8 slice_select_fusion
  1.5 5.5 %collective-permute-start.1 = (f32[128,128]{1,0:T(8,128)S(1)}, f32[128,128]{1,0:T(8,128)S(1)}, u32[]{:S(2)}, u32[]{:S(2)}) collective-permute-start(f32[128,128]{1,0:T(8,128)S(1)} %slice_select_fusion), channel_id=1, source_target_pairs={{0,16},{1,17},{2,18},{3,19},{32,48},{33,49},{34,50},{35,51},{64,80... | collective-permute-start | bytes 196616 | tf_op jit(solution)/shard_map/ppermute | solution.py:349
  7.0 1.3 collective-permute-start.2
  8.3 1.3 collective-permute-start
  9.6 1.6 %collective-permute-done = f32[128,128]{1,0:T(8,128)S(1)} collective-permute-done((f32[128,128]{1,0:T(8,128)S(1)}, f32[128,128]{1,0:T(8,128)S(1)}, u32[]{:S(2)}, u32[]{:S(2)}) %collective-permute-start) | collective-permute-done | bytes 65568 | tf_op jit(solution)/shard_map/ppermute | solution.py:349
  11.2 0.9 add_add_fusion.3
  12.0 1.3 collective-permute-start.3
  13.4 1.1 slice.30
  14.5 0.2 collective-permute-done.3
  14.7 3.0 %collective-permute-start.9 = (f32[128,128]{1,0:T(8,128)S(1)}, f32[128,128]{1,0:T(8,128)S(1)}, u32[]{:S(2)}, u32[]{:S(2)}) collective-permute-start(f32[128,128]{1,0:T(8,128)S(1)} %add.67), channel_id=1, source_target_pairs={{0,384},{32,416},{64,448},{96,480},{1,385},{33,417},{65,449},{97,4... | collective-permute-start | bytes 196616 | tf_op jit(solution)/shard_map/ppermute | solution.py:22
  17.7 1.3 collective-permute-start.8
  19.0 1.3 collective-permute-start.7
  20.3 3.1 %collective-permute-start.4 = (f32[2,128,128]{2,1,0:T(8,128)S(1)}, f32[2,128,128]{2,1,0:T(8,128)S(1)}, u32[]{:S(2)}, u32[]{:S(2)}) collective-permute-start(f32[2,128,128]{2,1,0:T(8,128)S(1)} %get-tuple-element.76), channel_id=1, source_target_pairs={{0,8},{1,9},{2,10},{3,11},{32,40},{33,41},{34,42},{35,43},{64,72},... | collective-permute-start | bytes 393224 | tf_op jit(solution)/shard_map/ppermute | solution.py:18
  23.5 1.9 %collective-permute-start.6 = (f32[2,128,128]{2,1,0:T(8,128)S(1)}, f32[2,128,128]{2,1,0:T(8,128)S(1)}, u32[]{:S(2)}, u32[]{:S(2)}) collective-permute-start(f32[2,128,128]{2,1,0:T(8,128)S(1)} %get-tuple-element.77), channel_id=1, source_target_pairs={{0,24},{1,25},{2,26},{3,27},{32,56},{33,57},{34,58},{35,59},{64,88... | collective-permute-start | bytes 393224 | tf_op jit(solution)/shard_map/ppermute | solution.py:18
  25.4 1.3 %collective-permute-start.5 = (f32[2,128,128]{2,1,0:T(8,128)S(1)}, f32[2,128,128]{2,1,0:T(8,128)S(1)}, u32[]{:S(2)}, u32[]{:S(2)}) collective-permute-start(f32[2,128,128]{2,1,0:T(8,128)S(1)} %get-tuple-element.78), channel_id=1, source_target_pairs={{0,16},{1,17},{2,18},{3,19},{32,48},{33,49},{34,50},{35,51},{64,80... | collective-permute-start | bytes 393224 | tf_op jit(solution)/shard_map/ppermute | solution.py:18
  26.8 0.5 collective-permute-done.6
  27.3 2.7 %collective-permute-done.5 = f32[2,128,128]{2,1,0:T(8,128)S(1)} collective-permute-done((f32[2,128,128]{2,1,0:T(8,128)S(1)}, f32[2,128,128]{2,1,0:T(8,128)S(1)}, u32[]{:S(2)}, u32[]{:S(2)}) %collective-permute-start.5) | collective-permute-done | bytes 131104 | tf_op jit(solution)/shard_map/ppermute | solution.py:18
  30.1 3.0 %collective-permute-start.11 = (f32[128,128]{1,0:T(8,128)S(1)}, f32[128,128]{1,0:T(8,128)S(1)}, u32[]{:S(2)}, u32[]{:S(2)}) collective-permute-start(f32[128,128]{1,0:T(8,128)S(1)} %add_add_fusion.2), channel_id=1, source_target_pairs={{0,2},{1,3},{2,0},{3,1},{4,6},{5,7},{6,4},{7,5},{8,10},{9,11},{10,... | collective-permute-start | bytes 196616 | tf_op jit(solution)/shard_map/ppermute | solution.py:18
  33.1 1.3 %collective-permute-start.10 = (f32[2,128,128]{2,1,0:T(8,128)S(1)}, f32[2,128,128]{2,1,0:T(8,128)S(1)}, u32[]{:S(2)}, u32[]{:S(2)}) collective-permute-start(f32[2,128,128]{2,1,0:T(8,128)S(1)} %add_add_fusion.1), channel_id=1, source_target_pairs={{0,7},{1,6},{2,5},{3,4},{8,15},{9,14},{10,13},{11,12},{16,23},{17,... | collective-permute-start | bytes 393224 | tf_op jit(solution)/shard_map/ppermute | solution.py:18
  34.4 2.1 %collective-permute-done.11 = f32[128,128]{1,0:T(8,128)S(1)} collective-permute-done((f32[128,128]{1,0:T(8,128)S(1)}, f32[128,128]{1,0:T(8,128)S(1)}, u32[]{:S(2)}, u32[]{:S(2)}) %collective-permute-start.11) | collective-permute-done | bytes 65568 | tf_op jit(solution)/shard_map/ppermute | solution.py:18
  36.5 1.9 %collective-permute-start.12 = (f32[2,128,128]{2,1,0:T(8,128)S(1)}, f32[2,128,128]{2,1,0:T(8,128)S(1)}, u32[]{:S(2)}, u32[]{:S(2)}) collective-permute-start(f32[2,128,128]{2,1,0:T(8,128)S(1)} %get-tuple-element.82), channel_id=1, source_target_pairs={{0,1},{1,0},{2,3},{3,2},{4,5},{5,4},{6,7},{7,6},{8,9},{9,8},{10,11... | collective-permute-start | bytes 393224 | tf_op jit(solution)/shard_map/ppermute | solution.py:18
  38.5 3.7 %collective-permute-done.12 = f32[2,128,128]{2,1,0:T(8,128)S(1)} collective-permute-done((f32[2,128,128]{2,1,0:T(8,128)S(1)}, f32[2,128,128]{2,1,0:T(8,128)S(1)}, u32[]{:S(2)}, u32[]{:S(2)}) %collective-permute-start.12) | collective-permute-done | bytes 131104 | tf_op jit(solution)/shard_map/ppermute | solution.py:18
  42.2 3.5 %collective-permute-start.14 = (f32[2,2,128,128]{3,2,1,0:T(8,128)S(1)}, f32[2,2,128,128]{3,2,1,0:T(8,128)S(1)}, u32[]{:S(2)}, u32[]{:S(2)}) collective-permute-start(f32[2,2,128,128]{3,2,1,0:T(8,128)S(1)} %pad_maximum_fusion.3), channel_id=1, source_target_pairs={{0,64},{32,96},{64,0},{96,32},{128,192},{160,224},{192,128},{224,1... | collective-permute-start | bytes 786440 | tf_op jit(solution)/shard_map/ppermute | solution.py:22
  45.7 3.0 %collective-permute-start.13 = (f32[2,128,128]{2,1,0:T(8,128)S(1)}, f32[2,128,128]{2,1,0:T(8,128)S(1)}, u32[]{:S(2)}, u32[]{:S(2)}) collective-permute-start(f32[2,128,128]{2,1,0:T(8,128)S(1)} %broadcast_select_fusion), channel_id=1, source_target_pairs={{0,2},{1,3},{2,0},{3,1},{4,6},{5,7},{6,4},{7,5},{8,10},{9,11},{10,... | collective-permute-start | bytes 393224 | tf_op jit(solution)/shard_map/ppermute | solution.py:18
  48.7 4.9 %collective-permute-done.13 = f32[2,128,128]{2,1,0:T(8,128)S(1)} collective-permute-done((f32[2,128,128]{2,1,0:T(8,128)S(1)}, f32[2,128,128]{2,1,0:T(8,128)S(1)}, u32[]{:S(2)}, u32[]{:S(2)}) %collective-permute-start.13) | collective-permute-done | bytes 131104 | tf_op jit(solution)/shard_map/ppermute | solution.py:18
  53.7 0.1 pad_maximum_fusion.1.own_ref
  53.7 5.9 %collective-permute-start.16 = (f32[2,2,2,128,128]{4,3,2,1,0:T(8,128)S(1)}, f32[2,2,2,128,128]{4,3,2,1,0:T(8,128)S(1)}, u32[]{:S(2)}, u32[]{:S(2)}) collective-permute-start(f32[2,2,2,128,128]{4,3,2,1,0:T(8,128)S(1)} %pad_maximum_fusion.1.own_ref), channel_id=1, source_target_pairs={{0,32},{32,0},{64,96},{96,64},{128,160},{160,128},{192,224},{224,1... | collective-permute-start | bytes 1572872 | tf_op jit(solution)/shard_map/ppermute | solution.py:22
  59.6 0.1 concatenate.6.at_ref
  59.8 4.7 %collective-permute-start.23 = (f32[128,640]{1,0:T(8,128)S(1)}, f32[128,640]{1,0:T(8,128)S(1)}, u32[]{:S(2)}, u32[]{:S(2)}) collective-permute-start(f32[128,640]{1,0:T(8,128)S(1)} %maximum_select_fusion), channel_id=1, source_target_pairs={{0,384},{32,416},{64,448},{96,480},{1,385},{33,417},{65,449},{97,4... | collective-permute-start | bytes 983048 | tf_op jit(solution)/shard_map/ppermute | solution.py:22
  64.4 1.3 %collective-permute-start.22 = (f32[128,640]{1,0:T(8,128)S(1)}, f32[128,640]{1,0:T(8,128)S(1)}, u32[]{:S(2)}, u32[]{:S(2)}) collective-permute-start(f32[128,640]{1,0:T(8,128)S(1)} %maximum_select_fusion), channel_id=1, source_target_pairs={{0,256},{32,288},{64,320},{96,352},{1,257},{33,289},{65,321},{97,3... | collective-permute-start | bytes 983048 | tf_op jit(solution)/shard_map/ppermute | solution.py:22
  65.8 1.3 %collective-permute-start.21 = (f32[128,640]{1,0:T(8,128)S(1)}, f32[128,640]{1,0:T(8,128)S(1)}, u32[]{:S(2)}, u32[]{:S(2)}) collective-permute-start(f32[128,640]{1,0:T(8,128)S(1)} %maximum_select_fusion), channel_id=1, source_target_pairs={{0,128},{32,160},{64,192},{96,224},{1,129},{33,161},{65,193},{97,2... | collective-permute-start | bytes 983048 | tf_op jit(solution)/shard_map/ppermute | solution.py:22
  67.1 2.6 %collective-permute-start.15 = (f32[2,2,128,128]{3,2,1,0:T(8,128)S(1)}, f32[2,2,128,128]{3,2,1,0:T(8,128)S(1)}, u32[]{:S(2)}, u32[]{:S(2)}) collective-permute-start(f32[2,2,128,128]{3,2,1,0:T(8,128)S(1)} %get-tuple-element.45), channel_id=1, source_target_pairs={{0,1},{1,0},{2,3},{3,2},{4,5},{5,4},{6,7},{7,6},{8,9},{9,8},{10,11... | collective-permute-start | bytes 786440 | tf_op jit(solution)/shard_map/ppermute | solution.py:18
  69.7 7.0 %shard_map.50 = (f32[512,128]{1,0:T(8,128)S(1)}, f32[128,128]{1,0:T(8,128)S(1)}, f32[384,384]{1,0:T(8,128)S(1)}) custom-call(s32[8]{0:T(128)S(1)} %concatenate.6.at_ref, f32[2,2,2,128,128]{4,3,2,1,0:T(8,128)S(1)} %pad_maximum_fusion.1.own_ref, f32[2,2,2,128,128]{4,3,2,1,0:T(8,128)S(1)} %collective-permute-done.16.got_ref), custom_call_target="tpu_custom_call" | custom-call | flops 6000000000 | bytes 1048576 | tf_op jit(solution)/shard_map/pallas_call | solution.py:164
  76.8 1.9 %collective-permute-start.18 = (f32[2,2,2,128,128]{4,3,2,1,0:T(8,128)S(1)}, f32[2,2,2,128,128]{4,3,2,1,0:T(8,128)S(1)}, u32[]{:S(2)}, u32[]{:S(2)}) collective-permute-start(f32[2,2,2,128,128]{4,3,2,1,0:T(8,128)S(1)} %pad_maximum_fusion.2.q0_ref), channel_id=1, source_target_pairs={{0,24},{1,25},{2,26},{3,27},{4,28},{5,29},{6,30},{7,31},{8,0},{9,1... | collective-permute-start | bytes 1572872 | tf_op jit(solution)/shard_map/ppermute | solution.py:18
  78.8 3.5 %collective-permute-start.17 = (f32[2,2,2,128,128]{4,3,2,1,0:T(8,128)S(1)}, f32[2,2,2,128,128]{4,3,2,1,0:T(8,128)S(1)}, u32[]{:S(2)}, u32[]{:S(2)}) collective-permute-start(f32[2,2,2,128,128]{4,3,2,1,0:T(8,128)S(1)} %pad_maximum_fusion.2.q0_ref), channel_id=1, source_target_pairs={{0,8},{1,9},{2,10},{3,11},{4,12},{5,13},{6,14},{7,15},{8,16},{9,17... | collective-permute-start | bytes 1572872 | tf_op jit(solution)/shard_map/ppermute | solution.py:18
  82.3 6.1 %shard_map.51 = (f32[384,128]{1,0:T(8,128)S(1)}, f32[128,256]{1,0:T(8,128)S(1)}, f32[256,256]{1,0:T(8,128)S(1)}) custom-call(f32[512,128]{1,0:T(8,128)S(1)} %get-tuple-element.48.refs_0_.f0, f32[128,128]{1,0:T(8,128)S(1)} %get-tuple-element.49.refs_1_.refs_2_.refs_3_.g0, f32[384,384]{1,0:T(8,128)S(1)} %get-tuple-element.50.refs_2_), custom_call_target="tpu_custom_call" | custom-call | flops 6000000000 | bytes 1048576 | tf_op jit(solution)/shard_map/pallas_call | solution.py:179
  88.4 5.9 %shard_map.52 = (f32[256,128]{1,0:T(8,128)S(1)}, f32[128,384]{1,0:T(8,128)S(1)}, f32[128,128]{1,0:T(8,128)S(1)}) custom-call(f32[512,128]{1,0:T(8,128)S(1)} %get-tuple-element.48.refs_0_.f0, f32[384,128]{1,0:T(8,128)S(1)} %get-tuple-element.51.refs_1_.f1, f32[128,128]{1,0:T(8,128)S(1)} %get-tuple-element.49.refs_1_.refs_2_.refs_3_.g0, ...), custom_call_target="tpu_custom_call" | custom-call | flops 6000000000 | bytes 1048576 | tf_op jit(solution)/shard_map/pallas_call | solution.py:179
  94.4 0.1 add_add_fusion
  94.5 4.2 %collective-permute-start.19 = (f32[2,2,128,128]{3,2,1,0:T(8,128)S(1)}, f32[2,2,128,128]{3,2,1,0:T(8,128)S(1)}, u32[]{:S(2)}, u32[]{:S(2)}) collective-permute-start(f32[2,2,128,128]{3,2,1,0:T(8,128)S(1)} %slice_bitcast_fusion.1), channel_id=1, source_target_pairs={{0,24},{1,25},{2,26},{3,27},{4,28},{5,29},{6,30},{7,31},{8,0},{9,1... | collective-permute-start | bytes 786440 | tf_op jit(solution)/shard_map/ppermute | solution.py:18
  98.8 1.9 %collective-permute-start.20 = (f32[2,2,128,128]{3,2,1,0:T(8,128)S(1)}, f32[2,2,128,128]{3,2,1,0:T(8,128)S(1)}, u32[]{:S(2)}, u32[]{:S(2)}) collective-permute-start(f32[2,2,128,128]{3,2,1,0:T(8,128)S(1)} %slice_bitcast_fusion), channel_id=1, source_target_pairs={{0,8},{1,9},{2,10},{3,11},{4,12},{5,13},{6,14},{7,15},{8,16},{9,17... | collective-permute-start | bytes 786440 | tf_op jit(solution)/shard_map/ppermute | solution.py:18
  100.7 3.9 %collective-permute-start.24 = (f32[128,640]{1,0:T(8,128)S(1)}, f32[128,640]{1,0:T(8,128)S(1)}, u32[]{:S(2)}, u32[]{:S(2)}) collective-permute-start(f32[128,640]{1,0:T(8,128)S(1)} %add_add_fusion), channel_id=1, source_target_pairs={{0,64},{32,96},{64,0},{96,32},{128,192},{160,224},{192,128},{224,1... | collective-permute-start | bytes 983048 | tf_op jit(solution)/shard_map/ppermute | solution.py:22
  104.6 5.5 %shard_map.53 = (f32[128,128]{1,0:T(8,128)S(1)}, f32[128,512]{1,0:T(8,128)S(1)}) custom-call(f32[512,128]{1,0:T(8,128)S(1)} %get-tuple-element.48.refs_0_.f0, f32[384,128]{1,0:T(8,128)S(1)} %get-tuple-element.51.refs_1_.f1, f32[256,128]{1,0:T(8,128)S(1)} %get-tuple-element.57.refs_2_.f2, f32[128,128]{1,0:T(8,128)S(1)} %get-tuple-element.49.refs_1_.refs_2_.refs_3_.g0, ...), custom_call_target="tpu_custom_call" | custom-call | flops 6000000000 | bytes 1048576 | tf_op jit(solution)/shard_map/pallas_call | solution.py:179
  110.1 0.8 collective-permute-done.24
  111.0 4.0 %collective-permute-start.25 = (f32[2,128,640]{2,1,0:T(8,128)S(1)}, f32[2,128,640]{2,1,0:T(8,128)S(1)}, u32[]{:S(2)}, u32[]{:S(2)}) collective-permute-start(f32[2,128,640]{2,1,0:T(8,128)S(1)} %pad_maximum_fusion.own_ref), channel_id=1, source_target_pairs={{0,32},{32,0},{64,96},{96,64},{128,160},{160,128},{192,224},{224,1... | collective-permute-start | bytes 1966088 | tf_op jit(solution)/shard_map/ppermute | solution.py:22
  115.0 0.3 shard_map.54
  115.3 1.4 %collective-permute-done.25.got_ref = f32[2,128,640]{2,1,0:T(8,128)S(1)} collective-permute-done((f32[2,128,640]{2,1,0:T(8,128)S(1)}, f32[2,128,640]{2,1,0:T(8,128)S(1)}, u32[]{:S(2)}, u32[]{:S(2)}) %collective-permute-start.25) | collective-permute-done | bytes 655392 | tf_op jit(solution)/shard_map/ppermute | solution.py:22
  116.7 2.6 %shard_map.55 = (bf16[512,640]{1,0:T(8,128)(2,1)S(1)}, bf16[512,640]{1,0:T(8,128)(2,1)S(1)}, f32[512,128]{1,0:T(8,128)S(1)}) custom-call(s32[8]{0:T(128)S(1)} %concatenate.6.at_ref, f32[2,128,640]{2,1,0:T(8,128)S(1)} %pad_maximum_fusion.own_ref, f32[2,128,640]{2,1,0:T(8,128)S(1)} %collective-permute-done.25.got_ref, ...), custom_call_target="tpu_custom_call" | custom-call | flops 4000000000 | bytes 4194304 | tf_op jit(solution)/shard_map/pallas_call | solution.py:239
  119.3 10.1 %shard_map.56 = (f32[1024,512]{1,0:T(8,128)}, f32[1024,128]{1,0:T(8,128)}) custom-call(s32[8]{0:T(128)S(1)} %concatenate.6.at_ref, f32[2,2,2,128,128]{4,3,2,1,0:T(8,128)S(1)} %pad_maximum_fusion.2.q0_ref, f32[2,2,2,128,128]{4,3,2,1,0:T(8,128)S(1)} %collective-permute-done.17.q1_ref, f32[2,2,2,128,128]{4,3,2,1,0:T(8,128)S(1)} %collective-permute-done.18.q2_ref, ...), custom_call_target="tpu_custom_call" | custom-call | flops 10000000000 | bytes 6291456 | tf_op jit(solution)/shard_map/pallas_call | solution.py:309
  (41 shorter events, 0.4 us)
Async XLA Ops:
  1.5 8.1 %collective-permute-start.1 = (f32[128,128]{1,0:T(8,128)S(1)}, f32[128,128]{1,0:T(8,128)S(1)}, u32[]{:S(2)}, u32[]{:S(2)}) collective-permute-start(f32[128,128]{1,0:T(8,128)S(1)} %slice_select_fusion), channel_id=1, source_target_pairs={{0,16},{1,17},{2,18},{3,19},{32,48},{33,49},{34,50},{35,51},{64,80... | collective-permute-start | bytes 196616 | tf_op jit(solution)/shard_map/ppermute | solution.py:349
  7.0 2.6 %collective-permute-start.2 = (f32[128,128]{1,0:T(8,128)S(1)}, f32[128,128]{1,0:T(8,128)S(1)}, u32[]{:S(2)}, u32[]{:S(2)}) collective-permute-start(f32[128,128]{1,0:T(8,128)S(1)} %slice_select_fusion), channel_id=1, source_target_pairs={{0,24},{1,25},{2,26},{3,27},{32,56},{33,57},{34,58},{35,59},{64,88... | collective-permute-start | bytes 196616 | tf_op jit(solution)/shard_map/ppermute | solution.py:349
  8.3 2.9 %collective-permute-start = (f32[128,128]{1,0:T(8,128)S(1)}, f32[128,128]{1,0:T(8,128)S(1)}, u32[]{:S(2)}, u32[]{:S(2)}) collective-permute-start(f32[128,128]{1,0:T(8,128)S(1)} %slice_select_fusion), channel_id=1, source_target_pairs={{0,8},{1,9},{2,10},{3,11},{32,40},{33,41},{34,42},{35,43},{64,72},... | collective-permute-start | bytes 196616 | tf_op jit(solution)/shard_map/ppermute | solution.py:349
  12.0 2.6 %collective-permute-start.3 = (f32[128,128]{1,0:T(8,128)S(1)}, f32[128,128]{1,0:T(8,128)S(1)}, u32[]{:S(2)}, u32[]{:S(2)}) collective-permute-start(f32[128,128]{1,0:T(8,128)S(1)} %add_add_fusion.3), channel_id=1, source_target_pairs={{0,7},{1,6},{2,5},{3,4},{8,15},{9,14},{10,13},{11,12},{16,23},{17,... | collective-permute-start | bytes 196616 | tf_op jit(solution)/shard_map/ppermute | solution.py:353
  14.7 10.7 %collective-permute-start.9 = (f32[128,128]{1,0:T(8,128)S(1)}, f32[128,128]{1,0:T(8,128)S(1)}, u32[]{:S(2)}, u32[]{:S(2)}) collective-permute-start(f32[128,128]{1,0:T(8,128)S(1)} %add.67), channel_id=1, source_target_pairs={{0,384},{32,416},{64,448},{96,480},{1,385},{33,417},{65,449},{97,4... | collective-permute-start | bytes 196616 | tf_op jit(solution)/shard_map/ppermute | solution.py:22
  17.7 9.0 %collective-permute-start.8 = (f32[128,128]{1,0:T(8,128)S(1)}, f32[128,128]{1,0:T(8,128)S(1)}, u32[]{:S(2)}, u32[]{:S(2)}) collective-permute-start(f32[128,128]{1,0:T(8,128)S(1)} %add.67), channel_id=1, source_target_pairs={{0,256},{32,288},{64,320},{96,352},{1,257},{33,289},{65,321},{97,3... | collective-permute-start | bytes 196616 | tf_op jit(solution)/shard_map/ppermute | solution.py:22
  19.0 7.7 %collective-permute-start.7 = (f32[128,128]{1,0:T(8,128)S(1)}, f32[128,128]{1,0:T(8,128)S(1)}, u32[]{:S(2)}, u32[]{:S(2)}) collective-permute-start(f32[128,128]{1,0:T(8,128)S(1)} %add.67), channel_id=1, source_target_pairs={{0,128},{32,160},{64,192},{96,224},{1,129},{33,161},{65,193},{97,2... | collective-permute-start | bytes 196616 | tf_op jit(solution)/shard_map/ppermute | solution.py:22
  20.3 6.5 %collective-permute-start.4 = (f32[2,128,128]{2,1,0:T(8,128)S(1)}, f32[2,128,128]{2,1,0:T(8,128)S(1)}, u32[]{:S(2)}, u32[]{:S(2)}) collective-permute-start(f32[2,128,128]{2,1,0:T(8,128)S(1)} %get-tuple-element.76), channel_id=1, source_target_pairs={{0,8},{1,9},{2,10},{3,11},{32,40},{33,41},{34,42},{35,43},{64,72},... | collective-permute-start | bytes 393224 | tf_op jit(solution)/shard_map/ppermute | solution.py:18
  23.5 3.9 %collective-permute-start.6 = (f32[2,128,128]{2,1,0:T(8,128)S(1)}, f32[2,128,128]{2,1,0:T(8,128)S(1)}, u32[]{:S(2)}, u32[]{:S(2)}) collective-permute-start(f32[2,128,128]{2,1,0:T(8,128)S(1)} %get-tuple-element.77), channel_id=1, source_target_pairs={{0,24},{1,25},{2,26},{3,27},{32,56},{33,57},{34,58},{35,59},{64,88... | collective-permute-start | bytes 393224 | tf_op jit(solution)/shard_map/ppermute | solution.py:18
  25.4 4.6 %collective-permute-start.5 = (f32[2,128,128]{2,1,0:T(8,128)S(1)}, f32[2,128,128]{2,1,0:T(8,128)S(1)}, u32[]{:S(2)}, u32[]{:S(2)}) collective-permute-start(f32[2,128,128]{2,1,0:T(8,128)S(1)} %get-tuple-element.78), channel_id=1, source_target_pairs={{0,16},{1,17},{2,18},{3,19},{32,48},{33,49},{34,50},{35,51},{64,80... | collective-permute-start | bytes 393224 | tf_op jit(solution)/shard_map/ppermute | solution.py:18
  26.8 32.8 %copy-start.2 = (s32[4]{0:T(128)S(1)}, s32[4]{0:T(128)}, u32[]{:S(2)}) copy-start(s32[4]{0:T(128)} %constant.58.clone) | copy-start | bytes 52
  30.1 29.7 %slice-start = ((f32[1024,512]{1,0:T(8,128)}), f32[128,512]{1,0:T(8,128)S(1)}, s32[]{:S(2)}) async-start(f32[1024,512]{1,0:T(8,128)} %k_ref.1), calls=%async_computation | async-start | bytes 524288 | tf_op jit(solution)/shard_map/slice | solution.py:374
  30.1 29.7 %slice-start.1 = ((f32[1024,128]{1,0:T(8,128)}), f32[128,128]{1,0:T(8,128)S(1)}, s32[]{:S(2)}) async-start(f32[1024,128]{1,0:T(8,128)} %y_ref.1), calls=%async_computation.1 | async-start | bytes 131072 | tf_op jit(solution)/shard_map/slice | solution.py:374
  30.1 6.4 %collective-permute-start.11 = (f32[128,128]{1,0:T(8,128)S(1)}, f32[128,128]{1,0:T(8,128)S(1)}, u32[]{:S(2)}, u32[]{:S(2)}) collective-permute-start(f32[128,128]{1,0:T(8,128)S(1)} %add_add_fusion.2), channel_id=1, source_target_pairs={{0,2},{1,3},{2,0},{3,1},{4,6},{5,7},{6,4},{7,5},{8,10},{9,11},{10,... | collective-permute-start | bytes 196616 | tf_op jit(solution)/shard_map/ppermute | solution.py:18
  33.1 5.4 %collective-permute-start.10 = (f32[2,128,128]{2,1,0:T(8,128)S(1)}, f32[2,128,128]{2,1,0:T(8,128)S(1)}, u32[]{:S(2)}, u32[]{:S(2)}) collective-permute-start(f32[2,128,128]{2,1,0:T(8,128)S(1)} %add_add_fusion.1), channel_id=1, source_target_pairs={{0,7},{1,6},{2,5},{3,4},{8,15},{9,14},{10,13},{11,12},{16,23},{17,... | collective-permute-start | bytes 393224 | tf_op jit(solution)/shard_map/ppermute | solution.py:18
  36.5 5.7 %collective-permute-start.12 = (f32[2,128,128]{2,1,0:T(8,128)S(1)}, f32[2,128,128]{2,1,0:T(8,128)S(1)}, u32[]{:S(2)}, u32[]{:S(2)}) collective-permute-start(f32[2,128,128]{2,1,0:T(8,128)S(1)} %get-tuple-element.82), channel_id=1, source_target_pairs={{0,1},{1,0},{2,3},{3,2},{4,5},{5,4},{6,7},{7,6},{8,9},{9,8},{10,11... | collective-permute-start | bytes 393224 | tf_op jit(solution)/shard_map/ppermute | solution.py:18
  42.2 11.4 %collective-permute-start.14 = (f32[2,2,128,128]{3,2,1,0:T(8,128)S(1)}, f32[2,2,128,128]{3,2,1,0:T(8,128)S(1)}, u32[]{:S(2)}, u32[]{:S(2)}) collective-permute-start(f32[2,2,128,128]{3,2,1,0:T(8,128)S(1)} %pad_maximum_fusion.3), channel_id=1, source_target_pairs={{0,64},{32,96},{64,0},{96,32},{128,192},{160,224},{192,128},{224,1... | collective-permute-start | bytes 786440 | tf_op jit(solution)/shard_map/ppermute | solution.py:22
  45.7 7.9 %collective-permute-start.13 = (f32[2,128,128]{2,1,0:T(8,128)S(1)}, f32[2,128,128]{2,1,0:T(8,128)S(1)}, u32[]{:S(2)}, u32[]{:S(2)}) collective-permute-start(f32[2,128,128]{2,1,0:T(8,128)S(1)} %broadcast_select_fusion), channel_id=1, source_target_pairs={{0,2},{1,3},{2,0},{3,1},{4,6},{5,7},{6,4},{7,5},{8,10},{9,11},{10,... | collective-permute-start | bytes 393224 | tf_op jit(solution)/shard_map/ppermute | solution.py:18
  53.7 16.0 %collective-permute-start.16 = (f32[2,2,2,128,128]{4,3,2,1,0:T(8,128)S(1)}, f32[2,2,2,128,128]{4,3,2,1,0:T(8,128)S(1)}, u32[]{:S(2)}, u32[]{:S(2)}) collective-permute-start(f32[2,2,2,128,128]{4,3,2,1,0:T(8,128)S(1)} %pad_maximum_fusion.1.own_ref), channel_id=1, source_target_pairs={{0,32},{32,0},{64,96},{96,64},{128,160},{160,128},{192,224},{224,1... | collective-permute-start | bytes 1572872 | tf_op jit(solution)/shard_map/ppermute | solution.py:22
  59.8 34.6 %collective-permute-start.23 = (f32[128,640]{1,0:T(8,128)S(1)}, f32[128,640]{1,0:T(8,128)S(1)}, u32[]{:S(2)}, u32[]{:S(2)}) collective-permute-start(f32[128,640]{1,0:T(8,128)S(1)} %maximum_select_fusion), channel_id=1, source_target_pairs={{0,384},{32,416},{64,448},{96,480},{1,385},{33,417},{65,449},{97,4... | collective-permute-start | bytes 983048 | tf_op jit(solution)/shard_map/ppermute | solution.py:22
  64.4 29.9 %collective-permute-start.22 = (f32[128,640]{1,0:T(8,128)S(1)}, f32[128,640]{1,0:T(8,128)S(1)}, u32[]{:S(2)}, u32[]{:S(2)}) collective-permute-start(f32[128,640]{1,0:T(8,128)S(1)} %maximum_select_fusion), channel_id=1, source_target_pairs={{0,256},{32,288},{64,320},{96,352},{1,257},{33,289},{65,321},{97,3... | collective-permute-start | bytes 983048 | tf_op jit(solution)/shard_map/ppermute | solution.py:22
  65.8 28.6 %collective-permute-start.21 = (f32[128,640]{1,0:T(8,128)S(1)}, f32[128,640]{1,0:T(8,128)S(1)}, u32[]{:S(2)}, u32[]{:S(2)}) collective-permute-start(f32[128,640]{1,0:T(8,128)S(1)} %maximum_select_fusion), channel_id=1, source_target_pairs={{0,128},{32,160},{64,192},{96,224},{1,129},{33,161},{65,193},{97,2... | collective-permute-start | bytes 983048 | tf_op jit(solution)/shard_map/ppermute | solution.py:22
  67.1 9.7 %collective-permute-start.15 = (f32[2,2,128,128]{3,2,1,0:T(8,128)S(1)}, f32[2,2,128,128]{3,2,1,0:T(8,128)S(1)}, u32[]{:S(2)}, u32[]{:S(2)}) collective-permute-start(f32[2,2,128,128]{3,2,1,0:T(8,128)S(1)} %get-tuple-element.45), channel_id=1, source_target_pairs={{0,1},{1,0},{2,3},{3,2},{4,5},{5,4},{6,7},{7,6},{8,9},{9,8},{10,11... | collective-permute-start | bytes 786440 | tf_op jit(solution)/shard_map/ppermute | solution.py:18
  76.8 17.7 %collective-permute-start.18 = (f32[2,2,2,128,128]{4,3,2,1,0:T(8,128)S(1)}, f32[2,2,2,128,128]{4,3,2,1,0:T(8,128)S(1)}, u32[]{:S(2)}, u32[]{:S(2)}) collective-permute-start(f32[2,2,2,128,128]{4,3,2,1,0:T(8,128)S(1)} %pad_maximum_fusion.2.q0_ref), channel_id=1, source_target_pairs={{0,24},{1,25},{2,26},{3,27},{4,28},{5,29},{6,30},{7,31},{8,0},{9,1... | collective-permute-start | bytes 1572872 | tf_op jit(solution)/shard_map/ppermute | solution.py:18
  78.8 20.0 %collective-permute-start.17 = (f32[2,2,2,128,128]{4,3,2,1,0:T(8,128)S(1)}, f32[2,2,2,128,128]{4,3,2,1,0:T(8,128)S(1)}, u32[]{:S(2)}, u32[]{:S(2)}) collective-permute-start(f32[2,2,2,128,128]{4,3,2,1,0:T(8,128)S(1)} %pad_maximum_fusion.2.q0_ref), channel_id=1, source_target_pairs={{0,8},{1,9},{2,10},{3,11},{4,12},{5,13},{6,14},{7,15},{8,16},{9,17... | collective-permute-start | bytes 1572872 | tf_op jit(solution)/shard_map/ppermute | solution.py:18
  94.5 16.5 %collective-permute-start.19 = (f32[2,2,128,128]{3,2,1,0:T(8,128)S(1)}, f32[2,2,128,128]{3,2,1,0:T(8,128)S(1)}, u32[]{:S(2)}, u32[]{:S(2)}) collective-permute-start(f32[2,2,128,128]{3,2,1,0:T(8,128)S(1)} %slice_bitcast_fusion.1), channel_id=1, source_target_pairs={{0,24},{1,25},{2,26},{3,27},{4,28},{5,29},{6,30},{7,31},{8,0},{9,1... | collective-permute-start | bytes 786440 | tf_op jit(solution)/shard_map/ppermute | solution.py:18
  98.8 12.2 %collective-permute-start.20 = (f32[2,2,128,128]{3,2,1,0:T(8,128)S(1)}, f32[2,2,128,128]{3,2,1,0:T(8,128)S(1)}, u32[]{:S(2)}, u32[]{:S(2)}) collective-permute-start(f32[2,2,128,128]{3,2,1,0:T(8,128)S(1)} %slice_bitcast_fusion), channel_id=1, source_target_pairs={{0,8},{1,9},{2,10},{3,11},{4,12},{5,13},{6,14},{7,15},{8,16},{9,17... | collective-permute-start | bytes 786440 | tf_op jit(solution)/shard_map/ppermute | solution.py:18
  100.7 10.2 %collective-permute-start.24 = (f32[128,640]{1,0:T(8,128)S(1)}, f32[128,640]{1,0:T(8,128)S(1)}, u32[]{:S(2)}, u32[]{:S(2)}) collective-permute-start(f32[128,640]{1,0:T(8,128)S(1)} %add_add_fusion), channel_id=1, source_target_pairs={{0,64},{32,96},{64,0},{96,32},{128,192},{160,224},{192,128},{224,1... | collective-permute-start | bytes 983048 | tf_op jit(solution)/shard_map/ppermute | solution.py:22
  111.0 5.7 %collective-permute-start.25 = (f32[2,128,640]{2,1,0:T(8,128)S(1)}, f32[2,128,640]{2,1,0:T(8,128)S(1)}, u32[]{:S(2)}, u32[]{:S(2)}) collective-permute-start(f32[2,128,640]{2,1,0:T(8,128)S(1)} %pad_maximum_fusion.own_ref), channel_id=1, source_target_pairs={{0,32},{32,0},{64,96},{96,64},{128,160},{160,128},{192,224},{224,1... | collective-permute-start | bytes 1966088 | tf_op jit(solution)/shard_map/ppermute | solution.py:22
  116.7 2.6 %copy-start = (f32[1024,512]{1,0:T(8,128)S(1)}, f32[1024,512]{1,0:T(8,128)}, u32[]{:S(2)}) copy-start(f32[1024,512]{1,0:T(8,128)} %k_ref.1) | copy-start | bytes 6291460
  116.7 2.6 %copy-start.1 = (f32[1024,128]{1,0:T(8,128)S(1)}, f32[1024,128]{1,0:T(8,128)}, u32[]{:S(2)}) copy-start(f32[1024,128]{1,0:T(8,128)} %y_ref.1) | copy-start | bytes 1572868

commit v8 on v7

--- a/solution.py
+++ b/solution.py
@@ -227,9 +227,15 @@
     for i in range(4):
         u = at_ref[0] ^ i
         tmp[i * n : (i + 1) * n, :] = jnp.where(u % 2 == 0, own_ref[u // 2], got_ref[u // 2])
+    top = split(tmp[...], 3)
     for i, g_ref in enumerate((g0, g1, g2, g3)):
         here = slice(i * n, (i + 1) * n)
-        value = dot(g_ref[...], tmp[: (i + 1) * n, :])
+        a = split(g_ref[...], 3)
+        b = [part[: (i + 1) * n, :] for part in top]
+        value = once(
+            jnp.concatenate([a[2], a[1], a[0], a[1], a[0], a[0]], 1),
+            jnp.concatenate([b[0], b[1], b[2], b[0], b[1], b[0]], 0),
+        )
         high_ref[here, :], low_ref[here, :] = split(value, 2)
         z_ref[here, :] = value[:, ORDER:]
 

time: 130 us -> 130 us (level)
  no operation moved by 1% of the time
where the time goes in v8:
time: 130 us; the launch traced here: 129 us
  starting transfers between devices  69.3 us (53%)
  Pallas kernels  37.3 us (29%)
  waiting for transfers between devices  18.1 us (14%)
  other arithmetic  2.1 us (2%)
    ppermute x10, starting transfers between devices, over_row(): return lax.ppermute(value, 'row', pairs)  30.1 us
    ppermute x12, starting transfers between devices, over_col(): return lax.ppermute(value, 'col', pairs)  29.8 us
    pallas_call x3, Pallas kernels, factor_step(): pl.pallas_call(functools.partial(step_kernel, k), out_shape=shapes, in_sp...  17.5 us
    ppermute x12, waiting for transfers between devices, over_col(): return lax.ppermute(value, 'col', pairs)  14 us
    pallas_call x1, Pallas kernels, update(): pl.pallas_call(update_kernel, out_shape=[f32(*kernel.shape), f32(*targets...  10.1 us
    ppermute x3, starting transfers between devices, per_device(): got.append(lax.ppermute(a0, ('row', 'col'), pairs))  8.05 us
    pallas_call x1, Pallas kernels, factor_first(): pl.pallas_call(first_kernel, out_shape=[f32(ORDER, BLOCK), f32(BLOCK, BLO...  7.04 us
  transfers between devices with their start and end apart: 26, of which 9 were waited for; matrix products, arithmetic and copies ran while one was open for 1% of the time, Pallas kernels for 19%

profile of v8, /device:TPU:1, one launch (start us, length us, event | category | flops | bytes accessed | tf_op | source)
XLA Modules:
  0.0 129.2 jit_solution(16321357521863935264)
XLA Ops:
  0.6 0.8 slice_select_fusion
  1.5 5.5 %collective-permute-start.1 = (f32[128,128]{1,0:T(8,128)S(1)}, f32[128,128]{1,0:T(8,128)S(1)}, u32[]{:S(2)}, u32[]{:S(2)}) collective-permute-start(f32[128,128]{1,0:T(8,128)S(1)} %slice_select_fusion), channel_id=1, source_target_pairs={{0,16},{1,17},{2,18},{3,19},{32,48},{33,49},{34,50},{35,51},{64,80... | collective-permute-start | bytes 196616 | tf_op jit(solution)/shard_map/ppermute | solution.py:355
  7.0 1.3 %collective-permute-start.2 = (f32[128,128]{1,0:T(8,128)S(1)}, f32[128,128]{1,0:T(8,128)S(1)}, u32[]{:S(2)}, u32[]{:S(2)}) collective-permute-start(f32[128,128]{1,0:T(8,128)S(1)} %slice_select_fusion), channel_id=1, source_target_pairs={{0,24},{1,25},{2,26},{3,27},{32,56},{33,57},{34,58},{35,59},{64,88... | collective-permute-start | bytes 196616 | tf_op jit(solution)/shard_map/ppermute | solution.py:355
  8.3 1.3 %collective-permute-start = (f32[128,128]{1,0:T(8,128)S(1)}, f32[128,128]{1,0:T(8,128)S(1)}, u32[]{:S(2)}, u32[]{:S(2)}) collective-permute-start(f32[128,128]{1,0:T(8,128)S(1)} %slice_select_fusion), channel_id=1, source_target_pairs={{0,8},{1,9},{2,10},{3,11},{32,40},{33,41},{34,42},{35,43},{64,72},... | collective-permute-start | bytes 196616 | tf_op jit(solution)/shard_map/ppermute | solution.py:355
  9.6 1.6 %collective-permute-done = f32[128,128]{1,0:T(8,128)S(1)} collective-permute-done((f32[128,128]{1,0:T(8,128)S(1)}, f32[128,128]{1,0:T(8,128)S(1)}, u32[]{:S(2)}, u32[]{:S(2)}) %collective-permute-start) | collective-permute-done | bytes 65568 | tf_op jit(solution)/shard_map/ppermute | solution.py:355
  11.2 0.9 add_add_fusion.3
  12.0 1.3 %collective-permute-start.3 = (f32[128,128]{1,0:T(8,128)S(1)}, f32[128,128]{1,0:T(8,128)S(1)}, u32[]{:S(2)}, u32[]{:S(2)}) collective-permute-start(f32[128,128]{1,0:T(8,128)S(1)} %add_add_fusion.3), channel_id=1, source_target_pairs={{0,7},{1,6},{2,5},{3,4},{8,15},{9,14},{10,13},{11,12},{16,23},{17,... | collective-permute-start | bytes 196616 | tf_op jit(solution)/shard_map/ppermute | solution.py:359
  13.4 1.1 slice.30
  14.5 0.2 collective-permute-done.3
  14.7 3.0 %collective-permute-start.9 = (f32[128,128]{1,0:T(8,128)S(1)}, f32[128,128]{1,0:T(8,128)S(1)}, u32[]{:S(2)}, u32[]{:S(2)}) collective-permute-start(f32[128,128]{1,0:T(8,128)S(1)} %add.67), channel_id=1, source_target_pairs={{0,384},{32,416},{64,448},{96,480},{1,385},{33,417},{65,449},{97,4... | collective-permute-start | bytes 196616 | tf_op jit(solution)/shard_map/ppermute | solution.py:22
  17.7 1.3 %collective-permute-start.8 = (f32[128,128]{1,0:T(8,128)S(1)}, f32[128,128]{1,0:T(8,128)S(1)}, u32[]{:S(2)}, u32[]{:S(2)}) collective-permute-start(f32[128,128]{1,0:T(8,128)S(1)} %add.67), channel_id=1, source_target_pairs={{0,256},{32,288},{64,320},{96,352},{1,257},{33,289},{65,321},{97,3... | collective-permute-start | bytes 196616 | tf_op jit(solution)/shard_map/ppermute | solution.py:22
  19.0 1.3 %collective-permute-start.7 = (f32[128,128]{1,0:T(8,128)S(1)}, f32[128,128]{1,0:T(8,128)S(1)}, u32[]{:S(2)}, u32[]{:S(2)}) collective-permute-start(f32[128,128]{1,0:T(8,128)S(1)} %add.67), channel_id=1, source_target_pairs={{0,128},{32,160},{64,192},{96,224},{1,129},{33,161},{65,193},{97,2... | collective-permute-start | bytes 196616 | tf_op jit(solution)/shard_map/ppermute | solution.py:22
  20.3 3.1 %collective-permute-start.4 = (f32[2,128,128]{2,1,0:T(8,128)S(1)}, f32[2,128,128]{2,1,0:T(8,128)S(1)}, u32[]{:S(2)}, u32[]{:S(2)}) collective-permute-start(f32[2,128,128]{2,1,0:T(8,128)S(1)} %get-tuple-element.76), channel_id=1, source_target_pairs={{0,8},{1,9},{2,10},{3,11},{32,40},{33,41},{34,42},{35,43},{64,72},... | collective-permute-start | bytes 393224 | tf_op jit(solution)/shard_map/ppermute | solution.py:18
  23.5 1.9 %collective-permute-start.6 = (f32[2,128,128]{2,1,0:T(8,128)S(1)}, f32[2,128,128]{2,1,0:T(8,128)S(1)}, u32[]{:S(2)}, u32[]{:S(2)}) collective-permute-start(f32[2,128,128]{2,1,0:T(8,128)S(1)} %get-tuple-element.77), channel_id=1, source_target_pairs={{0,24},{1,25},{2,26},{3,27},{32,56},{33,57},{34,58},{35,59},{64,88... | collective-permute-start | bytes 393224 | tf_op jit(solution)/shard_map/ppermute | solution.py:18
  25.4 1.3 %collective-permute-start.5 = (f32[2,128,128]{2,1,0:T(8,128)S(1)}, f32[2,128,128]{2,1,0:T(8,128)S(1)}, u32[]{:S(2)}, u32[]{:S(2)}) collective-permute-start(f32[2,128,128]{2,1,0:T(8,128)S(1)} %get-tuple-element.78), channel_id=1, source_target_pairs={{0,16},{1,17},{2,18},{3,19},{32,48},{33,49},{34,50},{35,51},{64,80... | collective-permute-start | bytes 393224 | tf_op jit(solution)/shard_map/ppermute | solution.py:18
  26.8 0.5 collective-permute-done.6
  27.3 2.7 %collective-permute-done.5 = f32[2,128,128]{2,1,0:T(8,128)S(1)} collective-permute-done((f32[2,128,128]{2,1,0:T(8,128)S(1)}, f32[2,128,128]{2,1,0:T(8,128)S(1)}, u32[]{:S(2)}, u32[]{:S(2)}) %collective-permute-start.5) | collective-permute-done | bytes 131104 | tf_op jit(solution)/shard_map/ppermute | solution.py:18
  30.1 3.0 %collective-permute-start.11 = (f32[128,128]{1,0:T(8,128)S(1)}, f32[128,128]{1,0:T(8,128)S(1)}, u32[]{:S(2)}, u32[]{:S(2)}) collective-permute-start(f32[128,128]{1,0:T(8,128)S(1)} %add_add_fusion.2), channel_id=1, source_target_pairs={{0,2},{1,3},{2,0},{3,1},{4,6},{5,7},{6,4},{7,5},{8,10},{9,11},{10,... | collective-permute-start | bytes 196616 | tf_op jit(solution)/shard_map/ppermute | solution.py:18
  33.1 1.3 %collective-permute-start.10 = (f32[2,128,128]{2,1,0:T(8,128)S(1)}, f32[2,128,128]{2,1,0:T(8,128)S(1)}, u32[]{:S(2)}, u32[]{:S(2)}) collective-permute-start(f32[2,128,128]{2,1,0:T(8,128)S(1)} %add_add_fusion.1), channel_id=1, source_target_pairs={{0,7},{1,6},{2,5},{3,4},{8,15},{9,14},{10,13},{11,12},{16,23},{17,... | collective-permute-start | bytes 393224 | tf_op jit(solution)/shard_map/ppermute | solution.py:18
  34.4 2.1 %collective-permute-done.11 = f32[128,128]{1,0:T(8,128)S(1)} collective-permute-done((f32[128,128]{1,0:T(8,128)S(1)}, f32[128,128]{1,0:T(8,128)S(1)}, u32[]{:S(2)}, u32[]{:S(2)}) %collective-permute-start.11) | collective-permute-done | bytes 65568 | tf_op jit(solution)/shard_map/ppermute | solution.py:18
  36.5 1.9 %collective-permute-start.12 = (f32[2,128,128]{2,1,0:T(8,128)S(1)}, f32[2,128,128]{2,1,0:T(8,128)S(1)}, u32[]{:S(2)}, u32[]{:S(2)}) collective-permute-start(f32[2,128,128]{2,1,0:T(8,128)S(1)} %get-tuple-element.82), channel_id=1, source_target_pairs={{0,1},{1,0},{2,3},{3,2},{4,5},{5,4},{6,7},{7,6},{8,9},{9,8},{10,11... | collective-permute-start | bytes 393224 | tf_op jit(solution)/shard_map/ppermute | solution.py:18
  38.5 3.7 %collective-permute-done.12 = f32[2,128,128]{2,1,0:T(8,128)S(1)} collective-permute-done((f32[2,128,128]{2,1,0:T(8,128)S(1)}, f32[2,128,128]{2,1,0:T(8,128)S(1)}, u32[]{:S(2)}, u32[]{:S(2)}) %collective-permute-start.12) | collective-permute-done | bytes 131104 | tf_op jit(solution)/shard_map/ppermute | solution.py:18
  42.2 3.5 %collective-permute-start.14 = (f32[2,2,128,128]{3,2,1,0:T(8,128)S(1)}, f32[2,2,128,128]{3,2,1,0:T(8,128)S(1)}, u32[]{:S(2)}, u32[]{:S(2)}) collective-permute-start(f32[2,2,128,128]{3,2,1,0:T(8,128)S(1)} %pad_maximum_fusion.3), channel_id=1, source_target_pairs={{0,64},{32,96},{64,0},{96,32},{128,192},{160,224},{192,128},{224,1... | collective-permute-start | bytes 786440 | tf_op jit(solution)/shard_map/ppermute | solution.py:22
  45.7 3.0 %collective-permute-start.13 = (f32[2,128,128]{2,1,0:T(8,128)S(1)}, f32[2,128,128]{2,1,0:T(8,128)S(1)}, u32[]{:S(2)}, u32[]{:S(2)}) collective-permute-start(f32[2,128,128]{2,1,0:T(8,128)S(1)} %broadcast_select_fusion), channel_id=1, source_target_pairs={{0,2},{1,3},{2,0},{3,1},{4,6},{5,7},{6,4},{7,5},{8,10},{9,11},{10,... | collective-permute-start | bytes 393224 | tf_op jit(solution)/shard_map/ppermute | solution.py:18
  48.7 4.9 %collective-permute-done.13 = f32[2,128,128]{2,1,0:T(8,128)S(1)} collective-permute-done((f32[2,128,128]{2,1,0:T(8,128)S(1)}, f32[2,128,128]{2,1,0:T(8,128)S(1)}, u32[]{:S(2)}, u32[]{:S(2)}) %collective-permute-start.13) | collective-permute-done | bytes 131104 | tf_op jit(solution)/shard_map/ppermute | solution.py:18
  53.7 0.1 pad_maximum_fusion.1.own_ref
  53.7 5.9 %collective-permute-start.16 = (f32[2,2,2,128,128]{4,3,2,1,0:T(8,128)S(1)}, f32[2,2,2,128,128]{4,3,2,1,0:T(8,128)S(1)}, u32[]{:S(2)}, u32[]{:S(2)}) collective-permute-start(f32[2,2,2,128,128]{4,3,2,1,0:T(8,128)S(1)} %pad_maximum_fusion.1.own_ref), channel_id=1, source_target_pairs={{0,32},{32,0},{64,96},{96,64},{128,160},{160,128},{192,224},{224,1... | collective-permute-start | bytes 1572872 | tf_op jit(solution)/shard_map/ppermute | solution.py:22
  59.6 0.1 concatenate.6.at_ref
  59.8 4.7 %collective-permute-start.23 = (f32[128,640]{1,0:T(8,128)S(1)}, f32[128,640]{1,0:T(8,128)S(1)}, u32[]{:S(2)}, u32[]{:S(2)}) collective-permute-start(f32[128,640]{1,0:T(8,128)S(1)} %maximum_select_fusion), channel_id=1, source_target_pairs={{0,384},{32,416},{64,448},{96,480},{1,385},{33,417},{65,449},{97,4... | collective-permute-start | bytes 983048 | tf_op jit(solution)/shard_map/ppermute | solution.py:22
  64.4 1.3 %collective-permute-start.22 = (f32[128,640]{1,0:T(8,128)S(1)}, f32[128,640]{1,0:T(8,128)S(1)}, u32[]{:S(2)}, u32[]{:S(2)}) collective-permute-start(f32[128,640]{1,0:T(8,128)S(1)} %maximum_select_fusion), channel_id=1, source_target_pairs={{0,256},{32,288},{64,320},{96,352},{1,257},{33,289},{65,321},{97,3... | collective-permute-start | bytes 983048 | tf_op jit(solution)/shard_map/ppermute | solution.py:22
  65.8 1.3 %collective-permute-start.21 = (f32[128,640]{1,0:T(8,128)S(1)}, f32[128,640]{1,0:T(8,128)S(1)}, u32[]{:S(2)}, u32[]{:S(2)}) collective-permute-start(f32[128,640]{1,0:T(8,128)S(1)} %maximum_select_fusion), channel_id=1, source_target_pairs={{0,128},{32,160},{64,192},{96,224},{1,129},{33,161},{65,193},{97,2... | collective-permute-start | bytes 983048 | tf_op jit(solution)/shard_map/ppermute | solution.py:22
  67.1 2.6 %collective-permute-start.15 = (f32[2,2,128,128]{3,2,1,0:T(8,128)S(1)}, f32[2,2,128,128]{3,2,1,0:T(8,128)S(1)}, u32[]{:S(2)}, u32[]{:S(2)}) collective-permute-start(f32[2,2,128,128]{3,2,1,0:T(8,128)S(1)} %get-tuple-element.45), channel_id=1, source_target_pairs={{0,1},{1,0},{2,3},{3,2},{4,5},{5,4},{6,7},{7,6},{8,9},{9,8},{10,11... | collective-permute-start | bytes 786440 | tf_op jit(solution)/shard_map/ppermute | solution.py:18
  69.7 7.0 %shard_map.50 = (f32[512,128]{1,0:T(8,128)S(1)}, f32[128,128]{1,0:T(8,128)S(1)}, f32[384,384]{1,0:T(8,128)S(1)}) custom-call(s32[8]{0:T(128)S(1)} %concatenate.6.at_ref, f32[2,2,2,128,128]{4,3,2,1,0:T(8,128)S(1)} %pad_maximum_fusion.1.own_ref, f32[2,2,2,128,128]{4,3,2,1,0:T(8,128)S(1)} %collective-permute-done.16.got_ref), custom_call_target="tpu_custom_call" | custom-call | flops 6000000000 | bytes 1048576 | tf_op jit(solution)/shard_map/pallas_call | solution.py:164
  76.8 1.9 %collective-permute-start.18 = (f32[2,2,2,128,128]{4,3,2,1,0:T(8,128)S(1)}, f32[2,2,2,128,128]{4,3,2,1,0:T(8,128)S(1)}, u32[]{:S(2)}, u32[]{:S(2)}) collective-permute-start(f32[2,2,2,128,128]{4,3,2,1,0:T(8,128)S(1)} %pad_maximum_fusion.2.q0_ref), channel_id=1, source_target_pairs={{0,24},{1,25},{2,26},{3,27},{4,28},{5,29},{6,30},{7,31},{8,0},{9,1... | collective-permute-start | bytes 1572872 | tf_op jit(solution)/shard_map/ppermute | solution.py:18
  78.8 3.5 %collective-permute-start.17 = (f32[2,2,2,128,128]{4,3,2,1,0:T(8,128)S(1)}, f32[2,2,2,128,128]{4,3,2,1,0:T(8,128)S(1)}, u32[]{:S(2)}, u32[]{:S(2)}) collective-permute-start(f32[2,2,2,128,128]{4,3,2,1,0:T(8,128)S(1)} %pad_maximum_fusion.2.q0_ref), channel_id=1, source_target_pairs={{0,8},{1,9},{2,10},{3,11},{4,12},{5,13},{6,14},{7,15},{8,16},{9,17... | collective-permute-start | bytes 1572872 | tf_op jit(solution)/shard_map/ppermute | solution.py:18
  82.3 6.1 %shard_map.51 = (f32[384,128]{1,0:T(8,128)S(1)}, f32[128,256]{1,0:T(8,128)S(1)}, f32[256,256]{1,0:T(8,128)S(1)}) custom-call(f32[512,128]{1,0:T(8,128)S(1)} %get-tuple-element.48.refs_0_.f0, f32[128,128]{1,0:T(8,128)S(1)} %get-tuple-element.49.refs_1_.refs_2_.refs_3_.g0, f32[384,384]{1,0:T(8,128)S(1)} %get-tuple-element.50.refs_2_), custom_call_target="tpu_custom_call" | custom-call | flops 6000000000 | bytes 1048576 | tf_op jit(solution)/shard_map/pallas_call | solution.py:179
  88.4 5.9 %shard_map.52 = (f32[256,128]{1,0:T(8,128)S(1)}, f32[128,384]{1,0:T(8,128)S(1)}, f32[128,128]{1,0:T(8,128)S(1)}) custom-call(f32[512,128]{1,0:T(8,128)S(1)} %get-tuple-element.48.refs_0_.f0, f32[384,128]{1,0:T(8,128)S(1)} %get-tuple-element.51.refs_1_.f1, f32[128,128]{1,0:T(8,128)S(1)} %get-tuple-element.49.refs_1_.refs_2_.refs_3_.g0, ...), custom_call_target="tpu_custom_call" | custom-call | flops 6000000000 | bytes 1048576 | tf_op jit(solution)/shard_map/pallas_call | solution.py:179
  94.4 0.1 add_add_fusion
  94.5 4.2 %collective-permute-start.19 = (f32[2,2,128,128]{3,2,1,0:T(8,128)S(1)}, f32[2,2,128,128]{3,2,1,0:T(8,128)S(1)}, u32[]{:S(2)}, u32[]{:S(2)}) collective-permute-start(f32[2,2,128,128]{3,2,1,0:T(8,128)S(1)} %slice_bitcast_fusion.1), channel_id=1, source_target_pairs={{0,24},{1,25},{2,26},{3,27},{4,28},{5,29},{6,30},{7,31},{8,0},{9,1... | collective-permute-start | bytes 786440 | tf_op jit(solution)/shard_map/ppermute | solution.py:18
  98.8 1.9 %collective-permute-start.20 = (f32[2,2,128,128]{3,2,1,0:T(8,128)S(1)}, f32[2,2,128,128]{3,2,1,0:T(8,128)S(1)}, u32[]{:S(2)}, u32[]{:S(2)}) collective-permute-start(f32[2,2,128,128]{3,2,1,0:T(8,128)S(1)} %slice_bitcast_fusion), channel_id=1, source_target_pairs={{0,8},{1,9},{2,10},{3,11},{4,12},{5,13},{6,14},{7,15},{8,16},{9,17... | collective-permute-start | bytes 786440 | tf_op jit(solution)/shard_map/ppermute | solution.py:18
  100.7 3.9 %collective-permute-start.24 = (f32[128,640]{1,0:T(8,128)S(1)}, f32[128,640]{1,0:T(8,128)S(1)}, u32[]{:S(2)}, u32[]{:S(2)}) collective-permute-start(f32[128,640]{1,0:T(8,128)S(1)} %add_add_fusion), channel_id=1, source_target_pairs={{0,64},{32,96},{64,0},{96,32},{128,192},{160,224},{192,128},{224,1... | collective-permute-start | bytes 983048 | tf_op jit(solution)/shard_map/ppermute | solution.py:22
  104.6 5.5 %shard_map.53 = (f32[128,128]{1,0:T(8,128)S(1)}, f32[128,512]{1,0:T(8,128)S(1)}) custom-call(f32[512,128]{1,0:T(8,128)S(1)} %get-tuple-element.48.refs_0_.f0, f32[384,128]{1,0:T(8,128)S(1)} %get-tuple-element.51.refs_1_.f1, f32[256,128]{1,0:T(8,128)S(1)} %get-tuple-element.57.refs_2_.f2, f32[128,128]{1,0:T(8,128)S(1)} %get-tuple-element.49.refs_1_.refs_2_.refs_3_.g0, ...), custom_call_target="tpu_custom_call" | custom-call | flops 6000000000 | bytes 1048576 | tf_op jit(solution)/shard_map/pallas_call | solution.py:179
  110.1 0.8 collective-permute-done.24
  111.0 4.0 %collective-permute-start.25 = (f32[2,128,640]{2,1,0:T(8,128)S(1)}, f32[2,128,640]{2,1,0:T(8,128)S(1)}, u32[]{:S(2)}, u32[]{:S(2)}) collective-permute-start(f32[2,128,640]{2,1,0:T(8,128)S(1)} %pad_maximum_fusion.own_ref), channel_id=1, source_target_pairs={{0,32},{32,0},{64,96},{96,64},{128,160},{160,128},{192,224},{224,1... | collective-permute-start | bytes 1966088 | tf_op jit(solution)/shard_map/ppermute | solution.py:22
  115.0 0.3 shard_map.54
  115.3 1.4 %collective-permute-done.25.got_ref = f32[2,128,640]{2,1,0:T(8,128)S(1)} collective-permute-done((f32[2,128,640]{2,1,0:T(8,128)S(1)}, f32[2,128,640]{2,1,0:T(8,128)S(1)}, u32[]{:S(2)}, u32[]{:S(2)}) %collective-permute-start.25) | collective-permute-done | bytes 655392 | tf_op jit(solution)/shard_map/ppermute | solution.py:22
  116.7 2.4 %shard_map.55 = (bf16[512,640]{1,0:T(8,128)(2,1)S(1)}, bf16[512,640]{1,0:T(8,128)(2,1)S(1)}, f32[512,128]{1,0:T(8,128)S(1)}) custom-call(s32[8]{0:T(128)S(1)} %concatenate.6.at_ref, f32[2,128,640]{2,1,0:T(8,128)S(1)} %pad_maximum_fusion.own_ref, f32[2,128,640]{2,1,0:T(8,128)S(1)} %collective-permute-done.25.got_ref, ...), custom_call_target="tpu_custom_call" | custom-call | flops 4000000000 | bytes 4194304 | tf_op jit(solution)/shard_map/pallas_call | solution.py:245
  119.1 10.1 %shard_map.56 = (f32[1024,512]{1,0:T(8,128)}, f32[1024,128]{1,0:T(8,128)}) custom-call(s32[8]{0:T(128)S(1)} %concatenate.6.at_ref, f32[2,2,2,128,128]{4,3,2,1,0:T(8,128)S(1)} %pad_maximum_fusion.2.q0_ref, f32[2,2,2,128,128]{4,3,2,1,0:T(8,128)S(1)} %collective-permute-done.17.q1_ref, f32[2,2,2,128,128]{4,3,2,1,0:T(8,128)S(1)} %collective-permute-done.18.q2_ref, ...), custom_call_target="tpu_custom_call" | custom-call | flops 10000000000 | bytes 6291456 | tf_op jit(solution)/shard_map/pallas_call | solution.py:315
  (41 shorter events, 0.4 us)
Async XLA Ops:
  1.5 8.1 %collective-permute-start.1 = (f32[128,128]{1,0:T(8,128)S(1)}, f32[128,128]{1,0:T(8,128)S(1)}, u32[]{:S(2)}, u32[]{:S(2)}) collective-permute-start(f32[128,128]{1,0:T(8,128)S(1)} %slice_select_fusion), channel_id=1, source_target_pairs={{0,16},{1,17},{2,18},{3,19},{32,48},{33,49},{34,50},{35,51},{64,80... | collective-permute-start | bytes 196616 | tf_op jit(solution)/shard_map/ppermute | solution.py:355
  7.0 2.6 %collective-permute-start.2 = (f32[128,128]{1,0:T(8,128)S(1)}, f32[128,128]{1,0:T(8,128)S(1)}, u32[]{:S(2)}, u32[]{:S(2)}) collective-permute-start(f32[128,128]{1,0:T(8,128)S(1)} %slice_select_fusion), channel_id=1, source_target_pairs={{0,24},{1,25},{2,26},{3,27},{32,56},{33,57},{34,58},{35,59},{64,88... | collective-permute-start | bytes 196616 | tf_op jit(solution)/shard_map/ppermute | solution.py:355
  8.3 2.9 %collective-permute-start = (f32[128,128]{1,0:T(8,128)S(1)}, f32[128,128]{1,0:T(8,128)S(1)}, u32[]{:S(2)}, u32[]{:S(2)}) collective-permute-start(f32[128,128]{1,0:T(8,128)S(1)} %slice_select_fusion), channel_id=1, source_target_pairs={{0,8},{1,9},{2,10},{3,11},{32,40},{33,41},{34,42},{35,43},{64,72},... | collective-permute-start | bytes 196616 | tf_op jit(solution)/shard_map/ppermute | solution.py:355
  12.0 2.6 %collective-permute-start.3 = (f32[128,128]{1,0:T(8,128)S(1)}, f32[128,128]{1,0:T(8,128)S(1)}, u32[]{:S(2)}, u32[]{:S(2)}) collective-permute-start(f32[128,128]{1,0:T(8,128)S(1)} %add_add_fusion.3), channel_id=1, source_target_pairs={{0,7},{1,6},{2,5},{3,4},{8,15},{9,14},{10,13},{11,12},{16,23},{17,... | collective-permute-start | bytes 196616 | tf_op jit(solution)/shard_map/ppermute | solution.py:359
  14.7 10.7 %collective-permute-start.9 = (f32[128,128]{1,0:T(8,128)S(1)}, f32[128,128]{1,0:T(8,128)S(1)}, u32[]{:S(2)}, u32[]{:S(2)}) collective-permute-start(f32[128,128]{1,0:T(8,128)S(1)} %add.67), channel_id=1, source_target_pairs={{0,384},{32,416},{64,448},{96,480},{1,385},{33,417},{65,449},{97,4... | collective-permute-start | bytes 196616 | tf_op jit(solution)/shard_map/ppermute | solution.py:22
  17.7 9.0 %collective-permute-start.8 = (f32[128,128]{1,0:T(8,128)S(1)}, f32[128,128]{1,0:T(8,128)S(1)}, u32[]{:S(2)}, u32[]{:S(2)}) collective-permute-start(f32[128,128]{1,0:T(8,128)S(1)} %add.67), channel_id=1, source_target_pairs={{0,256},{32,288},{64,320},{96,352},{1,257},{33,289},{65,321},{97,3... | collective-permute-start | bytes 196616 | tf_op jit(solution)/shard_map/ppermute | solution.py:22
  19.0 7.7 %collective-permute-start.7 = (f32[128,128]{1,0:T(8,128)S(1)}, f32[128,128]{1,0:T(8,128)S(1)}, u32[]{:S(2)}, u32[]{:S(2)}) collective-permute-start(f32[128,128]{1,0:T(8,128)S(1)} %add.67), channel_id=1, source_target_pairs={{0,128},{32,160},{64,192},{96,224},{1,129},{33,161},{65,193},{97,2... | collective-permute-start | bytes 196616 | tf_op jit(solution)/shard_map/ppermute | solution.py:22
  20.3 6.5 %collective-permute-start.4 = (f32[2,128,128]{2,1,0:T(8,128)S(1)}, f32[2,128,128]{2,1,0:T(8,128)S(1)}, u32[]{:S(2)}, u32[]{:S(2)}) collective-permute-start(f32[2,128,128]{2,1,0:T(8,128)S(1)} %get-tuple-element.76), channel_id=1, source_target_pairs={{0,8},{1,9},{2,10},{3,11},{32,40},{33,41},{34,42},{35,43},{64,72},... | collective-permute-start | bytes 393224 | tf_op jit(solution)/shard_map/ppermute | solution.py:18
  23.5 3.9 %collective-permute-start.6 = (f32[2,128,128]{2,1,0:T(8,128)S(1)}, f32[2,128,128]{2,1,0:T(8,128)S(1)}, u32[]{:S(2)}, u32[]{:S(2)}) collective-permute-start(f32[2,128,128]{2,1,0:T(8,128)S(1)} %get-tuple-element.77), channel_id=1, source_target_pairs={{0,24},{1,25},{2,26},{3,27},{32,56},{33,57},{34,58},{35,59},{64,88... | collective-permute-start | bytes 393224 | tf_op jit(solution)/shard_map/ppermute | solution.py:18
  25.4 4.6 %collective-permute-start.5 = (f32[2,128,128]{2,1,0:T(8,128)S(1)}, f32[2,128,128]{2,1,0:T(8,128)S(1)}, u32[]{:S(2)}, u32[]{:S(2)}) collective-permute-start(f32[2,128,128]{2,1,0:T(8,128)S(1)} %get-tuple-element.78), channel_id=1, source_target_pairs={{0,16},{1,17},{2,18},{3,19},{32,48},{33,49},{34,50},{35,51},{64,80... | collective-permute-start | bytes 393224 | tf_op jit(solution)/shard_map/ppermute | solution.py:18
  26.8 32.8 %copy-start.2 = (s32[4]{0:T(128)S(1)}, s32[4]{0:T(128)}, u32[]{:S(2)}) copy-start(s32[4]{0:T(128)} %constant.58.clone) | copy-start | bytes 52
  30.1 29.7 %slice-start = ((f32[1024,512]{1,0:T(8,128)}), f32[128,512]{1,0:T(8,128)S(1)}, s32[]{:S(2)}) async-start(f32[1024,512]{1,0:T(8,128)} %k_ref.1), calls=%async_computation | async-start | bytes 524288 | tf_op jit(solution)/shard_map/slice | solution.py:380
  30.1 29.7 %slice-start.1 = ((f32[1024,128]{1,0:T(8,128)}), f32[128,128]{1,0:T(8,128)S(1)}, s32[]{:S(2)}) async-start(f32[1024,128]{1,0:T(8,128)} %y_ref.1), calls=%async_computation.1 | async-start | bytes 131072 | tf_op jit(solution)/shard_map/slice | solution.py:380
  30.1 6.4 %collective-permute-start.11 = (f32[128,128]{1,0:T(8,128)S(1)}, f32[128,128]{1,0:T(8,128)S(1)}, u32[]{:S(2)}, u32[]{:S(2)}) collective-permute-start(f32[128,128]{1,0:T(8,128)S(1)} %add_add_fusion.2), channel_id=1, source_target_pairs={{0,2},{1,3},{2,0},{3,1},{4,6},{5,7},{6,4},{7,5},{8,10},{9,11},{10,... | collective-permute-start | bytes 196616 | tf_op jit(solution)/shard_map/ppermute | solution.py:18
  33.1 5.4 %collective-permute-start.10 = (f32[2,128,128]{2,1,0:T(8,128)S(1)}, f32[2,128,128]{2,1,0:T(8,128)S(1)}, u32[]{:S(2)}, u32[]{:S(2)}) collective-permute-start(f32[2,128,128]{2,1,0:T(8,128)S(1)} %add_add_fusion.1), channel_id=1, source_target_pairs={{0,7},{1,6},{2,5},{3,4},{8,15},{9,14},{10,13},{11,12},{16,23},{17,... | collective-permute-start | bytes 393224 | tf_op jit(solution)/shard_map/ppermute | solution.py:18
  36.5 5.7 %collective-permute-start.12 = (f32[2,128,128]{2,1,0:T(8,128)S(1)}, f32[2,128,128]{2,1,0:T(8,128)S(1)}, u32[]{:S(2)}, u32[]{:S(2)}) collective-permute-start(f32[2,128,128]{2,1,0:T(8,128)S(1)} %get-tuple-element.82), channel_id=1, source_target_pairs={{0,1},{1,0},{2,3},{3,2},{4,5},{5,4},{6,7},{7,6},{8,9},{9,8},{10,11... | collective-permute-start | bytes 393224 | tf_op jit(solution)/shard_map/ppermute | solution.py:18
  42.2 11.4 %collective-permute-start.14 = (f32[2,2,128,128]{3,2,1,0:T(8,128)S(1)}, f32[2,2,128,128]{3,2,1,0:T(8,128)S(1)}, u32[]{:S(2)}, u32[]{:S(2)}) collective-permute-start(f32[2,2,128,128]{3,2,1,0:T(8,128)S(1)} %pad_maximum_fusion.3), channel_id=1, source_target_pairs={{0,64},{32,96},{64,0},{96,32},{128,192},{160,224},{192,128},{224,1... | collective-permute-start | bytes 786440 | tf_op jit(solution)/shard_map/ppermute | solution.py:22
  45.7 7.9 %collective-permute-start.13 = (f32[2,128,128]{2,1,0:T(8,128)S(1)}, f32[2,128,128]{2,1,0:T(8,128)S(1)}, u32[]{:S(2)}, u32[]{:S(2)}) collective-permute-start(f32[2,128,128]{2,1,0:T(8,128)S(1)} %broadcast_select_fusion), channel_id=1, source_target_pairs={{0,2},{1,3},{2,0},{3,1},{4,6},{5,7},{6,4},{7,5},{8,10},{9,11},{10,... | collective-permute-start | bytes 393224 | tf_op jit(solution)/shard_map/ppermute | solution.py:18
  53.7 16.0 %collective-permute-start.16 = (f32[2,2,2,128,128]{4,3,2,1,0:T(8,128)S(1)}, f32[2,2,2,128,128]{4,3,2,1,0:T(8,128)S(1)}, u32[]{:S(2)}, u32[]{:S(2)}) collective-permute-start(f32[2,2,2,128,128]{4,3,2,1,0:T(8,128)S(1)} %pad_maximum_fusion.1.own_ref), channel_id=1, source_target_pairs={{0,32},{32,0},{64,96},{96,64},{128,160},{160,128},{192,224},{224,1... | collective-permute-start | bytes 1572872 | tf_op jit(solution)/shard_map/ppermute | solution.py:22
  59.8 34.6 %collective-permute-start.23 = (f32[128,640]{1,0:T(8,128)S(1)}, f32[128,640]{1,0:T(8,128)S(1)}, u32[]{:S(2)}, u32[]{:S(2)}) collective-permute-start(f32[128,640]{1,0:T(8,128)S(1)} %maximum_select_fusion), channel_id=1, source_target_pairs={{0,384},{32,416},{64,448},{96,480},{1,385},{33,417},{65,449},{97,4... | collective-permute-start | bytes 983048 | tf_op jit(solution)/shard_map/ppermute | solution.py:22
  64.4 29.9 %collective-permute-start.22 = (f32[128,640]{1,0:T(8,128)S(1)}, f32[128,640]{1,0:T(8,128)S(1)}, u32[]{:S(2)}, u32[]{:S(2)}) collective-permute-start(f32[128,640]{1,0:T(8,128)S(1)} %maximum_select_fusion), channel_id=1, source_target_pairs={{0,256},{32,288},{64,320},{96,352},{1,257},{33,289},{65,321},{97,3... | collective-permute-start | bytes 983048 | tf_op jit(solution)/shard_map/ppermute | solution.py:22
  65.8 28.6 %collective-permute-start.21 = (f32[128,640]{1,0:T(8,128)S(1)}, f32[128,640]{1,0:T(8,128)S(1)}, u32[]{:S(2)}, u32[]{:S(2)}) collective-permute-start(f32[128,640]{1,0:T(8,128)S(1)} %maximum_select_fusion), channel_id=1, source_target_pairs={{0,128},{32,160},{64,192},{96,224},{1,129},{33,161},{65,193},{97,2... | collective-permute-start | bytes 983048 | tf_op jit(solution)/shard_map/ppermute | solution.py:22
  67.1 9.7 %collective-permute-start.15 = (f32[2,2,128,128]{3,2,1,0:T(8,128)S(1)}, f32[2,2,128,128]{3,2,1,0:T(8,128)S(1)}, u32[]{:S(2)}, u32[]{:S(2)}) collective-permute-start(f32[2,2,128,128]{3,2,1,0:T(8,128)S(1)} %get-tuple-element.45), channel_id=1, source_target_pairs={{0,1},{1,0},{2,3},{3,2},{4,5},{5,4},{6,7},{7,6},{8,9},{9,8},{10,11... | collective-permute-start | bytes 786440 | tf_op jit(solution)/shard_map/ppermute | solution.py:18
  76.8 17.7 %collective-permute-start.18 = (f32[2,2,2,128,128]{4,3,2,1,0:T(8,128)S(1)}, f32[2,2,2,128,128]{4,3,2,1,0:T(8,128)S(1)}, u32[]{:S(2)}, u32[]{:S(2)}) collective-permute-start(f32[2,2,2,128,128]{4,3,2,1,0:T(8,128)S(1)} %pad_maximum_fusion.2.q0_ref), channel_id=1, source_target_pairs={{0,24},{1,25},{2,26},{3,27},{4,28},{5,29},{6,30},{7,31},{8,0},{9,1... | collective-permute-start | bytes 1572872 | tf_op jit(solution)/shard_map/ppermute | solution.py:18
  78.8 20.0 %collective-permute-start.17 = (f32[2,2,2,128,128]{4,3,2,1,0:T(8,128)S(1)}, f32[2,2,2,128,128]{4,3,2,1,0:T(8,128)S(1)}, u32[]{:S(2)}, u32[]{:S(2)}) collective-permute-start(f32[2,2,2,128,128]{4,3,2,1,0:T(8,128)S(1)} %pad_maximum_fusion.2.q0_ref), channel_id=1, source_target_pairs={{0,8},{1,9},{2,10},{3,11},{4,12},{5,13},{6,14},{7,15},{8,16},{9,17... | collective-permute-start | bytes 1572872 | tf_op jit(solution)/shard_map/ppermute | solution.py:18
  94.5 16.5 %collective-permute-start.19 = (f32[2,2,128,128]{3,2,1,0:T(8,128)S(1)}, f32[2,2,128,128]{3,2,1,0:T(8,128)S(1)}, u32[]{:S(2)}, u32[]{:S(2)}) collective-permute-start(f32[2,2,128,128]{3,2,1,0:T(8,128)S(1)} %slice_bitcast_fusion.1), channel_id=1, source_target_pairs={{0,24},{1,25},{2,26},{3,27},{4,28},{5,29},{6,30},{7,31},{8,0},{9,1... | collective-permute-start | bytes 786440 | tf_op jit(solution)/shard_map/ppermute | solution.py:18
  98.8 12.2 %collective-permute-start.20 = (f32[2,2,128,128]{3,2,1,0:T(8,128)S(1)}, f32[2,2,128,128]{3,2,1,0:T(8,128)S(1)}, u32[]{:S(2)}, u32[]{:S(2)}) collective-permute-start(f32[2,2,128,128]{3,2,1,0:T(8,128)S(1)} %slice_bitcast_fusion), channel_id=1, source_target_pairs={{0,8},{1,9},{2,10},{3,11},{4,12},{5,13},{6,14},{7,15},{8,16},{9,17... | collective-permute-start | bytes 786440 | tf_op jit(solution)/shard_map/ppermute | solution.py:18
  100.7 10.2 %collective-permute-start.24 = (f32[128,640]{1,0:T(8,128)S(1)}, f32[128,640]{1,0:T(8,128)S(1)}, u32[]{:S(2)}, u32[]{:S(2)}) collective-permute-start(f32[128,640]{1,0:T(8,128)S(1)} %add_add_fusion), channel_id=1, source_target_pairs={{0,64},{32,96},{64,0},{96,32},{128,192},{160,224},{192,128},{224,1... | collective-permute-start | bytes 983048 | tf_op jit(solution)/shard_map/ppermute | solution.py:22
  111.0 5.7 %collective-permute-start.25 = (f32[2,128,640]{2,1,0:T(8,128)S(1)}, f32[2,128,640]{2,1,0:T(8,128)S(1)}, u32[]{:S(2)}, u32[]{:S(2)}) collective-permute-start(f32[2,128,640]{2,1,0:T(8,128)S(1)} %pad_maximum_fusion.own_ref), channel_id=1, source_target_pairs={{0,32},{32,0},{64,96},{96,64},{128,160},{160,128},{192,224},{224,1... | collective-permute-start | bytes 1966088 | tf_op jit(solution)/shard_map/ppermute | solution.py:22
  116.7 2.4 %copy-start = (f32[1024,512]{1,0:T(8,128)S(1)}, f32[1024,512]{1,0:T(8,128)}, u32[]{:S(2)}) copy-start(f32[1024,512]{1,0:T(8,128)} %k_ref.1) | copy-start | bytes 6291460
  116.7 2.4 %copy-start.1 = (f32[1024,128]{1,0:T(8,128)S(1)}, f32[1024,128]{1,0:T(8,128)}, u32[]{:S(2)}) copy-start(f32[1024,128]{1,0:T(8,128)} %y_ref.1) | copy-start | bytes 1572868
